TPU v7x, 32 devices: a whole 2x2x4 slice. The times are simulated.
32 devices in a mesh: dp: 4 (over z), seq: 8 (over y, x, core).
Axes of the slice: x: 2, y: 2, z: 4, core: 2. Of those that a mesh axis runs over, the one named last changes fastest.
Arguments:
- byte_ids: int32 [32, 2048], P('dp', 'seq'), may hold values from 1 to 258
- lengths: int32 [32], P('dp'), may hold values from 256 to 2048, as said below
- byte_table: bfloat16 [259, 768], replicated, may hold values from -6 to 6
- conv_kernel: float32 [5, 768], replicated, may hold values from -3 to 3
- score_vector: float32 [768], replicated, may hold values from -0.3 to 0.3
- norm_gain_one: float32 [768], replicated, may hold values from 0.5 to 1.5
- qkv_weight: bfloat16 [768, 2304], replicated, may hold values from -0.109375 to 0.109375
- bias_table: float32 [32, 12], replicated, may hold values from -4 to 4
- out_weight: bfloat16 [768, 768], replicated, may hold values from -2 to 2
- norm_gain_two: float32 [768], replicated, may hold values from 0.5 to 1.5
- in_weight: bfloat16 [768, 4096], replicated, may hold values from -0.21875 to 0.21875
- down_weight: bfloat16 [2048, 768], replicated, may hold values from -0.125 to 0.125
- cotangent: bfloat16 [32, 1024, 768], P('dp', 'seq'), may hold values from -6 to 6
Outputs:
- layer_out: float32 [32, 1024, 768], P('dp', 'seq')
- grad_byte_table: float32 [259, 768], replicated
- grad_conv_kernel: float32 [5, 768], replicated
- grad_score_vector: float32 [768], replicated
- grad_gain_one: float32 [768], replicated
- grad_qkv_weight: float32 [768, 2304], P('seq', 'dp')
- grad_bias_table: float32 [32, 12], replicated
- grad_out_weight: float32 [768, 768], P('seq', 'dp')
- grad_gain_two: float32 [768], replicated
- grad_in_weight: float32 [768, 4096], P('seq', 'dp')
- grad_down_weight: float32 [2048, 768], P('seq', 'dp')
Inputs may be any that keep to these rules, and one draw needn't show every extreme that they name: `lengths`: each sequence holds 2048 bytes or from 256 to 1024 bytes; among sequences k * 8 to k * 8 + 7 one or more hold 2048.
All inputs are finite; a program needn't handle non-finite values.
Results may differ from a plain program's by a relative error of at most 0.02.
Values may be sent and summed in bfloat16 or wider, within the bound.
A program may use at most 320 MiB of HBM per device.

v0:
```python
import jax
import jax.numpy as jnp
from jax import lax
from jax.sharding import PartitionSpec as P

highest = lax.Precision.HIGHEST
thresholds = (12, 16, 23, 32, 46, 64, 91)


def extended_2(block, sides, width):
    for axis, dim in sides:
        count = lax.axis_size(axis)
        forward = [(i, i + 1) for i in range(count - 1)]
        backward = [(target, source) for source, target in forward]
        low = lax.ppermute(
            lax.slice_in_dim(block, block.shape[dim] - width, None, axis=dim), axis, forward
        )
        high = lax.ppermute(lax.slice_in_dim(block, 0, width, axis=dim), axis, backward)
        block = jnp.concatenate([low, block, high], axis=dim)
    return block


def rel_bucket(relative):
    distance = jnp.abs(relative)
    larger = 8 + sum(((distance >= boundary).astype(jnp.int32) for boundary in thresholds))
    bucket = jnp.where(distance < 8, distance, larger)
    return bucket + 16 * (relative > 0).astype(jnp.int32)


def rms_scale(values, gain_row):
    return values * lax.rsqrt(jnp.mean(values * values, axis=-1, keepdims=True) + 1e-06) * gain_row


def block_pool(extended, kernel, score_vector, first_byte, total_bytes):
    local = extended.shape[1] - 8
    reach_span = local + 4
    convolved = sum(
        (
            kernel[offset] * extended[:, offset : offset + reach_span]
            for offset in range(kernel.shape[0])
        )
    )
    conv_position = first_byte - 2 + jnp.arange(reach_span, dtype=jnp.int32)
    inside = (conv_position >= 0) & (conv_position < total_bytes)
    convolved = jnp.where(inside[None, :, None], convolved, 0.0)
    padded_conv = jnp.pad(convolved, ((0, 0), (1, 1), (0, 0)))
    global_position = first_byte + jnp.arange(local, dtype=jnp.int32)
    pooled_list = []
    for block_size in range(1, 5):
        phase = global_position % block_size
        pooled_one = (
            sum(
                (
                    jnp.where(
                        (phase == lead)[None, :, None],
                        sum(
                            (
                                padded_conv[:, 3 - lead + member : 3 - lead + member + local]
                                for member in range(block_size)
                            )
                        ),
                        0.0,
                    )
                    for lead in range(block_size)
                )
            )
            / block_size
        )
        pooled_list.append(pooled_one)
    pooled = jnp.stack(pooled_list)
    scores = jnp.einsum("kbld,d->kbl", pooled, score_vector, precision=highest)
    weights = jax.nn.softmax(scores, axis=0)
    mixture = jnp.sum(weights[..., None] * pooled, axis=0)
    return jnp.mean(mixture.reshape(mixture.shape[0], local // 2, 2, mixture.shape[2]), axis=2)


def block_logits(query_block, key_block, bias_column, delta, key_first, valid_tokens, breadth):
    logits = jnp.dot(query_block, key_block.T, preferred_element_type=jnp.float32)
    steps_here = jnp.arange(breadth, dtype=jnp.int32)
    buckets = rel_bucket(delta + steps_here[None, :] - steps_here[:, None])
    table_hit = (
        buckets[:, :, None] == jnp.arange(bias_column.shape[0], dtype=jnp.int32)[None, None, :]
    )
    logits = logits + jnp.sum(jnp.where(table_hit, bias_column[None, None, :], 0.0), axis=2)
    key_position = key_first + steps_here
    return (jnp.where((key_position < valid_tokens)[None, :], logits, -1000000000.0), table_hit)


def attend_item(query_all, key_all, value_all, bias_column, valid_tokens):
    tokens, depth = query_all.shape
    breadth = min(512, tokens)
    key_blocks = (valid_tokens + breadth - 1) // breadth

    def attend_query_step(first_query):
        query_block = lax.dynamic_slice_in_dim(query_all, first_query, breadth, 0)

        def max_step(block_number, carried):
            running_max, running_sum = carried
            key_first = block_number * breadth
            key_block = lax.dynamic_slice_in_dim(key_all, key_first, breadth, 0)
            logits = block_logits(
                query_block,
                key_block,
                bias_column,
                key_first - first_query,
                key_first,
                valid_tokens,
                breadth,
            )[0]
            new_max = jnp.maximum(running_max, jnp.max(logits, axis=1))
            running_sum = running_sum * jnp.exp(running_max - new_max) + jnp.sum(
                jnp.exp(logits - new_max[:, None]), axis=1
            )
            return (new_max, running_sum)

        start_max = jnp.full((breadth,), -1e30, jnp.float32)
        final_max, final_sum = lax.fori_loop(
            0, key_blocks, max_step, (start_max, jnp.zeros((breadth,), jnp.float32))
        )
        log_total = final_max + jnp.log(final_sum)

        def value_step(block_number, accumulated):
            key_first = block_number * breadth
            key_block = lax.dynamic_slice_in_dim(key_all, key_first, breadth, 0)
            value_block = lax.dynamic_slice_in_dim(value_all, key_first, breadth, 0)
            logits = block_logits(
                query_block,
                key_block,
                bias_column,
                key_first - first_query,
                key_first,
                valid_tokens,
                breadth,
            )[0]
            probabilities = jnp.exp(logits - log_total[:, None]).astype(jnp.bfloat16)
            return accumulated + jnp.dot(
                probabilities, value_block, preferred_element_type=jnp.float32
            )

        output = lax.fori_loop(0, key_blocks, value_step, jnp.zeros((breadth, depth), jnp.float32))
        return (output, log_total)

    firsts = jnp.arange(tokens // breadth, dtype=jnp.int32) * breadth
    outputs, log_totals = lax.map(attend_query_step, firsts)
    return (outputs.reshape(tokens, depth), log_totals.reshape(tokens))


def attend_item_back(
    query_all, key_all, value_all, output_all, log_total, grad_out, bias_column, valid_tokens
):
    tokens, depth = query_all.shape
    breadth = min(512, tokens)
    key_blocks = (valid_tokens + breadth - 1) // breadth
    correction = jnp.sum(grad_out.astype(jnp.float32) * output_all, axis=1)
    query_count = tokens // breadth

    def key_step(block_number, carried):
        grad_query, grad_key, grad_value, grad_bias = carried
        key_first = block_number * breadth
        key_block = lax.dynamic_slice_in_dim(key_all, key_first, breadth, 0)
        value_block = lax.dynamic_slice_in_dim(value_all, key_first, breadth, 0)

        def key_query_step(inner, query_number):
            grad_query, key_accum, value_accum, grad_bias = inner
            first_query = query_number * breadth
            query_block = lax.dynamic_slice_in_dim(query_all, first_query, breadth, 0)
            grad_block = lax.dynamic_slice_in_dim(grad_out, first_query, breadth, 0)
            total_block = lax.dynamic_slice_in_dim(log_total, first_query, breadth, 0)
            shift_block = lax.dynamic_slice_in_dim(correction, first_query, breadth, 0)
            logits, table_hit = block_logits(
                query_block,
                key_block,
                bias_column,
                key_first - first_query,
                key_first,
                valid_tokens,
                breadth,
            )
            probabilities = jnp.exp(logits - total_block[:, None])
            probs_low = probabilities.astype(jnp.bfloat16)
            grad_probs = jnp.dot(grad_block, value_block.T, preferred_element_type=jnp.float32)
            grad_logits = (probabilities * (grad_probs - shift_block[:, None])).astype(jnp.bfloat16)
            query_piece = lax.dynamic_slice_in_dim(grad_query, first_query, breadth, 0)
            query_piece = query_piece + jnp.dot(
                grad_logits, key_block, preferred_element_type=jnp.float32
            )
            grad_query = lax.dynamic_update_slice_in_dim(grad_query, query_piece, first_query, 0)
            key_accum = key_accum + jnp.dot(
                grad_logits.T, query_block, preferred_element_type=jnp.float32
            )
            value_accum = value_accum + jnp.dot(
                probs_low.T, grad_block, preferred_element_type=jnp.float32
            )
            grad_bias = grad_bias + jnp.sum(
                jnp.where(table_hit, grad_logits.astype(jnp.float32)[:, :, None], 0.0), axis=(0, 1)
            )
            return ((grad_query, key_accum, value_accum, grad_bias), None)

        zero_block = jnp.zeros((breadth, depth), jnp.float32)
        finished, unused = lax.scan(
            key_query_step,
            (grad_query, zero_block, zero_block, grad_bias),
            jnp.arange(query_count, dtype=jnp.int32),
        )
        grad_query, key_accum, value_accum, grad_bias = finished
        grad_key = lax.dynamic_update_slice_in_dim(grad_key, key_accum, key_first, 0)
        grad_value = lax.dynamic_update_slice_in_dim(grad_value, value_accum, key_first, 0)
        return (grad_query, grad_key, grad_value, grad_bias)

    zero_all = jnp.zeros((tokens, depth), jnp.float32)
    return lax.fori_loop(
        0,
        key_blocks,
        key_step,
        (zero_all, zero_all, zero_all, jnp.zeros((bias_column.shape[0],), jnp.float32)),
    )


def to_items(token_rows):
    sequences, steps_local, heads_count, inner = token_rows.shape
    arranged = jnp.transpose(token_rows, (0, 2, 1, 3))
    return arranged.reshape(sequences * heads_count, steps_local * inner)


def from_items(item_rows, sequences, heads_count, inner):
    steps_local = item_rows.shape[1] // inner
    arranged = jnp.transpose(
        item_rows.reshape(sequences, heads_count, steps_local, inner), (0, 2, 1, 3)
    )
    return arranged.reshape(sequences, steps_local, heads_count * inner)


def body(
    byte_ids,
    lengths,
    byte_table,
    conv_kernel,
    score_vector,
    norm_gain_one,
    qkv_weight,
    bias_table,
    out_weight,
    norm_gain_two,
    in_weight,
    down_weight,
    cotangent,
):
    sequences, local_bytes = byte_ids.shape
    total_bytes = local_bytes * lax.axis_size("seq")
    first_byte = lax.axis_index("seq") * local_bytes
    model_width = byte_table.shape[1]
    vocab_rows = byte_table.shape[0]
    padded_rows = -(-vocab_rows // 128) * 128
    table_padded = jnp.concatenate(
        [byte_table, jnp.zeros((padded_rows - vocab_rows, model_width), jnp.bfloat16)], axis=0
    )
    positions = first_byte + jnp.arange(local_bytes, dtype=jnp.int32)
    picked = jnp.where(positions[None, :] < lengths[:, None], byte_ids, 0)
    one_hot = (
        picked.reshape(-1)[:, None] == jnp.arange(padded_rows, dtype=jnp.int32)[None, :]
    ).astype(jnp.bfloat16)
    embedded = jnp.dot(one_hot, table_padded, preferred_element_type=jnp.float32).astype(
        jnp.bfloat16
    )
    embedded = embedded.reshape(sequences, local_bytes, model_width)
    extended = extended_2(embedded, (("seq", 1),), 4)

    def pool_local(extended_rows, kernel, vector):
        return block_pool(extended_rows, kernel, vector, first_byte, total_bytes)

    hidden_in, pool_back = jax.vjp(
        pool_local, extended.astype(jnp.float32), conv_kernel, score_vector
    )
    normed, norm_back_one = jax.vjp(rms_scale, hidden_in, norm_gain_one)
    normed_low = normed.astype(jnp.bfloat16)
    projected = jnp.dot(normed_low, qkv_weight, preferred_element_type=jnp.float32).astype(
        jnp.bfloat16
    )
    steps_local = projected.shape[1]
    heads_count = bias_table.shape[1]
    depth = model_width // heads_count
    sent = to_items(projected.reshape(sequences, steps_local, heads_count, 3 * depth))
    received = lax.all_to_all(sent, "seq", split_axis=0, concat_axis=1, tiled=True)
    item_count = received.shape[0]
    tokens = received.shape[1] // (3 * depth)
    arranged = received.reshape(item_count, tokens, 3, depth)
    query_all = arranged[:, :, 0]
    key_all = arranged[:, :, 1]
    value_all = arranged[:, :, 2]
    item_index = lax.axis_index("seq") * item_count + jnp.arange(item_count, dtype=jnp.int32)
    seq_of = item_index // heads_count
    head_of = item_index % heads_count
    match_head = head_of[:, None] == jnp.arange(heads_count, dtype=jnp.int32)[None, :]
    bias_columns = jnp.sum(jnp.where(match_head[:, None, :], bias_table[None, :, :], 0.0), axis=2)
    match_seq = seq_of[:, None] == jnp.arange(sequences, dtype=jnp.int32)[None, :]
    item_lengths = jnp.sum(jnp.where(match_seq, lengths[None, :], 0), axis=1)
    valid_tokens = (item_lengths + 1) // 2

    def forward_item(item):
        query_one, key_one, value_one, column_one, valid_one = item
        return attend_item(query_one, key_one, value_one, column_one, valid_one)

    outputs_full, log_totals = lax.map(
        forward_item, (query_all, key_all, value_all, bias_columns, valid_tokens)
    )
    outputs_low = outputs_full.astype(jnp.bfloat16)
    returned = lax.all_to_all(
        outputs_low.reshape(item_count, tokens * depth),
        "seq",
        split_axis=1,
        concat_axis=0,
        tiled=True,
    )
    attended = from_items(returned, sequences, heads_count, depth)
    residual = hidden_in + jnp.dot(attended, out_weight, preferred_element_type=jnp.float32)
    normed_two, norm_back_two = jax.vjp(rms_scale, residual, norm_gain_two)
    normed_two_low = normed_two.astype(jnp.bfloat16)
    gate_up = jnp.dot(normed_two_low, in_weight, preferred_element_type=jnp.float32)
    hidden_units = gate_up.shape[-1] // 2

    def activate(gate_up_rows):
        return (
            jax.nn.gelu(gate_up_rows[..., :hidden_units], approximate=True)
            * gate_up_rows[..., hidden_units:]
        )

    activated, activate_back = jax.vjp(activate, gate_up)
    activated_low = activated.astype(jnp.bfloat16)
    layer_out = residual + jnp.dot(activated_low, down_weight, preferred_element_type=jnp.float32)
    grad_down = jnp.einsum(
        "bti,btd->id", activated_low, cotangent, preferred_element_type=jnp.float32
    )
    grad_activated = jnp.einsum(
        "btd,id->bti", cotangent, down_weight, preferred_element_type=jnp.float32
    )
    grad_gate_up = activate_back(grad_activated)[0].astype(jnp.bfloat16)
    grad_in = jnp.einsum(
        "btd,bti->di", normed_two_low, grad_gate_up, preferred_element_type=jnp.float32
    )
    grad_normed_two = jnp.einsum(
        "bti,di->btd", grad_gate_up, in_weight, preferred_element_type=jnp.float32
    )
    grad_residual_two, grad_gain_two = norm_back_two(grad_normed_two)
    grad_residual = cotangent.astype(jnp.float32) + grad_residual_two
    grad_branch = grad_residual.astype(jnp.bfloat16)
    grad_out_weight = jnp.einsum(
        "btd,bte->de", attended, grad_branch, preferred_element_type=jnp.float32
    )
    grad_attended = jnp.einsum(
        "bte,de->btd", grad_branch, out_weight, preferred_element_type=jnp.float32
    ).astype(jnp.bfloat16)
    sent_back = to_items(grad_attended.reshape(sequences, steps_local, heads_count, depth))
    grad_items = lax.all_to_all(sent_back, "seq", split_axis=0, concat_axis=1, tiled=True).reshape(
        item_count, tokens, depth
    )

    def backward_item(item):
        query_one, key_one, value_one, output_one, total_one, grad_one, column_one, valid_one = item
        return attend_item_back(
            query_one, key_one, value_one, output_one, total_one, grad_one, column_one, valid_one
        )

    grad_query, grad_key, grad_value, item_bias_grads = lax.map(
        backward_item,
        (
            query_all,
            key_all,
            value_all,
            outputs_full,
            log_totals,
            grad_items,
            bias_columns,
            valid_tokens,
        ),
    )
    stacked = jnp.stack([grad_query, grad_key, grad_value], axis=2).astype(jnp.bfloat16)
    back_tokens = lax.all_to_all(
        stacked.reshape(item_count, tokens * 3 * depth),
        "seq",
        split_axis=1,
        concat_axis=0,
        tiled=True,
    )
    grad_projected = from_items(back_tokens, sequences, heads_count, 3 * depth)
    grad_qkv = jnp.einsum(
        "btd,bte->de", normed_low, grad_projected, preferred_element_type=jnp.float32
    )
    grad_normed = jnp.einsum(
        "bte,de->btd", grad_projected, qkv_weight, preferred_element_type=jnp.float32
    )
    grad_hidden_one, grad_gain_one = norm_back_one(grad_normed)
    grad_hidden = grad_residual + grad_hidden_one
    grad_extended, grad_kernel, grad_vector = pool_back(grad_hidden)
    owned = grad_extended[:, 4 : 4 + local_bytes]
    rims = jnp.concatenate([grad_extended[:, :4], grad_extended[:, 4 + local_bytes :]], axis=1)
    arrived = extended_2(rims.astype(jnp.bfloat16), (("seq", 1),), 4).astype(rims.dtype)
    grad_bytes = owned.at[:, :4].add(arrived[:, :4]).at[:, local_bytes - 4 :].add(arrived[:, 12:16])
    grad_table = jnp.dot(
        one_hot.astype(jnp.float32).T, grad_bytes.reshape(-1, model_width), precision=highest
    )[:vocab_rows]
    grad_bias_table = jnp.sum(
        jnp.where(match_head[:, None, :], item_bias_grads[:, :, None], 0.0), axis=0
    )
    rows_qkv, rows_out, rows_in, rows_down = (
        lax.psum_scatter(
            grad_qkv.astype(jnp.bfloat16), "seq", scatter_dimension=0, tiled=True
        ).astype(jnp.float32),
        lax.psum_scatter(
            grad_out_weight.astype(jnp.bfloat16), "seq", scatter_dimension=0, tiled=True
        ).astype(jnp.float32),
        lax.psum_scatter(
            grad_in.astype(jnp.bfloat16), "seq", scatter_dimension=0, tiled=True
        ).astype(jnp.float32),
        lax.psum_scatter(
            grad_down.astype(jnp.bfloat16), "seq", scatter_dimension=0, tiled=True
        ).astype(jnp.float32),
    )
    summed_qkv, summed_out, summed_in, summed_down = (
        lax.psum_scatter(
            rows_qkv.astype(jnp.bfloat16), "dp", scatter_dimension=1, tiled=True
        ).astype(jnp.float32),
        lax.psum_scatter(
            rows_out.astype(jnp.bfloat16), "dp", scatter_dimension=1, tiled=True
        ).astype(jnp.float32),
        lax.psum_scatter(
            rows_in.astype(jnp.bfloat16), "dp", scatter_dimension=1, tiled=True
        ).astype(jnp.float32),
        lax.psum_scatter(
            rows_down.astype(jnp.bfloat16), "dp", scatter_dimension=1, tiled=True
        ).astype(jnp.float32),
    )
    small_totals = lax.psum(
        (grad_table, grad_kernel, grad_vector, grad_gain_one, grad_bias_table, grad_gain_two),
        ("dp", "seq"),
    )
    return (
        layer_out,
        small_totals[0],
        small_totals[1],
        small_totals[2],
        small_totals[3],
        summed_qkv,
        small_totals[4],
        summed_out,
        small_totals[5],
        summed_in,
        summed_down,
    )


def solution(mesh):
    return jax.shard_map(
        body,
        mesh=mesh,
        in_specs=(
            P("dp", "seq"),
            P("dp"),
            P(),
            P(),
            P(),
            P(),
            P(),
            P(),
            P(),
            P(),
            P(),
            P(),
            P("dp", "seq", None),
        ),
        out_specs=(
            P("dp", "seq", None),
            P(),
            P(),
            P(),
            P(),
            P("seq", "dp"),
            P(),
            P("seq", "dp"),
            P(),
            P("seq", "dp"),
            P("seq", "dp"),
        ),
        check_vma=False,
    )
```

profile of v0, /device:TPU:0, one launch (start us, length us, event | category | flops | bytes accessed | tf_op | source)
XLA Modules:
  0.0 5507.2 jit_solution(16009602801260554893)
XLA Ops:
  255.5 1397.6 %while.181 = (s32[]{:T(128)}, f32[12,1024,64]{2,1,0:T(8,128)}, f32[12,1024]{1,0:T(8,128)}, bf16[12,1024,64]{2,1,0:T(8,128)(2,1)}, s32[12]{0:T(128)}, /*index=5*/...) while((s32[]{:T(128)}, f32[12,1024,64]{2,1,0:T(8,128)}, ...), condition=%wide.region_18.19_spmd, body=%wide.region_7.18_spmd.sunk | while | flops 167547408 | bytes 18553988 | solution.py:303
  261.9 103.7 %while.184 = (s32[]{:T(128)}, f32[2,512,64]{1,2,0:T(8,128)}, f32[2,512]{1,0:T(2,128)}, s32[2]{0:T(128)S(1)}, bf16[1024,64]{1,0:T(8,128)(2,1)}, /*index=5*/s32[]{...) while((s32[]{:T(128)}, f32[2,512,64]{1,2,0:T(8,128)}, ...), condition=%wide.region_17.17_spmd, body=%wide.region_8.16_spmd.sunk | while | flops 167547392 | bytes 16177421 | solution.py:144
  377.6 103.7 %while.184 = (s32[]{:T(128)}, f32[2,512,64]{1,2,0:T(8,128)}, f32[2,512]{1,0:T(2,128)}, s32[2]{0:T(128)S(1)}, bf16[1024,64]{1,0:T(8,128)(2,1)}, /*index=5*/s32[]{...) while((s32[]{:T(128)}, f32[2,512,64]{1,2,0:T(8,128)}, ...), condition=%wide.region_17.17_spmd, body=%wide.region_8.16_spmd.sunk | while | flops 167547392 | bytes 16177421 | solution.py:144
  493.4 103.7 %while.184 = (s32[]{:T(128)}, f32[2,512,64]{1,2,0:T(8,128)}, f32[2,512]{1,0:T(2,128)}, s32[2]{0:T(128)S(1)}, bf16[1024,64]{1,0:T(8,128)(2,1)}, /*index=5*/s32[]{...) while((s32[]{:T(128)}, f32[2,512,64]{1,2,0:T(8,128)}, ...), condition=%wide.region_17.17_spmd, body=%wide.region_8.16_spmd.sunk | while | flops 167547392 | bytes 16177421 | solution.py:144
  609.2 103.7 %while.184 = (s32[]{:T(128)}, f32[2,512,64]{1,2,0:T(8,128)}, f32[2,512]{1,0:T(2,128)}, s32[2]{0:T(128)S(1)}, bf16[1024,64]{1,0:T(8,128)(2,1)}, /*index=5*/s32[]{...) while((s32[]{:T(128)}, f32[2,512,64]{1,2,0:T(8,128)}, ...), condition=%wide.region_17.17_spmd, body=%wide.region_8.16_spmd.sunk | while | flops 167547392 | bytes 16177421 | solution.py:144
  725.0 103.7 %while.184 = (s32[]{:T(128)}, f32[2,512,64]{1,2,0:T(8,128)}, f32[2,512]{1,0:T(2,128)}, s32[2]{0:T(128)S(1)}, bf16[1024,64]{1,0:T(8,128)(2,1)}, /*index=5*/s32[]{...) while((s32[]{:T(128)}, f32[2,512,64]{1,2,0:T(8,128)}, ...), condition=%wide.region_17.17_spmd, body=%wide.region_8.16_spmd.sunk | while | flops 167547392 | bytes 16177421 | solution.py:144
  840.8 103.7 %while.184 = (s32[]{:T(128)}, f32[2,512,64]{1,2,0:T(8,128)}, f32[2,512]{1,0:T(2,128)}, s32[2]{0:T(128)S(1)}, bf16[1024,64]{1,0:T(8,128)(2,1)}, /*index=5*/s32[]{...) while((s32[]{:T(128)}, f32[2,512,64]{1,2,0:T(8,128)}, ...), condition=%wide.region_17.17_spmd, body=%wide.region_8.16_spmd.sunk | while | flops 167547392 | bytes 16177421 | solution.py:144
  956.5 103.7 %while.184 = (s32[]{:T(128)}, f32[2,512,64]{1,2,0:T(8,128)}, f32[2,512]{1,0:T(2,128)}, s32[2]{0:T(128)S(1)}, bf16[1024,64]{1,0:T(8,128)(2,1)}, /*index=5*/s32[]{...) while((s32[]{:T(128)}, f32[2,512,64]{1,2,0:T(8,128)}, ...), condition=%wide.region_17.17_spmd, body=%wide.region_8.16_spmd.sunk | while | flops 167547392 | bytes 16177421 | solution.py:144
  1072.3 103.7 %while.184 = (s32[]{:T(128)}, f32[2,512,64]{1,2,0:T(8,128)}, f32[2,512]{1,0:T(2,128)}, s32[2]{0:T(128)S(1)}, bf16[1024,64]{1,0:T(8,128)(2,1)}, /*index=5*/s32[]{...) while((s32[]{:T(128)}, f32[2,512,64]{1,2,0:T(8,128)}, ...), condition=%wide.region_17.17_spmd, body=%wide.region_8.16_spmd.sunk | while | flops 167547392 | bytes 16177421 | solution.py:144
  1188.1 103.7 %while.184 = (s32[]{:T(128)}, f32[2,512,64]{1,2,0:T(8,128)}, f32[2,512]{1,0:T(2,128)}, s32[2]{0:T(128)S(1)}, bf16[1024,64]{1,0:T(8,128)(2,1)}, /*index=5*/s32[]{...) while((s32[]{:T(128)}, f32[2,512,64]{1,2,0:T(8,128)}, ...), condition=%wide.region_17.17_spmd, body=%wide.region_8.16_spmd.sunk | while | flops 167547392 | bytes 16177421 | solution.py:144
  1304.0 103.7 %while.184 = (s32[]{:T(128)}, f32[2,512,64]{1,2,0:T(8,128)}, f32[2,512]{1,0:T(2,128)}, s32[2]{0:T(128)S(1)}, bf16[1024,64]{1,0:T(8,128)(2,1)}, /*index=5*/s32[]{...) while((s32[]{:T(128)}, f32[2,512,64]{1,2,0:T(8,128)}, ...), condition=%wide.region_17.17_spmd, body=%wide.region_8.16_spmd.sunk | while | flops 167547392 | bytes 16177421 | solution.py:144
  1419.7 103.7 %while.184 = (s32[]{:T(128)}, f32[2,512,64]{1,2,0:T(8,128)}, f32[2,512]{1,0:T(2,128)}, s32[2]{0:T(128)S(1)}, bf16[1024,64]{1,0:T(8,128)(2,1)}, /*index=5*/s32[]{...) while((s32[]{:T(128)}, f32[2,512,64]{1,2,0:T(8,128)}, ...), condition=%wide.region_17.17_spmd, body=%wide.region_8.16_spmd.sunk | while | flops 167547392 | bytes 16177421 | solution.py:144
  1535.5 103.7 %while.184 = (s32[]{:T(128)}, f32[2,512,64]{1,2,0:T(8,128)}, f32[2,512]{1,0:T(2,128)}, s32[2]{0:T(128)S(1)}, bf16[1024,64]{1,0:T(8,128)(2,1)}, /*index=5*/s32[]{...) while((s32[]{:T(128)}, f32[2,512,64]{1,2,0:T(8,128)}, ...), condition=%wide.region_17.17_spmd, body=%wide.region_8.16_spmd.sunk | while | flops 167547392 | bytes 16177421 | solution.py:144
  1665.8 1095.3 %all_to_all.61 = bf16[12,8,8192]{2,0,1:T(8,128)(2,1)S(1)} all-to-all(bf16[12,8,8192]{2,0,1:T(8,128)(2,1)S(1)} %copy.196), channel_id=1, replica_groups=mesh['dp'=4,'seq'=8] {'seq'}, dimensions={1} | all-to-all | bytes 3145728 | tf_op jit(solution)/shard_map/all_to_all | solution.py:307
  2900.4 1152.1 %while.183 = (s32[]{:T(128)}, bf16[12,1024,64]{1,2,0:T(8,128)(2,1)}, bf16[12,1024,64]{1,2,0:T(8,128)(2,1)}, bf16[12,1024,64]{1,2,0:T(8,128)(2,1)}, f32[12,32]{1,...) while((s32[]{:T(128)}, bf16[12,1024,64]{1,2,0:T(8,128)(2,1)}, ...), condition=%wide.region_29.30_spmd, body=%wide.region_21.29_spmd.sunk | while | flops 227705360 | bytes 18251388 | solution.py:363
  2914.5 78.4 %while.185 = (s32[]{:T(128)}, f32[1024,64]{0,1:T(8,128)}, bf16[1024,64]{0,1:T(8,128)(2,1)}, bf16[1024,64]{0,1:T(8,128)(2,1)}, f32[32]{0:T(128)}, /*index=5*/s32[...) while((s32[]{:T(128)}, f32[1024,64]{0,1:T(8,128)}, ...), condition=%wide.region_28.28_spmd, body=%wide.region_23.27_spmd.sunk | while | flops 227444224 | bytes 14567765 | solution.py:211
  2918.1 73.1 %while.186 = (s32[]{:T(128)}, f32[1024,64]{0,1:T(8,128)}, f32[512,64]{0,1:T(8,128)}, f32[512,64]{0,1:T(8,128)}, f32[32]{0:T(128)}, /*index=5*/s32[2]{0:T(128)}, ...) while((s32[]{:T(128)}, f32[1024,64]{0,1:T(8,128)}, ...), condition=%wide.region_27.26_spmd.clone, body=%wide.region_24.25_spmd.clone.sunk | while | flops 227444224 | bytes 13780910 | solution.py:200
  3011.3 77.4 %while.185 = (s32[]{:T(128)}, f32[1024,64]{0,1:T(8,128)}, bf16[1024,64]{0,1:T(8,128)(2,1)}, bf16[1024,64]{0,1:T(8,128)(2,1)}, f32[32]{0:T(128)}, /*index=5*/s32[...) while((s32[]{:T(128)}, f32[1024,64]{0,1:T(8,128)}, ...), condition=%wide.region_28.28_spmd, body=%wide.region_23.27_spmd.sunk | while | flops 227444224 | bytes 14567765 | solution.py:211
  3107.2 77.4 %while.185 = (s32[]{:T(128)}, f32[1024,64]{0,1:T(8,128)}, bf16[1024,64]{0,1:T(8,128)(2,1)}, bf16[1024,64]{0,1:T(8,128)(2,1)}, f32[32]{0:T(128)}, /*index=5*/s32[...) while((s32[]{:T(128)}, f32[1024,64]{0,1:T(8,128)}, ...), condition=%wide.region_28.28_spmd, body=%wide.region_23.27_spmd.sunk | while | flops 227444224 | bytes 14567765 | solution.py:211
  3203.1 77.4 %while.185 = (s32[]{:T(128)}, f32[1024,64]{0,1:T(8,128)}, bf16[1024,64]{0,1:T(8,128)(2,1)}, bf16[1024,64]{0,1:T(8,128)(2,1)}, f32[32]{0:T(128)}, /*index=5*/s32[...) while((s32[]{:T(128)}, f32[1024,64]{0,1:T(8,128)}, ...), condition=%wide.region_28.28_spmd, body=%wide.region_23.27_spmd.sunk | while | flops 227444224 | bytes 14567765 | solution.py:211
  3206.7 72.1 %while.186 = (s32[]{:T(128)}, f32[1024,64]{0,1:T(8,128)}, f32[512,64]{0,1:T(8,128)}, f32[512,64]{0,1:T(8,128)}, f32[32]{0:T(128)}, /*index=5*/s32[2]{0:T(128)}, ...) while((s32[]{:T(128)}, f32[1024,64]{0,1:T(8,128)}, ...), condition=%wide.region_27.26_spmd.clone, body=%wide.region_24.25_spmd.clone.sunk | while | flops 227444224 | bytes 13780910 | solution.py:200
  3298.9 77.4 %while.185 = (s32[]{:T(128)}, f32[1024,64]{0,1:T(8,128)}, bf16[1024,64]{0,1:T(8,128)(2,1)}, bf16[1024,64]{0,1:T(8,128)(2,1)}, f32[32]{0:T(128)}, /*index=5*/s32[...) while((s32[]{:T(128)}, f32[1024,64]{0,1:T(8,128)}, ...), condition=%wide.region_28.28_spmd, body=%wide.region_23.27_spmd.sunk | while | flops 227444224 | bytes 14567765 | solution.py:211
  3394.8 77.4 %while.185 = (s32[]{:T(128)}, f32[1024,64]{0,1:T(8,128)}, bf16[1024,64]{0,1:T(8,128)(2,1)}, bf16[1024,64]{0,1:T(8,128)(2,1)}, f32[32]{0:T(128)}, /*index=5*/s32[...) while((s32[]{:T(128)}, f32[1024,64]{0,1:T(8,128)}, ...), condition=%wide.region_28.28_spmd, body=%wide.region_23.27_spmd.sunk | while | flops 227444224 | bytes 14567765 | solution.py:211
  3490.7 77.4 %while.185 = (s32[]{:T(128)}, f32[1024,64]{0,1:T(8,128)}, bf16[1024,64]{0,1:T(8,128)(2,1)}, bf16[1024,64]{0,1:T(8,128)(2,1)}, f32[32]{0:T(128)}, /*index=5*/s32[...) while((s32[]{:T(128)}, f32[1024,64]{0,1:T(8,128)}, ...), condition=%wide.region_28.28_spmd, body=%wide.region_23.27_spmd.sunk | while | flops 227444224 | bytes 14567765 | solution.py:211
  3494.4 72.1 %while.186 = (s32[]{:T(128)}, f32[1024,64]{0,1:T(8,128)}, f32[512,64]{0,1:T(8,128)}, f32[512,64]{0,1:T(8,128)}, f32[32]{0:T(128)}, /*index=5*/s32[2]{0:T(128)}, ...) while((s32[]{:T(128)}, f32[1024,64]{0,1:T(8,128)}, ...), condition=%wide.region_27.26_spmd.clone, body=%wide.region_24.25_spmd.clone.sunk | while | flops 227444224 | bytes 13780910 | solution.py:200
  3586.6 77.4 %while.185 = (s32[]{:T(128)}, f32[1024,64]{0,1:T(8,128)}, bf16[1024,64]{0,1:T(8,128)(2,1)}, bf16[1024,64]{0,1:T(8,128)(2,1)}, f32[32]{0:T(128)}, /*index=5*/s32[...) while((s32[]{:T(128)}, f32[1024,64]{0,1:T(8,128)}, ...), condition=%wide.region_28.28_spmd, body=%wide.region_23.27_spmd.sunk | while | flops 227444224 | bytes 14567765 | solution.py:211
  3682.5 77.4 %while.185 = (s32[]{:T(128)}, f32[1024,64]{0,1:T(8,128)}, bf16[1024,64]{0,1:T(8,128)(2,1)}, bf16[1024,64]{0,1:T(8,128)(2,1)}, f32[32]{0:T(128)}, /*index=5*/s32[...) while((s32[]{:T(128)}, f32[1024,64]{0,1:T(8,128)}, ...), condition=%wide.region_28.28_spmd, body=%wide.region_23.27_spmd.sunk | while | flops 227444224 | bytes 14567765 | solution.py:211
  3778.4 77.4 %while.185 = (s32[]{:T(128)}, f32[1024,64]{0,1:T(8,128)}, bf16[1024,64]{0,1:T(8,128)(2,1)}, bf16[1024,64]{0,1:T(8,128)(2,1)}, f32[32]{0:T(128)}, /*index=5*/s32[...) while((s32[]{:T(128)}, f32[1024,64]{0,1:T(8,128)}, ...), condition=%wide.region_28.28_spmd, body=%wide.region_23.27_spmd.sunk | while | flops 227444224 | bytes 14567765 | solution.py:211
  3782.0 72.1 %while.186 = (s32[]{:T(128)}, f32[1024,64]{0,1:T(8,128)}, f32[512,64]{0,1:T(8,128)}, f32[512,64]{0,1:T(8,128)}, f32[32]{0:T(128)}, /*index=5*/s32[2]{0:T(128)}, ...) while((s32[]{:T(128)}, f32[1024,64]{0,1:T(8,128)}, ...), condition=%wide.region_27.26_spmd.clone, body=%wide.region_24.25_spmd.clone.sunk | while | flops 227444224 | bytes 13780910 | solution.py:200
  3874.2 77.4 %while.185 = (s32[]{:T(128)}, f32[1024,64]{0,1:T(8,128)}, bf16[1024,64]{0,1:T(8,128)(2,1)}, bf16[1024,64]{0,1:T(8,128)(2,1)}, f32[32]{0:T(128)}, /*index=5*/s32[...) while((s32[]{:T(128)}, f32[1024,64]{0,1:T(8,128)}, ...), condition=%wide.region_28.28_spmd, body=%wide.region_23.27_spmd.sunk | while | flops 227444224 | bytes 14567765 | solution.py:211
  3970.1 77.4 %while.185 = (s32[]{:T(128)}, f32[1024,64]{0,1:T(8,128)}, bf16[1024,64]{0,1:T(8,128)(2,1)}, bf16[1024,64]{0,1:T(8,128)(2,1)}, f32[32]{0:T(128)}, /*index=5*/s32[...) while((s32[]{:T(128)}, f32[1024,64]{0,1:T(8,128)}, ...), condition=%wide.region_28.28_spmd, body=%wide.region_23.27_spmd.sunk | while | flops 227444224 | bytes 14567765 | solution.py:211
  4098.4 929.7 %all-to-all-start.3 = ((bf16[12,8,24576]{2,0,1:T(8,128)(2,1)}), bf16[12,8,24576]{2,0,1:T(8,128)(2,1)}, u32[]{:S(2)}, u32[]{:S(2)}) async-start(bf16[12,8,24576]{2,0,1:T(8,128)(2,1)} %copy.208), calls=%async_computation.3 | async-start | bytes 12582912 | tf_op jit(solution)/shard_map/all_to_all | solution.py:377
  (1788 shorter events, 5000.4 us)
Async XLA Ops:
  8.0 81.3 %copy-start = (bf16[768,2304]{1,0:T(8,128)(2,1)S(1)}, bf16[768,2304]{1,0:T(8,128)(2,1)}, u32[]{:S(2)}) copy-start(bf16[768,2304]{1,0:T(8,128)(2,1)} %param.37) | copy-start | bytes 10616836
  14.6 7.2 collective-permute-start
  17.6 5.0 collective-permute-start.1
  46.6 26.1 copy-start.3
  46.6 26.1 copy-start.4
  46.6 26.8 copy-start.5
  46.6 26.8 copy-start.7
  121.4 77.8 %all-to-all-start = ((bf16[8,12,24576]{2,1,0:T(8,128)(2,1)}), bf16[8,12,24576]{2,1,0:T(8,128)(2,1)}, u32[]{:S(2)}, u32[]{:S(2)}) async-start(bf16[8,12,24576]{2,1,0:T(8,128)(2,1)} %reshape.546), calls=%async_computation | async-start | bytes 12582912 | tf_op jit(solution)/shard_map/all_to_all | solution.py:283
  127.6 4900.6 %reduce-scatter.17.cloned.1.call-start = ((), (), s32[]{:S(2)}) async-start(), calls=%async_computation.14 | async-start | bytes 1327104 | tf_op jit(solution)/shard_map/reduce_scatter | solution.py:408
  289.6 24.2 copy-start.80
  457.2 24.2 copy-start.80
  573.0 24.2 copy-start.80
  752.7 24.2 copy-start.80
  868.5 24.2 copy-start.80
  1267.7 24.2 copy-start.80
  1331.6 24.2 copy-start.80
  2833.4 2313.8 %reduce-scatter.23.cloned.1.call-start = ((), (), s32[]{:S(2)}) async-start(), calls=%async_computation.17 | async-start | bytes 3538944 | tf_op jit(solution)/shard_map/reduce_scatter | solution.py:414
  2858.5 32.6 all-to-all-start.2
  2862.9 2449.0 %reduce-scatter.19.cloned.1.call-start = ((), (), s32[]{:S(2)}) async-start(), calls=%async_computation.15 | async-start | bytes 7077888 | tf_op jit(solution)/shard_map/reduce_scatter | solution.py:411
  4098.4 1001.8 %all-to-all-start.3 = ((bf16[12,8,24576]{2,0,1:T(8,128)(2,1)}), bf16[12,8,24576]{2,0,1:T(8,128)(2,1)}, u32[]{:S(2)}, u32[]{:S(2)}) async-start(bf16[12,8,24576]{2,0,1:T(8,128)(2,1)} %copy.208), calls=%async_computation.3 | async-start | bytes 12582912 | tf_op jit(solution)/shard_map/all_to_all | solution.py:377
  5028.1 314.4 %reduce-scatter.27.cloned.1.call-start = ((), (), s32[]{:S(2)}) async-start(), calls=%async_computation.19 | async-start | bytes 245760
  5029.9 321.6 %reduce-scatter.15.cloned.1.call-start = ((), (), s32[]{:S(2)}) async-start(), calls=%async_computation.13 | async-start | bytes 3981312 | tf_op jit(solution)/shard_map/reduce_scatter | solution.py:405
  5135.8 289.1 %reduce-scatter.29.cloned.1.call-start = ((), (), s32[]{:S(2)}) async-start(), calls=%async_computation.20 | async-start | bytes 491520
  5149.3 278.9 %reduce-scatter.21.cloned.1.call-start = ((), (), s32[]{:S(2)}) async-start(), calls=%async_computation.16 | async-start | bytes 983040 | tf_op jit(solution)/shard_map/reduce_scatter | solution.py:425
  5281.4 30.5 copy-start.27
  5281.4 30.5 copy-start.29
  5281.5 30.5 copy-start.31
  5281.5 30.5 copy-start.33
  5311.9 118.0 %reduce-scatter.25.cloned.1.call-start = ((), (), s32[]{:S(2)}) async-start(), calls=%async_computation.18 | async-start | bytes 737280
  5339.1 14.6 collective-permute-start.2
  5341.0 12.7 collective-permute-start.3
  5353.7 143.8 %all-reduce.47.cloned.1.call-start = ((), (), s32[]{:S(2)}) async-start(), calls=%async_computation.12 | async-start | bytes 1622016 | tf_op jit(solution)/shard_map/psum | solution.py:432
  (122 other events, 1181.5 us)
Sparse Core Ops, SparseCore 0:
  2833.6 38.8 reduce-scatter.16
  2876.3 51.0 reduce-scatter.22
  2930.7 61.7 reduce-scatter.18
  5031.5 23.4 reduce-scatter.26
  5135.9 49.4 reduce-scatter.14
  5188.2 20.5 reduce-scatter.28
  5312.1 24.7 reduce-scatter.20
  5353.8 26.6 reduce-scatter.24
Sparse Core Ops, SparseCore 1:
  5365.0 132.4 all-reduce.46
where the time goes:
time: 5550 us; the launch traced here: 5510 us
  other arithmetic  1630 us (29%)
  blocking collectives  1140 us (21%)
  starting transfers between devices  949 us (17%)
  local copies, waits for them, and re-layouts  938 us (17%)
  matrix products  513 us (9%)
  waiting for transfers between devices  216 us (4%)
  loops' own time  109 us (2%)
    all_to_all x1, blocking collectives, body(): lax.all_to_all(outputs_low.reshape(item_count, tokens * depth), 'seq', sp...  1100 us
    reduce_sum x72, other arithmetic, block_logits(): jnp.sum(jnp.where(table_hit, bias_column[None, None, :], 0.0), axis=2)  1020 us
    all_to_all x1, starting transfers between devices, body(): lax.all_to_all(stacked.reshape(item_count, tokens * 3 * depth), 'seq', sp...  930 us
    add x72, other arithmetic, rel_bucket(): return bucket + 16 * (relative > 0).astype(jnp.int32)  147 us
    squeeze x96, local copies, waits for them, and re-layouts, body(): lax.map(forward_item, (query_all, key_all, value_all, bias_columns, valid...  146 us
    reduce_sum x24, other arithmetic, key_query_step(): jnp.sum(jnp.where(table_hit, grad_logits.astype(jnp.float32)[:, :, None],...  135 us
    reduce_sum x48, local copies, waits for them, and re-layouts, block_logits(): jnp.sum(jnp.where(table_hit, bias_column[None, None, :], 0.0), axis=2)  124 us
  transfers between devices with their start and end apart: 16, of which 5 were waited for; matrix products, arithmetic and copies ran while one was open for 27% of the time, Pallas kernels for 0%

commit v1 on v0

v1 whole, which is shorter than its diff:
```python
import functools
import jax
import jax.numpy as jnp
from jax import lax
from jax.experimental import pallas as pl
from jax.experimental.pallas import tpu as pltpu
from jax.sharding import PartitionSpec as P

thresholds = (12, 16, 23, 32, 46, 64, 91)
KB = 256
NEAR = 1024
F32 = jnp.float32
BF16 = jnp.bfloat16
NT = (((1,), (1,)), ((), ()))
NN = (((1,), (0,)), ((), ()))


def rel_bucket(relative):
    distance = jnp.abs(relative)
    larger = 8 + sum(((distance >= boundary).astype(jnp.int32) for boundary in thresholds))
    bucket = jnp.where(distance < 8, distance, larger)
    return bucket + 16 * (relative > 0).astype(jnp.int32)


def near_one_hot():
    place = jnp.arange(NEAR, dtype=jnp.int32)
    relative = jnp.where(place < NEAR - 128, KB - place, KB + NEAR - place)
    return (rel_bucket(relative)[:, None] == jnp.arange(32, dtype=jnp.int32)[None, :]).astype(F32)


def dot(a, b, dims):
    return lax.dot_general(a, b, dims, preferred_element_type=F32)


def fill_bias(strip, head, row, blocks):
    base = KB * (blocks - 2)
    width = KB * (2 * blocks - 1)
    spread = jnp.broadcast_to(row, (128, NEAR))
    rolled = pltpu.roll(spread, 0, 1, stride=1, stride_axis=0)
    far_right = jnp.broadcast_to(row[:, NEAR - 1 :], (KB, 128))
    far_left = jnp.broadcast_to(row[:, 768:769], (KB, 128))
    for start in range(0, base, 128):
        strip[head, :, start : start + 128] = far_right
    strip[head, 0:128, base : base + 768] = rolled[:, :768]
    strip[head, 128:256, base : base + 128] = far_right[:128]
    strip[head, 128:256, base + 128 : base + 768] = rolled[:, :640]
    for start in range(base + 768, width, 128):
        strip[head, :, start : start + 128] = far_left


def lanes_of(head, shape):
    lane = lax.broadcasted_iota(jnp.int32, shape, 1)
    own = (lane < 64) if head == 0 else (lane >= 64)
    return own, lane - (64 if head == 0 else 0)


def fill_keys(ka, head, keys, valid):
    own, spare = lanes_of(head, keys.shape)
    row = lax.broadcasted_iota(jnp.int32, keys.shape, 0)
    masked = jnp.where(row < valid, 0.0, -1e9)
    extra = jnp.where(spare == 0, masked, jnp.where((spare >= 1) & (spare <= 3), 1.0, 0.0))
    ka[head] = jnp.where(own, keys, extra.astype(BF16))


def fwd_kernel(blocks, valid_ref, pair_ref, qkv_ref, row_ref, out_ref, aug_ref, qa, ka, vt, strip, peak, acc, probs):
    item = pl.program_id(0)
    valid = valid_ref[item]
    tokens = blocks * KB
    joined = qkv_ref[:, 0].reshape(tokens, 384)
    queries = joined[:, 0:128]
    keys = joined[:, 128:256]
    turned = joined[:, 256:384].T
    filler = jnp.where(lax.broadcasted_iota(jnp.int32, (16, tokens), 0) == 0, 1.0, 0.0).astype(BF16)
    for head in range(2):
        own, spare = lanes_of(head, queries.shape)
        qa[head] = jnp.where(own, queries, jnp.where(spare == 0, 1.0, 0.0).astype(BF16))
        fill_keys(ka, head, keys, valid)
        vt[head, 0:64] = turned[64 * head : 64 * head + 64]
        vt[head, 64:80] = filler
        fill_bias(strip, head, row_ref[0, head : head + 1, :], blocks)
    peak[...] = jnp.full_like(peak, -1e30)
    acc[...] = jnp.zeros_like(acc)

    def step(block, unused):
        first = pl.multiple_of(block * KB, KB)
        shift = pl.multiple_of((blocks - 1 - block) * KB, KB)
        for head in range(2):
            alphas = []
            for part in range(blocks):
                here = slice(part * KB, part * KB + KB)
                logits = dot(ka[head, pl.ds(first, KB), :], qa[head, here, :], NT)
                logits = logits + strip[head, :, pl.ds(shift + part * KB, KB)]
                before = peak[head, :, here]
                after = jnp.maximum(before, jnp.max(logits, axis=0, keepdims=True))
                probs[head, :, here] = jnp.exp(logits - after).astype(BF16)
                peak[head, :, here] = after
                alphas.append(jnp.exp(before - after))
            acc[head] = acc[head] * jnp.concatenate(alphas, axis=1) + dot(
                    vt[head, :, pl.ds(first, KB)], probs[head], NN
                )
        return unused

    lax.fori_loop(0, (valid + KB - 1) // KB, step, 0)
    outs = []
    rows = []
    place = lax.broadcasted_iota(jnp.int32, (64, tokens), 0)
    for head in range(2):
        total = acc[head, 64:65, :]
        outs.append(acc[head, 0:64, :] / total)
        minus = -(peak[head] + jnp.log(total))
        high = minus.astype(BF16).astype(F32)
        rest = minus - high
        middle = rest.astype(BF16).astype(F32)
        low = rest - middle
        rows.append(jnp.where(place == 0, 1.0, jnp.where(place == 1, high, jnp.where(place == 2, middle, jnp.where(place == 3, low, 0.0)))))
    out_ref[:, 0] = jnp.concatenate(outs, axis=0).T.astype(BF16).reshape(out_ref.shape[0], out_ref.shape[2], 128)
    aug_ref[0] = jnp.concatenate([rows[1], rows[0]], axis=0).T.astype(BF16)


def bwd_kernel(
    blocks, valid_ref, pair_ref, qkv_ref, out_ref, aug_ref, grad_ref, row_ref,
    dqkv_ref, bias_ref, qa, ka, va, ga, kt, strip, tally, probs, slopes, dq,
):
    item = pl.program_id(0)
    valid = valid_ref[item]
    tokens = blocks * KB
    width = KB * (2 * blocks - 1)
    local = qkv_ref.shape[2]
    joined = qkv_ref[:, 0].reshape(tokens, 384)
    queries = joined[:, 0:128]
    keys = joined[:, 128:256]
    values = joined[:, 256:384]
    grads = grad_ref[:, 0].reshape(tokens, 128)
    outs = out_ref[:, 0].reshape(tokens, 128)
    kt[...] = keys.T
    product = grads.astype(F32) * outs.astype(F32)
    high = product.astype(BF16)
    low = (product - high.astype(F32)).astype(BF16)
    row_at = lax.broadcasted_iota(jnp.int32, (128, 128), 0)
    lane_at = lax.broadcasted_iota(jnp.int32, (128, 128), 1)
    pick = jnp.where((row_at < 64) == (lane_at >= 64), -1.0, 0.0).astype(BF16)
    shifts = dot(high, pick, NN) + dot(low, pick, NN)
    shift_high = shifts.astype(BF16)
    shift_low = (shifts - shift_high.astype(F32)).astype(BF16)
    for head in range(2):
        own, spare = lanes_of(head, queries.shape)
        qa[head] = jnp.where(own, queries, aug_ref[0])
        fill_keys(ka, head, keys, valid)
        va[head] = jnp.where(own, values, jnp.where((spare == 0) | (spare == 1), 1.0, 0.0).astype(BF16))
        ga[head] = jnp.where(own, grads, jnp.where(spare == 0, shift_high, jnp.where(spare == 1, shift_low, jnp.zeros_like(shift_low))))
        fill_bias(strip, head, row_ref[0, head : head + 1, :], blocks)
    tally[...] = jnp.zeros_like(tally)
    dq[...] = jnp.zeros_like(dq)
    dqkv_ref[...] = jnp.zeros_like(dqkv_ref)

    def step(block, unused):
        first = pl.multiple_of(block * KB, KB)
        shift = pl.multiple_of((blocks - 1 - block) * KB, KB)
        key_parts = []
        value_parts = []
        for head in range(2):
            for part in range(blocks):
                here = slice(part * KB, part * KB + KB)
                there = pl.ds(shift + part * KB, KB)
                logits = dot(ka[head, pl.ds(first, KB), :], qa[head, here, :], NT)
                weights = jnp.exp(logits + strip[head, :, there])
                change = dot(va[head, pl.ds(first, KB), :], ga[head, here, :], NT)
                slope = weights * change
                tally[head, :, there] += slope
                probs[head, :, here] = weights.astype(BF16)
                slopes[head, :, here] = slope.astype(BF16)
            value_parts.append(dot(probs[head], ga[head], NN))
            key_parts.append(dot(slopes[head], qa[head], NN))
            dq[pl.ds(64 * head, 64), :] += dot(kt[pl.ds(64 * head, 64), pl.ds(first, KB)], slopes[head], NN)
        own, unused_spare = lanes_of(0, (KB, 128))
        count = KB // local
        where = pl.ds(block * count, count)
        dqkv_ref[where, 0, :, 128:256] = jnp.where(own, key_parts[0], key_parts[1]).astype(BF16).reshape(count, local, 128)
        dqkv_ref[where, 0, :, 256:384] = jnp.where(own, value_parts[0], value_parts[1]).astype(BF16).reshape(count, local, 128)
        return unused

    lax.fori_loop(0, (valid + KB - 1) // KB, step, 0)
    dqkv_ref[:, 0, :, 0:128] = dq[...].T.astype(BF16).reshape(dqkv_ref.shape[0], local, 128)
    base = KB * (blocks - 2)
    lane = lax.broadcasted_iota(jnp.int32, (1, NEAR), 1)
    flip = jnp.where(row_at + lane_at == 127, 1.0, 0.0).astype(BF16)
    for head in range(2):
        far_right = sum(tally[head, :, start : start + 128] for start in range(0, base, 128)) if base else jnp.zeros((KB, 128), F32)
        far_right = far_right[:128] + far_right[128:] + tally[head, 128:256, base : base + 128]
        left_list = [tally[head, :, start : start + 128] for start in range(base + 768, width, 128)]
        far_left = sum(left_list) if left_list else jnp.zeros((KB, 128), F32)
        near = tally[head, 0:128, base : base + 768]
        near_low = tally[head, 128:256, base + 128 : base + 768]
        near = near + jnp.concatenate([near_low, jnp.zeros((128, 128), F32)], axis=1)
        near = jnp.concatenate([near, jnp.zeros((128, NEAR - 768), F32)], axis=1)
        near_high = near.astype(BF16)
        flipped = dot(flip, near_high, NN) + dot(flip, (near - near_high.astype(F32)).astype(BF16), NN)
        rolled = pltpu.roll(flipped, NEAR - 127, 1, stride=1, stride_axis=0)
        row = jnp.sum(rolled, axis=0, keepdims=True)
        row = row + jnp.where(lane == NEAR - 1, jnp.sum(far_right), 0.0) + jnp.where(lane == 768, jnp.sum(far_left), 0.0)
        bias_ref[0, head : head + 1, :] = row


def attention_forward(qkv, rows, valid, pair):
    sources, items, local, unused = qkv.shape
    blocks = sources * local // KB
    tokens = sources * local
    width = KB * (2 * blocks - 1)
    spec = pltpu.PrefetchScalarGridSpec(
        num_scalar_prefetch=2,
        grid=(items,),
        in_specs=[
            pl.BlockSpec((sources, 1, local, 384), lambda i, v, p: (0, i, 0, 0)),
            pl.BlockSpec((1, 2, NEAR), lambda i, v, p: (p[i], 0, 0)),
        ],
        out_specs=[
            pl.BlockSpec((sources, 1, local, 128), lambda i, v, p: (0, i, 0, 0)),
            pl.BlockSpec((1, tokens, 128), lambda i, v, p: (i, 0, 0)),
        ],
        scratch_shapes=[
            pltpu.VMEM((2, tokens, 128), BF16),
            pltpu.VMEM((2, tokens, 128), BF16),
            pltpu.VMEM((2, 80, tokens), BF16),
            pltpu.VMEM((2, KB, width), F32),
            pltpu.VMEM((2, 1, tokens), F32),
            pltpu.VMEM((2, 80, tokens), F32),
            pltpu.VMEM((2, KB, tokens), BF16),
        ],
    )
    return pl.pallas_call(
        functools.partial(fwd_kernel, blocks),
        grid_spec=spec,
        out_shape=[
            jax.ShapeDtypeStruct((sources, items, local, 128), BF16),
            jax.ShapeDtypeStruct((items, tokens, 128), BF16),
        ],
        compiler_params=pltpu.CompilerParams(vmem_limit_bytes=50 * 2**20),
        cost_estimate=pl.CostEstimate(flops=items * tokens * tokens * 512, bytes_accessed=items * tokens * 2048, transcendentals=items * tokens * tokens * 2),
        name="attention_forward",
    )(valid, pair, qkv, rows)


def attention_backward(qkv, outs, aug, grads, rows, valid, pair):
    sources, items, local, unused = qkv.shape
    blocks = sources * local // KB
    tokens = sources * local
    width = KB * (2 * blocks - 1)
    big = lambda lanes: pl.BlockSpec((sources, 1, local, lanes), lambda i, v, p: (0, i, 0, 0))
    spec = pltpu.PrefetchScalarGridSpec(
        num_scalar_prefetch=2,
        grid=(items,),
        in_specs=[
            big(384),
            big(128),
            pl.BlockSpec((1, tokens, 128), lambda i, v, p: (i, 0, 0)),
            big(128),
            pl.BlockSpec((1, 2, NEAR), lambda i, v, p: (p[i], 0, 0)),
        ],
        out_specs=[
            big(384),
            pl.BlockSpec((1, 2, NEAR), lambda i, v, p: (i, 0, 0)),
        ],
        scratch_shapes=[
            pltpu.VMEM((2, tokens, 128), BF16),
            pltpu.VMEM((2, tokens, 128), BF16),
            pltpu.VMEM((2, tokens, 128), BF16),
            pltpu.VMEM((2, tokens, 128), BF16),
            pltpu.VMEM((128, tokens), BF16),
            pltpu.VMEM((2, KB, width), F32),
            pltpu.VMEM((2, KB, width), F32),
            pltpu.VMEM((2, KB, tokens), BF16),
            pltpu.VMEM((2, KB, tokens), BF16),
            pltpu.VMEM((128, tokens), F32),
        ],
    )
    return pl.pallas_call(
        functools.partial(bwd_kernel, blocks),
        grid_spec=spec,
        out_shape=[
            jax.ShapeDtypeStruct((sources, items, local, 384), BF16),
            jax.ShapeDtypeStruct((items, 2, NEAR), F32),
        ],
        compiler_params=pltpu.CompilerParams(vmem_limit_bytes=50 * 2**20),
        cost_estimate=pl.CostEstimate(flops=items * tokens * tokens * 1280, bytes_accessed=items * tokens * 4096, transcendentals=items * tokens * tokens * 2),
        name="attention_backward",
    )(valid, pair, qkv, outs, aug, grads, rows)


VPAD = 384
HALVES = 2
PAIRS = 6
TN = (((0,), (0,)), ((), ()))
SQRT_2_OVER_PI = 0.7978845608028654


def block_masks(masks, first_byte, total_bytes):
    shape = masks.shape[2:]
    conv_at = first_byte - 2 + lax.broadcasted_iota(jnp.int32, shape, 1)
    token = lax.broadcasted_iota(jnp.int32, shape, 0)
    for side in range(2):
        place = first_byte + 2 * token + side
        for size in range(1, 5):
            start = (place // size) * size
            inside = (conv_at >= start) & (conv_at < start + size) & (conv_at < total_bytes)
            masks[side, size - 1] = jnp.where(inside, 1.0 / size, 0.0)


def split_two(values):
    high = values.astype(BF16)
    return high, (values - high.astype(F32)).astype(BF16)


def permute_weight(weight, out):
    rows = weight.shape[0]
    low = lax.broadcasted_iota(jnp.int32, (rows, 128), 1) < 64
    for pair in range(PAIRS):
        at = pair * 384
        one, two, three = (weight[:, at + 128 * k : at + 128 * k + 128] for k in range(3))
        out[:, at : at + 128] = jnp.where(low, one, two)
        out[:, at + 128 : at + 256] = pltpu.roll(jnp.where(low, three, one).astype(F32), 64, 1).astype(BF16)
        out[:, at + 256 : at + 384] = jnp.where(low, two, three)


def front_kernel(
    sizes, half, place_ref, ids_ref, taps_ref, weight_ref, gain_ref, score_ref,
    hidden_ref, normed_ref, conv_ref, mix_ref, share_ref, items_ref, masks, wide, permuted,
):
    local_tokens, window, devices, span = sizes
    step = pl.program_id(0)

    @pl.when(step == 0)
    def _():
        block_masks(masks, place_ref[0], place_ref[1])
        permute_weight(weight_ref, permuted)
        if devices * items_ref.shape[1] > PAIRS * span:
            items_ref[...] = jnp.zeros_like(items_ref)

    together = ids_ref.shape[0]
    score = score_ref[...]
    score_high, score_low = split_two(score)
    row8 = lax.broadcasted_iota(jnp.int32, (16, score.shape[1]), 0)
    score_rows = jnp.where(row8 == 0, score_high.astype(F32), jnp.where(row8 == 1, score_low.astype(F32), 0.0)).astype(BF16)
    lane = lax.broadcasted_iota(jnp.int32, (window, VPAD), 1)
    width = masks.shape[3]
    for one in range(together):
        ids = ids_ref[one]
        conv = jnp.zeros((window, score.shape[1]), F32)
        for tap in range(taps_ref.shape[0]):
            hot = jnp.where(ids[:, tap : tap + 1] == lane, 1.0, 0.0).astype(BF16)
            conv = conv + dot(hot, taps_ref[tap], NN)
        high, low = split_two(conv)
        conv_ref[one, 0:window] = high
        wide[one, 0, 0:window] = high
        wide[one, 1, 0:window] = low
        if width > window:
            wide[one, :, window:width] = jnp.zeros((2, width - window, score.shape[1]), BF16)
            conv_ref[one, window:width] = jnp.zeros((width - window, score.shape[1]), BF16)
        high = wide[one, 0]
        low = wide[one, 1]
        along = jnp.sum(dot(score_rows, high, NT), axis=0, keepdims=True) + dot(score_rows, low, NT)[0:1]
        total = jnp.zeros((local_tokens, width), F32)
        kept = jnp.zeros((local_tokens, 128), F32)
        lane128 = lax.broadcasted_iota(jnp.int32, (local_tokens, 128), 1)
        for side in range(2):
            scores = [jnp.sum(masks[side, k] * along, axis=1, keepdims=True) for k in range(4)]
            top = jnp.maximum(jnp.maximum(scores[0], scores[1]), jnp.maximum(scores[2], scores[3]))
            powers = [jnp.exp(value - top) for value in scores]
            under = 1.0 / (powers[0] + powers[1] + powers[2] + powers[3])
            for k in range(4):
                share = powers[k] * under
                total = total + share * masks[side, k]
                kept = jnp.where(lane128 == 4 * side + k, share, kept)
        share_ref[one] = kept
        mix_high, mix_low = split_two(total * 0.5)
        mix_ref[one] = mix_high
        hidden = dot(mix_high, high, NN) + dot(mix_high, low, NN) + dot(mix_low, high, NN)
        hidden_ref[one] = hidden
        scale = lax.rsqrt(jnp.mean(hidden * hidden, axis=1, keepdims=True) + 1e-06)
        normed_ref[one] = (hidden * scale * gain_ref[...]).astype(BF16)
    normed = normed_ref[...].reshape(together * local_tokens, score.shape[1])
    for pair in range(PAIRS):
        piece = dot(normed, permuted[:, pair * 384 : pair * 384 + 384], NN).astype(BF16)
        for one in range(together):
            item = (step * together + one) * PAIRS + pair
            items_ref[lax.rem(item, devices), item // devices] = piece[one * local_tokens : (one + 1) * local_tokens]


def mid_kernel(
    sizes, order_ref, att_ref, hidden_ref, cot_ref, out_weight_ref, in_weight_ref, down_ref, gain_ref, *refs,
):
    local_tokens, devices, span, aliased = sizes
    refs = refs[aliased:]
    (layer_ref, act_ref, gate_up_ref, normed_ref, attended_ref, branch_ref, residual_ref, items_ref, gain_out, keep_gain) = refs
    step = pl.program_id(0)
    pieces = []
    for pair in range(PAIRS):
        item = step * PAIRS + pair
        pieces.append(att_ref[lax.rem(item, devices), item // devices])
    attended = jnp.concatenate(pieces, axis=1)
    attended_ref[0] = attended
    residual = hidden_ref[0] + dot(attended, out_weight_ref[...], NN)
    gain = gain_ref[...]
    scale = lax.rsqrt(jnp.mean(residual * residual, axis=1, keepdims=True) + 1e-06)
    normed = (residual * scale * gain).astype(BF16)
    normed_ref[0] = normed
    cot = cot_ref[0]
    hidden_units = down_ref.shape[0]
    chunk = 512
    layer = residual
    back = jnp.zeros_like(residual)
    for first in range(0, hidden_units, chunk):
        here = slice(first, first + chunk)
        there = slice(hidden_units + first, hidden_units + first + chunk)
        gate = dot(normed, in_weight_ref[:, here], NN)
        up = dot(normed, in_weight_ref[:, there], NN)
        grad = dot(cot, down_ref[here, :], NT)
        square = gate * gate
        inner = gate * (SQRT_2_OVER_PI + (SQRT_2_OVER_PI * 0.044715) * square)
        curve = jnp.tanh(inner)
        half_plus = 0.5 + 0.5 * curve
        smooth = gate * half_plus
        slope = half_plus + (0.5 * gate) * (1.0 - curve * curve) * (SQRT_2_OVER_PI + (3 * SQRT_2_OVER_PI * 0.044715) * square)
        act = (smooth * up).astype(BF16)
        grad_gate = (grad * up * slope).astype(BF16)
        grad_up = (grad * smooth).astype(BF16)
        act_ref[0, :, here] = act
        gate_up_ref[0, :, here] = grad_gate
        gate_up_ref[0, :, there] = grad_up
        layer = layer + dot(act, down_ref[here, :], NN)
        back = back + dot(grad_gate, in_weight_ref[:, here], NT) + dot(grad_up, in_weight_ref[:, there], NT)
    layer_ref[0] = layer
    weighted = gain * back
    inner_mean = jnp.mean(residual * weighted, axis=1, keepdims=True)
    grad_residual = cot.astype(F32) + scale * weighted - residual * (scale * scale * scale * inner_mean)
    residual_ref[0] = grad_residual
    branch = grad_residual.astype(BF16)
    branch_ref[0] = branch
    grad_attended = dot(branch, out_weight_ref[...], NT).astype(BF16)
    for pair in range(PAIRS):
        item = step * PAIRS + pair
        items_ref[lax.rem(item, devices), item // devices] = grad_attended[:, pair * 128 : pair * 128 + 128]

    @pl.when(step == 0)
    def _():
        keep_gain[...] = jnp.zeros_like(keep_gain)

    keep_gain[...] += jnp.sum((back * residual * scale).reshape(local_tokens // 8, 8, residual.shape[1]), axis=0)
    gain_out[...] = jnp.sum(keep_gain[...], axis=0, keepdims=True)


def back_kernel(
    sizes, place_ref, grads_ref, hidden_ref, residual_ref, conv_ref, mix_ref, share_ref, ids_ref, weight_ref, taps_ref,
    table_ref, gain_ref, score_ref, table_out, small_out, flat_out, masks, permuted, slopes, keep_gain, keep_score,
):
    local_tokens, window, devices, span = sizes
    step = pl.program_id(0)
    model = gain_ref.shape[1]

    @pl.when(step == 0)
    def _():
        block_masks(masks, place_ref[0], place_ref[1])
        permute_weight(weight_ref, permuted)
        keep_gain[...] = jnp.zeros_like(keep_gain)
        keep_score[...] = jnp.zeros_like(keep_score)

    together = hidden_ref.shape[0]
    width = masks.shape[3]
    rows = together * local_tokens
    gathered = []
    for one in range(together):
        pieces = []
        for pair in range(PAIRS):
            item = (step * together + one) * PAIRS + pair
            pieces.append(grads_ref[lax.rem(item, devices), item // devices])
        gathered.append(jnp.concatenate(pieces, axis=1))
    projected = jnp.concatenate(gathered, axis=0)
    flat_out[...] = projected.reshape(flat_out.shape)
    grad_normed = dot(projected, permuted[...], NT)
    hidden = hidden_ref[...].reshape(rows, model)
    gain = gain_ref[...]
    scale = lax.rsqrt(jnp.mean(hidden * hidden, axis=1, keepdims=True) + 1e-06)
    weighted = gain * grad_normed
    inner_mean = jnp.mean(hidden * weighted, axis=1, keepdims=True)
    grad_hidden = residual_ref[...].reshape(rows, model) + scale * weighted - hidden * (scale * scale * scale * inner_mean)
    keep_gain[...] += jnp.sum((grad_normed * hidden * scale).reshape(rows // 8, 8, model), axis=0)
    high, low = split_two(grad_hidden)
    score_high, score_low = split_two(score_ref[...])
    row_at = lax.broadcasted_iota(jnp.int32, (local_tokens, model), 0)
    vector = jnp.broadcast_to(score_ref[...].astype(BF16), (local_tokens, model))
    for one in range(together):
        own = slice(one * local_tokens, (one + 1) * local_tokens)
        conv = conv_ref[one]
        cross = 0.5 * (dot(high[own], conv, NT) + dot(low[own], conv, NT))
        kept = share_ref[one]
        total = jnp.zeros((local_tokens, width), F32)
        for side in range(2):
            shares = [kept[:, 4 * side + k : 4 * side + k + 1] for k in range(4)]
            grads = [jnp.sum(masks[side, k] * cross, axis=1, keepdims=True) for k in range(4)]
            mean = sum(share * grad for share, grad in zip(shares, grads))
            for k in range(4):
                total = total + (shares[k] * (grads[k] - mean)) * masks[side, k]
        column = jnp.sum(total, axis=0, keepdims=True)
        column_high, column_low = split_two(column)
        row16 = lax.broadcasted_iota(jnp.int32, (16, width), 0)
        column_rows = jnp.where(row16 == 0, column_high.astype(F32), jnp.where(row16 == 1, column_low.astype(F32), 0.0)).astype(BF16)
        keep_score[...] += dot(column_rows, conv, NN)
        left = jnp.concatenate([mix_ref[one], total.astype(BF16)], axis=0)
        right = jnp.concatenate([high[own], vector], axis=0)
        slope = dot(left, right, TN)
        slopes[pl.ds((step * together + one) * window, window), :] = slope[0:window].astype(BF16)

    @pl.when(step == pl.num_programs(0) - 1)
    def _():
        count = slopes.shape[0]
        row = lax.broadcasted_iota(jnp.int32, (VPAD, count), 0)
        table_grad = jnp.zeros((VPAD, model), F32)
        table = table_ref[...].astype(F32)
        small_row = lax.broadcasted_iota(jnp.int32, (8, model), 0)
        small = jnp.where(small_row == 5, jnp.sum(keep_gain[...], axis=0, keepdims=True), 0.0)
        small = jnp.where(small_row == 6, jnp.sum(keep_score[...], axis=0, keepdims=True), small)
        for tap in range(taps_ref.shape[0]):
            hot = jnp.where(ids_ref[tap : tap + 1, :] == row, 1.0, 0.0).astype(BF16)
            sums = dot(hot, slopes[...], NN)
            table_grad = table_grad + taps_ref[tap : tap + 1, :] * sums
            small = jnp.where(small_row == tap, jnp.sum(sums * table, axis=0, keepdims=True), small)
        table_out[...] = table_grad
        small_out[...] = small


VMEM_LIMIT = 56 * 2**20


def call_front(half, place, ids, taps, weight, gain, score, local_tokens, devices, per_device):
    span = ids.shape[0]
    window = ids.shape[1]
    width = -(-window // 128) * 128
    model = weight.shape[0]
    together = 2
    whole = lambda *shape: pl.BlockSpec(shape, lambda s, *_: (0,) * len(shape))
    part = lambda *shape: pl.BlockSpec(shape, lambda s, *_: (s,) + (0,) * (len(shape) - 1))
    return pl.pallas_call(
        functools.partial(front_kernel, (local_tokens, window, devices, span), half),
        grid_spec=pltpu.PrefetchScalarGridSpec(
            num_scalar_prefetch=1,
            grid=(span // together,),
            in_specs=[part(together, window, 8), whole(*taps.shape), whole(*weight.shape), whole(1, model), whole(1, model)],
            out_specs=[
                part(together, local_tokens, model),
                part(together, local_tokens, model),
                part(together, width, model),
                part(together, local_tokens, width),
                part(together, local_tokens, 128),
                whole(devices, per_device, local_tokens, 384),
            ],
            scratch_shapes=[
                pltpu.VMEM((2, 4, local_tokens, width), F32),
                pltpu.VMEM((together, 2, width, model), BF16),
                pltpu.VMEM(weight.shape, BF16),
            ],
        ),
        out_shape=[
            jax.ShapeDtypeStruct((span, local_tokens, model), F32),
            jax.ShapeDtypeStruct((span, local_tokens, model), BF16),
            jax.ShapeDtypeStruct((span, width, model), BF16),
            jax.ShapeDtypeStruct((span, local_tokens, width), BF16),
            jax.ShapeDtypeStruct((span, local_tokens, 128), F32),
            jax.ShapeDtypeStruct((devices, per_device, local_tokens, 384), BF16),
        ],
        compiler_params=pltpu.CompilerParams(vmem_limit_bytes=VMEM_LIMIT),
        cost_estimate=pl.CostEstimate(flops=8 * 10**9, bytes_accessed=2 * 10**7, transcendentals=10**5),
        name="front",
    )(place, ids, taps, weight, gain, score)


def call_mid(half, order, att, hidden, cot, out_weight, in_weight, down_weight, gain, before):
    devices, per_device, local_tokens, unused = att.shape
    span, unused, model = hidden.shape
    sequences = cot.shape[0]
    hidden_units = down_weight.shape[0]
    aliased = len(before)
    whole = lambda *shape: pl.BlockSpec(shape, lambda s, *_: (0,) * len(shape))
    moved = lambda lanes: pl.BlockSpec((1, local_tokens, lanes), lambda s, order: (order[half * span + s], 0, 0))
    part = lambda lanes: pl.BlockSpec((1, local_tokens, lanes), lambda s, order: (s, 0, 0))
    full = lambda lanes, kind: jax.ShapeDtypeStruct((sequences, local_tokens, lanes), kind)
    return pl.pallas_call(
        functools.partial(mid_kernel, (local_tokens, devices, span, aliased)),
        grid_spec=pltpu.PrefetchScalarGridSpec(
            num_scalar_prefetch=1,
            grid=(span,),
            in_specs=[
                whole(*att.shape),
                part(model),
                moved(model),
                whole(*out_weight.shape),
                whole(*in_weight.shape),
                whole(*down_weight.shape),
                whole(1, model),
            ]
            + [pl.BlockSpec(memory_space=pl.ANY)] * aliased,
            out_specs=[
                moved(model),
                moved(hidden_units),
                moved(2 * hidden_units),
                moved(model),
                moved(model),
                moved(model),
                part(model),
                whole(*att.shape),
                whole(1, model),
            ],
            scratch_shapes=[pltpu.VMEM((8, model), F32)],
        ),
        out_shape=[
            full(model, F32),
            full(hidden_units, BF16),
            full(2 * hidden_units, BF16),
            full(model, BF16),
            full(model, BF16),
            full(model, BF16),
            jax.ShapeDtypeStruct((span, local_tokens, model), F32),
            jax.ShapeDtypeStruct(att.shape, BF16),
            jax.ShapeDtypeStruct((1, model), F32),
        ],
        input_output_aliases={8 + k: k for k in range(aliased)},
        compiler_params=pltpu.CompilerParams(vmem_limit_bytes=VMEM_LIMIT),
        cost_estimate=pl.CostEstimate(flops=11 * 10**9, bytes_accessed=4 * 10**7, transcendentals=10**6),
        name="middle",
    )(order, att, hidden, cot, out_weight, in_weight, down_weight, gain, *before)


def call_back(place, grads, hidden, residual, conv, mix, share, ids, weight, taps, table, gain, score):
    devices, per_device, local_tokens, unused = grads.shape
    span, unused, model = hidden.shape
    width = conv.shape[1]
    window = ids.shape[1] // span
    together = 2
    whole = lambda *shape: pl.BlockSpec(shape, lambda s, *_: (0,) * len(shape))
    part = lambda *shape: pl.BlockSpec(shape, lambda s, *_: (s,) + (0,) * (len(shape) - 1))
    return pl.pallas_call(
        functools.partial(back_kernel, (local_tokens, window, devices, span)),
        grid_spec=pltpu.PrefetchScalarGridSpec(
            num_scalar_prefetch=1,
            grid=(span // together,),
            in_specs=[
                whole(*grads.shape),
                part(together, local_tokens, model),
                part(together, local_tokens, model),
                part(together, width, model),
                part(together, local_tokens, width),
                part(together, local_tokens, 128),
                whole(*ids.shape),
                whole(*weight.shape),
                whole(*taps.shape),
                whole(*table.shape),
                whole(1, model),
                whole(1, model),
            ],
            out_specs=[whole(VPAD, model), whole(8, model), part(together, local_tokens, PAIRS * 384)],
            scratch_shapes=[
                pltpu.VMEM((2, 4, local_tokens, width), F32),
                pltpu.VMEM(weight.shape, BF16),
                pltpu.VMEM((span * window, model), BF16),
                pltpu.VMEM((8, model), F32),
                pltpu.VMEM((16, model), F32),
            ],
        ),
        out_shape=[
            jax.ShapeDtypeStruct((VPAD, model), F32),
            jax.ShapeDtypeStruct((8, model), F32),
            jax.ShapeDtypeStruct((span, local_tokens, PAIRS * 384), BF16),
        ],
        compiler_params=pltpu.CompilerParams(vmem_limit_bytes=VMEM_LIMIT),
        cost_estimate=pl.CostEstimate(flops=8 * 10**9, bytes_accessed=2 * 10**7, transcendentals=10**5),
        name="back",
    )(place, grads, hidden, residual, conv, mix, share, ids, weight, taps, table, gain, score)


def body(
    byte_ids,
    lengths,
    byte_table,
    conv_kernel,
    score_vector,
    norm_gain_one,
    qkv_weight,
    bias_table,
    out_weight,
    norm_gain_two,
    in_weight,
    down_weight,
    cotangent,
):
    devices = lax.axis_size("seq")
    me = lax.axis_index("seq")
    sequences, local_bytes = byte_ids.shape
    local_tokens = local_bytes // 2
    total_bytes = local_bytes * devices
    first_byte = me * local_bytes
    vocab, model = byte_table.shape
    span = sequences // HALVES
    window = local_bytes + 16
    per_device = -(-span * PAIRS // devices)
    place = jnp.stack([first_byte, jnp.int32(total_bytes)]).astype(jnp.int32)

    number = jnp.arange(sequences, dtype=jnp.int32)
    ahead = (lengths[None, :] > lengths[:, None]) | (
        (lengths[None, :] == lengths[:, None]) & (number[None, :] < number[:, None])
    )
    rank = jnp.sum(ahead.astype(jnp.int32), axis=1)
    placed = rank[None, :] == number[:, None]
    order = jnp.sum(jnp.where(placed, number[None, :], 0), axis=1)
    sorted_lengths = jnp.sum(jnp.where(placed, lengths[None, :], 0), axis=1)
    positions = first_byte + jnp.arange(local_bytes, dtype=jnp.int32)
    picked = jnp.where(positions[None, :] < lengths[:, None], byte_ids, 0)
    forward = [(i, i + 1) for i in range(devices - 1)]
    backward = [(target, source) for source, target in forward]
    before = jnp.where(me > 0, lax.ppermute(picked[:, -4:], "seq", forward), -1)
    after = jnp.where(me < devices - 1, lax.ppermute(picked[:, :4], "seq", backward), -1)
    outside = jnp.full((sequences, 12), -1, jnp.int32)
    extended = jnp.concatenate([before, picked, after, outside], axis=1)
    extended = jnp.sum(jnp.where(placed[:, :, None], extended[None, :, :], 0), axis=1)
    shifted = jnp.stack([extended[:, tap : tap + window] for tap in range(5)])
    ids_columns = jnp.concatenate([jnp.moveaxis(shifted, 0, 2), jnp.full((sequences, window, 3), -1, jnp.int32)], axis=2)

    table_padded = jnp.concatenate([byte_table, jnp.zeros((VPAD - vocab, model), BF16)], axis=0)
    taps = (conv_kernel[:, None, :] * table_padded.astype(F32)[None]).astype(BF16)
    rows = jnp.dot(near_one_hot(), bias_table, precision="highest").T.reshape(PAIRS, 2, NEAR)
    gain_one = norm_gain_one[None, :]
    gain_two = norm_gain_two[None, :]
    score = score_vector[None, :]

    def exchange(items):
        return lax.all_to_all(items, "seq", split_axis=0, concat_axis=0, tiled=True)

    valids, pairs = [], []
    for half in range(HALVES):
        item = me + devices * jnp.arange(per_device, dtype=jnp.int32)
        real = item < span * PAIRS
        at = half * span + item // PAIRS
        length = jnp.sum(jnp.where(at[:, None] == number[None, :], sorted_lengths[None, :], 0), axis=1)
        valids.append(jnp.where(real, (length + 1) // 2, 0).astype(jnp.int32))
        pairs.append(lax.rem(item, PAIRS).astype(jnp.int32))

    fronts, received, outs, augs, returned = [], [], [], [], []
    for half in range(HALVES):
        here = slice(half * span, half * span + span)
        front = call_front(half, place, ids_columns[here], taps, qkv_weight, gain_one, score, local_tokens, devices, per_device)
        fronts.append(front)
        received.append(exchange(front[5]))
    for half in range(HALVES):
        out, aug = attention_forward(received[half], rows, valids[half], pairs[half])
        outs.append(out)
        augs.append(aug)
        returned.append(exchange(out))
    mids, grad_items = [], []
    before_mid = ()
    for half in range(HALVES):
        mid = call_mid(half, order, returned[half], fronts[half][0], cotangent, out_weight, in_weight, down_weight, gain_two, before_mid)
        before_mid = tuple(mid[:6])
        mids.append(mid)
        grad_items.append(exchange(mid[7]))
    layer_out, act, gate_up, normed_two, attended, branch = mids[-1][:6]
    grad_gain_two = mids[0][8] + mids[1][8]
    grad_down = jnp.einsum("bti,btd->id", act, cotangent, preferred_element_type=F32).astype(BF16)
    grad_in = jnp.einsum("btd,bti->di", normed_two, gate_up, preferred_element_type=F32).astype(BF16)
    grad_out = jnp.einsum("btd,bte->de", attended, branch, preferred_element_type=F32).astype(BF16)

    def scatter(grad):
        rows_own = lax.psum_scatter(grad, "seq", scatter_dimension=0, tiled=True)
        return lax.psum_scatter(rows_own, "dp", scatter_dimension=1, tiled=True).astype(F32)

    summed_down = scatter(grad_down)
    summed_in = scatter(grad_in)
    summed_out = scatter(grad_out)
    back_items, bias_rows = [], []
    for half in range(HALVES):
        dqkv, bias_row = attention_backward(received[half], outs[half], augs[half], grad_items[half], rows, valids[half], pairs[half])
        back_items.append(exchange(dqkv))
        bias_rows.append(bias_row)
    backs = []
    for half in range(HALVES):
        hidden, normed, conv, mix, share, unused = fronts[half]
        ids_rows = shifted[:, half * span : half * span + span].reshape(5, span * window)
        backs.append(
            call_back(place, back_items[half], hidden, mids[half][6], conv, mix, share, ids_rows, qkv_weight, conv_kernel, table_padded, gain_one, score)
        )
    normed_all = jnp.concatenate([front[1] for front in fronts], axis=0)
    projected_all = jnp.concatenate([back[2] for back in backs], axis=0)
    grad_qkv = jnp.einsum("btd,bte->de", normed_all, projected_all, preferred_element_type=F32).astype(BF16)
    grad_qkv = jnp.swapaxes(grad_qkv.reshape(model, PAIRS, 3, 2, 64), 2, 3).reshape(model, PAIRS * 384)
    summed_qkv = scatter(grad_qkv)
    item_rows = jnp.concatenate(bias_rows, axis=0)
    item_bias = jnp.einsum("ihy,yb->bih", item_rows, near_one_hot(), precision="highest")
    pair_hot = (jnp.concatenate(pairs)[:, None] == jnp.arange(PAIRS, dtype=jnp.int32)[None, :]).astype(F32)
    grad_bias = jnp.einsum("bih,ip->bph", item_bias, pair_hot, precision="highest").reshape(32, 2 * PAIRS)
    grad_table = (backs[0][0] + backs[1][0])[:vocab]
    small = backs[0][1] + backs[1][1]
    totals = lax.psum((grad_table, small[0:5], small[6], small[5], grad_bias, grad_gain_two[0]), ("dp", "seq"))
    return (
        layer_out,
        totals[0],
        totals[1],
        totals[2],
        totals[3],
        summed_qkv,
        totals[4],
        summed_out,
        totals[5],
        summed_in,
        summed_down,
    )


def solution(mesh):
    return jax.shard_map(
        body,
        mesh=mesh,
        in_specs=(
            P("dp", "seq"),
            P("dp"),
            P(),
            P(),
            P(),
            P(),
            P(),
            P(),
            P(),
            P(),
            P(),
            P(),
            P("dp", "seq", None),
        ),
        out_specs=(
            P("dp", "seq", None),
            P(),
            P(),
            P(),
            P(),
            P("seq", "dp"),
            P(),
            P("seq", "dp"),
            P(),
            P("seq", "dp"),
            P("seq", "dp"),
        ),
        check_vma=False,
    )
```

time: 5550 us -> 632 us (0.11)
  other arithmetic: 1630 us -> 11.8 us
  blocking collectives: 1140 us -> 39.8 us
  starting transfers between devices: 949 us -> 40.4 us
  local copies, waits for them, and re-layouts: 938 us -> 42 us
  matrix products: 513 us -> 31.6 us
  Pallas kernels: 0 us -> 217 us
  loops' own time: 109 us -> 0 us
    reduce_sum x142 -> x4, other arithmetic: 1230 us -> 1.85 us  [the longest x1 0.91 us: body(): rank = jnp.sum(ahead.astype(jnp.int32), axis=1)]
    all_to_all x1 -> x0, blocking collectives: 1100 us -> none  [body(): lax.all_to_all(outputs_low.reshape(item_count, tokens * depth), 'seq', sp...]
    all_to_all x3 -> x8, starting transfers between devices: 940 us -> 36 us  [exchange(): return lax.all_to_all(items, 'seq', split_axis=0, concat_axis=0, tiled=True)]
    dot_general x184 -> x7, matrix products: 513 us -> 31.6 us  [the longest x1 12.2 us: body(): jnp.einsum('btd,bti->di', normed_two, gate_up, preferred_element_type=F32)]
    pallas_call x0 -> x10, Pallas kernels: none -> 217 us  [the longest x2 59.1 us: call_mid(): pl.pallas_call(functools.partial(mid_kernel, (local_tokens, devices, span...]
    dynamic_update_slice x120 -> x0, local copies, waits for them, and re-layouts: 183 us -> none  [the longest x48 78.9 us: body(): lax.map(forward_item, (query_all, key_all, value_all, bias_columns, valid...]
    dynamic_slice x180 -> x0, local copies, waits for them, and re-layouts: 160 us -> none  [the longest x48 42.1 us: attend_item(): outputs, log_totals = lax.map(attend_query_step, firsts)]
    squeeze x99 -> x0, local copies, waits for them, and re-layouts: 153 us -> none  [the longest x96 146 us: body(): lax.map(forward_item, (query_all, key_all, value_all, bias_columns, valid...]
  transfers between devices with their start and end apart: 16 -> 19, of which waited for: 5 -> 11; matrix products, arithmetic and copies ran while one was open for 27% -> 12% of each run, Pallas kernels for 0% -> 31%
where the time goes in v1:
time: 632 us; the launch traced here: 625 us
  waiting for transfers between devices  226 us (36%)
  Pallas kernels  217 us (34%)
  local copies, waits for them, and re-layouts  42 us (7%)
  starting transfers between devices  40.4 us (6%)
  blocking collectives  39.8 us (6%)
  matrix products  31.6 us (5%)
  between operations  16.2 us (3%)
  other arithmetic  11.8 us (2%)
    reduce_scatter x3, waiting for transfers between devices, scatter(): rows_own = lax.psum_scatter(grad, 'seq', scatter_dimension=0, tiled=True)  62.8 us
    pallas_call x2, Pallas kernels, call_mid(): pl.pallas_call(functools.partial(mid_kernel, (local_tokens, devices, span...  59.1 us
    unnamed x12, waiting for transfers between devices  54.6 us
    psum x1, waiting for transfers between devices, body(): lax.psum((grad_table, small[0:5], small[6], small[5], grad_bias, grad_gai...  47.7 us
    pallas_call x2, Pallas kernels, attention_backward(): pl.pallas_call(functools.partial(bwd_kernel, blocks), grid_spec=spec, out...  43.5 us
    pallas_call x2, Pallas kernels, call_back(): pl.pallas_call(functools.partial(back_kernel, (local_tokens, window, devi...  42.7 us
    pallas_call x2, Pallas kernels, call_front(): pl.pallas_call(functools.partial(front_kernel, (local_tokens, window, dev...  42.3 us
    psum x1, blocking collectives, body(): lax.psum((grad_table, small[0:5], small[6], small[5], grad_bias, grad_gai...  39.8 us
  transfers between devices with their start and end apart: 19, of which 11 were waited for; matrix products, arithmetic and copies ran while one was open for 12% of the time, Pallas kernels for 31%

profile of v1, /device:TPU:0, one launch (start us, length us, event | category | flops | bytes accessed | tf_op | source)
XLA Modules:
  0.0 625.5 jit_solution(8130714527876983125)
XLA Ops:
  23.0 21.1 %front.3 = (f32[4,128,768]{2,1,0:T(8,128)}, bf16[4,128,768]{2,1,0:T(8,128)(2,1)}, bf16[4,384,768]{2,1,0:T(8,128)(2,1)}, bf16[4,128,384]{2,1,0:T(8,128)(2,1)}, f3...) custom-call(s32[2]{0:T(128)} %pad_add_fusion.place_ref, s32[4,272,8]{2,1,0:T(8,128)} %get-tuple-element.198.ids_ref, ...), custom_call_target="tpu_custom_call" | custom-call | flops 8000000000 | bytes 20000000 | tf_op jit(solution)/shard_map/front/pallas_call | solution.py:541
  44.2 7.4 %all-to-all-start.2 = ((bf16[8,3,128,384]{3,2,1,0:T(8,128)(2,1)}), bf16[8,3,128,384]{3,2,1,0:T(8,128)(2,1)S(1)}, u32[]{:S(2)}, u32[]{:S(2)}) async-start(bf16[8,3,128,384]{3,2,1,0:T(8,128)(2,1)} %get-tuple-element.58), calls=%async_computation.2 | async-start | bytes 4718592 | tf_op jit(solution)/shard_map/all_to_all | solution.py:733
  51.6 21.2 %front.2 = (f32[4,128,768]{2,1,0:T(8,128)}, bf16[4,128,768]{2,1,0:T(8,128)(2,1)}, bf16[4,384,768]{2,1,0:T(8,128)(2,1)}, bf16[4,128,384]{2,1,0:T(8,128)(2,1)}, f3...) custom-call(s32[2]{0:T(128)} %pad_add_fusion.place_ref, s32[4,272,8]{2,1,0:T(8,128)} %get-tuple-element.199.ids_ref, ...), custom_call_target="tpu_custom_call" | custom-call | flops 8000000000 | bytes 20000000 | tf_op jit(solution)/shard_map/front/pallas_call | solution.py:541
  72.8 8.2 %all-to-all-done.2.qkv_ref = bf16[8,3,128,384]{3,2,1,0:T(8,128)(2,1)S(1)} async-done(((bf16[8,3,128,384]{3,2,1,0:T(8,128)(2,1)}), bf16[8,3,128,384]{3,2,1,0:T(8,128)(2,1)S(1)}, u32[]{:S(2)}, u32[]{:S(2)}) %all-to-all-start.2) | async-done | bytes 2359328 | tf_op jit(solution)/shard_map/all_to_all | solution.py:733
  89.0 18.2 %attention_forward.3 = (bf16[8,3,128,128]{3,2,1,0:T(8,128)(2,1)}, bf16[3,1024,128]{2,1,0:T(8,128)(2,1)S(1)}) custom-call(s32[3]{0:T(128)S(1)} %compare_select_fusion.8.valid_ref, s32[3]{0:T(128)S(1)} %broadcast_remainder_fusion.pair_ref, bf16[8,3,128,384]{3,2,1,0:T(8,128)(2,1)S(1)} %copy-done.4, f32[6,2,1024]{2,1,0:T(2,128)S(1)} %reshape.120.row_ref), custom_call_target="tpu_custom_call" | custom-call | flops 1610612736 | bytes 6291456 | tf_op jit(solution)/shard_map/attention_forward/pallas_call | solution.py:230
  108.1 7.5 %all-to-all-done.qkv_ref = bf16[8,3,128,384]{3,2,1,0:T(8,128)(2,1)S(1)} async-done(((bf16[8,3,128,384]{3,2,1,0:T(8,128)(2,1)}), bf16[8,3,128,384]{3,2,1,0:T(8,128)(2,1)S(1)}, u32[]{:S(2)}, u32[]{:S(2)}) %all-to-all-start) | async-done | bytes 2359328 | tf_op jit(solution)/shard_map/all_to_all | solution.py:733
  115.6 4.2 all-to-all-start.3
  120.4 11.4 %attention_forward.2 = (bf16[8,3,128,128]{3,2,1,0:T(8,128)(2,1)}, bf16[3,1024,128]{2,1,0:T(8,128)(2,1)S(1)}) custom-call(s32[3]{0:T(128)S(1)} %compare_select_fusion.9.valid_ref, s32[3]{0:T(128)S(1)} %broadcast_remainder_fusion.pair_ref, bf16[8,3,128,384]{3,2,1,0:T(8,128)(2,1)S(1)} %all-to-all-done.qkv_ref, f32[6,2,1024]{2,1,0:T(2,128)S(1)} %reshape.120.row_ref), custom_call_target="tpu_custom_call" | custom-call | flops 1610612736 | bytes 6291456 | tf_op jit(solution)/shard_map/attention_forward/pallas_call | solution.py:230
  136.5 29.5 %middle.2 = (f32[8,128,768]{2,1,0:T(8,128)}, bf16[8,128,2048]{2,1,0:T(8,128)(2,1)}, bf16[8,128,4096]{2,1,0:T(8,128)(2,1)}, bf16[8,128,768]{2,1,0:T(8,128)(2,1)},...) custom-call(s32[8]{0:T(128)} %get-tuple-element.192.order_ref, ...), custom_call_target="tpu_custom_call" | custom-call | flops 11000000512 | bytes 40000000 | tf_op jit(solution)/shard_map/middle/pallas_call | solution.py:585
  166.0 4.2 all-to-all-start.4
  170.2 29.6 %middle.3 = (f32[8,128,768]{2,1,0:T(8,128)}, bf16[8,128,2048]{2,1,0:T(8,128)(2,1)}, bf16[8,128,4096]{2,1,0:T(8,128)(2,1)}, bf16[8,128,768]{2,1,0:T(8,128)(2,1)},...) custom-call(s32[8]{0:T(128)} %get-tuple-element.192.order_ref, ...), custom_call_target="tpu_custom_call", output_to_operand_aliasing={{0}: (8, {}), {1}: (9, {}), {2}: (10, {}), {3}: (11, {}), {... | custom-call | flops 11000000512 | bytes 40000000 | tf_op jit(solution)/shard_map/middle/pallas_call | solution.py:585
  199.8 4.2 all-to-all-start.6
  204.2 4.3 bitcast_convert_fusion.3
  209.7 26.2 %attention_backward.2 = (bf16[8,3,128,384]{3,2,1,0:T(8,128)(2,1)}, f32[3,2,1024]{2,1,0:T(2,128)S(1)}) custom-call(s32[3]{0:T(128)S(1)} %compare_select_fusion.8.valid_ref, s32[3]{0:T(128)S(1)} %broadcast_remainder_fusion.pair_ref, bf16[8,3,128,384]{3,2,1,0:T(8,128)(2,1)} %copy-done.3, bf16[8,3,128,128]{3,2,1,0:T(8,128)(2,1)} %get-tuple-element.59.out_ref, ...), custom_call_target="tpu_custom_call" | custom-call | flops 4026531840 | bytes 12582912 | tf_op jit(solution)/shard_map/attention_backward/pallas_call | solution.py:276
  235.9 4.5 all-to-all-start.5
  240.5 7.5 %bitcast_convert_fusion.2 = bf16[2048,768]{1,0:T(8,128)(2,1)} fusion(bf16[8,128,2048]{2,1,0:T(8,128)(2,1)} %get-tuple-element.98, bf16[8,128,768]{2,1,0:T(8,128)(2,1)S(1)} %copy-done.18), kind=kOutput, calls=%fused_computation.2 | convolution fusion | flops 3222798336 | bytes 8912896 | tf_op jit(solution)/shard_map/bti,btd->id/dot_general | solution.py:764
  248.0 17.3 %attention_backward.3 = (bf16[8,3,128,384]{3,2,1,0:T(8,128)(2,1)}, f32[3,2,1024]{2,1,0:T(2,128)S(1)}) custom-call(s32[3]{0:T(128)S(1)} %compare_select_fusion.9.valid_ref, s32[3]{0:T(128)S(1)} %broadcast_remainder_fusion.pair_ref, bf16[8,3,128,384]{3,2,1,0:T(8,128)(2,1)} %copy-done.2, bf16[8,3,128,128]{3,2,1,0:T(8,128)(2,1)} %get-tuple-element.56.out_ref, ...), custom_call_target="tpu_custom_call" | custom-call | flops 4026531840 | bytes 12582912 | tf_op jit(solution)/shard_map/attention_backward/pallas_call | solution.py:276
  265.4 6.1 all-to-all-done.5.grads_ref
  276.8 21.0 %back.2 = (f32[384,768]{1,0:T(8,128)}, f32[8,768]{1,0:T(8,128)}, bf16[4,128,2304]{2,1,0:T(8,128)(2,1)}) custom-call(s32[2]{0:T(128)} %pad_add_fusion.place_ref, bf16[8,3,128,384]{3,2,1,0:T(8,128)(2,1)} %all-to-all-done.5.grads_ref, f32[4,128,768]{2,1,0:T(8,128)} %get-tuple-element.60.hidden_ref, f32[4,128,768]{2,1,0:T(8,128)} %get-tuple-element.71.residual_ref, ...), custom_call_target="tpu_custom_call" | custom-call | flops 8000000000 | bytes 20000000 | tf_op jit(solution)/shard_map/back/pallas_call | solution.py:639
  297.8 15.1 %all-to-all-done.7.grads_ref = bf16[8,3,128,384]{3,2,1,0:T(8,128)(2,1)S(1)} async-done(((bf16[8,3,128,384]{3,2,1,0:T(8,128)(2,1)}), bf16[8,3,128,384]{3,2,1,0:T(8,128)(2,1)S(1)}, u32[]{:S(2)}, u32[]{:S(2)}) %all-to-all-start.7) | async-done | bytes 2359328 | tf_op jit(solution)/shard_map/all_to_all | solution.py:733
  314.3 21.7 %back.3 = (f32[384,768]{1,0:T(8,128)}, f32[8,768]{1,0:T(8,128)}, bf16[4,128,2304]{2,1,0:T(8,128)(2,1)}) custom-call(s32[2]{0:T(128)} %pad_add_fusion.place_ref, bf16[8,3,128,384]{3,2,1,0:T(8,128)(2,1)} %copy-done.7, f32[4,128,768]{2,1,0:T(8,128)} %get-tuple-element.57.hidden_ref, f32[4,128,768]{2,1,0:T(8,128)} %get-tuple-element.79.residual_ref, ...), custom_call_target="tpu_custom_call" | custom-call | flops 8000000000 | bytes 20000000 | tf_op jit(solution)/shard_map/back/pallas_call | solution.py:639
  336.1 7.0 %bitcast_convert_fusion.1 = bf16[768,2304]{1,0:T(8,128)(2,1)} fusion(bf16[4,128,2304]{2,1,0:T(8,128)(2,1)} %get-tuple-element.89, bf16[4,128,2304]{2,1,0:T(8,128)(2,1)S(1)} %copy-done.20, bf16[4,128,768]{2,1,0:T(8,128)(2,1)S(1)} %copy-done.22, bf16[4,128,768]{2,1,0:T(8,128)(2,1)S(1)} %copy-done.21), kind=kOutput, calls=%fused_computation.1 | convolution fusion | flops 3628793856 | bytes 9830400 | tf_op jit(solution)/shard_map/btd,bte->de/dot_general | solution.py:789
  343.1 5.8 copy.135
  348.9 4.1 copy.136
  353.1 5.8 copy.148
  360.3 12.2 %bitcast_convert_fusion = bf16[768,4096]{1,0:T(8,128)(2,1)} fusion(bf16[8,128,768]{2,1,0:T(8,128)(2,1)S(1)} %copy-done.19, bf16[8,128,4096]{2,1,0:T(8,128)(2,1)} %get-tuple-element.97), kind=kOutput, calls=%fused_computation | convolution fusion | flops 6445596672 | bytes 16252928 | tf_op jit(solution)/shard_map/btd,bti->di/dot_general | solution.py:765
  376.7 33.8 %reduce-scatter.25.cloned.1.call-done = bf16[96,2304]{1,0:T(8,128)(2,1)} async-done(((bf16[768,2304]{1,0:T(8,128)(2,1)}), bf16[96,2304]{1,0:T(8,128)(2,1)}) %reduce-scatter.25.cloned.1.call-update) | async-done | bytes 442384
  412.7 62.8 %reduce-scatter.19.cloned.1.call-done = bf16[96,4096]{1,0:T(8,128)(2,1)} async-done(((bf16[768,4096]{1,0:T(8,128)(2,1)}), bf16[96,4096]{1,0:T(8,128)(2,1)}) %reduce-scatter.19.cloned.1.call-update) | async-done | bytes 786448 | tf_op jit(solution)/shard_map/reduce_scatter | solution.py:769
  477.0 20.6 %reduce-scatter.27.cloned.1.call-done = bf16[192,96]{1,0:T(8,128)(2,1)} async-done(((bf16[768,96]{1,0:T(8,128)(2,1)}), bf16[192,96]{1,0:T(8,128)(2,1)}) %reduce-scatter.27.cloned.1.call-update) | async-done | bytes 36880
  499.3 39.8 %all-reduce.2 = (f32[5,768]{1,0:T(8,128)}, f32[768]{0:T(1024)}, f32[768]{0:T(1024)}, f32[32,12]{0,1:T(8,128)}, f32[768]{0:T(1024)}) all-reduce(f32[5,768]{1,0:T(8,128)S(1)} %bitcast.65, f32[768]{0:T(1024)S(1)} %get-tuple-element.188, f32[768]{0:T(1024)S(1)} %get-tuple-element.187, ...), channel_id=1, replica_groups=mesh['dp'=4,'seq'=8] {'dp','seq'}, use_global_device_ids=true, to_apply=%region_7.8 | all-reduce | flops 6528 | bytes 52224 | tf_op jit(solution)/shard_map/psum | solution.py:798
  543.7 22.6 %reduce-scatter.21.cloned.1.call-done = bf16[96,1024]{1,0:T(8,128)(2,1)} async-done(((bf16[96,4096]{1,0:T(8,128)(2,1)}), bf16[96,1024]{1,0:T(8,128)(2,1)}) %reduce-scatter.21.cloned.1.call-update) | async-done | bytes 196624 | tf_op jit(solution)/shard_map/reduce_scatter | solution.py:770
  568.0 47.7 %all-reduce.5.cloned.1.call-done = f32[259,768]{1,0:T(8,128)} async-done(((f32[259,768]{1,0:T(8,128)}), f32[259,768]{1,0:T(8,128)}) %all-reduce.5.cloned.1.call-update) | async-done | bytes 795664 | tf_op jit(solution)/shard_map/psum | solution.py:798
  (135 shorter events, 56.4 us)
Async XLA Ops:
  8.0 78.2 %copy-start = (f32[32,12]{0,1:T(8,128)S(1)}, f32[32,12]{0,1:T(8,128)}, u32[]{:S(2)}) copy-start(f32[32,12]{0,1:T(8,128)} %param.20) | copy-start | bytes 4612
  8.9 12.1 %collective-permute-start = (s32[8,4]{1,0:T(8,128)S(1)}, s32[8,4]{1,0:T(8,128)S(1)}, u32[]{:S(2)}, u32[]{:S(2)}) collective-permute-start(s32[8,4]{1,0:T(8,128)S(1)} %get-tuple-element.204), channel_id=1, source_target_pairs={{0,1},{1,2},{2,3},{3,4},{4,5},{5,6},{6,7},{8,9},{9,10},{10,11},{11... | collective-permute-start | bytes 392 | tf_op jit(solution)/shard_map/ppermute | solution.py:717
  11.2 9.8 %collective-permute-start.1 = (s32[8,4]{1,0:T(8,128)S(1)}, s32[8,4]{1,0:T(8,128)S(1)}, u32[]{:S(2)}, u32[]{:S(2)}) collective-permute-start(s32[8,4]{1,0:T(8,128)S(1)} %get-tuple-element.205), channel_id=1, source_target_pairs={{1,0},{2,1},{3,2},{4,3},{5,4},{6,5},{7,6},{9,8},{10,9},{11,10},{12... | collective-permute-start | bytes 392 | tf_op jit(solution)/shard_map/ppermute | solution.py:718
  44.2 36.8 %all-to-all-start.2 = ((bf16[8,3,128,384]{3,2,1,0:T(8,128)(2,1)}), bf16[8,3,128,384]{3,2,1,0:T(8,128)(2,1)S(1)}, u32[]{:S(2)}, u32[]{:S(2)}) async-start(bf16[8,3,128,384]{3,2,1,0:T(8,128)(2,1)} %get-tuple-element.58), calls=%async_computation.2 | async-start | bytes 4718592 | tf_op jit(solution)/shard_map/all_to_all | solution.py:733
  82.5 33.1 %all-to-all-start = ((bf16[8,3,128,384]{3,2,1,0:T(8,128)(2,1)}), bf16[8,3,128,384]{3,2,1,0:T(8,128)(2,1)S(1)}, u32[]{:S(2)}, u32[]{:S(2)}) async-start(bf16[8,3,128,384]{3,2,1,0:T(8,128)(2,1)} %get-tuple-element.55), calls=%async_computation | async-start | bytes 4718592 | tf_op jit(solution)/shard_map/all_to_all | solution.py:733
  89.0 30.8 %copy-start.14 = (f32[768]{0:T(1024)S(1)}, f32[768]{0:T(1024)}, u32[]{:S(2)}) copy-start(f32[768]{0:T(1024)} %param.22) | copy-start | bytes 9220
  115.6 16.2 %copy-start.2 = (bf16[8,3,128,384]{3,2,1,0:T(8,128)(2,1)}, bf16[8,3,128,384]{3,2,1,0:T(8,128)(2,1)S(1)}, u32[]{:S(2)}) copy-start(bf16[8,3,128,384]{3,2,1,0:T(8,128)(2,1)S(1)} %all-to-all-done.qkv_ref) | copy-start | bytes 7077892
  115.6 16.8 %all-to-all-start.3 = ((bf16[8,3,128,128]{3,2,1,0:T(8,128)(2,1)}), bf16[8,3,128,128]{3,2,1,0:T(8,128)(2,1)}, u32[]{:S(2)}, u32[]{:S(2)}) async-start(bf16[8,3,128,128]{3,2,1,0:T(8,128)(2,1)} %get-tuple-element.59.out_ref), calls=%async_computation.3 | async-start | bytes 1572864 | tf_op jit(solution)/shard_map/all_to_all | solution.py:733
  132.4 33.6 %all-to-all-start.1 = ((bf16[8,3,128,128]{3,2,1,0:T(8,128)(2,1)}), bf16[8,3,128,128]{3,2,1,0:T(8,128)(2,1)S(1)}, u32[]{:S(2)}, u32[]{:S(2)}) async-start(bf16[8,3,128,128]{3,2,1,0:T(8,128)(2,1)} %get-tuple-element.56.out_ref), calls=%async_computation.1 | async-start | bytes 1572864 | tf_op jit(solution)/shard_map/all_to_all | solution.py:733
  166.0 33.8 %all-to-all-start.4 = ((bf16[8,3,128,128]{3,2,1,0:T(8,128)(2,1)}), bf16[8,3,128,128]{3,2,1,0:T(8,128)(2,1)S(1)}, u32[]{:S(2)}, u32[]{:S(2)}) async-start(bf16[8,3,128,128]{3,2,1,0:T(8,128)(2,1)} %get-tuple-element.69), calls=%async_computation.4 | async-start | bytes 1572864 | tf_op jit(solution)/shard_map/all_to_all | solution.py:733
  199.8 36.1 %all-to-all-start.6 = ((bf16[8,3,128,128]{3,2,1,0:T(8,128)(2,1)}), bf16[8,3,128,128]{3,2,1,0:T(8,128)(2,1)S(1)}, u32[]{:S(2)}, u32[]{:S(2)}) async-start(bf16[8,3,128,128]{3,2,1,0:T(8,128)(2,1)} %get-tuple-element.77), calls=%async_computation.6 | async-start | bytes 1572864 | tf_op jit(solution)/shard_map/all_to_all | solution.py:733
  204.0 168.6 %reduce-scatter.17.cloned.1.call-start = ((), (), s32[]{:S(2)}) async-start(), calls=%async_computation.18 | async-start | bytes 1327104 | tf_op jit(solution)/shard_map/reduce_scatter | solution.py:769
  235.9 35.6 %all-to-all-start.5 = ((bf16[8,3,128,384]{3,2,1,0:T(8,128)(2,1)}), bf16[8,3,128,384]{3,2,1,0:T(8,128)(2,1)}, u32[]{:S(2)}, u32[]{:S(2)}) async-start(bf16[8,3,128,384]{3,2,1,0:T(8,128)(2,1)} %get-tuple-element.70), calls=%async_computation.5 | async-start | bytes 4718592 | tf_op jit(solution)/shard_map/all_to_all | solution.py:733
  240.4 134.2 %reduce-scatter.23.cloned.1.call-start = ((), (), s32[]{:S(2)}) async-start(), calls=%async_computation.21 | async-start | bytes 3538944 | tf_op jit(solution)/shard_map/reduce_scatter | solution.py:769
  271.5 41.4 %all-to-all-start.7 = ((bf16[8,3,128,384]{3,2,1,0:T(8,128)(2,1)}), bf16[8,3,128,384]{3,2,1,0:T(8,128)(2,1)S(1)}, u32[]{:S(2)}, u32[]{:S(2)}) async-start(bf16[8,3,128,384]{3,2,1,0:T(8,128)(2,1)} %get-tuple-element.78), calls=%async_computation.7 | async-start | bytes 4718592 | tf_op jit(solution)/shard_map/all_to_all | solution.py:733
  275.1 135.3 %reduce-scatter.25.cloned.1.call-start = ((), (), s32[]{:S(2)}) async-start(), calls=%async_computation.22 | async-start | bytes 3981312
  314.3 21.7 %copy-start.20 = (bf16[4,128,2304]{2,1,0:T(8,128)(2,1)S(1)}, bf16[4,128,2304]{2,1,0:T(8,128)(2,1)}, u32[]{:S(2)}) copy-start(bf16[4,128,2304]{2,1,0:T(8,128)(2,1)} %get-tuple-element.88) | copy-start | bytes 7077892
  314.3 21.7 %copy-start.21 = (bf16[4,128,768]{2,1,0:T(8,128)(2,1)S(1)}, bf16[4,128,768]{2,1,0:T(8,128)(2,1)}, u32[]{:S(2)}) copy-start(bf16[4,128,768]{2,1,0:T(8,128)(2,1)} %get-tuple-element.86) | copy-start | bytes 2359300
  314.3 21.8 %copy-start.22 = (bf16[4,128,768]{2,1,0:T(8,128)(2,1)S(1)}, bf16[4,128,768]{2,1,0:T(8,128)(2,1)}, u32[]{:S(2)}) copy-start(bf16[4,128,768]{2,1,0:T(8,128)(2,1)} %get-tuple-element.87) | copy-start | bytes 2359300
  358.9 116.5 %reduce-scatter.19.cloned.1.call-start = ((), (), s32[]{:S(2)}) async-start(), calls=%async_computation.19 | async-start | bytes 7077888 | tf_op jit(solution)/shard_map/reduce_scatter | solution.py:769
  372.5 103.1 %copy-start.15 = (f32[1,768]{1,0:T(1,128)S(1)}, f32[1,768]{1,0:T(1,128)}, u32[]{:S(2)}) copy-start(f32[1,768]{1,0:T(1,128)} %get-tuple-element.94) | copy-start | bytes 9220
  372.5 103.1 %copy-start.16 = (f32[1,768]{1,0:T(1,128)S(1)}, f32[1,768]{1,0:T(1,128)}, u32[]{:S(2)}) copy-start(f32[1,768]{1,0:T(1,128)} %get-tuple-element.95) | copy-start | bytes 9220
  372.5 103.1 %copy-start.9 = (f32[384,768]{1,0:T(8,128)S(1)}, f32[384,768]{1,0:T(8,128)}, u32[]{:S(2)}) copy-start(f32[384,768]{1,0:T(8,128)} %get-tuple-element.75) | copy-start | bytes 3538948
  372.5 103.1 %copy-start.10 = (f32[384,768]{1,0:T(8,128)S(1)}, f32[384,768]{1,0:T(8,128)}, u32[]{:S(2)}) copy-start(f32[384,768]{1,0:T(8,128)} %get-tuple-element.83) | copy-start | bytes 3538948
  372.6 125.1 %reduce-scatter.27.cloned.1.call-start = ((), (), s32[]{:S(2)}) async-start(), calls=%async_computation.23 | async-start | bytes 245760
  374.6 164.5 %reduce-scatter.29.cloned.1.call-start = ((), (), s32[]{:S(2)}) async-start(), calls=%async_computation.24 | async-start | bytes 491520
  376.6 165.4 %reduce-scatter.15.cloned.1.call-start = ((), (), s32[]{:S(2)}) async-start(), calls=%async_computation.17 | async-start | bytes 737280 | tf_op jit(solution)/shard_map/reduce_scatter | solution.py:770
  412.6 86.6 %copy-start.11 = (f32[8,768]{1,0:T(8,128)S(1)}, f32[8,768]{1,0:T(8,128)}, u32[]{:S(2)}) copy-start(f32[8,768]{1,0:T(8,128)} %get-tuple-element.84) | copy-start | bytes 73732
  412.6 86.6 %copy-start.12 = (f32[8,768]{1,0:T(8,128)S(1)}, f32[8,768]{1,0:T(8,128)}, u32[]{:S(2)}) copy-start(f32[8,768]{1,0:T(8,128)} %get-tuple-element.85) | copy-start | bytes 73732
  412.6 153.7 %reduce-scatter.21.cloned.1.call-start = ((), (), s32[]{:S(2)}) async-start(), calls=%async_computation.20 | async-start | bytes 983040 | tf_op jit(solution)/shard_map/reduce_scatter | solution.py:770
  475.5 140.3 %all-reduce.5.cloned.1.call-start = ((), (), s32[]{:S(2)}) async-start(), calls=%async_computation.16 | async-start | bytes 1622016 | tf_op jit(solution)/shard_map/psum | solution.py:798
  475.7 142.1 %copy-start.1 = (f32[32,12]{0,1:T(8,128)S(1)}, f32[32,12]{0,1:T(8,128)}, u32[]{:S(2)}) copy-start(f32[32,12]{0,1:T(8,128)} %param.20) | copy-start | bytes 4612
  (10 other events, 24.4 us)
Sparse Core Ops, SparseCore 0:
  208.7 44.1 reduce-scatter.16
  256.6 69.3 reduce-scatter.22
  359.0 51.3 reduce-scatter.24
  413.7 61.7 reduce-scatter.18
  478.2 19.3 reduce-scatter.26
  500.4 18.8 reduce-scatter.28
  521.7 20.3 reduce-scatter.14
  544.4 21.8 reduce-scatter.20
Sparse Core Ops, SparseCore 1:
  481.8 133.9 all-reduce.4

commit v2 on v1

--- a/solution.py
+++ b/solution.py
@@ -118,7 +118,7 @@
 
 
 def bwd_kernel(
-    blocks, valid_ref, pair_ref, qkv_ref, out_ref, aug_ref, grad_ref, row_ref,
+    blocks, valid_ref, pair_ref, qkv_ref, out_ref, aug_ref, grad_ref, row_ref, after,
     dqkv_ref, bias_ref, qa, ka, va, ga, kt, strip, tally, probs, slopes, dq,
 ):
     item = pl.program_id(0)
@@ -240,7 +240,7 @@
     )(valid, pair, qkv, rows)
 
 
-def attention_backward(qkv, outs, aug, grads, rows, valid, pair):
+def attention_backward(qkv, outs, aug, grads, rows, valid, pair, after):
     sources, items, local, unused = qkv.shape
     blocks = sources * local // KB
     tokens = sources * local
@@ -255,6 +255,7 @@
             pl.BlockSpec((1, tokens, 128), lambda i, v, p: (i, 0, 0)),
             big(128),
             pl.BlockSpec((1, 2, NEAR), lambda i, v, p: (p[i], 0, 0)),
+            pl.BlockSpec(memory_space=pl.ANY),
         ],
         out_specs=[
             big(384),
@@ -283,11 +284,10 @@
         compiler_params=pltpu.CompilerParams(vmem_limit_bytes=50 * 2**20),
         cost_estimate=pl.CostEstimate(flops=items * tokens * tokens * 1280, bytes_accessed=items * tokens * 4096, transcendentals=items * tokens * tokens * 2),
         name="attention_backward",
-    )(valid, pair, qkv, outs, aug, grads, rows)
+    )(valid, pair, qkv, outs, aug, grads, rows, after)
 
 
 VPAD = 384
-HALVES = 2
 PAIRS = 6
 TN = (((0,), (0,)), ((), ()))
 SQRT_2_OVER_PI = 0.7978845608028654
@@ -321,44 +321,117 @@
         out[:, at + 256 : at + 384] = jnp.where(low, two, three)
 
 
+def greet(axis, here, count):
+    barrier = pltpu.get_barrier_semaphore()
+
+    def signal(step, unused):
+        pl.semaphore_signal(barrier, inc=1, device_id={axis: lax.rem(here + step, count)}, device_id_type=pl.DeviceIdType.MESH)
+        return unused
+
+    lax.fori_loop(1, count, signal, 0)
+
+
+def item_copy(devices, me, source, target, other, slot, sems):
+    send, recv, unused = sems
+
+    def outward():
+        offset = lax.rem(other - me + devices, devices)
+        return pltpu.make_async_remote_copy(
+            src_ref=source, dst_ref=target, send_sem=send.at[offset, slot], recv_sem=recv.at[offset, slot],
+            device_id={"seq": other}, device_id_type=pl.DeviceIdType.MESH,
+        )
+
+    def inward():
+        offset = lax.rem(me - other + devices, devices)
+        return pltpu.make_async_remote_copy(
+            src_ref=source, dst_ref=target, send_sem=send.at[offset, slot], recv_sem=recv.at[offset, slot],
+            device_id={"seq": other}, device_id_type=pl.DeviceIdType.MESH,
+        )
+
+    return outward, inward
+
+
+def start_item(devices, me, source, target, other, slot, sems):
+    @pl.when(other == me)
+    def _():
+        pltpu.make_async_copy(source, target, sems[2].at[slot]).start()
+
+    @pl.when(other != me)
+    def _():
+        item_copy(devices, me, source, target, other, slot, sems)[0]().start()
+
+
+def finish_sends(devices, me, total, source_of, target_of, sems):
+    def wait(item, unused):
+        other, slot = lax.rem(item, devices), item // devices
+
+        @pl.when(other != me)
+        def _():
+            item_copy(devices, me, source_of(other, slot), target_of(other, slot), other, slot, sems)[0]().wait_send()
+
+        return unused
+
+    lax.fori_loop(0, total, wait, 0)
+
+
+def finish_receives(devices, me, total, source_of, target_of, sems):
+    per_device = -(-total // devices)
+
+    def wait(at, unused):
+        other, slot = at // per_device, lax.rem(at, per_device)
+
+        @pl.when((slot * devices + me < total) & (other != me))
+        def _():
+            item_copy(devices, me, source_of(other, slot), target_of(other, slot), other, slot, sems)[1]().wait_recv()
+
+        @pl.when((slot * devices + me < total) & (other == me))
+        def _():
+            pltpu.make_async_copy(source_of(other, slot), target_of(other, slot), sems[2].at[slot]).wait()
+
+        return unused
+
+    lax.fori_loop(0, devices * per_device, wait, 0)
+
+
 def front_kernel(
-    sizes, half, place_ref, ids_ref, taps_ref, weight_ref, gain_ref, score_ref,
-    hidden_ref, normed_ref, conv_ref, mix_ref, share_ref, items_ref, masks, wide, permuted,
+    sizes, ids_ref, taps_ref, weight_ref, gain_ref, score_ref,
+    hidden_ref, normed_ref, conv_ref, mix_ref, share_ref, items_ref, masks, wide, permuted, stage, *sems,
 ):
-    local_tokens, window, devices, span = sizes
+    local_tokens, window, devices, total = sizes
     step = pl.program_id(0)
+    me = lax.axis_index("seq")
 
     @pl.when(step == 0)
     def _():
-        block_masks(masks, place_ref[0], place_ref[1])
+        greet("seq", me, devices)
+        block_masks(masks, me * 2 * local_tokens, devices * 2 * local_tokens)
         permute_weight(weight_ref, permuted)
-        if devices * items_ref.shape[1] > PAIRS * span:
-            items_ref[...] = jnp.zeros_like(items_ref)
 
     together = ids_ref.shape[0]
     score = score_ref[...]
+    model = score.shape[1]
     score_high, score_low = split_two(score)
-    row8 = lax.broadcasted_iota(jnp.int32, (16, score.shape[1]), 0)
-    score_rows = jnp.where(row8 == 0, score_high.astype(F32), jnp.where(row8 == 1, score_low.astype(F32), 0.0)).astype(BF16)
-    lane = lax.broadcasted_iota(jnp.int32, (window, VPAD), 1)
+    row16 = lax.broadcasted_iota(jnp.int32, (16, model), 0)
+    score_rows = jnp.where(row16 == 0, score_high.astype(F32), jnp.where(row16 == 1, score_low.astype(F32), 0.0)).astype(BF16)
+    lane = lax.broadcasted_iota(jnp.int32, (together * window, VPAD), 1)
     width = masks.shape[3]
+    ids = ids_ref[...].reshape(together * window, 8)
+    conv_all = jnp.zeros((together * window, model), F32)
+    for tap in range(taps_ref.shape[0]):
+        hot = jnp.where(ids[:, tap : tap + 1] == lane, 1.0, 0.0).astype(BF16)
+        conv_all = conv_all + dot(hot, taps_ref[tap], NN)
     for one in range(together):
-        ids = ids_ref[one]
-        conv = jnp.zeros((window, score.shape[1]), F32)
-        for tap in range(taps_ref.shape[0]):
-            hot = jnp.where(ids[:, tap : tap + 1] == lane, 1.0, 0.0).astype(BF16)
-            conv = conv + dot(hot, taps_ref[tap], NN)
-        high, low = split_two(conv)
+        high, low = split_two(conv_all[one * window : (one + 1) * window])
         conv_ref[one, 0:window] = high
         wide[one, 0, 0:window] = high
         wide[one, 1, 0:window] = low
         if width > window:
-            wide[one, :, window:width] = jnp.zeros((2, width - window, score.shape[1]), BF16)
-            conv_ref[one, window:width] = jnp.zeros((width - window, score.shape[1]), BF16)
+            wide[one, :, window:width] = jnp.zeros((2, width - window, model), BF16)
+            conv_ref[one, window:width] = jnp.zeros((width - window, model), BF16)
         high = wide[one, 0]
         low = wide[one, 1]
         along = jnp.sum(dot(score_rows, high, NT), axis=0, keepdims=True) + dot(score_rows, low, NT)[0:1]
-        total = jnp.zeros((local_tokens, width), F32)
+        mixed = jnp.zeros((local_tokens, width), F32)
         kept = jnp.zeros((local_tokens, 128), F32)
         lane128 = lax.broadcasted_iota(jnp.int32, (local_tokens, 128), 1)
         for side in range(2):
@@ -368,42 +441,92 @@
             under = 1.0 / (powers[0] + powers[1] + powers[2] + powers[3])
             for k in range(4):
                 share = powers[k] * under
-                total = total + share * masks[side, k]
+                mixed = mixed + share * masks[side, k]
                 kept = jnp.where(lane128 == 4 * side + k, share, kept)
         share_ref[one] = kept
-        mix_high, mix_low = split_two(total * 0.5)
+        mix_high, mix_low = split_two(mixed * 0.5)
         mix_ref[one] = mix_high
         hidden = dot(mix_high, high, NN) + dot(mix_high, low, NN) + dot(mix_low, high, NN)
         hidden_ref[one] = hidden
         scale = lax.rsqrt(jnp.mean(hidden * hidden, axis=1, keepdims=True) + 1e-06)
         normed_ref[one] = (hidden * scale * gain_ref[...]).astype(BF16)
-    normed = normed_ref[...].reshape(together * local_tokens, score.shape[1])
+    normed = normed_ref[...].reshape(together * local_tokens, model)
+
+    @pl.when(step == 0)
+    def _():
+        pl.semaphore_wait(pltpu.get_barrier_semaphore(), devices - 1)
+
     for pair in range(PAIRS):
         piece = dot(normed, permuted[:, pair * 384 : pair * 384 + 384], NN).astype(BF16)
         for one in range(together):
             item = (step * together + one) * PAIRS + pair
-            items_ref[lax.rem(item, devices), item // devices] = piece[one * local_tokens : (one + 1) * local_tokens]
+            other, slot = lax.rem(item, devices), item // devices
+            stage[other, slot] = piece[one * local_tokens : (one + 1) * local_tokens]
+            start_item(devices, me, stage.at[other, slot], items_ref.at[me, slot], other, slot, sems)
+
+    @pl.when(step == pl.num_programs(0) - 1)
+    def _():
+        finish_sends(devices, me, total, lambda other, slot: stage.at[other, slot], lambda other, slot: items_ref.at[me, slot], sems)
+        finish_receives(devices, me, total, lambda other, slot: stage.at[other, slot], lambda other, slot: items_ref.at[other, slot], sems)
 
 
 def mid_kernel(
-    sizes, order_ref, att_ref, hidden_ref, cot_ref, out_weight_ref, in_weight_ref, down_ref, gain_ref, *refs,
+    sizes, att_ref, hidden_ref, cot_ref, out_weight_ref, in_weight_ref, down_ref, gain_ref,
+    layer_ref, act_ref, gate_up_ref, normed_ref, attended_ref, branch_ref, residual_ref, items_ref, gain_out,
+    arrived, stage, keep_gain, *sems,
 ):
-    local_tokens, devices, span, aliased = sizes
-    refs = refs[aliased:]
-    (layer_ref, act_ref, gate_up_ref, normed_ref, attended_ref, branch_ref, residual_ref, items_ref, gain_out, keep_gain) = refs
+    local_tokens, devices, total = sizes
+    in_sems, out_sems = sems[:3], sems[3:]
     step = pl.program_id(0)
-    pieces = []
-    for pair in range(PAIRS):
-        item = step * PAIRS + pair
-        pieces.append(att_ref[lax.rem(item, devices), item // devices])
-    attended = jnp.concatenate(pieces, axis=1)
-    attended_ref[0] = attended
-    residual = hidden_ref[0] + dot(attended, out_weight_ref[...], NN)
+    me = lax.axis_index("seq")
+    per_device = -(-total // devices)
+
+    @pl.when(step == 0)
+    def _():
+        greet("seq", me, devices)
+        keep_gain[...] = jnp.zeros_like(keep_gain)
+        pl.semaphore_wait(pltpu.get_barrier_semaphore(), devices - 1)
+
+        def send(at, unused):
+            slot, offset = at // devices, lax.rem(at, devices)
+            other = lax.rem(me + offset, devices)
+
+            @pl.when(slot * devices + me < total)
+            def _():
+                start_item(devices, me, att_ref.at[other, slot], arrived.at[me, slot], other, slot, in_sems)
+
+            return unused
+
+        lax.fori_loop(0, devices * per_device, send, 0)
+
+    together = hidden_ref.shape[0]
+    rows = together * local_tokens
+    model = gain_ref.shape[1]
+    gathered = []
+    for one in range(together):
+        pieces = []
+        for pair in range(PAIRS):
+            item = (step * together + one) * PAIRS + pair
+            other, slot = lax.rem(item, devices), item // devices
+
+            @pl.when(other == me)
+            def _():
+                pltpu.make_async_copy(att_ref.at[me, slot], arrived.at[me, slot], in_sems[2].at[slot]).wait()
+
+            @pl.when(other != me)
+            def _():
+                item_copy(devices, me, att_ref.at[other, slot], arrived.at[other, slot], other, slot, in_sems)[1]().wait_recv()
+
+            pieces.append(arrived[other, slot])
+        gathered.append(jnp.concatenate(pieces, axis=1))
+    attended = jnp.concatenate(gathered, axis=0)
+    attended_ref[...] = attended.reshape(attended_ref.shape)
+    residual = hidden_ref[...].reshape(rows, model) + dot(attended, out_weight_ref[...], NN)
     gain = gain_ref[...]
     scale = lax.rsqrt(jnp.mean(residual * residual, axis=1, keepdims=True) + 1e-06)
     normed = (residual * scale * gain).astype(BF16)
-    normed_ref[0] = normed
-    cot = cot_ref[0]
+    normed_ref[...] = normed.reshape(normed_ref.shape)
+    cot = cot_ref[...].reshape(rows, model)
     hidden_units = down_ref.shape[0]
     chunk = 512
     layer = residual
@@ -423,45 +546,75 @@
         act = (smooth * up).astype(BF16)
         grad_gate = (grad * up * slope).astype(BF16)
         grad_up = (grad * smooth).astype(BF16)
-        act_ref[0, :, here] = act
-        gate_up_ref[0, :, here] = grad_gate
-        gate_up_ref[0, :, there] = grad_up
+        act_ref[:, :, here] = act.reshape(together, local_tokens, chunk)
+        gate_up_ref[:, :, here] = grad_gate.reshape(together, local_tokens, chunk)
+        gate_up_ref[:, :, there] = grad_up.reshape(together, local_tokens, chunk)
         layer = layer + dot(act, down_ref[here, :], NN)
         back = back + dot(grad_gate, in_weight_ref[:, here], NT) + dot(grad_up, in_weight_ref[:, there], NT)
-    layer_ref[0] = layer
+    layer_ref[...] = layer.reshape(layer_ref.shape)
     weighted = gain * back
     inner_mean = jnp.mean(residual * weighted, axis=1, keepdims=True)
     grad_residual = cot.astype(F32) + scale * weighted - residual * (scale * scale * scale * inner_mean)
-    residual_ref[0] = grad_residual
+    residual_ref[...] = grad_residual.reshape(residual_ref.shape)
     branch = grad_residual.astype(BF16)
-    branch_ref[0] = branch
+    branch_ref[...] = branch.reshape(branch_ref.shape)
     grad_attended = dot(branch, out_weight_ref[...], NT).astype(BF16)
-    for pair in range(PAIRS):
-        item = step * PAIRS + pair
-        items_ref[lax.rem(item, devices), item // devices] = grad_attended[:, pair * 128 : pair * 128 + 128]
+    for one in range(together):
+        for pair in range(PAIRS):
+            item = (step * together + one) * PAIRS + pair
+            other, slot = lax.rem(item, devices), item // devices
+            stage[other, slot] = grad_attended[one * local_tokens : (one + 1) * local_tokens, pair * 128 : pair * 128 + 128]
+            start_item(devices, me, stage.at[other, slot], items_ref.at[me, slot], other, slot, out_sems)
+    keep_gain[...] += jnp.sum((back * residual * scale).reshape(rows // 8, 8, model), axis=0)
+    gain_out[...] = jnp.sum(keep_gain[...], axis=0, keepdims=True)
+
+    @pl.when(step == pl.num_programs(0) - 1)
+    def _():
+        def wait(at, unused):
+            slot, offset = at // devices, lax.rem(at, devices)
+            other = lax.rem(me + offset, devices)
+
+            @pl.when((slot * devices + me < total) & (offset != 0))
+            def _():
+                item_copy(devices, me, att_ref.at[other, slot], arrived.at[me, slot], other, slot, in_sems)[0]().wait_send()
+
+            return unused
+
+        lax.fori_loop(0, devices * per_device, wait, 0)
+        finish_sends(devices, me, total, lambda other, slot: stage.at[other, slot], lambda other, slot: items_ref.at[me, slot], out_sems)
+        finish_receives(devices, me, total, lambda other, slot: stage.at[other, slot], lambda other, slot: items_ref.at[other, slot], out_sems)
+
+
+def back_kernel(
+    sizes, grads_ref, hidden_ref, residual_ref, conv_ref, mix_ref, share_ref, ids_ref, weight_ref, taps_ref,
+    table_ref, gain_ref, score_ref, after, table_out, flat_out, masks, permuted, slopes, keep_gain, keep_score, arrived, *sems,
+):
+    local_tokens, window, devices, item_total = sizes
+    step = pl.program_id(0)
+    me = lax.axis_index("seq")
+    model = gain_ref.shape[1]
+    per_device = -(-item_total // devices)
 
     @pl.when(step == 0)
     def _():
-        keep_gain[...] = jnp.zeros_like(keep_gain)
-
-    keep_gain[...] += jnp.sum((back * residual * scale).reshape(local_tokens // 8, 8, residual.shape[1]), axis=0)
-    gain_out[...] = jnp.sum(keep_gain[...], axis=0, keepdims=True)
-
-
-def back_kernel(
-    sizes, place_ref, grads_ref, hidden_ref, residual_ref, conv_ref, mix_ref, share_ref, ids_ref, weight_ref, taps_ref,
-    table_ref, gain_ref, score_ref, table_out, small_out, flat_out, masks, permuted, slopes, keep_gain, keep_score,
-):
-    local_tokens, window, devices, span = sizes
-    step = pl.program_id(0)
-    model = gain_ref.shape[1]
-
-    @pl.when(step == 0)
-    def _():
-        block_masks(masks, place_ref[0], place_ref[1])
+        greet("seq", me, devices)
+        block_masks(masks, me * 2 * local_tokens, devices * 2 * local_tokens)
         permute_weight(weight_ref, permuted)
         keep_gain[...] = jnp.zeros_like(keep_gain)
         keep_score[...] = jnp.zeros_like(keep_score)
+        pl.semaphore_wait(pltpu.get_barrier_semaphore(), devices - 1)
+
+        def send(at, unused):
+            slot, offset = at // devices, lax.rem(at, devices)
+            other = lax.rem(me + offset, devices)
+
+            @pl.when(slot * devices + me < item_total)
+            def _():
+                start_item(devices, me, grads_ref.at[other, slot], arrived.at[me, slot], other, slot, sems)
+
+            return unused
+
+        lax.fori_loop(0, devices * per_device, send, 0)
 
     together = hidden_ref.shape[0]
     width = masks.shape[3]
@@ -471,7 +624,17 @@
         pieces = []
         for pair in range(PAIRS):
             item = (step * together + one) * PAIRS + pair
-            pieces.append(grads_ref[lax.rem(item, devices), item // devices])
+            other, slot = lax.rem(item, devices), item // devices
+
+            @pl.when(other == me)
+            def _():
+                pltpu.make_async_copy(grads_ref.at[me, slot], arrived.at[me, slot], sems[2].at[slot]).wait()
+
+            @pl.when(other != me)
+            def _():
+                item_copy(devices, me, grads_ref.at[other, slot], arrived.at[other, slot], other, slot, sems)[1]().wait_recv()
+
+            pieces.append(arrived[other, slot])
         gathered.append(jnp.concatenate(pieces, axis=1))
     projected = jnp.concatenate(gathered, axis=0)
     flat_out[...] = projected.reshape(flat_out.shape)
@@ -511,105 +674,128 @@
 
     @pl.when(step == pl.num_programs(0) - 1)
     def _():
+        def wait(at, unused):
+            slot, offset = at // devices, lax.rem(at, devices)
+            other = lax.rem(me + offset, devices)
+
+            @pl.when((slot * devices + me < item_total) & (offset != 0))
+            def _():
+                item_copy(devices, me, grads_ref.at[other, slot], arrived.at[me, slot], other, slot, sems)[0]().wait_send()
+
+            return unused
+
+        lax.fori_loop(0, devices * per_device, wait, 0)
         count = slopes.shape[0]
-        row = lax.broadcasted_iota(jnp.int32, (VPAD, count), 0)
-        table_grad = jnp.zeros((VPAD, model), F32)
+        row = lax.broadcasted_iota(jnp.int32, (SMALL_ROWS, count), 0)
+        table_grad = jnp.zeros((SMALL_ROWS, model), F32)
         table = table_ref[...].astype(F32)
-        small_row = lax.broadcasted_iota(jnp.int32, (8, model), 0)
-        small = jnp.where(small_row == 5, jnp.sum(keep_gain[...], axis=0, keepdims=True), 0.0)
-        small = jnp.where(small_row == 6, jnp.sum(keep_score[...], axis=0, keepdims=True), small)
+        place = lax.broadcasted_iota(jnp.int32, (SMALL_ROWS, model), 0)
+        extra = []
         for tap in range(taps_ref.shape[0]):
             hot = jnp.where(ids_ref[tap : tap + 1, :] == row, 1.0, 0.0).astype(BF16)
             sums = dot(hot, slopes[...], NN)
             table_grad = table_grad + taps_ref[tap : tap + 1, :] * sums
-            small = jnp.where(small_row == tap, jnp.sum(sums * table, axis=0, keepdims=True), small)
+            extra.append(jnp.sum(sums * table, axis=0, keepdims=True))
+        extra.append(jnp.sum(keep_gain[...], axis=0, keepdims=True))
+        extra.append(jnp.sum(keep_score[...], axis=0, keepdims=True))
+        for index, value in enumerate(extra):
+            table_grad = jnp.where(place == 259 + index, value, table_grad)
         table_out[...] = table_grad
-        small_out[...] = small
-
-
-VMEM_LIMIT = 56 * 2**20
-
-
-def call_front(half, place, ids, taps, weight, gain, score, local_tokens, devices, per_device):
-    span = ids.shape[0]
-    window = ids.shape[1]
+
+
+VMEM_LIMIT = 58 * 2**20
+TOGETHER = 2
+
+
+def item_sems(devices, per_device):
+    dma = pltpu.SemaphoreType.DMA
+    return [dma((devices, per_device)), dma((devices, per_device)), dma((per_device,))]
+
+
+def whole(*shape):
+    return pl.BlockSpec(shape, lambda s, *_: (0,) * len(shape))
+
+
+def part(*shape):
+    return pl.BlockSpec(shape, lambda s, *_: (s,) + (0,) * (len(shape) - 1))
+
+
+ANYWHERE = pl.BlockSpec(memory_space=pl.ANY)
+
+
+def remote_params(number):
+    return pltpu.CompilerParams(vmem_limit_bytes=VMEM_LIMIT, collective_id=number, has_side_effects=True)
+
+
+def call_front(ids, taps, weight, gain, score, local_tokens, devices, per_device):
+    sequences, window, unused = ids.shape
     width = -(-window // 128) * 128
     model = weight.shape[0]
-    together = 2
-    whole = lambda *shape: pl.BlockSpec(shape, lambda s, *_: (0,) * len(shape))
-    part = lambda *shape: pl.BlockSpec(shape, lambda s, *_: (s,) + (0,) * (len(shape) - 1))
     return pl.pallas_call(
-        functools.partial(front_kernel, (local_tokens, window, devices, span), half),
-        grid_spec=pltpu.PrefetchScalarGridSpec(
-            num_scalar_prefetch=1,
-            grid=(span // together,),
-            in_specs=[part(together, window, 8), whole(*taps.shape), whole(*weight.shape), whole(1, model), whole(1, model)],
-            out_specs=[
-                part(together, local_tokens, model),
-                part(together, local_tokens, model),
-                part(together, width, model),
-                part(together, local_tokens, width),
-                part(together, local_tokens, 128),
-                whole(devices, per_device, local_tokens, 384),
-            ],
-            scratch_shapes=[
-                pltpu.VMEM((2, 4, local_tokens, width), F32),
-                pltpu.VMEM((together, 2, width, model), BF16),
-                pltpu.VMEM(weight.shape, BF16),
-            ],
-        ),
+        functools.partial(front_kernel, (local_tokens, window, devices, sequences * PAIRS)),
+        grid=(sequences // TOGETHER,),
+        in_specs=[part(TOGETHER, window, 8), whole(*taps.shape), whole(*weight.shape), whole(1, model), whole(1, model)],
+        out_specs=[
+            part(TOGETHER, local_tokens, model),
+            part(TOGETHER, local_tokens, model),
+            part(TOGETHER, width, model),
+            part(TOGETHER, local_tokens, width),
+            part(TOGETHER, local_tokens, 128),
+            ANYWHERE,
+        ],
+        scratch_shapes=[
+            pltpu.VMEM((2, 4, local_tokens, width), F32),
+            pltpu.VMEM((TOGETHER, 2, width, model), BF16),
+            pltpu.VMEM(weight.shape, BF16),
+            pltpu.VMEM((devices, per_device, local_tokens, 384), BF16),
+        ]
+        + item_sems(devices, per_device),
         out_shape=[
-            jax.ShapeDtypeStruct((span, local_tokens, model), F32),
-            jax.ShapeDtypeStruct((span, local_tokens, model), BF16),
-            jax.ShapeDtypeStruct((span, width, model), BF16),
-            jax.ShapeDtypeStruct((span, local_tokens, width), BF16),
-            jax.ShapeDtypeStruct((span, local_tokens, 128), F32),
+            jax.ShapeDtypeStruct((sequences, local_tokens, model), F32),
+            jax.ShapeDtypeStruct((sequences, local_tokens, model), BF16),
+            jax.ShapeDtypeStruct((sequences, width, model), BF16),
+            jax.ShapeDtypeStruct((sequences, local_tokens, width), BF16),
+            jax.ShapeDtypeStruct((sequences, local_tokens, 128), F32),
             jax.ShapeDtypeStruct((devices, per_device, local_tokens, 384), BF16),
         ],
-        compiler_params=pltpu.CompilerParams(vmem_limit_bytes=VMEM_LIMIT),
-        cost_estimate=pl.CostEstimate(flops=8 * 10**9, bytes_accessed=2 * 10**7, transcendentals=10**5),
+        compiler_params=remote_params(3),
+        cost_estimate=pl.CostEstimate(flops=5 * 10**10, bytes_accessed=2 * 10**7, transcendentals=10**5),
         name="front",
-    )(place, ids, taps, weight, gain, score)
-
-
-def call_mid(half, order, att, hidden, cot, out_weight, in_weight, down_weight, gain, before):
+    )(ids, taps, weight, gain, score)
+
+
+def call_mid(att, hidden, cot, out_weight, in_weight, down_weight, gain):
     devices, per_device, local_tokens, unused = att.shape
-    span, unused, model = hidden.shape
-    sequences = cot.shape[0]
+    sequences, unused, model = hidden.shape
     hidden_units = down_weight.shape[0]
-    aliased = len(before)
-    whole = lambda *shape: pl.BlockSpec(shape, lambda s, *_: (0,) * len(shape))
-    moved = lambda lanes: pl.BlockSpec((1, local_tokens, lanes), lambda s, order: (order[half * span + s], 0, 0))
-    part = lambda lanes: pl.BlockSpec((1, local_tokens, lanes), lambda s, order: (s, 0, 0))
+    rows = lambda lanes: part(TOGETHER, local_tokens, lanes)
     full = lambda lanes, kind: jax.ShapeDtypeStruct((sequences, local_tokens, lanes), kind)
     return pl.pallas_call(
-        functools.partial(mid_kernel, (local_tokens, devices, span, aliased)),
-        grid_spec=pltpu.PrefetchScalarGridSpec(
-            num_scalar_prefetch=1,
-            grid=(span,),
-            in_specs=[
-                whole(*att.shape),
-                part(model),
-                moved(model),
-                whole(*out_weight.shape),
-                whole(*in_weight.shape),
-                whole(*down_weight.shape),
-                whole(1, model),
-            ]
-            + [pl.BlockSpec(memory_space=pl.ANY)] * aliased,
-            out_specs=[
-                moved(model),
-                moved(hidden_units),
-                moved(2 * hidden_units),
-                moved(model),
-                moved(model),
-                moved(model),
-                part(model),
-                whole(*att.shape),
-                whole(1, model),
-            ],
-            scratch_shapes=[pltpu.VMEM((8, model), F32)],
-        ),
+        functools.partial(mid_kernel, (local_tokens, devices, sequences * PAIRS)),
+        grid=(sequences // TOGETHER,),
+        in_specs=[
+            ANYWHERE,
+            rows(model),
+            rows(model),
+            whole(*out_weight.shape),
+            whole(*in_weight.shape),
+            whole(*down_weight.shape),
+            whole(1, model),
+        ],
+        out_specs=[
+            rows(model),
+            rows(hidden_units),
+            rows(2 * hidden_units),
+            rows(model),
+            rows(model),
+            rows(model),
+            rows(model),
+            ANYWHERE,
+            whole(1, model),
+        ],
+        scratch_shapes=[pltpu.VMEM(att.shape, BF16), pltpu.VMEM(att.shape, BF16), pltpu.VMEM((8, model), F32)]
+        + item_sems(devices, per_device)
+        + item_sems(devices, per_device),
         out_shape=[
             full(model, F32),
             full(hidden_units, BF16),
@@ -617,62 +803,478 @@
             full(model, BF16),
             full(model, BF16),
             full(model, BF16),
-            jax.ShapeDtypeStruct((span, local_tokens, model), F32),
+            full(model, F32),
             jax.ShapeDtypeStruct(att.shape, BF16),
             jax.ShapeDtypeStruct((1, model), F32),
         ],
-        input_output_aliases={8 + k: k for k in range(aliased)},
-        compiler_params=pltpu.CompilerParams(vmem_limit_bytes=VMEM_LIMIT),
-        cost_estimate=pl.CostEstimate(flops=11 * 10**9, bytes_accessed=4 * 10**7, transcendentals=10**6),
+        compiler_params=remote_params(4),
+        cost_estimate=pl.CostEstimate(flops=5 * 10**10, bytes_accessed=4 * 10**7, transcendentals=10**6),
         name="middle",
-    )(order, att, hidden, cot, out_weight, in_weight, down_weight, gain, *before)
-
-
-def call_back(place, grads, hidden, residual, conv, mix, share, ids, weight, taps, table, gain, score):
+    )(att, hidden, cot, out_weight, in_weight, down_weight, gain)
+
+
+def call_back(grads, hidden, residual, conv, mix, share, ids, weight, taps, table, gain, score, after):
     devices, per_device, local_tokens, unused = grads.shape
-    span, unused, model = hidden.shape
+    sequences, unused, model = hidden.shape
     width = conv.shape[1]
-    window = ids.shape[1] // span
-    together = 2
-    whole = lambda *shape: pl.BlockSpec(shape, lambda s, *_: (0,) * len(shape))
-    part = lambda *shape: pl.BlockSpec(shape, lambda s, *_: (s,) + (0,) * (len(shape) - 1))
+    window = ids.shape[1] // sequences
     return pl.pallas_call(
-        functools.partial(back_kernel, (local_tokens, window, devices, span)),
+        functools.partial(back_kernel, (local_tokens, window, devices, sequences * PAIRS)),
+        grid=(sequences // TOGETHER,),
+        in_specs=[
+            ANYWHERE,
+            part(TOGETHER, local_tokens, model),
+            part(TOGETHER, local_tokens, model),
+            part(TOGETHER, width, model),
+            part(TOGETHER, local_tokens, width),
+            part(TOGETHER, local_tokens, 128),
+            whole(*ids.shape),
+            whole(*weight.shape),
+            whole(*taps.shape),
+            whole(*table.shape),
+            whole(1, model),
+            whole(1, model),
+            ANYWHERE,
+        ],
+        out_specs=[whole(SMALL_ROWS, model), part(TOGETHER, local_tokens, PAIRS * 384)],
+        scratch_shapes=[
+            pltpu.VMEM((2, 4, local_tokens, width), F32),
+            pltpu.VMEM(weight.shape, BF16),
+            pltpu.VMEM((sequences * window, model), BF16),
+            pltpu.VMEM((8, model), F32),
+            pltpu.VMEM((16, model), F32),
+            pltpu.VMEM(grads.shape, BF16),
+        ]
+        + item_sems(devices, per_device),
+        out_shape=[
+            jax.ShapeDtypeStruct((SMALL_ROWS, model), F32),
+            jax.ShapeDtypeStruct((sequences, local_tokens, PAIRS * 384), BF16),
+        ],
+        compiler_params=remote_params(5),
+        cost_estimate=pl.CostEstimate(flops=5 * 10**10, bytes_accessed=2 * 10**7, transcendentals=10**5),
+        name="back",
+    )(grads, hidden, residual, conv, mix, share, ids, weight, taps, table, gain, score, after)
+
+
+def move_kernel(order_ref, source_ref, out_ref):
+    out_ref[...] = source_ref[...]
+
+
+def reorder(source, order, inverse):
+    block = (1,) + source.shape[1:]
+    moved = pl.BlockSpec(block, lambda s, order: (order[s], 0, 0))
+    plain = pl.BlockSpec(block, lambda s, order: (s, 0, 0))
+    return pl.pallas_call(
+        move_kernel,
         grid_spec=pltpu.PrefetchScalarGridSpec(
             num_scalar_prefetch=1,
-            grid=(span // together,),
-            in_specs=[
-                whole(*grads.shape),
-                part(together, local_tokens, model),
-                part(together, local_tokens, model),
-                part(together, width, model),
-                part(together, local_tokens, width),
-                part(together, local_tokens, 128),
-                whole(*ids.shape),
-                whole(*weight.shape),
-                whole(*taps.shape),
-                whole(*table.shape),
-                whole(1, model),
-                whole(1, model),
-            ],
-            out_specs=[whole(VPAD, model), whole(8, model), part(together, local_tokens, PAIRS * 384)],
-            scratch_shapes=[
-                pltpu.VMEM((2, 4, local_tokens, width), F32),
-                pltpu.VMEM(weight.shape, BF16),
-                pltpu.VMEM((span * window, model), BF16),
-                pltpu.VMEM((8, model), F32),
-                pltpu.VMEM((16, model), F32),
-            ],
+            grid=(source.shape[0],),
+            in_specs=[plain if inverse else moved],
+            out_specs=moved if inverse else plain,
         ),
+        out_shape=jax.ShapeDtypeStruct(source.shape, source.dtype),
+        cost_estimate=pl.CostEstimate(flops=0, bytes_accessed=2 * source.size * source.dtype.itemsize, transcendentals=0),
+        name="reorder",
+    )(order, source)
+
+
+EARLY_ROWS = 8 * 96 + 2 * 192 + 2 * 96
+LATE_ROWS = 5 * 96
+
+
+def meet_sibling(core):
+    barrier = pltpu.get_barrier_semaphore()
+    sibling = lax.axis_index("seq") + 1 - 2 * core
+    pl.semaphore_signal(barrier, inc=1, device_id={"seq": sibling}, device_id_type=pl.DeviceIdType.MESH)
+    pl.semaphore_wait(barrier, 1)
+
+
+def to_sibling(core, source, target, send_sem, recv_sem):
+    sibling = lax.axis_index("seq") + 1 - 2 * core
+    return pltpu.make_async_remote_copy(
+        src_ref=source, dst_ref=target, send_sem=send_sem, recv_sem=recv_sem,
+        device_id={"seq": sibling}, device_id_type=pl.DeviceIdType.MESH,
+    )
+
+
+def spread_rows(core, source, lanes, keep_ref, send_ref, column, first):
+    for chip in range(4):
+        for other, ref in ((0, keep_ref), (1, send_ref)):
+            device = 2 * chip + lax.rem(core + other, 2)
+            rows = pl.ds(pl.multiple_of(device * 96, 32), 96)
+            ref[chip, column, pl.ds(first, 96)] = source[rows, lanes]
+
+
+def add_received(keep_ref, got):
+    def add(at, unused):
+        chip, column = at // 4, at % 4
+        keep_ref[chip, column] = (keep_ref[chip, column].astype(F32) + got[chip, column].astype(F32)).astype(BF16)
+        return unused
+
+    lax.fori_loop(0, 16, add, 0)
+
+
+def early_kernel(
+    act_ref, cot_ref, normed_ref, gate_up_ref, attended_ref, branch_ref, keep_ref,
+    send_ref, got, cot_t, normed_t, result, send_in, recv_in, send_down, recv_down, send_out, recv_out,
+):
+    step = pl.program_id(0)
+    core = lax.rem(lax.axis_index("seq"), 2)
+    model = cot_t.shape[0]
+    tokens = cot_t.shape[1]
+    out_rows = pl.ds(1152, 192)
+    down_rows = pl.ds(768, 384)
+    out_copy = to_sibling(core, send_ref.at[:, :, out_rows], got.at[:, :, out_rows], send_out, recv_out)
+
+    def in_copy(at):
+        rows = pl.ds(pl.multiple_of(384 * lax.rem(at, 2), 384), 384)
+        return to_sibling(core, send_ref.at[:, at // 2, rows], got.at[:, at // 2, rows], send_in.at[at], recv_in.at[at])
+
+    def down_copy(chip):
+        return to_sibling(core, send_ref.at[chip, :, down_rows], got.at[chip, :, down_rows], send_down.at[chip], recv_down.at[chip])
+
+    @pl.when(step == 0)
+    def _():
+        meet_sibling(core)
+        cot_t[...] = cot_ref[...].reshape(tokens, model).T
+        normed_t[...] = attended_ref[...].reshape(tokens, model).T
+        for first in range(0, model, 256):
+            result[:, 0:256] = dot(normed_t[...], branch_ref[:, :, first : first + 256].reshape(tokens, 256), NN).astype(BF16)
+            for part in range(2):
+                tile = first // 128 + part
+                for column, slot in {0: ((0, 0),), 1: ((0, 1), (1, 0)), 2: ((1, 1),), 3: ((2, 0),), 4: ((2, 1), (3, 0)), 5: ((3, 1),)}[tile]:
+                    spread_rows(core, result, slice(128 * part, 128 * part + 128), keep_ref, send_ref, column, 1152 + 96 * slot)
+        out_copy.start()
+        normed_t[...] = normed_ref[...].reshape(tokens, model).T
+
+    result[...] = dot(normed_t[...], gate_up_ref[...].reshape(tokens, 512), NN).astype(BF16)
+    for part in range(4):
+        first = pl.multiple_of((4 * lax.rem(step, 2) + part) * 96, 32)
+        spread_rows(core, result, slice(128 * part, 128 * part + 128), keep_ref, send_ref, step // 2, first)
+    in_copy(step).start()
+    down = dot(cot_t[...], act_ref[...].reshape(tokens, 256), NN).astype(BF16)
+
+    def put_down(ref):
+        for column in range(4):
+            for part in range(2):
+                ref[step // 2, column, 768 + 192 * part : 960 + 192 * part] = down[192 * column : 192 * column + 192, 128 * part : 128 * part + 128]
+
+    @pl.when(lax.rem(step, 2) == core)
+    def _():
+        put_down(keep_ref)
+
+    @pl.when(lax.rem(step, 2) != core)
+    def _():
+        put_down(send_ref)
+        down_copy(step // 2).start()
+
+    @pl.when(step == 7)
+    def _():
+        out_copy.wait()
+        for at in range(8):
+            in_copy(at).wait()
+        for chip in range(4):
+            down_copy(chip).wait()
+        add_received(keep_ref, got)
+
+
+def call_early(act, cot, normed, gate_up, attended, branch):
+    sequences, local_tokens, model = cot.shape
+    tokens = sequences * local_tokens
+    whole = pl.BlockSpec((sequences, local_tokens, model), lambda s: (0, 0, 0))
+    shape = (4, 4, EARLY_ROWS, 128)
+    dma = pltpu.SemaphoreType.DMA
+    return pl.pallas_call(
+        early_kernel,
+        grid=(8,),
+        in_specs=[
+            pl.BlockSpec((sequences, local_tokens, 256), lambda s: (0, 0, s)),
+            whole,
+            whole,
+            pl.BlockSpec((sequences, local_tokens, 512), lambda s: (0, 0, s)),
+            whole,
+            whole,
+        ],
+        out_specs=pl.BlockSpec(shape, lambda s: (0, 0, 0, 0)),
+        scratch_shapes=[
+            pltpu.VMEM(shape, BF16),
+            pltpu.VMEM(shape, BF16),
+            pltpu.VMEM((model, tokens), BF16),
+            pltpu.VMEM((model, tokens), BF16),
+            pltpu.VMEM((model, 512), BF16),
+            dma((8,)), dma((8,)), dma((4,)), dma((4,)), dma, dma,
+        ],
+        out_shape=jax.ShapeDtypeStruct(shape, BF16),
+        compiler_params=pltpu.CompilerParams(vmem_limit_bytes=VMEM_LIMIT, collective_id=1, has_side_effects=True),
+        cost_estimate=pl.CostEstimate(flops=11 * 10**9, bytes_accessed=3 * 10**7, transcendentals=0),
+        name="early_gradients",
+    )(act, cot, normed, gate_up, attended, branch)
+
+
+def tail_kernel(
+    normed_ref, grads_ref, plane_ref, one_ref, tail_ref, late_out, early_out, out_ref,
+    keep, send_ref, got, normed_t, result, got_chips, planes_late, got_late, got_early,
+    held, got_seq, planes, got_dp, whole_small, *sems,
+):
+    small_sems, (send_a, recv_a, send_b, recv_b, send_c, recv_c, send_e, recv_e) = sems[:8], sems[8:]
+    me = lax.axis_index("seq")
+    plane = lax.axis_index("dp")
+    core = lax.rem(me, 2)
+    chip = me // 2
+    sequences, local_tokens, model = normed_ref.shape
+    small = SmallSums(one_ref, tail_ref, out_ref, held, got_seq, planes, got_dp, whole_small, small_sems)
+    greet("seq", me, 8)
+    greet("dp", plane, 4)
+    small.pack()
+    normed_t[...] = normed_ref[...].reshape(sequences * local_tokens, model).T
+    pl.semaphore_wait(pltpu.get_barrier_semaphore(), 10)
+    small.one_start()
+
+    def to_plane(offset, source, target, send, recv):
+        return pltpu.make_async_remote_copy(
+            src_ref=source, dst_ref=target, send_sem=send.at[offset - 1], recv_sem=recv.at[offset - 1],
+            device_id={"dp": lax.rem(plane + offset, 4)}, device_id_type=pl.DeviceIdType.MESH,
+        )
+
+    early_copies = [to_plane(offset, plane_ref.at[lax.rem(plane + offset, 4)], got_early.at[offset - 1], send_e, recv_e) for offset in (1, 2, 3)]
+    for copy in early_copies:
+        copy.start()
+    low = lax.broadcasted_iota(jnp.int32, (model, 128), 1) < 64
+    copies = [to_sibling(core, send_ref.at[:, column], got.at[:, column], send_a.at[column], recv_a.at[column]) for column in range(4)]
+    for pair in range(PAIRS):
+        rows = grads_ref[:, :, pair * 384 : pair * 384 + 384].reshape(sequences * local_tokens, 384)
+        sums = dot(normed_t[...], rows, NN)
+        query, key, value = sums[:, 0:128], pltpu.roll(sums[:, 128:256], 64, 1), sums[:, 256:384]
+        result[0] = jnp.where(low, query, key).astype(BF16)
+        result[1] = jnp.where(low, value, query).astype(BF16)
+        result[2] = jnp.where(low, key, value).astype(BF16)
+        for third in range(3):
+            tile = 3 * pair + third
+            within = tile % 9
+            spots = [(2 * (tile // 9), within)] if within <= 4 else []
+            spots += [(2 * (tile // 9) + 1, within - 4)] if within >= 4 else []
+            for column, slot in spots:
+                spread_rows(core, result.at[third], slice(0, 128), keep, send_ref, column, 96 * slot)
+        if pair in (1, 2, 4, 5):
+            copies[(1, 2, 4, 5).index(pair)].start()
+    small.one_finish()
+
+    def chip_copy(offset, column):
+        other = lax.rem(chip + offset, 4)
+        return pltpu.make_async_remote_copy(
+            src_ref=keep.at[other, column], dst_ref=got_chips.at[offset - 1, column],
+            send_sem=send_b.at[offset - 1, column], recv_sem=recv_b.at[offset - 1, column],
+            device_id={"seq": 2 * other + core}, device_id_type=pl.DeviceIdType.MESH,
+        )
+
+    for column in range(4):
+        copies[column].wait()
+        for at in range(4):
+            keep[at, column] = (keep[at, column].astype(F32) + got[at, column].astype(F32)).astype(BF16)
+        for offset in (1, 2, 3):
+            chip_copy(offset, column).start()
+    small.two_finish()
+    for column in range(4):
+        total = keep[chip, column].astype(F32)
+        for offset in (1, 2, 3):
+            chip_copy(offset, column).wait()
+            total = total + got_chips[offset - 1, column].astype(F32)
+        planes_late[column] = total.astype(BF16)
+    late_copies = [to_plane(offset, planes_late.at[lax.rem(plane + offset, 4)], got_late.at[offset - 1], send_c, recv_c) for offset in (1, 2, 3)]
+    for copy in late_copies:
+        copy.start()
+    small.three_finish()
+    total = plane_ref[plane].astype(F32)
+    for offset in (1, 2, 3):
+        early_copies[offset - 1].wait()
+        total = total + got_early[offset - 1].astype(F32)
+    early_out[...] = total
+    total = planes_late[plane].astype(F32)
+    for offset in (1, 2, 3):
+        late_copies[offset - 1].wait()
+        total = total + got_late[offset - 1].astype(F32)
+    late_out[...] = total
+    small.four_finish()
+
+
+def call_tail(normed, grads, plane, one, tail):
+    model = normed.shape[2]
+    tokens = normed.shape[0] * normed.shape[1]
+    shape = (4, 4, LATE_ROWS, 128)
+    dma = pltpu.SemaphoreType.DMA
+    vmem = pl.BlockSpec(memory_space=pltpu.VMEM)
+    return pl.pallas_call(
+        tail_kernel,
+        in_specs=[vmem] * 5,
+        out_specs=[vmem] * 3,
         out_shape=[
-            jax.ShapeDtypeStruct((VPAD, model), F32),
-            jax.ShapeDtypeStruct((8, model), F32),
-            jax.ShapeDtypeStruct((span, local_tokens, PAIRS * 384), BF16),
-        ],
+            jax.ShapeDtypeStruct((LATE_ROWS, 128), F32),
+            jax.ShapeDtypeStruct((EARLY_ROWS, 128), F32),
+            jax.ShapeDtypeStruct(tail.shape, F32),
+        ],
+        scratch_shapes=[
+            pltpu.VMEM(shape, BF16),
+            pltpu.VMEM(shape, BF16),
+            pltpu.VMEM(shape, BF16),
+            pltpu.VMEM((model, tokens), BF16),
+            pltpu.VMEM((3, model, 128), BF16),
+            pltpu.VMEM((3, 4, LATE_ROWS, 128), BF16),
+            pltpu.VMEM((4, LATE_ROWS, 128), BF16),
+            pltpu.VMEM((3, LATE_ROWS, 128), BF16),
+            pltpu.VMEM((3, EARLY_ROWS, 128), BF16),
+        ]
+        + small_scratch(8, 4)
+        + [dma((4,)), dma((4,)), dma((3, 4)), dma((3, 4)), dma((3,)), dma((3,)), dma((3,)), dma((3,))],
+        compiler_params=remote_params(2),
+        cost_estimate=pl.CostEstimate(flops=5 * 10**10, bytes_accessed=10**7, transcendentals=0),
+        name="tail",
+    )(normed, grads, plane, one, tail)
+
+
+def sum_kernel(parts_ref, after, out_ref):
+    out_ref[0] = sum(parts_ref[k, 0].astype(F32) for k in range(parts_ref.shape[0])).astype(out_ref.dtype)
+
+
+def sum_parts(parts, kind, after):
+    count, columns, rows, lanes = parts.shape
+    return pl.pallas_call(
+        sum_kernel,
+        grid=(columns,),
+        in_specs=[pl.BlockSpec((count, 1, rows, lanes), lambda s: (0, s, 0, 0)), pl.BlockSpec(memory_space=pl.ANY)],
+        out_specs=pl.BlockSpec((1, rows, lanes), lambda s: (s, 0, 0)),
+        out_shape=jax.ShapeDtypeStruct((columns, rows, lanes), kind),
         compiler_params=pltpu.CompilerParams(vmem_limit_bytes=VMEM_LIMIT),
-        cost_estimate=pl.CostEstimate(flops=8 * 10**9, bytes_accessed=2 * 10**7, transcendentals=10**5),
-        name="back",
-    )(place, grads, hidden, residual, conv, mix, share, ids, weight, taps, table, gain, score)
+        cost_estimate=pl.CostEstimate(flops=10**6, bytes_accessed=parts.size * 3, transcendentals=0),
+        name="sum_parts",
+    )(parts, after)
+
+
+def over_chips(chips):
+    return lax.all_to_all(chips, "seq", split_axis=0, concat_axis=0, axis_index_groups=[[0, 2, 4, 6], [1, 3, 5, 7]], tiled=True)
+
+
+def over_planes(plane):
+    return lax.all_to_all(plane, "dp", split_axis=0, concat_axis=0, tiled=True)
+
+
+SMALL_ROWS = 288
+
+
+class SmallSums:
+    def __init__(self, one, tail, out, held, got_seq, planes, got_dp, whole_small, sems):
+        self.one, self.tail, self.out = one, tail, out
+        self.held, self.got_seq, self.planes, self.got_dp, self.whole = held, got_seq, planes, got_dp, whole_small
+        self.sems = sems
+        self.me, self.plane = lax.axis_index("seq"), lax.axis_index("dp")
+        self.across, self.along = held.shape[0], held.shape[1]
+
+    def places(self):
+        half = self.held.shape[2] // 2
+        units = SMALL_ROWS // half
+        tiles = self.one.shape[1] // 128
+        for at in range(2 * self.along * self.across):
+            spot = (at // (2 * self.along), at // 2 % self.along, slice((at % 2) * half, (at % 2) * half + half))
+            tile, unit = at // units, at % units
+            if tile < tiles:
+                yield spot, (slice(unit * half, unit * half + half), slice(128 * tile, 128 * tile + 128))
+            else:
+                yield spot, None
+
+    def pack(self):
+        for spot, source in self.places():
+            if source is None:
+                self.held[spot] = jnp.zeros((self.held.shape[2] // 2, 128), BF16)
+            else:
+                self.held[spot] = (self.one[source] + self.tail[source]).astype(BF16)
+
+    def copies(self, axis, source, target, number):
+        here, count = (self.me, self.across) if axis == "seq" else (self.plane, self.along)
+        send, recv = self.sems[2 * number], self.sems[2 * number + 1]
+        made = []
+        for step in range(1, count):
+            peer = lax.rem(here + step, count)
+            made.append(
+                pltpu.make_async_remote_copy(
+                    src_ref=source(peer), dst_ref=target(step - 1), send_sem=send.at[step - 1], recv_sem=recv.at[step - 1],
+                    device_id={axis: peer}, device_id_type=pl.DeviceIdType.MESH,
+                )
+            )
+        for copy in made:
+            copy.start()
+        return made
+
+    def one_start(self):
+        self.waiting = self.copies("seq", lambda peer: self.held.at[peer], lambda slot: self.got_seq.at[slot], 0)
+
+    def one_finish(self):
+        for copy in self.waiting:
+            copy.wait()
+        total = self.held[self.me].astype(F32)
+        for slot in range(self.across - 1):
+            total = total + self.got_seq[slot].astype(F32)
+        self.planes[...] = total.astype(BF16)
+        self.waiting = self.copies("dp", lambda peer: self.planes.at[peer], lambda slot: self.got_dp.at[slot], 1)
+
+    def two_finish(self):
+        for copy in self.waiting:
+            copy.wait()
+        mine = self.planes[self.plane].astype(F32)
+        for slot in range(self.along - 1):
+            mine = mine + self.got_dp[slot].astype(F32)
+        self.whole[self.me, self.plane] = mine.astype(BF16)
+        self.waiting = self.copies("dp", lambda peer: self.whole.at[self.me, self.plane], lambda slot: self.whole.at[self.me, self.plane], 2)
+
+    def three_finish(self):
+        for copy in self.waiting:
+            copy.wait()
+        self.waiting = self.copies("seq", lambda peer: self.whole.at[self.me], lambda slot: self.whole.at[self.me], 3)
+
+    def four_finish(self):
+        for copy in self.waiting:
+            copy.wait()
+        for spot, target in self.places():
+            if target is not None:
+                self.out[target] = self.whole[spot].astype(F32)
+
+
+def small_scratch(across, along):
+    chunk = max(16, 2048 // (across * along))
+    dma = lambda count: pltpu.SemaphoreType.DMA((count,))
+    return [
+        pltpu.VMEM((across, along, chunk, 128), BF16),
+        pltpu.VMEM((across - 1, along, chunk, 128), BF16),
+        pltpu.VMEM((along, chunk, 128), BF16),
+        pltpu.VMEM((along - 1, chunk, 128), BF16),
+        pltpu.VMEM((across, along, chunk, 128), BF16),
+        dma(across - 1), dma(across - 1), dma(along - 1), dma(along - 1),
+        dma(along - 1), dma(along - 1), dma(across - 1), dma(across - 1),
+    ]
+
+
+def small_kernel(one_ref, tail_ref, out_ref, held, got_seq, planes, got_dp, whole_small, *sems):
+    small = SmallSums(one_ref, tail_ref, out_ref, held, got_seq, planes, got_dp, whole_small, sems)
+    greet("seq", small.me, small.across)
+    greet("dp", small.plane, small.along)
+    small.pack()
+    pl.semaphore_wait(pltpu.get_barrier_semaphore(), small.across + small.along - 2)
+    small.one_start()
+    small.one_finish()
+    small.two_finish()
+    small.three_finish()
+    small.four_finish()
+
+
+def call_small(one, tail, across, along):
+    return pl.pallas_call(
+        small_kernel,
+        in_specs=[pl.BlockSpec(memory_space=pltpu.VMEM)] * 2,
+        out_specs=pl.BlockSpec(memory_space=pltpu.VMEM),
+        out_shape=jax.ShapeDtypeStruct(tail.shape, F32),
+        scratch_shapes=small_scratch(across, along),
+        compiler_params=remote_params(0),
+        cost_estimate=pl.CostEstimate(flops=10**6, bytes_accessed=3 * 10**6, transcendentals=0),
+        name="small_sums",
+    )(one, tail)
 
 
 def body(
@@ -697,10 +1299,9 @@
     total_bytes = local_bytes * devices
     first_byte = me * local_bytes
     vocab, model = byte_table.shape
-    span = sequences // HALVES
     window = local_bytes + 16
-    per_device = -(-span * PAIRS // devices)
-    place = jnp.stack([first_byte, jnp.int32(total_bytes)]).astype(jnp.int32)
+    total = sequences * PAIRS
+    per_device = -(-total // devices)
 
     number = jnp.arange(sequences, dtype=jnp.int32)
     ahead = (lengths[None, :] > lengths[:, None]) | (
@@ -729,83 +1330,82 @@
     gain_two = norm_gain_two[None, :]
     score = score_vector[None, :]
 
-    def exchange(items):
-        return lax.all_to_all(items, "seq", split_axis=0, concat_axis=0, tiled=True)
-
-    valids, pairs = [], []
-    for half in range(HALVES):
-        item = me + devices * jnp.arange(per_device, dtype=jnp.int32)
-        real = item < span * PAIRS
-        at = half * span + item // PAIRS
-        length = jnp.sum(jnp.where(at[:, None] == number[None, :], sorted_lengths[None, :], 0), axis=1)
-        valids.append(jnp.where(real, (length + 1) // 2, 0).astype(jnp.int32))
-        pairs.append(lax.rem(item, PAIRS).astype(jnp.int32))
-
-    fronts, received, outs, augs, returned = [], [], [], [], []
-    for half in range(HALVES):
-        here = slice(half * span, half * span + span)
-        front = call_front(half, place, ids_columns[here], taps, qkv_weight, gain_one, score, local_tokens, devices, per_device)
-        fronts.append(front)
-        received.append(exchange(front[5]))
-    for half in range(HALVES):
-        out, aug = attention_forward(received[half], rows, valids[half], pairs[half])
-        outs.append(out)
-        augs.append(aug)
-        returned.append(exchange(out))
-    mids, grad_items = [], []
-    before_mid = ()
-    for half in range(HALVES):
-        mid = call_mid(half, order, returned[half], fronts[half][0], cotangent, out_weight, in_weight, down_weight, gain_two, before_mid)
-        before_mid = tuple(mid[:6])
-        mids.append(mid)
-        grad_items.append(exchange(mid[7]))
-    layer_out, act, gate_up, normed_two, attended, branch = mids[-1][:6]
-    grad_gain_two = mids[0][8] + mids[1][8]
-    grad_down = jnp.einsum("bti,btd->id", act, cotangent, preferred_element_type=F32).astype(BF16)
-    grad_in = jnp.einsum("btd,bti->di", normed_two, gate_up, preferred_element_type=F32).astype(BF16)
-    grad_out = jnp.einsum("btd,bte->de", attended, branch, preferred_element_type=F32).astype(BF16)
+    item = me + devices * jnp.arange(per_device, dtype=jnp.int32)
+    length = jnp.sum(jnp.where((item // PAIRS)[:, None] == number[None, :], sorted_lengths[None, :], 0), axis=1)
+    valid = jnp.where(item < total, (length + 1) // 2, 0).astype(jnp.int32)
+    pair = lax.rem(item, PAIRS).astype(jnp.int32)
+    cot = reorder(cotangent, order, False)
+
+    hidden, normed, conv, mix, share, received = call_front(ids_columns, taps, qkv_weight, gain_one, score, local_tokens, devices, per_device)
+    out, aug = attention_forward(received, rows, valid, pair)
+    layer, act, gate_up, normed_two, attended, branch, grad_residual, grad_items, grad_gain_two = call_mid(
+        out, hidden, cot, out_weight, in_weight, down_weight, gain_two
+    )
+    layer_out = reorder(layer, order, True)
+    along_count = lax.axis_size("dp")
+    custom = devices == 8 and along_count == 4
 
     def scatter(grad):
         rows_own = lax.psum_scatter(grad, "seq", scatter_dimension=0, tiled=True)
         return lax.psum_scatter(rows_own, "dp", scatter_dimension=1, tiled=True).astype(F32)
 
-    summed_down = scatter(grad_down)
-    summed_in = scatter(grad_in)
-    summed_out = scatter(grad_out)
-    back_items, bias_rows = [], []
-    for half in range(HALVES):
-        dqkv, bias_row = attention_backward(received[half], outs[half], augs[half], grad_items[half], rows, valids[half], pairs[half])
-        back_items.append(exchange(dqkv))
-        bias_rows.append(bias_row)
-    backs = []
-    for half in range(HALVES):
-        hidden, normed, conv, mix, share, unused = fronts[half]
-        ids_rows = shifted[:, half * span : half * span + span].reshape(5, span * window)
-        backs.append(
-            call_back(place, back_items[half], hidden, mids[half][6], conv, mix, share, ids_rows, qkv_weight, conv_kernel, table_padded, gain_one, score)
-        )
-    normed_all = jnp.concatenate([front[1] for front in fronts], axis=0)
-    projected_all = jnp.concatenate([back[2] for back in backs], axis=0)
-    grad_qkv = jnp.einsum("btd,bte->de", normed_all, projected_all, preferred_element_type=F32).astype(BF16)
-    grad_qkv = jnp.swapaxes(grad_qkv.reshape(model, PAIRS, 3, 2, 64), 2, 3).reshape(model, PAIRS * 384)
-    summed_qkv = scatter(grad_qkv)
-    item_rows = jnp.concatenate(bias_rows, axis=0)
-    item_bias = jnp.einsum("ihy,yb->bih", item_rows, near_one_hot(), precision="highest")
-    pair_hot = (jnp.concatenate(pairs)[:, None] == jnp.arange(PAIRS, dtype=jnp.int32)[None, :]).astype(F32)
-    grad_bias = jnp.einsum("bih,ip->bph", item_bias, pair_hot, precision="highest").reshape(32, 2 * PAIRS)
-    grad_table = (backs[0][0] + backs[1][0])[:vocab]
-    small = backs[0][1] + backs[1][1]
-    totals = lax.psum((grad_table, small[0:5], small[6], small[5], grad_bias, grad_gain_two[0]), ("dp", "seq"))
+    if custom:
+        early_chips = call_early(act, cot, normed_two, gate_up, attended, branch)
+        early_across = over_chips(early_chips)
+        after = early_chips
+    else:
+        summed_down = scatter(jnp.einsum("bti,btd->id", act, cot, preferred_element_type=F32).astype(BF16))
+        summed_in = scatter(jnp.einsum("btd,bti->di", normed_two, gate_up, preferred_element_type=F32).astype(BF16))
+        summed_out = scatter(jnp.einsum("btd,bte->de", attended, branch, preferred_element_type=F32).astype(BF16))
+        after = grad_gain_two
+    dqkv, bias_rows = attention_backward(received, out, aug, grad_items, rows, valid, pair, after)
+    after = bias_rows
+    if custom:
+        early_plane = sum_parts(early_across, BF16, bias_rows)
+        after = early_plane
+    ids_rows = shifted.reshape(5, sequences * window)
+    table_block, projected = call_back(
+        dqkv, hidden, grad_residual, conv, mix, share, ids_rows, qkv_weight, conv_kernel, table_padded[:SMALL_ROWS], gain_one, score, after
+    )
+    item_bias = jnp.einsum("ihy,yb->bih", bias_rows, near_one_hot(), precision="highest")
+    pair_hot = (pair[:, None] == jnp.arange(PAIRS, dtype=jnp.int32)[None, :]).astype(F32)
+    grad_bias = jnp.einsum("bih,ip->bph", item_bias, pair_hot, precision="highest").reshape(32 * 2 * PAIRS)
+    tail = jnp.concatenate(
+        [
+            jnp.zeros((267, model), F32),
+            grad_gain_two,
+            jnp.pad(grad_bias, (0, model - grad_bias.shape[0]))[None, :],
+            jnp.zeros((SMALL_ROWS - 269, model), F32),
+        ],
+        axis=0,
+    )
+    if custom:
+        late, early, sums = call_tail(normed, projected, early_plane, table_block, tail)
+        odd = lax.rem(lax.axis_index("dp"), 2) == 1
+
+        def joined(block, tiles, columns):
+            block = jnp.concatenate([block[96 * k : 96 * k + 96] for k in range(tiles)], axis=1)
+            return jnp.where(odd, block[:, 64 : 64 + columns], block[:, :columns])
+
+        summed_in = jnp.concatenate([early[96 * k : 96 * k + 96] for k in range(8)], axis=1)
+        summed_down = jnp.concatenate([early[768:960], early[960:1152]], axis=1).T
+        summed_out = joined(early[1152:1344], 2, 192)
+        summed_qkv = joined(late, 5, 576)
+    else:
+        grad_qkv = jnp.einsum("btd,bte->de", normed, projected, preferred_element_type=F32).astype(BF16)
+        grad_qkv = jnp.swapaxes(grad_qkv.reshape(model, PAIRS, 3, 2, 64), 2, 3).reshape(model, PAIRS * 384)
+        summed_qkv = scatter(grad_qkv)
+        sums = call_small(table_block, tail, devices, along_count)
     return (
         layer_out,
-        totals[0],
-        totals[1],
-        totals[2],
-        totals[3],
+        sums[:vocab],
+        sums[259:264],
+        sums[265],
+        sums[264],
         summed_qkv,
-        totals[4],
+        sums[268, : 32 * 2 * PAIRS].reshape(32, 2 * PAIRS),
         summed_out,
-        totals[5],
+        sums[267],
         summed_in,
         summed_down,
     )

time: 632 us -> 442 us (0.70)
  waiting for transfers between devices: 226 us -> 13.2 us
  Pallas kernels: 217 us -> 366 us
  blocking collectives: 39.8 us -> 0 us
  matrix products: 31.6 us -> 0.47 us
  starting transfers between devices: 40.4 us -> 19.8 us
  between operations: 16.2 us -> 1.2 us
  local copies, waits for them, and re-layouts: 42 us -> 27.2 us
    pallas_call x2 -> x6, Pallas kernels: 59.1 us -> 163 us  [the longest x1 60.2 us: call_tail(): pl.pallas_call(tail_kernel, in_specs=[vmem] * 5, out_specs=[vmem] * 3, ou...]
    reduce_scatter x5 -> x0, waiting for transfers between devices: 86.6 us -> none  [the longest x3 62.8 us: scatter(): rows_own = lax.psum_scatter(grad, 'seq', scatter_dimension=0, tiled=True)]
    unnamed x12 -> x0, waiting for transfers between devices: 54.6 us -> none
    psum x1 -> x0, waiting for transfers between devices: 47.7 us -> none  [body(): lax.psum((grad_table, small[0:5], small[6], small[5], grad_bias, grad_gai...]
    psum x1 -> x0, blocking collectives: 39.8 us -> none  [body(): lax.psum((grad_table, small[0:5], small[6], small[5], grad_bias, grad_gai...]
    dot_general x5 -> x1, matrix products: 31.3 us -> 0.14 us  [body(): jnp.einsum('ihy,yb->bih', bias_rows, near_one_hot(), precision='highest')]
    pallas_call x2 -> x1, Pallas kernels: 42.7 us -> 70.2 us  [call_back(): pl.pallas_call(functools.partial(back_kernel, (local_tokens, window, devi...]
    pallas_call x2 -> x1, Pallas kernels: 42.3 us -> 68 us  [call_front(): pl.pallas_call(functools.partial(front_kernel, (local_tokens, window, dev...]
  transfers between devices with their start and end apart: 19 -> 3, of which waited for: 11 -> 1; matrix products, arithmetic and copies ran while one was open for 12% -> 3% of each run, Pallas kernels for 31% -> 12%
where the time goes in v2:
time: 442 us; the launch traced here: 439 us
  Pallas kernels  366 us (83%)
  local copies, waits for them, and re-layouts  27.2 us (6%)
  starting transfers between devices  19.8 us (4%)
  waiting for transfers between devices  13.2 us (3%)
  other arithmetic  10.8 us (2%)
    pallas_call x1, Pallas kernels, call_back(): pl.pallas_call(functools.partial(back_kernel, (local_tokens, window, devi...  70.2 us
    pallas_call x1, Pallas kernels, call_front(): pl.pallas_call(functools.partial(front_kernel, (local_tokens, window, dev...  68 us
    pallas_call x1, Pallas kernels, call_tail(): pl.pallas_call(tail_kernel, in_specs=[vmem] * 5, out_specs=[vmem] * 3, ou...  60.2 us
    pallas_call x1, Pallas kernels, call_mid(): pl.pallas_call(functools.partial(mid_kernel, (local_tokens, devices, sequ...  53.7 us
    pallas_call x1, Pallas kernels, attention_backward(): pl.pallas_call(functools.partial(bwd_kernel, blocks), grid_spec=spec, out...  38.3 us
    pallas_call x1, Pallas kernels, call_early(): pl.pallas_call(early_kernel, grid=(8,), in_specs=[pl.BlockSpec((sequences...  31.9 us
    pallas_call x1, Pallas kernels, attention_forward(): pl.pallas_call(functools.partial(fwd_kernel, blocks), grid_spec=spec, out...  26.2 us
    all_to_all x1, starting transfers between devices, over_chips(): lax.all_to_all(chips, 'seq', split_axis=0, concat_axis=0, axis_index_grou...  15.5 us
  transfers between devices with their start and end apart: 3, of which 1 were waited for; matrix products, arithmetic and copies ran while one was open for 3% of the time, Pallas kernels for 12%

profile of v2, /device:TPU:0, one launch (start us, length us, event | category | flops | bytes accessed | tf_op | source)
XLA Modules:
  0.0 438.9 jit_solution(10599325651632625314)
XLA Ops:
  1.5 1.3 collective-permute-start.1
  2.8 3.0 collective-permute-start
  5.8 0.9 convert_reduce_fusion
  6.8 1.3 select_reduce_fusion.2
  8.4 1.1 pad_convert_fusion
  9.5 1.3 broadcast_in_dim.114.gain_ref
  10.7 1.3 broadcast_in_dim.115.score_ref
  12.2 1.3 broadcast_in_dim.116.gain_ref
  13.5 3.0 multiply_convert_fusion.taps_ref
  16.4 6.1 %reorder.2.cot_ref = bf16[8,128,768]{2,1,0:T(8,128)(2,1)} custom-call(s32[8]{0:T(128)} %get-tuple-element.151.order_ref, bf16[8,128,768]{2,1,0:T(8,128)(2,1)} %source_ref.1), custom_call_target="tpu_custom_call" | custom-call | bytes 3145728 | tf_op jit(solution)/shard_map/reorder/pallas_call | solution.py:867
  23.5 1.1 concatenate.26.ids_ref
  24.6 68.0 %front.1 = (f32[8,128,768]{2,1,0:T(8,128)}, bf16[8,128,768]{2,1,0:T(8,128)(2,1)}, bf16[8,384,768]{2,1,0:T(8,128)(2,1)}, bf16[8,128,384]{2,1,0:T(8,128)(2,1)}, f3...) custom-call(s32[8,272,8]{2,1,0:T(8,128)} %concatenate.26.ids_ref, ...), custom_call_target="tpu_custom_call" | custom-call | flops 49999998976 | bytes 20000000 | tf_op jit(solution)/shard_map/front/pallas_call | solution.py:734
  92.6 26.2 %attention_forward.1 = (bf16[8,6,128,128]{3,2,1,0:T(8,128)(2,1)S(1)}, bf16[6,1024,128]{2,1,0:T(8,128)(2,1)S(1)}) custom-call(s32[6]{0:T(128)S(1)} %compare_select_fusion.2.valid_ref, s32[6]{0:T(128)S(1)} %get-tuple-element.165.pair_ref, bf16[8,6,128,384]{3,2,1,0:T(8,128)(2,1)} %get-tuple-element.35.qkv_ref, f32[6,2,1024]{2,1,0:T(2,128)S(1)} %reshape.117.row_ref), custom_call_target="tpu_custom_call" | custom-call | flops 3221225472 | bytes 12582912 | tf_op jit(solution)/shard_map/attention_forward/pallas_call | solution.py:230
  118.9 1.1 copy-done.3
  120.0 53.7 %middle.1 = (f32[8,128,768]{2,1,0:T(8,128)}, bf16[8,128,2048]{2,1,0:T(8,128)(2,1)}, bf16[8,128,4096]{2,1,0:T(8,128)(2,1)}, bf16[8,128,768]{2,1,0:T(8,128)(2,1)},...) custom-call(bf16[8,6,128,128]{3,2,1,0:T(8,128)(2,1)} %copy-done.3, ...), custom_call_target="tpu_custom_call" | custom-call | flops 49999998976 | bytes 40000000 | tf_op jit(solution)/shard_map/middle/pallas_call | solution.py:773
  173.7 31.9 %early_gradients.1.after = bf16[4,4,1344,128]{3,2,1,0:T(8,128)(2,1)} custom-call(bf16[8,128,2048]{2,1,0:T(8,128)(2,1)} %get-tuple-element.42.act_ref, bf16[8,128,768]{2,1,0:T(8,128)(2,1)} %reorder.2.cot_ref, bf16[8,128,768]{2,1,0:T(8,128)(2,1)} %get-tuple-element.43.normed_ref, bf16[8,128,4096]{2,1,0:T(8,128)(2,1)} %get-tuple-element.44.gate_up_ref, ...), custom_call_target="tpu_custom_call" | custom-call | flops 11000000512 | bytes 30000000 | tf_op jit(solution)/shard_map/early_gradients/pallas_call | solution.py:987
  205.7 15.5 %all-to-all-start = ((bf16[4,4,1344,128]{3,2,1,0:T(8,128)(2,1)}), bf16[4,4,1344,128]{3,2,1,0:T(8,128)(2,1)}, u32[]{:S(2)}, u32[]{:S(2)}) async-start(bf16[4,4,1344,128]{3,2,1,0:T(8,128)(2,1)} %early_gradients.1.after), calls=%async_computation | async-start | bytes 11010048 | tf_op jit(solution)/shard_map/all_to_all | solution.py:1153
  222.0 6.9 %reorder.3 = f32[8,128,768]{2,1,0:T(8,128)} custom-call(s32[8]{0:T(128)} %get-tuple-element.151.order_ref, f32[8,128,768]{2,1,0:T(8,128)} %get-tuple-element.38.source_ref), custom_call_target="tpu_custom_call" | custom-call | bytes 6291456 | tf_op jit(solution)/shard_map/reorder/pallas_call | solution.py:867
  229.5 38.3 %attention_backward.1 = (bf16[8,6,128,384]{3,2,1,0:T(8,128)(2,1)}, f32[6,2,1024]{2,1,0:T(2,128)S(1)}) custom-call(s32[6]{0:T(128)S(1)} %compare_select_fusion.2.valid_ref, s32[6]{0:T(128)S(1)} %get-tuple-element.165.pair_ref, bf16[8,6,128,384]{3,2,1,0:T(8,128)(2,1)} %get-tuple-element.35.qkv_ref, bf16[8,6,128,128]{3,2,1,0:T(8,128)(2,1)S(1)} %copy-done.4, ...), custom_call_target="tpu_custom_call" | custom-call | flops 8053063680 | bytes 25165824 | tf_op jit(solution)/shard_map/attention_backward/pallas_call | solution.py:277
  269.1 1.1 maximum_maximum_fusion.tail_ref
  270.2 13.2 %all-to-all-done.parts_ref = bf16[4,4,1344,128]{3,2,1,0:T(8,128)(2,1)} async-done(((bf16[4,4,1344,128]{3,2,1,0:T(8,128)(2,1)}), bf16[4,4,1344,128]{3,2,1,0:T(8,128)(2,1)}, u32[]{:S(2)}, u32[]{:S(2)}) %all-to-all-start) | async-done | bytes 5505056 | tf_op jit(solution)/shard_map/all_to_all | solution.py:1153
  283.4 4.6 %sum_parts.1.after.plane_ref = bf16[4,1344,128]{2,1,0:T(8,128)(2,1)} custom-call(bf16[4,4,1344,128]{3,2,1,0:T(8,128)(2,1)} %all-to-all-done.parts_ref, f32[6,2,1024]{2,1,0:T(2,128)} %copy-done.2), custom_call_target="tpu_custom_call" | custom-call | flops 1000000 | bytes 8257536 | tf_op jit(solution)/shard_map/sum_parts/pallas_call | solution.py:1140
  288.0 70.2 %back.1 = (f32[288,768]{1,0:T(8,128)}, bf16[8,128,2304]{2,1,0:T(8,128)(2,1)}) custom-call(bf16[8,6,128,384]{3,2,1,0:T(8,128)(2,1)} %get-tuple-element.47.grads_ref, f32[8,128,768]{2,1,0:T(8,128)} %get-tuple-element.37.hidden_ref, f32[8,128,768]{2,1,0:T(8,128)} %get-tuple-element.48.residual_ref, bf16[8,384,768]{2,1,0:T(8,128)(2,1)} %get-tuple-element.49.conv_ref, ...), custom_call_target="tpu_custom_call" | custom-call | flops 49999998976 | bytes 20000000 | tf_op jit(solution)/shard_map/back/pallas_call | solution.py:821
  358.3 60.2 %tail.1 = (f32[480,128]{1,0:T(8,128)}, f32[1344,128]{1,0:T(8,128)}, f32[288,768]{1,0:T(8,128)}) custom-call(bf16[8,128,768]{2,1,0:T(8,128)(2,1)} %get-tuple-element.39.normed_ref, bf16[8,128,2304]{2,1,0:T(8,128)(2,1)} %get-tuple-element.53.grads_ref, bf16[4,1344,128]{2,1,0:T(8,128)(2,1)} %sum_parts.1.after.plane_ref, f32[288,768]{1,0:T(8,128)} %get-tuple-element.54.one_ref, ...), custom_call_target="tpu_custom_call" | custom-call | flops 49999998976 | bytes 10000000 | tf_op jit(solution)/shard_map/tail/pallas_call | solution.py:1106
  418.4 2.1 slice.116
  420.5 1.3 slice.117
  421.9 1.5 slice_reduce_fusion
  424.9 1.0 fusion.23
  425.8 0.8 slice_dynamic-update-slice_fusion.12
  431.4 0.8 slice_dynamic-update-slice_fusion.5
  435.5 0.9 slice_dynamic-update-slice_fusion
  436.3 0.8 slice_select_fusion
  (72 shorter events, 15.9 us)
Async XLA Ops:
  0.6 11.4 %copy-start = (f32[32,12]{0,1:T(8,128)S(1)}, f32[32,12]{0,1:T(8,128)}, u32[]{:S(2)}) copy-start(f32[32,12]{0,1:T(8,128)} %param.20) | copy-start | bytes 4612
  1.5 21.0 %collective-permute-start.1 = (s32[8,4]{1,0:T(8,128)S(1)}, s32[8,4]{1,0:T(8,128)S(1)}, u32[]{:S(2)}, u32[]{:S(2)}) collective-permute-start(s32[8,4]{1,0:T(8,128)S(1)} %get-tuple-element.163), channel_id=1, source_target_pairs={{1,0},{2,1},{3,2},{4,3},{5,4},{6,5},{7,6},{9,8},{10,9},{11,10},{12... | collective-permute-start | bytes 392 | tf_op jit(solution)/shard_map/ppermute | solution.py:1319
  2.8 19.7 %collective-permute-start = (s32[8,4]{1,0:T(8,128)S(1)}, s32[8,4]{1,0:T(8,128)S(1)}, u32[]{:S(2)}, u32[]{:S(2)}) collective-permute-start(s32[8,4]{1,0:T(8,128)S(1)} %get-tuple-element.162), channel_id=1, source_target_pairs={{0,1},{1,2},{2,3},{3,4},{4,5},{5,6},{6,7},{8,9},{9,10},{10,11},{11... | collective-permute-start | bytes 392 | tf_op jit(solution)/shard_map/ppermute | solution.py:1318
  118.9 1.2 copy-start.3
  205.7 15.6 %copy-start.5 = (bf16[259,768]{1,0:T(8,128)(2,1)S(1)}, bf16[259,768]{1,0:T(8,128)(2,1)}, u32[]{:S(2)}) copy-start(bf16[259,768]{1,0:T(8,128)(2,1)} %param.15) | copy-start | bytes 1193476
  205.7 77.7 %all-to-all-start = ((bf16[4,4,1344,128]{3,2,1,0:T(8,128)(2,1)}), bf16[4,4,1344,128]{3,2,1,0:T(8,128)(2,1)}, u32[]{:S(2)}, u32[]{:S(2)}) async-start(bf16[4,4,1344,128]{3,2,1,0:T(8,128)(2,1)} %early_gradients.1.after), calls=%async_computation | async-start | bytes 11010048 | tf_op jit(solution)/shard_map/all_to_all | solution.py:1153
  222.0 7.5 %copy-start.4 = (bf16[8,6,128,128]{3,2,1,0:T(8,128)(2,1)S(1)}, bf16[8,6,128,128]{3,2,1,0:T(8,128)(2,1)}, u32[]{:S(2)}) copy-start(bf16[8,6,128,128]{3,2,1,0:T(8,128)(2,1)} %copy-done.3) | copy-start | bytes 4718596
  229.5 39.6 %copy-start.7 = (f32[1,768]{1,0:T(1,128)S(1)}, f32[1,768]{1,0:T(1,128)}, u32[]{:S(2)}) copy-start(f32[1,768]{1,0:T(1,128)} %get-tuple-element.55) | copy-start | bytes 9220
  267.8 15.6 %copy-start.2 = (f32[6,2,1024]{2,1,0:T(2,128)}, f32[6,2,1024]{2,1,0:T(2,128)S(1)}, u32[]{:S(2)}) copy-start(f32[6,2,1024]{2,1,0:T(2,128)S(1)} %get-tuple-element.52.after) | copy-start | bytes 147460
  358.2 80.4 %copy-start.1 = (f32[32,12]{0,1:T(8,128)S(1)}, f32[32,12]{0,1:T(8,128)}, u32[]{:S(2)}) copy-start(f32[32,12]{0,1:T(8,128)} %param.20) | copy-start | bytes 4612
  436.3 2.3 copy-start.6

commit v3 on v2

v3 whole, which is shorter than its diff:
```python
import functools
import jax
import jax.numpy as jnp
from jax import lax
from jax.experimental import pallas as pl
from jax.experimental.pallas import tpu as pltpu
from jax.sharding import PartitionSpec as P

thresholds = (12, 16, 23, 32, 46, 64, 91)
KB = 256
NEAR = 1024
F32 = jnp.float32
BF16 = jnp.bfloat16
NT = (((1,), (1,)), ((), ()))
NN = (((1,), (0,)), ((), ()))


def rel_bucket(relative):
    distance = jnp.abs(relative)
    larger = 8 + sum(((distance >= boundary).astype(jnp.int32) for boundary in thresholds))
    bucket = jnp.where(distance < 8, distance, larger)
    return bucket + 16 * (relative > 0).astype(jnp.int32)


def near_one_hot():
    place = jnp.arange(NEAR, dtype=jnp.int32)
    relative = jnp.where(place < NEAR - 128, KB - place, KB + NEAR - place)
    return (rel_bucket(relative)[:, None] == jnp.arange(32, dtype=jnp.int32)[None, :]).astype(F32)


def dot(a, b, dims):
    return lax.dot_general(a, b, dims, preferred_element_type=F32)


def fill_bias(strip, head, row, blocks):
    base = KB * (blocks - 2)
    width = KB * (2 * blocks - 1)
    spread = jnp.broadcast_to(row, (128, NEAR))
    rolled = pltpu.roll(spread, 0, 1, stride=1, stride_axis=0)
    far_right = jnp.broadcast_to(row[:, NEAR - 1 :], (KB, 128))
    far_left = jnp.broadcast_to(row[:, 768:769], (KB, 128))
    for start in range(0, base, 128):
        strip[head, :, start : start + 128] = far_right
    strip[head, 0:128, base : base + 768] = rolled[:, :768]
    strip[head, 128:256, base : base + 128] = far_right[:128]
    strip[head, 128:256, base + 128 : base + 768] = rolled[:, :640]
    for start in range(base + 768, width, 128):
        strip[head, :, start : start + 128] = far_left


def lanes_of(head, shape):
    lane = lax.broadcasted_iota(jnp.int32, shape, 1)
    own = (lane < 64) if head == 0 else (lane >= 64)
    return own, lane - (64 if head == 0 else 0)


def fill_keys(ka, head, keys, valid):
    own, spare = lanes_of(head, keys.shape)
    row = lax.broadcasted_iota(jnp.int32, keys.shape, 0)
    masked = jnp.where(row < valid, 0.0, -1e9)
    extra = jnp.where(spare == 0, masked, jnp.where((spare >= 1) & (spare <= 3), 1.0, 0.0))
    ka[head] = jnp.where(own, keys, extra.astype(BF16))


def move_rows(item, order_ref, source, buffer, target, sems, sorting):
    def inward(number):
        place = order_ref[number] if sorting else number
        return pltpu.make_async_copy(source.at[place], buffer.at[number], sems.at[0, number])

    def outward(number):
        place = number if sorting else order_ref[number]
        return pltpu.make_async_copy(buffer.at[number], target.at[place], sems.at[1, number])

    count = source.shape[0]

    @pl.when(item == 0)
    def _():
        for number in range(count):
            inward(number).start()

    @pl.when(item == jnp.minimum(1, pl.num_programs(0) - 1))
    def _():
        for number in range(count):
            inward(number).wait()
            outward(number).start()

    def finish():
        @pl.when(item == pl.num_programs(0) - 1)
        def _():
            for number in range(count):
                outward(number).wait()

    return finish


def fwd_kernel(
    blocks, valid_ref, pair_ref, order_ref, qkv_ref, row_ref, cot_ref, out_ref, aug_ref, sorted_ref,
    qa, ka, vt, strip, peak, acc, probs, moving, sems,
):
    item = pl.program_id(0)
    finish = move_rows(item, order_ref, cot_ref, moving, sorted_ref, sems, True)
    valid = valid_ref[item]
    tokens = blocks * KB
    joined = qkv_ref[:, 0].reshape(tokens, 384)
    queries = joined[:, 0:128]
    keys = joined[:, 128:256]
    turned = joined[:, 256:384].T
    filler = jnp.where(lax.broadcasted_iota(jnp.int32, (16, tokens), 0) == 0, 1.0, 0.0).astype(BF16)
    for head in range(2):
        own, spare = lanes_of(head, queries.shape)
        qa[head] = jnp.where(own, queries, jnp.where(spare == 0, 1.0, 0.0).astype(BF16))
        fill_keys(ka, head, keys, valid)
        vt[head, 0:64] = turned[64 * head : 64 * head + 64]
        vt[head, 64:80] = filler
        fill_bias(strip, head, row_ref[0, head : head + 1, :], blocks)
    peak[...] = jnp.full_like(peak, -1e30)
    acc[...] = jnp.zeros_like(acc)

    def step(block, unused):
        first = pl.multiple_of(block * KB, KB)
        shift = pl.multiple_of((blocks - 1 - block) * KB, KB)
        for head in range(2):
            alphas = []
            for part in range(blocks):
                here = slice(part * KB, part * KB + KB)
                logits = dot(ka[head, pl.ds(first, KB), :], qa[head, here, :], NT)
                logits = logits + strip[head, :, pl.ds(shift + part * KB, KB)]
                before = peak[head, :, here]
                after = jnp.maximum(before, jnp.max(logits, axis=0, keepdims=True))
                probs[head, :, here] = jnp.exp(logits - after).astype(BF16)
                peak[head, :, here] = after
                alphas.append(jnp.exp(before - after))
            acc[head] = acc[head] * jnp.concatenate(alphas, axis=1) + dot(
                    vt[head, :, pl.ds(first, KB)], probs[head], NN
                )
        return unused

    lax.fori_loop(0, (valid + KB - 1) // KB, step, 0)
    outs = []
    rows = []
    place = lax.broadcasted_iota(jnp.int32, (64, tokens), 0)
    for head in range(2):
        total = acc[head, 64:65, :]
        outs.append(acc[head, 0:64, :] / total)
        minus = -(peak[head] + jnp.log(total))
        high = minus.astype(BF16).astype(F32)
        rest = minus - high
        middle = rest.astype(BF16).astype(F32)
        low = rest - middle
        rows.append(jnp.where(place == 0, 1.0, jnp.where(place == 1, high, jnp.where(place == 2, middle, jnp.where(place == 3, low, 0.0)))))
    out_ref[:, 0] = jnp.concatenate(outs, axis=0).T.astype(BF16).reshape(out_ref.shape[0], out_ref.shape[2], 128)
    aug_ref[0] = jnp.concatenate([rows[1], rows[0]], axis=0).T.astype(BF16)
    finish()


def bwd_kernel(
    blocks, base_slot, moves, valid_ref, pair_ref, order_ref, qkv_ref, out_ref, aug_ref, grad_ref, row_ref, layer_ref, after,
    dqkv_ref, bias_ref, moved_ref, qa, ka, va, ga, kt, strip, tally, probs, slopes, dq, *moving,
):
    item = pl.program_id(0)
    finish = move_rows(item, order_ref, layer_ref, moving[0], moved_ref, moving[1], False) if moves else lambda: None
    valid = valid_ref[item + base_slot]
    tokens = blocks * KB
    width = KB * (2 * blocks - 1)
    local = qkv_ref.shape[2]
    joined = qkv_ref[:, 0].reshape(tokens, 384)
    queries = joined[:, 0:128]
    keys = joined[:, 128:256]
    values = joined[:, 256:384]
    grads = grad_ref[:, 0].reshape(tokens, 128)
    outs = out_ref[:, 0].reshape(tokens, 128)
    kt[...] = keys.T
    product = grads.astype(F32) * outs.astype(F32)
    high = product.astype(BF16)
    low = (product - high.astype(F32)).astype(BF16)
    row_at = lax.broadcasted_iota(jnp.int32, (128, 128), 0)
    lane_at = lax.broadcasted_iota(jnp.int32, (128, 128), 1)
    pick = jnp.where((row_at < 64) == (lane_at >= 64), -1.0, 0.0).astype(BF16)
    shifts = dot(high, pick, NN) + dot(low, pick, NN)
    shift_high = shifts.astype(BF16)
    shift_low = (shifts - shift_high.astype(F32)).astype(BF16)
    for head in range(2):
        own, spare = lanes_of(head, queries.shape)
        qa[head] = jnp.where(own, queries, aug_ref[0])
        fill_keys(ka, head, keys, valid)
        va[head] = jnp.where(own, values, jnp.where((spare == 0) | (spare == 1), 1.0, 0.0).astype(BF16))
        ga[head] = jnp.where(own, grads, jnp.where(spare == 0, shift_high, jnp.where(spare == 1, shift_low, jnp.zeros_like(shift_low))))
        fill_bias(strip, head, row_ref[0, head : head + 1, :], blocks)
    tally[...] = jnp.zeros_like(tally)
    dq[...] = jnp.zeros_like(dq)
    dqkv_ref[...] = jnp.zeros_like(dqkv_ref)

    def step(block, unused):
        first = pl.multiple_of(block * KB, KB)
        shift = pl.multiple_of((blocks - 1 - block) * KB, KB)
        key_parts = []
        value_parts = []
        for head in range(2):
            for part in range(blocks):
                here = slice(part * KB, part * KB + KB)
                there = pl.ds(shift + part * KB, KB)
                logits = dot(ka[head, pl.ds(first, KB), :], qa[head, here, :], NT)
                weights = jnp.exp(logits + strip[head, :, there])
                change = dot(va[head, pl.ds(first, KB), :], ga[head, here, :], NT)
                slope = weights * change
                tally[head, :, there] += slope
                probs[head, :, here] = weights.astype(BF16)
                slopes[head, :, here] = slope.astype(BF16)
            value_parts.append(dot(probs[head], ga[head], NN))
            key_parts.append(dot(slopes[head], qa[head], NN))
            dq[pl.ds(64 * head, 64), :] += dot(kt[pl.ds(64 * head, 64), pl.ds(first, KB)], slopes[head], NN)
        own, unused_spare = lanes_of(0, (KB, 128))
        count = KB // local
        where = pl.ds(block * count, count)
        dqkv_ref[where, 0, :, 128:256] = jnp.where(own, key_parts[0], key_parts[1]).astype(BF16).reshape(count, local, 128)
        dqkv_ref[where, 0, :, 256:384] = jnp.where(own, value_parts[0], value_parts[1]).astype(BF16).reshape(count, local, 128)
        return unused

    lax.fori_loop(0, (valid + KB - 1) // KB, step, 0)
    dqkv_ref[:, 0, :, 0:128] = dq[...].T.astype(BF16).reshape(dqkv_ref.shape[0], local, 128)
    base = KB * (blocks - 2)
    lane = lax.broadcasted_iota(jnp.int32, (1, NEAR), 1)
    flip = jnp.where(row_at + lane_at == 127, 1.0, 0.0).astype(BF16)
    for head in range(2):
        far_right = sum(tally[head, :, start : start + 128] for start in range(0, base, 128)) if base else jnp.zeros((KB, 128), F32)
        far_right = far_right[:128] + far_right[128:] + tally[head, 128:256, base : base + 128]
        left_list = [tally[head, :, start : start + 128] for start in range(base + 768, width, 128)]
        far_left = sum(left_list) if left_list else jnp.zeros((KB, 128), F32)
        near = tally[head, 0:128, base : base + 768]
        near_low = tally[head, 128:256, base + 128 : base + 768]
        near = near + jnp.concatenate([near_low, jnp.zeros((128, 128), F32)], axis=1)
        near = jnp.concatenate([near, jnp.zeros((128, NEAR - 768), F32)], axis=1)
        near_high = near.astype(BF16)
        flipped = dot(flip, near_high, NN) + dot(flip, (near - near_high.astype(F32)).astype(BF16), NN)
        rolled = pltpu.roll(flipped, NEAR - 127, 1, stride=1, stride_axis=0)
        row = jnp.sum(rolled, axis=0, keepdims=True)
        row = row + jnp.where(lane == NEAR - 1, jnp.sum(far_right), 0.0) + jnp.where(lane == 768, jnp.sum(far_left), 0.0)
        bias_ref[0, head : head + 1, :] = row
    finish()


def attention_forward(qkv, rows, valid, pair, order, cot):
    sources, items, local, unused = qkv.shape
    blocks = sources * local // KB
    tokens = sources * local
    width = KB * (2 * blocks - 1)
    spec = pltpu.PrefetchScalarGridSpec(
        num_scalar_prefetch=3,
        grid=(items,),
        in_specs=[
            pl.BlockSpec((sources, 1, local, 384), lambda i, v, p, o: (0, i, 0, 0)),
            pl.BlockSpec((1, 2, NEAR), lambda i, v, p, o: (p[i], 0, 0)),
            pl.BlockSpec(memory_space=pl.ANY),
        ],
        out_specs=[
            pl.BlockSpec((sources, 1, local, 128), lambda i, v, p, o: (0, i, 0, 0)),
            pl.BlockSpec((1, tokens, 128), lambda i, v, p, o: (i, 0, 0)),
            pl.BlockSpec(memory_space=pl.ANY),
        ],
        scratch_shapes=[
            pltpu.VMEM((2, tokens, 128), BF16),
            pltpu.VMEM((2, tokens, 128), BF16),
            pltpu.VMEM((2, 80, tokens), BF16),
            pltpu.VMEM((2, KB, width), F32),
            pltpu.VMEM((2, 1, tokens), F32),
            pltpu.VMEM((2, 80, tokens), F32),
            pltpu.VMEM((2, KB, tokens), BF16),
            pltpu.VMEM(cot.shape, cot.dtype),
            pltpu.SemaphoreType.DMA((2,) + cot.shape[:1]),
        ],
    )
    return pl.pallas_call(
        functools.partial(fwd_kernel, blocks),
        grid_spec=spec,
        out_shape=[
            jax.ShapeDtypeStruct((sources, items, local, 128), BF16),
            jax.ShapeDtypeStruct((items, tokens, 128), BF16),
            jax.ShapeDtypeStruct(cot.shape, cot.dtype),
        ],
        compiler_params=pltpu.CompilerParams(vmem_limit_bytes=50 * 2**20),
        cost_estimate=pl.CostEstimate(flops=items * tokens * tokens * 512, bytes_accessed=items * tokens * 2048, transcendentals=items * tokens * tokens * 2),
        name="attention_forward",
    )(valid, pair, order, qkv, rows, cot)


def attention_backward(qkv, outs, aug, grads, rows, valid, pair, order, layer, after, first, items):
    sources, unused, local, unused = qkv.shape
    moves = layer is not None
    layer = after if layer is None else layer
    moved = layer if moves else jnp.zeros((8, 128), F32)
    blocks = sources * local // KB
    tokens = sources * local
    width = KB * (2 * blocks - 1)
    big = lambda lanes: pl.BlockSpec((sources, 1, local, lanes), lambda i, v, p, o: (0, i + first, 0, 0))
    spec = pltpu.PrefetchScalarGridSpec(
        num_scalar_prefetch=3,
        grid=(items,),
        in_specs=[
            big(384),
            big(128),
            pl.BlockSpec((1, tokens, 128), lambda i, v, p, o: (i + first, 0, 0)),
            big(128),
            pl.BlockSpec((1, 2, NEAR), lambda i, v, p, o: (p[i + first], 0, 0)),
            pl.BlockSpec(memory_space=pl.ANY),
            pl.BlockSpec(memory_space=pl.ANY),
        ],
        out_specs=[
            pl.BlockSpec((sources, 1, local, 384), lambda i, v, p, o: (0, i, 0, 0)),
            pl.BlockSpec((1, 2, NEAR), lambda i, v, p, o: (i, 0, 0)),
            pl.BlockSpec(memory_space=pl.ANY),
        ],
        scratch_shapes=[
            pltpu.VMEM((2, tokens, 128), BF16),
            pltpu.VMEM((2, tokens, 128), BF16),
            pltpu.VMEM((2, tokens, 128), BF16),
            pltpu.VMEM((2, tokens, 128), BF16),
            pltpu.VMEM((128, tokens), BF16),
            pltpu.VMEM((2, KB, width), F32),
            pltpu.VMEM((2, KB, width), F32),
            pltpu.VMEM((2, KB, tokens), BF16),
            pltpu.VMEM((2, KB, tokens), BF16),
            pltpu.VMEM((128, tokens), F32),
        ]
        + ([pltpu.VMEM(layer.shape, layer.dtype), pltpu.SemaphoreType.DMA((2,) + layer.shape[:1])] if moves else []),
    )
    return pl.pallas_call(
        functools.partial(bwd_kernel, blocks, first, moves),
        grid_spec=spec,
        out_shape=[
            jax.ShapeDtypeStruct((sources, items, local, 384), BF16),
            jax.ShapeDtypeStruct((items, 2, NEAR), F32),
            jax.ShapeDtypeStruct(moved.shape, moved.dtype),
        ],
        compiler_params=pltpu.CompilerParams(vmem_limit_bytes=50 * 2**20),
        cost_estimate=pl.CostEstimate(flops=items * tokens * tokens * 1280, bytes_accessed=items * tokens * 4096, transcendentals=items * tokens * tokens * 2),
        name="attention_backward",
    )(valid, pair, order, qkv, outs, aug, grads, rows, layer, after)


VPAD = 384
PAIRS = 6
TN = (((0,), (0,)), ((), ()))
SQRT_2_OVER_PI = 0.7978845608028654


def block_masks(masks, first_byte, total_bytes):
    shape = masks.shape[2:]
    conv_at = first_byte - 2 + lax.broadcasted_iota(jnp.int32, shape, 1)
    token = lax.broadcasted_iota(jnp.int32, shape, 0)
    for side in range(2):
        place = first_byte + 2 * token + side
        for size in range(1, 5):
            start = (place // size) * size
            inside = (conv_at >= start) & (conv_at < start + size) & (conv_at < total_bytes)
            masks[side, size - 1] = jnp.where(inside, 1.0 / size, 0.0)


def split_two(values):
    high = values.astype(BF16)
    return high, (values - high.astype(F32)).astype(BF16)


def permute_weight(weight, out):
    rows = weight.shape[0]
    low = lax.broadcasted_iota(jnp.int32, (rows, 128), 1) < 64
    for pair in range(PAIRS):
        at = pair * 384
        one, two, three = (weight[:, at + 128 * k : at + 128 * k + 128] for k in range(3))
        out[:, at : at + 128] = jnp.where(low, one, two)
        out[:, at + 128 : at + 256] = pltpu.roll(jnp.where(low, three, one).astype(F32), 64, 1).astype(BF16)
        out[:, at + 256 : at + 384] = jnp.where(low, two, three)


def greet(axis, here, count):
    barrier = pltpu.get_barrier_semaphore()

    def signal(step, unused):
        pl.semaphore_signal(barrier, inc=1, device_id={axis: lax.rem(here + step, count)}, device_id_type=pl.DeviceIdType.MESH)
        return unused

    lax.fori_loop(1, count, signal, 0)


def item_copy(devices, me, source, target, other, slot, sems):
    send, recv, unused = sems

    def outward():
        offset = lax.rem(other - me + devices, devices)
        return pltpu.make_async_remote_copy(
            src_ref=source, dst_ref=target, send_sem=send.at[offset, slot], recv_sem=recv.at[offset, slot],
            device_id={"seq": other}, device_id_type=pl.DeviceIdType.MESH,
        )

    def inward():
        offset = lax.rem(me - other + devices, devices)
        return pltpu.make_async_remote_copy(
            src_ref=source, dst_ref=target, send_sem=send.at[offset, slot], recv_sem=recv.at[offset, slot],
            device_id={"seq": other}, device_id_type=pl.DeviceIdType.MESH,
        )

    return outward, inward


def start_item(devices, me, source, target, other, slot, sems):
    @pl.when(other == me)
    def _():
        pltpu.make_async_copy(source, target, sems[2].at[slot]).start()

    @pl.when(other != me)
    def _():
        item_copy(devices, me, source, target, other, slot, sems)[0]().start()


def finish_sends(devices, me, total, source_of, target_of, sems):
    def wait(item, unused):
        other, slot = lax.rem(item, devices), item // devices

        @pl.when(other != me)
        def _():
            item_copy(devices, me, source_of(other, slot), target_of(other, slot), other, slot, sems)[0]().wait_send()

        return unused

    lax.fori_loop(0, total, wait, 0)


def finish_receives(devices, me, total, source_of, target_of, sems):
    per_device = -(-total // devices)

    def wait(at, unused):
        other, slot = at // per_device, lax.rem(at, per_device)

        @pl.when((slot * devices + me < total) & (other != me))
        def _():
            item_copy(devices, me, source_of(other, slot), target_of(other, slot), other, slot, sems)[1]().wait_recv()

        @pl.when((slot * devices + me < total) & (other == me))
        def _():
            pltpu.make_async_copy(source_of(other, slot), target_of(other, slot), sems[2].at[slot]).wait()

        return unused

    lax.fori_loop(0, devices * per_device, wait, 0)


def front_kernel(
    sizes, ids_ref, table_ref, weight_ref, vectors_ref,
    hidden_ref, normed_ref, conv_ref, mix_ref, share_ref, items_ref, masks, wide, permuted, stage, taps, *sems,
):
    local_tokens, window, devices, total = sizes
    step = pl.program_id(0)
    me = lax.axis_index("seq")

    @pl.when(step == 0)
    def _():
        greet("seq", me, devices)
        block_masks(masks, me * 2 * local_tokens, devices * 2 * local_tokens)
        permute_weight(weight_ref, permuted)
        table = table_ref[...].astype(F32)
        for tap in range(5):
            taps[tap] = (vectors_ref[tap : tap + 1, :] * table).astype(BF16)

    together = ids_ref.shape[0]
    score = vectors_ref[7:8, :]
    gain = vectors_ref[5:6, :]
    model = score.shape[1]
    score_high, score_low = split_two(score)
    row16 = lax.broadcasted_iota(jnp.int32, (16, model), 0)
    score_rows = jnp.where(row16 == 0, score_high.astype(F32), jnp.where(row16 == 1, score_low.astype(F32), 0.0)).astype(BF16)
    lane = lax.broadcasted_iota(jnp.int32, (together * window, VPAD), 1)
    width = masks.shape[3]
    ids = ids_ref[...].reshape(together * window, 8)
    conv_all = jnp.zeros((together * window, model), F32)
    for tap in range(5):
        hot = jnp.where(ids[:, tap : tap + 1] == lane, 1.0, 0.0).astype(BF16)
        conv_all = conv_all + dot(hot, taps[tap], NN)
    for one in range(together):
        high, low = split_two(conv_all[one * window : (one + 1) * window])
        conv_ref[one, 0:window] = high
        wide[one, 0, 0:window] = high
        wide[one, 1, 0:window] = low
        if width > window:
            wide[one, :, window:width] = jnp.zeros((2, width - window, model), BF16)
            conv_ref[one, window:width] = jnp.zeros((width - window, model), BF16)
        high = wide[one, 0]
        low = wide[one, 1]
        along = jnp.sum(dot(score_rows, high, NT), axis=0, keepdims=True) + dot(score_rows, low, NT)[0:1]
        mixed = jnp.zeros((local_tokens, width), F32)
        kept = jnp.zeros((local_tokens, 128), F32)
        lane128 = lax.broadcasted_iota(jnp.int32, (local_tokens, 128), 1)
        for side in range(2):
            scores = [jnp.sum(masks[side, k] * along, axis=1, keepdims=True) for k in range(4)]
            top = jnp.maximum(jnp.maximum(scores[0], scores[1]), jnp.maximum(scores[2], scores[3]))
            powers = [jnp.exp(value - top) for value in scores]
            under = 1.0 / (powers[0] + powers[1] + powers[2] + powers[3])
            for k in range(4):
                share = powers[k] * under
                mixed = mixed + share * masks[side, k]
                kept = jnp.where(lane128 == 4 * side + k, share, kept)
        share_ref[one] = kept
        mix_high, mix_low = split_two(mixed * 0.5)
        mix_ref[one] = mix_high
        hidden = dot(mix_high, high, NN) + dot(mix_high, low, NN) + dot(mix_low, high, NN)
        hidden_ref[one] = hidden
        scale = lax.rsqrt(jnp.mean(hidden * hidden, axis=1, keepdims=True) + 1e-06)
        normed_ref[one] = (hidden * scale * gain).astype(BF16)
    normed = normed_ref[...].reshape(together * local_tokens, model)
    for pair in range(PAIRS):
        piece = dot(normed, permuted[:, pair * 384 : pair * 384 + 384], NN).astype(BF16)
        for one in range(together):
            item = (step * together + one) * PAIRS + pair
            other, slot = lax.rem(item, devices), item // devices
            stage[other, slot] = piece[one * local_tokens : (one + 1) * local_tokens]

    @pl.when(step == 0)
    def _():
        pl.semaphore_wait(pltpu.get_barrier_semaphore(), devices - 1)

    send_items(devices, me, step * together * PAIRS, together * PAIRS, stage, items_ref, sems)

    @pl.when(step == pl.num_programs(0) - 1)
    def _():
        finish_sends(devices, me, total, lambda other, slot: stage.at[other, slot], lambda other, slot: items_ref.at[me, slot], sems)
        finish_receives(devices, me, total, lambda other, slot: stage.at[other, slot], lambda other, slot: items_ref.at[other, slot], sems)


def send_group(devices, me, total, group, number, source, arrived, sems):
    for slot in range(-(-total // devices)):
        item = slot * devices + me

        @pl.when((item < total) & (item // group == number))
        def _():
            def send(offset, unused):
                other = lax.rem(me + offset, devices)
                start_item(devices, me, source.at[other, slot], arrived.at[me, slot], other, slot, sems)
                return unused

            lax.fori_loop(0, devices, send, 0)


def send_items(devices, me, first, count, stage, target, sems):
    def send(at, unused):
        item = first + at
        other, slot = lax.rem(item, devices), item // devices
        start_item(devices, me, stage.at[other, slot], target.at[me, slot], other, slot, sems)
        return unused

    lax.fori_loop(0, count, send, 0)


def take_items(devices, me, first, count, source, arrived, sems):
    def take(at, unused):
        item = first + at
        take_item(devices, me, lax.rem(item, devices), item // devices, source, arrived, sems)
        return unused

    lax.fori_loop(0, count, take, 0)


def finish_groups(devices, me, total, source, arrived, sems):
    per_device = -(-total // devices)

    def wait(at, unused):
        slot, offset = at // devices, lax.rem(at, devices)
        other = lax.rem(me + offset, devices)

        @pl.when((slot * devices + me < total) & (offset != 0))
        def _():
            item_copy(devices, me, source.at[other, slot], arrived.at[me, slot], other, slot, sems)[0]().wait_send()

        return unused

    lax.fori_loop(0, devices * per_device, wait, 0)


def take_item(devices, me, other, slot, source, arrived, sems):
    @pl.when(other == me)
    def _():
        pltpu.make_async_copy(source.at[me, slot], arrived.at[me, slot], sems[2].at[slot]).wait()

    @pl.when(other != me)
    def _():
        item_copy(devices, me, source.at[other, slot], arrived.at[other, slot], other, slot, sems)[1]().wait_recv()


def mid_kernel(
    sizes, att_ref, hidden_ref, cot_ref, out_weight_ref, in_weight_ref, down_ref, vectors_ref,
    layer_ref, act_ref, gate_up_ref, normed_ref, attended_ref, branch_ref, residual_ref, items_ref, gain_out,
    arrived, stage, keep_gain, grad_act, *sems,
):
    local_tokens, devices, total = sizes
    in_sems, out_sems = sems[:3], sems[3:]
    step = pl.program_id(0)
    me = lax.axis_index("seq")

    @pl.when(step == 0)
    def _():
        greet("seq", me, devices)
        keep_gain[...] = jnp.zeros_like(keep_gain)
        pl.semaphore_wait(pltpu.get_barrier_semaphore(), devices - 1)

    together = hidden_ref.shape[0]
    group = together * PAIRS
    rows = together * local_tokens
    model = vectors_ref.shape[1]

    here_rows = pl.ds(pl.multiple_of(step * rows, 128), rows)

    @pl.when(step == 0)
    def _():
        send_group(devices, me, total, group, 0, att_ref, arrived, in_sems)
        every = cot_ref[...].reshape(grad_act.shape[0], model)
        for first in range(0, down_ref.shape[0], 512):
            grad_act[:, first : first + 512] = dot(every, down_ref[first : first + 512, :], NT)

    take_items(devices, me, step * group, group, att_ref, arrived, in_sems)

    @pl.when(step + 1 < pl.num_programs(0))
    def _():
        send_group(devices, me, total, group, step + 1, att_ref, arrived, in_sems)

    gathered = []
    for one in range(together):
        pieces = []
        for pair in range(PAIRS):
            item = (step * together + one) * PAIRS + pair
            other, slot = lax.rem(item, devices), item // devices
            pieces.append(arrived[other, slot])
        gathered.append(jnp.concatenate(pieces, axis=1))
    attended = jnp.concatenate(gathered, axis=0)
    attended_ref[...] = attended.reshape(attended_ref.shape)
    residual = hidden_ref[...].reshape(rows, model) + dot(attended, out_weight_ref[...], NN)
    gain = vectors_ref[6:7, :]
    scale = lax.rsqrt(jnp.mean(residual * residual, axis=1, keepdims=True) + 1e-06)
    normed = (residual * scale * gain).astype(BF16)
    normed_ref[...] = normed.reshape(normed_ref.shape)
    cot = cot_ref[pl.ds(step * together, together)].reshape(rows, model)
    hidden_units = down_ref.shape[0]
    chunk = 512
    layer = residual
    back = jnp.zeros_like(residual)
    for first in range(0, hidden_units, chunk):
        here = slice(first, first + chunk)
        there = slice(hidden_units + first, hidden_units + first + chunk)
        gate = dot(normed, in_weight_ref[:, here], NN)
        up = dot(normed, in_weight_ref[:, there], NN)
        grad = grad_act[here_rows, here]
        square = gate * gate
        inner = gate * (SQRT_2_OVER_PI + (SQRT_2_OVER_PI * 0.044715) * square)
        curve = jnp.tanh(inner)
        half_plus = 0.5 + 0.5 * curve
        smooth = gate * half_plus
        slope = half_plus + (0.5 * gate) * (1.0 - curve * curve) * (SQRT_2_OVER_PI + (3 * SQRT_2_OVER_PI * 0.044715) * square)
        act = (smooth * up).astype(BF16)
        grad_gate = (grad * up * slope).astype(BF16)
        grad_up = (grad * smooth).astype(BF16)
        act_ref[:, :, here] = act.reshape(together, local_tokens, chunk)
        gate_up_ref[:, :, here] = grad_gate.reshape(together, local_tokens, chunk)
        gate_up_ref[:, :, there] = grad_up.reshape(together, local_tokens, chunk)
        layer = layer + dot(act, down_ref[here, :], NN)
        back = back + dot(grad_gate, in_weight_ref[:, here], NT) + dot(grad_up, in_weight_ref[:, there], NT)
    layer_ref[...] = layer.reshape(layer_ref.shape)
    weighted = gain * back
    inner_mean = jnp.mean(residual * weighted, axis=1, keepdims=True)
    grad_residual = cot.astype(F32) + scale * weighted - residual * (scale * scale * scale * inner_mean)
    residual_ref[...] = grad_residual.reshape(residual_ref.shape)
    branch = grad_residual.astype(BF16)
    branch_ref[...] = branch.reshape(branch_ref.shape)
    grad_attended = dot(branch, out_weight_ref[...], NT).astype(BF16)
    for one in range(together):
        for pair in range(PAIRS):
            item = (step * together + one) * PAIRS + pair
            other, slot = lax.rem(item, devices), item // devices
            stage[other, slot] = grad_attended[one * local_tokens : (one + 1) * local_tokens, pair * 128 : pair * 128 + 128]
    keep_gain[...] += jnp.sum((back * residual * scale).reshape(rows // 8, 8, model), axis=0)
    gain_out[...] = jnp.sum(keep_gain[...], axis=0, keepdims=True)
    send_items(devices, me, step * group, group, stage, items_ref, out_sems)

    @pl.when(step == pl.num_programs(0) - 1)
    def _():
        finish_groups(devices, me, total, att_ref, arrived, in_sems)
        finish_sends(devices, me, total, lambda other, slot: stage.at[other, slot], lambda other, slot: items_ref.at[me, slot], out_sems)
        finish_receives(devices, me, total, lambda other, slot: stage.at[other, slot], lambda other, slot: items_ref.at[other, slot], out_sems)


def back_kernel(
    sizes, custom, one_ref, two_ref, hidden_ref, residual_ref, conv_ref, mix_ref, share_ref, ids_ref, weight_ref,
    table_ref, vectors_ref, bias_ref, bias_hot_ref, gain_two_ref, *refs,
):
    local_tokens, window, devices = sizes
    step = pl.program_id(0)
    last = step == pl.num_programs(0) - 1
    me = lax.axis_index("seq")
    plane = lax.axis_index("dp")
    model = vectors_ref.shape[1]
    if custom:
        normed_ref, across_ref, planes_ref = refs[:3]
        block, qkv_out, in_out, down_out, weight_out = refs[3:8]
        refs = refs[8:]
    else:
        block, flat_out, refs = refs[0], refs[1], refs[2:]
    masks, permuted, tap_sums, keep_gain, keep_score = refs[:5]
    refs = refs[5:]
    small = SmallSums(block, refs[:5], refs[5:13])
    refs = refs[13:]

    @pl.when(step == 0)
    def _():
        greet("seq", me, devices)
        greet("dp", plane, small.along)
        keep_gain[...] = jnp.zeros_like(keep_gain)
        keep_score[...] = jnp.zeros_like(keep_score)
        tap_sums[...] = jnp.zeros_like(tap_sums)
        pl.semaphore_wait(pltpu.get_barrier_semaphore(), devices + small.along - 2)

    half = one_ref.shape[1]

    def block_of(item):
        other, slot = lax.rem(item, devices), item // devices
        if isinstance(item, int):
            return (one_ref if slot < half else two_ref)[other, slot % half]
        return jnp.where(slot < half, one_ref[other, jnp.minimum(slot, half - 1)], two_ref[other, jnp.maximum(slot - half, 0)])

    if custom:
        reduce = WeightSums(normed_ref, across_ref, planes_ref, block_of, refs)

        @pl.when(step == 0)
        def _():
            reduce.begin()
            reduce.late()

        @pl.when(step == 1)
        def _():
            reduce.second()

        @pl.when(step == 5)
        def _():
            reduce.third()
            reduce.between()

    @pl.when(step == 0)
    def _():
        block_masks(masks, me * 2 * local_tokens, devices * 2 * local_tokens)
        permute_weight(weight_ref, permuted)

    projected = jnp.concatenate([block_of(step * PAIRS + pair) for pair in range(PAIRS)], axis=1)
    if not custom:
        flat_out[0] = projected
    width = masks.shape[3]
    grad_normed = dot(projected, permuted[...], NT)
    hidden = hidden_ref[0]
    gain = vectors_ref[5:6, :]
    score = vectors_ref[7:8, :]
    scale = lax.rsqrt(jnp.mean(hidden * hidden, axis=1, keepdims=True) + 1e-06)
    weighted = gain * grad_normed
    inner_mean = jnp.mean(hidden * weighted, axis=1, keepdims=True)
    grad_hidden = residual_ref[0] + scale * weighted - hidden * (scale * scale * scale * inner_mean)
    keep_gain[...] += jnp.sum((grad_normed * hidden * scale).reshape(local_tokens // 8, 8, model), axis=0)
    high, low = split_two(grad_hidden)
    vector = jnp.broadcast_to(score.astype(BF16), (local_tokens, model))
    conv = conv_ref[0]
    cross = 0.5 * (dot(high, conv, NT) + dot(low, conv, NT))
    kept = share_ref[0]
    total = jnp.zeros((local_tokens, width), F32)
    for side in range(2):
        shares = [kept[:, 4 * side + k : 4 * side + k + 1] for k in range(4)]
        grads = [jnp.sum(masks[side, k] * cross, axis=1, keepdims=True) for k in range(4)]
        mean = sum(share * grad for share, grad in zip(shares, grads))
        for k in range(4):
            total = total + (shares[k] * (grads[k] - mean)) * masks[side, k]
    column = jnp.sum(total, axis=0, keepdims=True)
    column_high, column_low = split_two(column)
    row16 = lax.broadcasted_iota(jnp.int32, (16, width), 0)
    column_rows = jnp.where(row16 == 0, column_high.astype(F32), jnp.where(row16 == 1, column_low.astype(F32), 0.0)).astype(BF16)
    keep_score[...] += dot(column_rows, conv, NN)
    left = jnp.concatenate([mix_ref[0], total.astype(BF16)], axis=0)
    right = jnp.concatenate([high, vector], axis=0)
    slope = dot(left, right, TN)
    slope = slope[0:window].astype(BF16)
    row = lax.broadcasted_iota(jnp.int32, (SMALL_ROWS, window), 0)
    hots = [jnp.where(ids_ref[0, tap : tap + 1, :] == row, 1.0, 0.0).astype(BF16) for tap in range(5)]
    for tap in range(5):
        tap_sums[tap] += dot(hots[tap], slope, NN)

    @pl.when(last)
    def _():
        table_grad = jnp.zeros((SMALL_ROWS, model), F32)
        table = table_ref[0:SMALL_ROWS, :].astype(F32)
        place = lax.broadcasted_iota(jnp.int32, (SMALL_ROWS, model), 0)
        extra = []
        for tap in range(5):
            sums = tap_sums[tap]
            table_grad = table_grad + vectors_ref[tap : tap + 1, :] * sums
            extra.append(jnp.sum(sums * table, axis=0, keepdims=True))
        extra.append(jnp.sum(keep_gain[...], axis=0, keepdims=True))
        extra.append(jnp.sum(keep_score[...], axis=0, keepdims=True))
        extra.append(gain_two_ref[...])
        for index, value in enumerate(extra):
            table_grad = jnp.where(place == 259 + index, value, table_grad)
        block[...] = table_grad
        heads = jnp.zeros((16, 128), F32)
        head_row = lax.broadcasted_iota(jnp.int32, (16, 128), 0)
        for slot in range(bias_ref.shape[0]):
            first, second = split_two(bias_ref[slot])
            sums = dot(first, bias_hot_ref[...], NN) + dot(second, bias_hot_ref[...], NN)
            pair = lax.rem(slot * devices + me, PAIRS)
            heads = heads + jnp.where(head_row == 2 * pair, sums[0:1], 0.0) + jnp.where(head_row == 2 * pair + 1, sums[1:2], 0.0)
        block[272:288, 0:128] = heads
        small.pack()
        small.one_start()
        if custom:
            reduce.fourth()
        small.one_finish()
        small.two_finish()
        if custom:
            reduce.finish(in_out, down_out, weight_out)
        small.three_finish()
        if custom:
            reduce.finish_late(qkv_out)
        small.four_finish()


def finish_kernel(block, *refs):
    refs = list(refs)
    count = (len(refs) - 6) // 2
    for source, target in zip(refs[:count], refs[count : 2 * count]):
        target[...] = source[...]
    table_out, taps_out, one_out, score_out, two_out, bias_out = refs[2 * count :]
    table_out[...] = block[0:259, :]
    taps_out[...] = block[259:264, :]
    one_out[...] = block[264, :]
    score_out[...] = block[265, :]
    two_out[...] = block[266, :]
    bias_out[...] = block[272:288, 0:128].T[0:32, 0:12]


def call_finish(block, sums):
    model = block.shape[1]
    shape = lambda *dims: jax.ShapeDtypeStruct(dims, F32)
    return pl.pallas_call(
        finish_kernel,
        out_shape=[shape(*x.shape) for x in sums] + [shape(259, model), shape(5, model), shape(model), shape(model), shape(model), shape(32, 12)],
        compiler_params=pltpu.CompilerParams(vmem_limit_bytes=VMEM_LIMIT),
        name="finish",
    )(block, *sums)


VMEM_LIMIT = 58 * 2**20
TOGETHER = 2


def item_sems(devices, per_device):
    dma = pltpu.SemaphoreType.DMA
    return [dma((devices, per_device)), dma((devices, per_device)), dma((per_device,))]


def whole(*shape):
    return pl.BlockSpec(shape, lambda s, *_: (0,) * len(shape), pipeline_mode=pl.Buffered(1))


def part(*shape):
    return pl.BlockSpec(shape, lambda s, *_: (s,) + (0,) * (len(shape) - 1))


ANYWHERE = pl.BlockSpec(memory_space=pl.ANY)


def remote_params(number):
    return pltpu.CompilerParams(vmem_limit_bytes=VMEM_LIMIT, collective_id=number, has_side_effects=True)


def call_front(ids, table, weight, vectors, local_tokens, devices, per_device):
    sequences, window, unused = ids.shape
    width = -(-window // 128) * 128
    model = weight.shape[0]
    return pl.pallas_call(
        functools.partial(front_kernel, (local_tokens, window, devices, sequences * PAIRS)),
        grid=(sequences,),
        in_specs=[part(1, window, 8), whole(*table.shape), whole(*weight.shape), whole(*vectors.shape)],
        out_specs=[
            part(1, local_tokens, model),
            part(1, local_tokens, model),
            part(1, width, model),
            part(1, local_tokens, width),
            part(1, local_tokens, 128),
            ANYWHERE,
        ],
        scratch_shapes=[
            pltpu.VMEM((2, 4, local_tokens, width), F32),
            pltpu.VMEM((1, 2, width, model), BF16),
            pltpu.VMEM(weight.shape, BF16),
            pltpu.VMEM((devices, per_device, local_tokens, 384), BF16),
            pltpu.VMEM((5,) + table.shape, BF16),
        ]
        + item_sems(devices, per_device),
        out_shape=[
            jax.ShapeDtypeStruct((sequences, local_tokens, model), F32),
            jax.ShapeDtypeStruct((sequences, local_tokens, model), BF16),
            jax.ShapeDtypeStruct((sequences, width, model), BF16),
            jax.ShapeDtypeStruct((sequences, local_tokens, width), BF16),
            jax.ShapeDtypeStruct((sequences, local_tokens, 128), F32),
            jax.ShapeDtypeStruct((devices, per_device, local_tokens, 384), BF16),
        ],
        compiler_params=remote_params(3),
        cost_estimate=pl.CostEstimate(flops=5 * 10**10, bytes_accessed=2 * 10**7, transcendentals=10**5),
        name="front",
    )(ids, table, weight, vectors)


def call_mid(att, hidden, cot, out_weight, in_weight, down_weight, vectors):
    devices, per_device, local_tokens, unused = att.shape
    sequences, unused, model = hidden.shape
    hidden_units = down_weight.shape[0]
    rows = lambda lanes: part(TOGETHER, local_tokens, lanes)
    full = lambda lanes, kind: jax.ShapeDtypeStruct((sequences, local_tokens, lanes), kind)
    return pl.pallas_call(
        functools.partial(mid_kernel, (local_tokens, devices, sequences * PAIRS)),
        grid=(sequences // TOGETHER,),
        in_specs=[
            ANYWHERE,
            rows(model),
            whole(*cot.shape),
            whole(*out_weight.shape),
            whole(*in_weight.shape),
            whole(*down_weight.shape),
            whole(*vectors.shape),
        ],
        out_specs=[
            rows(model),
            rows(hidden_units),
            rows(2 * hidden_units),
            rows(model),
            rows(model),
            rows(model),
            rows(model),
            ANYWHERE,
            whole(1, model),
        ],
        scratch_shapes=[pltpu.VMEM(att.shape, BF16), pltpu.VMEM(att.shape, BF16), pltpu.VMEM((8, model), F32), pltpu.VMEM((sequences * local_tokens, hidden_units), F32)]
        + item_sems(devices, per_device)
        + item_sems(devices, per_device),
        out_shape=[
            full(model, F32),
            full(hidden_units, BF16),
            full(2 * hidden_units, BF16),
            full(model, BF16),
            full(model, BF16),
            full(model, BF16),
            full(model, F32),
            jax.ShapeDtypeStruct(att.shape, BF16),
            jax.ShapeDtypeStruct((1, model), F32),
        ],
        compiler_params=remote_params(4),
        cost_estimate=pl.CostEstimate(flops=5 * 10**10, bytes_accessed=4 * 10**7, transcendentals=10**6),
        name="middle",
    )(att, hidden, cot, out_weight, in_weight, down_weight, vectors)


def call_back(custom, one, two, hidden, residual, conv, mix, share, ids, weight, table, vectors, bias_rows, gain_two, along, extra):
    devices, unused, local_tokens, unused = one.shape
    sequences, unused, model = hidden.shape
    width = conv.shape[1]
    window = ids.shape[2]
    bias_hot = jnp.pad(near_one_hot(), ((0, 0), (0, 96))).astype(BF16)
    out_specs = [whole(SMALL_ROWS, model)]
    out_shape = [jax.ShapeDtypeStruct((SMALL_ROWS, model), F32)]
    scratch = []
    specs = []
    if custom:
        specs = [whole(*x.shape) for x in extra]
        sums = [(96, 576), (96, 1024), (256, 192), (96, 192)]
        out_specs = out_specs + [whole(*shape) for shape in sums]
        out_shape = out_shape + [jax.ShapeDtypeStruct(shape, F32) for shape in sums]
        scratch = weight_scratch(model, sequences * local_tokens)
    else:
        out_specs = out_specs + [part(1, local_tokens, PAIRS * 384)]
        out_shape = out_shape + [jax.ShapeDtypeStruct((sequences, local_tokens, PAIRS * 384), BF16)]
    return pl.pallas_call(
        functools.partial(back_kernel, (local_tokens, window, devices), custom),
        grid=(sequences,),
        in_specs=[
            whole(*one.shape),
            whole(*two.shape),
            part(1, local_tokens, model),
            part(1, local_tokens, model),
            part(1, width, model),
            part(1, local_tokens, width),
            part(1, local_tokens, 128),
            part(1, 8, window),
            whole(*weight.shape),
            whole(*table.shape),
            whole(*vectors.shape),
            whole(*bias_rows.shape),
            whole(*bias_hot.shape),
            whole(1, model),
        ]
        + specs,
        out_specs=out_specs,
        scratch_shapes=[
            pltpu.VMEM((2, 4, local_tokens, width), F32),
            pltpu.VMEM(weight.shape, BF16),
            pltpu.VMEM((5, SMALL_ROWS, model), F32),
            pltpu.VMEM((8, model), F32),
            pltpu.VMEM((16, model), F32),
        ]
        + small_scratch(devices, along)
        + scratch,
        out_shape=out_shape,
        compiler_params=remote_params(5),
        cost_estimate=pl.CostEstimate(flops=10**11, bytes_accessed=2 * 10**7, transcendentals=10**5),
        name="back",
    )(one, two, hidden, residual, conv, mix, share, ids, weight, table, vectors, bias_rows, bias_hot, gain_two, *extra)


IN_ROWS = 8 * 96 + 2 * 96
REST_ROWS = 2 * 192
LATE_ROWS = 5 * 96


def meet_sibling(core):
    barrier = pltpu.get_barrier_semaphore()
    sibling = lax.axis_index("seq") + 1 - 2 * core
    pl.semaphore_signal(barrier, inc=1, device_id={"seq": sibling}, device_id_type=pl.DeviceIdType.MESH)
    pl.semaphore_wait(barrier, 1)


def to_sibling(core, source, target, send_sem, recv_sem):
    sibling = lax.axis_index("seq") + 1 - 2 * core
    return pltpu.make_async_remote_copy(
        src_ref=source, dst_ref=target, send_sem=send_sem, recv_sem=recv_sem,
        device_id={"seq": sibling}, device_id_type=pl.DeviceIdType.MESH,
    )


def spread_rows(core, source, lanes, keep_ref, send_ref, index_of):
    for chip in range(4):
        for other, ref in ((0, keep_ref), (1, send_ref)):
            device = 2 * chip + lax.rem(core + other, 2)
            rows = pl.ds(pl.multiple_of(device * 96, 32), 96)
            ref[index_of(chip)] = source[rows, lanes]


def early_kernel(
    act_ref, cot_ref, normed_ref, gate_up_ref, attended_ref, branch_ref, after, keep_in, keep_rest,
    other_in, got_in, other_rest, got_rest, cot_t, normed_t, result, send_in, recv_in, send_down, recv_down, send_out, recv_out,
):
    step = pl.program_id(0)
    core = lax.rem(lax.axis_index("seq"), 2)
    model = cot_t.shape[0]
    tokens = cot_t.shape[1]
    out_rows = pl.ds(768, 192)
    out_copy = to_sibling(core, other_in.at[:, :, out_rows], got_in.at[:, :, out_rows], send_out, recv_out)

    def in_copy(at):
        rows = pl.ds(pl.multiple_of(384 * lax.rem(at, 2), 384), 384)
        return to_sibling(core, other_in.at[:, at // 2, rows], got_in.at[:, at // 2, rows], send_in.at[at], recv_in.at[at])

    def down_copy(chip):
        return to_sibling(core, other_rest.at[:, chip], got_rest.at[:, chip], send_down.at[chip], recv_down.at[chip])

    @pl.when(step == 0)
    def _():
        meet_sibling(core)
        cot_t[...] = cot_ref[...].reshape(tokens, model).T
        normed_t[...] = attended_ref[...].reshape(tokens, model).T
        for first in range(0, model, 256):
            result[:, 0:256] = dot(normed_t[...], branch_ref[:, :, first : first + 256].reshape(tokens, 256), NN).astype(BF16)
            for half in range(2):
                tile = first // 128 + half
                for column, slot in {0: ((0, 0),), 1: ((0, 1), (1, 0)), 2: ((1, 1),), 3: ((2, 0),), 4: ((2, 1), (3, 0)), 5: ((3, 1),)}[tile]:
                    rows = slice(768 + 96 * slot, 864 + 96 * slot)
                    spread_rows(core, result, slice(128 * half, 128 * half + 128), keep_in, other_in, lambda chip: (chip, column, rows))
        normed_t[...] = normed_ref[...].reshape(tokens, model).T

    result[...] = dot(normed_t[...], gate_up_ref[...].reshape(tokens, 512), NN).astype(BF16)
    column_at = step // 2
    for quarter in range(4):
        rows = pl.ds(pl.multiple_of((4 * lax.rem(step, 2) + quarter) * 96, 32), 96)
        spread_rows(core, result, slice(128 * quarter, 128 * quarter + 128), keep_in, other_in, lambda chip: (chip, column_at, rows))
    down = dot(cot_t[...], act_ref[...].reshape(tokens, 256), NN).astype(BF16)

    def put_down(ref):
        for column in range(4):
            for half in range(2):
                ref[column, step // 2, 192 * half : 192 * half + 192] = down[192 * column : 192 * column + 192, 128 * half : 128 * half + 128]

    @pl.when(lax.rem(step, 2) == core)
    def _():
        put_down(keep_rest)

    @pl.when(lax.rem(step, 2) != core)
    def _():
        put_down(other_rest)
        down_copy(step // 2).start()

    in_copy(step).start()

    @pl.when(step == 0)
    def _():
        out_copy.start()

    @pl.when(step == 7)
    def _():
        for at in range(8):
            in_copy(at).wait()
        out_copy.wait()
        for chip in range(4):
            down_copy(chip).wait()

        def add(at, unused):
            one, two = at // 4, lax.rem(at, 4)
            keep_in[one, two] = (keep_in[one, two].astype(F32) + got_in[one, two].astype(F32)).astype(BF16)
            keep_rest[one, two] = (keep_rest[one, two].astype(F32) + got_rest[one, two].astype(F32)).astype(BF16)
            return unused

        lax.fori_loop(0, 16, add, 0)


def call_early(act, cot, normed, gate_up, attended, branch, after):
    sequences, local_tokens, model = cot.shape
    tokens = sequences * local_tokens
    every = whole(sequences, local_tokens, model)
    shapes = [(4, 4, IN_ROWS, 128), (4, 4, REST_ROWS, 128)]
    dma = pltpu.SemaphoreType.DMA
    return pl.pallas_call(
        early_kernel,
        grid=(8,),
        in_specs=[
            pl.BlockSpec((sequences, local_tokens, 256), lambda s: (0, 0, s)),
            every,
            every,
            pl.BlockSpec((sequences, local_tokens, 512), lambda s: (0, 0, s)),
            every,
            every,
            ANYWHERE,
        ],
        out_specs=[whole(*shape) for shape in shapes],
        scratch_shapes=[
            pltpu.VMEM(shapes[0], BF16),
            pltpu.VMEM(shapes[0], BF16),
            pltpu.VMEM(shapes[1], BF16),
            pltpu.VMEM(shapes[1], BF16),
            pltpu.VMEM((model, tokens), BF16),
            pltpu.VMEM((model, tokens), BF16),
            pltpu.VMEM((model, 512), BF16),
            dma((8,)), dma((8,)), dma((4,)), dma((4,)), dma, dma,
        ],
        out_shape=[jax.ShapeDtypeStruct(shape, BF16) for shape in shapes],
        compiler_params=pltpu.CompilerParams(vmem_limit_bytes=VMEM_LIMIT, collective_id=1, has_side_effects=True),
        cost_estimate=pl.CostEstimate(flops=11 * 10**9, bytes_accessed=3 * 10**7, transcendentals=0),
        name="early_gradients",
    )(act, cot, normed, gate_up, attended, branch, after)


class WeightSums:
    def __init__(self, normed_ref, across_ref, planes_ref, block_of, refs):
        self.normed, self.across, self.planes, self.block_of = normed_ref, across_ref, planes_ref, block_of
        (
            self.in_sum, self.in_got, self.rest_got, self.rest_sum, self.rest_chips, self.normed_t, self.result,
            self.keep, self.other, self.got, self.chips, self.late_sum, self.late_got, self.in_chips,
        ) = refs[:14]
        (
            self.send_in, self.recv_in, self.send_rest, self.recv_rest, self.send_chip, self.recv_chip,
            self.send_a, self.recv_a, self.send_b, self.recv_b, self.send_c, self.recv_c, self.send_i, self.recv_i,
        ) = refs[14:]
        self.me, self.plane = lax.axis_index("seq"), lax.axis_index("dp")
        self.core, self.chip = lax.rem(self.me, 2), self.me // 2

    def to_plane(self, offset, source, target, send, recv):
        return pltpu.make_async_remote_copy(
            src_ref=source, dst_ref=target, send_sem=send.at[offset - 1], recv_sem=recv.at[offset - 1],
            device_id={"dp": lax.rem(self.plane + offset, 4)}, device_id_type=pl.DeviceIdType.MESH,
        )

    def to_chip(self, offset, source, target, send, recv):
        other = lax.rem(self.chip + offset, 4)
        return pltpu.make_async_remote_copy(
            src_ref=source, dst_ref=target, send_sem=send, recv_sem=recv,
            device_id={"seq": 2 * other + self.core}, device_id_type=pl.DeviceIdType.MESH,
        )

    def rest_plane(self, offset):
        peer = lax.rem(self.plane + offset, 4)
        return self.to_plane(offset, self.planes.at[peer], self.rest_got.at[offset - 1], self.send_rest, self.recv_rest)

    def in_plane(self, offset):
        peer = lax.rem(self.plane + offset, 4)
        return self.to_plane(offset, self.in_sum.at[peer], self.in_got.at[offset - 1], self.send_in, self.recv_in)

    def late_plane(self, offset):
        peer = lax.rem(self.plane + offset, 4)
        return self.to_plane(offset, self.late_sum.at[peer], self.late_got.at[offset - 1], self.send_c, self.recv_c)

    def rest_chip(self, offset):
        other = lax.rem(self.chip + offset, 4)
        return self.to_chip(offset, self.rest_sum.at[other], self.rest_chips.at[offset - 1], self.send_chip.at[offset - 1], self.recv_chip.at[offset - 1])

    def late_chip(self, offset, column):
        other = lax.rem(self.chip + offset, 4)
        return self.to_chip(
            offset, self.keep.at[other, column], self.chips.at[offset - 1, column], self.send_b.at[offset - 1, column], self.recv_b.at[offset - 1, column]
        )

    def late_core(self, column):
        return to_sibling(self.core, self.other.at[:, column], self.got.at[:, column], self.send_a.at[column], self.recv_a.at[column])

    def in_chip(self, offset):
        other = lax.rem(self.chip + offset, 4)
        return self.to_chip(offset, self.across.at[other], self.in_chips.at[offset - 1], self.send_i.at[offset - 1], self.recv_i.at[offset - 1])

    def begin(self):
        for offset in (1, 2, 3):
            self.in_chip(offset).start()
            self.rest_plane(offset).start()

    def late(self):
        sequences, count, model = self.normed.shape
        self.normed_t[...] = self.normed[...].reshape(sequences * count, model).T
        low = lax.broadcasted_iota(jnp.int32, (model, 128), 1) < 64
        for pair in range(PAIRS):
            rows = jnp.concatenate([self.block_of(one * PAIRS + pair) for one in range(sequences)], axis=0)
            sums = dot(self.normed_t[...], rows, NN)
            query, key, value = sums[:, 0:128], pltpu.roll(sums[:, 128:256], 64, 1), sums[:, 256:384]
            self.result[3 * pair] = jnp.where(low, query, key).astype(BF16)
            self.result[3 * pair + 1] = jnp.where(low, value, query).astype(BF16)
            self.result[3 * pair + 2] = jnp.where(low, key, value).astype(BF16)
        for tile in range(3 * PAIRS):
            within = tile % 9
            spots = [(2 * (tile // 9), within)] if within <= 4 else []
            spots += [(2 * (tile // 9) + 1, within - 4)] if within >= 4 else []
            for column, slot in spots:
                rows_at = slice(96 * slot, 96 * slot + 96)
                spread_rows(self.core, self.result.at[tile], slice(0, 128), self.keep, self.other, lambda chip: (chip, column, rows_at))
        for column in range(4):
            self.late_core(column).start()

    def second(self):
        for column in range(4):
            self.late_core(column).wait()
            for at in range(4):
                self.keep[at, column] = (self.keep[at, column].astype(F32) + self.got[at, column].astype(F32)).astype(BF16)
            for offset in (1, 2, 3):
                self.late_chip(offset, column).start()

    def third(self):
        for offset in (1, 2, 3):
            self.in_chip(offset).wait()
        for column in range(4):
            total = self.across[self.chip, column].astype(F32)
            for slot in range(3):
                total = total + self.in_chips[slot, column].astype(F32)
            self.in_sum[column] = total.astype(BF16)
        for offset in (1, 2, 3):
            self.in_plane(offset).start()

    def between(self):
        for offset in (1, 2, 3):
            self.rest_plane(offset).wait()
        for chip in range(4):
            total = self.planes[self.plane, chip].astype(F32)
            for slot in range(3):
                total = total + self.rest_got[slot, chip].astype(F32)
            self.rest_sum[chip] = total.astype(BF16)
        for offset in (1, 2, 3):
            self.rest_chip(offset).start()

    def fourth(self):
        for column in range(4):
            total = self.keep[self.chip, column].astype(F32)
            for offset in (1, 2, 3):
                self.late_chip(offset, column).wait()
                total = total + self.chips[offset - 1, column].astype(F32)
            self.late_sum[column] = total.astype(BF16)
        for offset in (1, 2, 3):
            self.late_plane(offset).start()

    def joined(self, block, columns):
        odd = lax.rem(self.plane, 2) == 1
        count = block.shape[1]
        return jnp.where(odd, pltpu.roll(block, count - 64, 1), block)[:, :columns]

    def finish(self, in_out, down_out, weight_out):
        total = self.in_sum[self.plane].astype(F32)
        for offset in (1, 2, 3):
            self.in_plane(offset).wait()
            total = total + self.in_got[offset - 1].astype(F32)
        for tile in range(8):
            in_out[:, 128 * tile : 128 * tile + 128] = total[96 * tile : 96 * tile + 96]
        weight_out[...] = self.joined(jnp.concatenate([total[768:864], total[864:960]], axis=1), 192)
        total = self.rest_sum[self.chip].astype(F32)
        for offset in (1, 2, 3):
            self.rest_chip(offset).wait()
            total = total + self.rest_chips[offset - 1].astype(F32)
        down_out[0:128, :] = total[0:192].T
        down_out[128:256, :] = total[192:384].T

    def finish_late(self, qkv_out):
        total = self.late_sum[self.plane].astype(F32)
        for offset in (1, 2, 3):
            self.late_plane(offset).wait()
            total = total + self.late_got[offset - 1].astype(F32)
        qkv_out[...] = self.joined(jnp.concatenate([total[96 * k : 96 * k + 96] for k in range(5)], axis=1), 576)


def weight_scratch(model, tokens):
    dma = pltpu.SemaphoreType.DMA
    late = (4, 4, LATE_ROWS, 128)
    return [
        pltpu.VMEM((4, IN_ROWS, 128), BF16),
        pltpu.VMEM((3, IN_ROWS, 128), BF16),
        pltpu.VMEM((3, 4, REST_ROWS, 128), BF16),
        pltpu.VMEM((4, REST_ROWS, 128), BF16),
        pltpu.VMEM((3, REST_ROWS, 128), BF16),
        pltpu.VMEM((model, tokens), BF16),
        pltpu.VMEM((3 * PAIRS, model, 128), BF16),
        pltpu.VMEM(late, BF16),
        pltpu.VMEM(late, BF16),
        pltpu.VMEM(late, BF16),
        pltpu.VMEM((3, 4, LATE_ROWS, 128), BF16),
        pltpu.VMEM((4, LATE_ROWS, 128), BF16),
        pltpu.VMEM((3, LATE_ROWS, 128), BF16),
        pltpu.VMEM((3, 4, IN_ROWS, 128), BF16),
        dma((3,)), dma((3,)), dma((3,)), dma((3,)), dma((3,)), dma((3,)),
        dma((4,)), dma((4,)), dma((3, 4)), dma((3, 4)), dma((3,)), dma((3,)), dma((3,)), dma((3,)),
    ]


SMALL_ROWS = 288


class SmallSums:
    def __init__(self, block, buffers, sems):
        self.block = block
        self.held, self.got_seq, self.planes, self.got_dp, self.whole = buffers
        self.sems = sems
        self.me, self.plane = lax.axis_index("seq"), lax.axis_index("dp")
        self.across, self.along = self.held.shape[0], self.held.shape[1]

    def places(self):
        half = self.held.shape[2] // 2
        units = SMALL_ROWS // half
        tiles = self.block.shape[1] // 128
        for at in range(2 * self.along * self.across):
            spot = (at // (2 * self.along), at // 2 % self.along, slice((at % 2) * half, (at % 2) * half + half))
            tile, unit = at // units, at % units
            if tile < tiles:
                yield spot, (slice(unit * half, unit * half + half), slice(128 * tile, 128 * tile + 128))
            else:
                yield spot, None

    def pack(self):
        for spot, source in self.places():
            if source is None:
                self.held[spot] = jnp.zeros((self.held.shape[2] // 2, 128), BF16)
            else:
                self.held[spot] = self.block[source].astype(BF16)

    def copies(self, axis, source, target, number):
        here, count = (self.me, self.across) if axis == "seq" else (self.plane, self.along)
        send, recv = self.sems[2 * number], self.sems[2 * number + 1]
        made = []
        for step in range(1, count):
            peer = lax.rem(here + step, count)
            made.append(
                pltpu.make_async_remote_copy(
                    src_ref=source(peer), dst_ref=target(step - 1), send_sem=send.at[step - 1], recv_sem=recv.at[step - 1],
                    device_id={axis: peer}, device_id_type=pl.DeviceIdType.MESH,
                )
            )
        for copy in made:
            copy.start()
        return made

    def one_start(self):
        self.waiting = self.copies("seq", lambda peer: self.held.at[peer], lambda slot: self.got_seq.at[slot], 0)

    def one_finish(self):
        for copy in self.waiting:
            copy.wait()
        total = self.held[self.me].astype(F32)
        for slot in range(self.across - 1):
            total = total + self.got_seq[slot].astype(F32)
        self.planes[...] = total.astype(BF16)
        self.waiting = self.copies("dp", lambda peer: self.planes.at[peer], lambda slot: self.got_dp.at[slot], 1)

    def two_finish(self):
        for copy in self.waiting:
            copy.wait()
        mine = self.planes[self.plane].astype(F32)
        for slot in range(self.along - 1):
            mine = mine + self.got_dp[slot].astype(F32)
        self.whole[self.me, self.plane] = mine.astype(BF16)
        self.waiting = self.copies("dp", lambda peer: self.whole.at[self.me, self.plane], lambda slot: self.whole.at[self.me, self.plane], 2)

    def three_finish(self):
        for copy in self.waiting:
            copy.wait()
        self.waiting = self.copies("seq", lambda peer: self.whole.at[self.me], lambda slot: self.whole.at[self.me], 3)

    def four_finish(self):
        for copy in self.waiting:
            copy.wait()
        for spot, target in self.places():
            if target is not None:
                self.block[target] = self.whole[spot].astype(F32)


def small_scratch(across, along):
    chunk = max(16, 2048 // (across * along))
    dma = lambda count: pltpu.SemaphoreType.DMA((count,))
    return [
        pltpu.VMEM((across, along, chunk, 128), BF16),
        pltpu.VMEM((across - 1, along, chunk, 128), BF16),
        pltpu.VMEM((along, chunk, 128), BF16),
        pltpu.VMEM((along - 1, chunk, 128), BF16),
        pltpu.VMEM((across, along, chunk, 128), BF16),
        dma(across - 1), dma(across - 1), dma(along - 1), dma(along - 1),
        dma(along - 1), dma(along - 1), dma(across - 1), dma(across - 1),
    ]


def body(
    byte_ids,
    lengths,
    byte_table,
    conv_kernel,
    score_vector,
    norm_gain_one,
    qkv_weight,
    bias_table,
    out_weight,
    norm_gain_two,
    in_weight,
    down_weight,
    cotangent,
):
    devices = lax.axis_size("seq")
    me = lax.axis_index("seq")
    sequences, local_bytes = byte_ids.shape
    local_tokens = local_bytes // 2
    total_bytes = local_bytes * devices
    first_byte = me * local_bytes
    vocab, model = byte_table.shape
    window = local_bytes + 16
    total = sequences * PAIRS
    per_device = -(-total // devices)

    number = jnp.arange(sequences, dtype=jnp.int32)
    ahead = (lengths[None, :] > lengths[:, None]) | (
        (lengths[None, :] == lengths[:, None]) & (number[None, :] < number[:, None])
    )
    rank = jnp.sum(ahead.astype(jnp.int32), axis=1)
    placed = rank[None, :] == number[:, None]
    order = jnp.sum(jnp.where(placed, number[None, :], 0), axis=1)
    sorted_lengths = jnp.sum(jnp.where(placed, lengths[None, :], 0), axis=1)
    positions = first_byte + jnp.arange(local_bytes, dtype=jnp.int32)
    picked = jnp.where(positions[None, :] < lengths[:, None], byte_ids, 0)
    forward = [(i, i + 1) for i in range(devices - 1)]
    backward = [(target, source) for source, target in forward]
    before = jnp.where(me > 0, lax.ppermute(picked[:, -4:], "seq", forward), -1)
    after = jnp.where(me < devices - 1, lax.ppermute(picked[:, :4], "seq", backward), -1)
    outside = jnp.full((sequences, 12), -1, jnp.int32)
    extended = jnp.concatenate([before, picked, after, outside], axis=1)
    extended = jnp.sum(jnp.where(placed[:, :, None], extended[None, :, :], 0), axis=1)
    shifted = jnp.stack([extended[:, tap : tap + window] for tap in range(5)])
    ids_columns = jnp.concatenate([jnp.moveaxis(shifted, 0, 2), jnp.full((sequences, window, 3), -1, jnp.int32)], axis=2)

    table_padded = jnp.concatenate([byte_table, jnp.zeros((VPAD - vocab, model), BF16)], axis=0)
    vectors = jnp.concatenate([conv_kernel, norm_gain_one[None, :], norm_gain_two[None, :], score_vector[None, :]], axis=0)
    rows = jnp.dot(near_one_hot(), bias_table, precision="highest").T.reshape(PAIRS, 2, NEAR)

    item = me + devices * jnp.arange(per_device, dtype=jnp.int32)
    length = jnp.sum(jnp.where((item // PAIRS)[:, None] == number[None, :], sorted_lengths[None, :], 0), axis=1)
    valid = jnp.where(item < total, (length + 1) // 2, 0).astype(jnp.int32)
    pair = lax.rem(item, PAIRS).astype(jnp.int32)
    def exchange(items):
        return lax.all_to_all(items, "seq", split_axis=0, concat_axis=0, tiled=True)

    hidden, normed, conv, mix, share, received = call_front(ids_columns, table_padded, qkv_weight, vectors, local_tokens, devices, per_device)
    out, aug, cot = attention_forward(received, rows, valid, pair, order, cotangent)
    layer, act, gate_up, normed_two, attended, branch, grad_residual, grad_items, grad_gain_two = call_mid(
        out, hidden, cot, out_weight, in_weight, down_weight, vectors
    )
    along_count = lax.axis_size("dp")
    custom = devices == 8 and along_count == 4

    def scatter(grad):
        rows_own = lax.psum_scatter(grad, "seq", scatter_dimension=0, tiled=True)
        return lax.psum_scatter(rows_own, "dp", scatter_dimension=1, tiled=True).astype(F32)

    if not custom:
        summed_down = scatter(jnp.einsum("bti,btd->id", act, cot, preferred_element_type=F32).astype(BF16))
        summed_in = scatter(jnp.einsum("btd,bti->di", normed_two, gate_up, preferred_element_type=F32).astype(BF16))
        summed_out = scatter(jnp.einsum("btd,bte->de", attended, branch, preferred_element_type=F32).astype(BF16))
    half = per_device // 2
    dqkv_two, bias_two, layer_out = attention_backward(received, out, aug, grad_items, rows, valid, pair, order, layer, grad_gain_two, half, per_device - half)
    items_two = exchange(dqkv_two)
    dqkv_one, bias_one, unused = attention_backward(received, out, aug, grad_items, rows, valid, pair, order, None, bias_two, 0, half)
    items_one = exchange(dqkv_one)
    bias_rows = jnp.concatenate([bias_one, bias_two], axis=0)
    if custom:
        in_chips, rest_planes = call_early(act, cot, normed_two, gate_up, attended, branch, items_two)
    ids_rows = jnp.concatenate([jnp.moveaxis(shifted, 0, 1), jnp.full((sequences, 3, window), -1, jnp.int32)], axis=1)
    extra = (normed, in_chips, rest_planes) if custom else ()
    results = call_back(
        custom, items_one, items_two, hidden, grad_residual, conv, mix, share, ids_rows, qkv_weight, table_padded, vectors, bias_rows, grad_gain_two, along_count, extra
    )
    if custom:
        summed_qkv, summed_in, summed_down, summed_out, *smalls = call_finish(results[0], results[1:])
    else:
        smalls = call_finish(results[0], ())
        grad_qkv = jnp.einsum("btd,bte->de", normed, results[1], preferred_element_type=F32).astype(BF16)
        grad_qkv = jnp.swapaxes(grad_qkv.reshape(model, PAIRS, 3, 2, 64), 2, 3).reshape(model, PAIRS * 384)
        summed_qkv = scatter(grad_qkv)
    grad_table, grad_taps, grad_gain_one, grad_score, grad_gain_two, grad_bias = smalls
    return (
        layer_out,
        grad_table,
        grad_taps,
        grad_score,
        grad_gain_one,
        summed_qkv,
        grad_bias,
        summed_out,
        grad_gain_two,
        summed_in,
        summed_down,
    )


def solution(mesh):
    return jax.shard_map(
        body,
        mesh=mesh,
        in_specs=(
            P("dp", "seq"),
            P("dp"),
            P(),
            P(),
            P(),
            P(),
            P(),
            P(),
            P(),
            P(),
            P(),
            P(),
            P("dp", "seq", None),
        ),
        out_specs=(
            P("dp", "seq", None),
            P(),
            P(),
            P(),
            P(),
            P("seq", "dp"),
            P(),
            P("seq", "dp"),
            P(),
            P("seq", "dp"),
            P("seq", "dp"),
        ),
        check_vma=False,
    )
```

time: 442 us -> 375 us (0.85)
  Pallas kernels: 366 us -> 330 us
  local copies, waits for them, and re-layouts: 27.2 us -> 12.9 us
  waiting for transfers between devices: 13.2 us -> 5.61 us
  starting transfers between devices: 19.8 us -> 12.3 us
  other arithmetic: 10.8 us -> 5.89 us
    pallas_call x5 -> x3, Pallas kernels: 116 us -> 44.9 us  [the longest x2 42.2 us: attention_backward(): pl.pallas_call(functools.partial(bwd_kernel, blocks, first, moves), grid_...]
    pallas_call x1, Pallas kernels: 70.2 us -> 110 us  [call_back(): pl.pallas_call(functools.partial(back_kernel, (local_tokens, window, devi...]
    all_to_all x1 -> x2, waiting for transfers between devices: 13.2 us -> 5.61 us  [exchange(): return lax.all_to_all(items, 'seq', split_axis=0, concat_axis=0, tiled=True)]
    all_to_all x1 -> x2, starting transfers between devices: 15.5 us -> 8 us  [exchange(): return lax.all_to_all(items, 'seq', split_axis=0, concat_axis=0, tiled=True)]
    slice x6 -> x0, local copies, waits for them, and re-layouts: 7.38 us -> none  [the longest x1 2.08 us: body(): sums[:vocab]]
    pallas_call x1, Pallas kernels: 31.9 us -> 25.1 us  [call_early(): pl.pallas_call(early_kernel, grid=(8,), in_specs=[pl.BlockSpec((sequences...]
    pallas_call x1, Pallas kernels: 53.7 us -> 59 us  [call_mid(): pl.pallas_call(functools.partial(mid_kernel, (local_tokens, devices, sequ...]
    pallas_call x1, Pallas kernels: 68 us -> 63.3 us  [call_front(): pl.pallas_call(functools.partial(front_kernel, (local_tokens, window, dev...]
  transfers between devices with their start and end apart: 3 -> 4, of which waited for: 1 -> 2; matrix products, arithmetic and copies ran while one was open for 3% -> 3% of each run, Pallas kernels for 12% -> 14%
where the time goes in v3:
time: 375 us; the launch traced here: 368 us
  Pallas kernels  330 us (88%)
  local copies, waits for them, and re-layouts  12.9 us (3%)
  starting transfers between devices  12.3 us (3%)
  other arithmetic  5.89 us (2%)
  waiting for transfers between devices  5.61 us (1%)
    pallas_call x1, Pallas kernels, call_back(): pl.pallas_call(functools.partial(back_kernel, (local_tokens, window, devi...  110 us
    pallas_call x1, Pallas kernels, call_front(): pl.pallas_call(functools.partial(front_kernel, (local_tokens, window, dev...  63.3 us
    pallas_call x1, Pallas kernels, call_mid(): pl.pallas_call(functools.partial(mid_kernel, (local_tokens, devices, sequ...  59 us
    pallas_call x2, Pallas kernels, attention_backward(): pl.pallas_call(functools.partial(bwd_kernel, blocks, first, moves), grid_...  42.2 us
    pallas_call x1, Pallas kernels, attention_forward(): pl.pallas_call(functools.partial(fwd_kernel, blocks), grid_spec=spec, out...  27.7 us
    pallas_call x1, Pallas kernels, call_early(): pl.pallas_call(early_kernel, grid=(8,), in_specs=[pl.BlockSpec((sequences...  25.1 us
    all_to_all x2, starting transfers between devices, exchange(): return lax.all_to_all(items, 'seq', split_axis=0, concat_axis=0, tiled=True)  8 us
  transfers between devices with their start and end apart: 4, of which 2 were waited for; matrix products, arithmetic and copies ran while one was open for 3% of the time, Pallas kernels for 14%

profile of v3, /device:TPU:0, one launch (start us, length us, event | category | flops | bytes accessed | tf_op | source)
XLA Modules:
  0.0 368.3 jit_solution(3623110422535109300)
XLA Ops:
  0.7 0.8 compare_select_fusion.1
  1.5 1.3 collective-permute-start.1
  2.8 3.0 collective-permute-start
  5.8 0.9 convert_reduce_fusion
  6.8 0.8 select_reduce_fusion.1
  7.9 0.7 broadcast_in_dim.104
  8.6 0.7 broadcast_in_dim.103
  9.3 0.7 broadcast_in_dim.102
  10.0 0.4 convolution_bitcast_fusion
  10.5 1.4 pad_maximum_fusion.1.vectors_ref
  11.8 1.9 concatenate.20.table_ref
  14.6 1.1 concatenate.19.clone.ids_ref
  15.7 63.3 %front.1 = (f32[8,128,768]{2,1,0:T(8,128)}, bf16[8,128,768]{2,1,0:T(8,128)(2,1)}, bf16[8,384,768]{2,1,0:T(8,128)(2,1)}, bf16[8,128,384]{2,1,0:T(8,128)(2,1)}, f3...) custom-call(s32[8,272,8]{2,1,0:T(8,128)} %concatenate.19.clone.ids_ref, bf16[384,768]{1,0:T(8,128)(2,1)} %concatenate.20.table_ref, ...), custom_call_target="tpu_custom_call" | custom-call | flops 49999998976 | bytes 20000000 | tf_op jit(solution)/shard_map/front/pallas_call | solution.py:876
  79.0 27.7 %attention_forward.1 = (bf16[8,6,128,128]{3,2,1,0:T(8,128)(2,1)S(1)}, bf16[6,1024,128]{2,1,0:T(8,128)(2,1)S(1)}, bf16[8,128,768]{2,1,0:T(8,128)(2,1)}) custom-call(s32[6]{0:T(128)S(1)} %compare_select_fusion.2.valid_ref, s32[6]{0:T(128)S(1)} %get-tuple-element.123.pair_ref, s32[8]{0:T(128)S(1)} %get-tuple-element.113.order_ref, ...), custom_call_target="tpu_custom_call" | custom-call | flops 3221225472 | bytes 12582912 | tf_op jit(solution)/shard_map/attention_forward/pallas_call | solution.py:272
  106.8 1.1 copy-done.2
  107.9 59.0 %middle.1 = (f32[8,128,768]{2,1,0:T(8,128)}, bf16[8,128,2048]{2,1,0:T(8,128)(2,1)}, bf16[8,128,4096]{2,1,0:T(8,128)(2,1)}, bf16[8,128,768]{2,1,0:T(8,128)(2,1)},...) custom-call(bf16[8,6,128,128]{3,2,1,0:T(8,128)(2,1)} %copy-done.2, ...), custom_call_target="tpu_custom_call" | custom-call | flops 49999998976 | bytes 40000000 | tf_op jit(solution)/shard_map/middle/pallas_call | solution.py:916
  166.9 0.7 copy-done.4
  167.6 16.3 %attention_backward.2 = (bf16[8,3,128,384]{3,2,1,0:T(8,128)(2,1)}, f32[3,2,1024]{2,1,0:T(2,128)S(1)}, f32[8,128,768]{2,1,0:T(8,128)}) custom-call(s32[6]{0:T(128)S(1)} %compare_select_fusion.2.valid_ref, s32[6]{0:T(128)S(1)} %get-tuple-element.123.pair_ref, s32[8]{0:T(128)S(1)} %get-tuple-element.113.order_ref, ...), custom_call_target="tpu_custom_call" | custom-call | flops 4026531840 | bytes 12582912 | tf_op jit(solution)/shard_map/attention_backward/pallas_call | solution.py:326
  183.9 4.4 %all-to-all-start.1 = ((bf16[8,3,128,384]{3,2,1,0:T(8,128)(2,1)}), bf16[8,3,128,384]{3,2,1,0:T(8,128)(2,1)}, u32[]{:S(2)}, u32[]{:S(2)}) async-start(bf16[8,3,128,384]{3,2,1,0:T(8,128)(2,1)} %get-tuple-element.62), calls=%async_computation.1 | async-start | bytes 4718592 | tf_op jit(solution)/shard_map/all_to_all | solution.py:1477
  188.3 25.9 %attention_backward.3 = (bf16[8,3,128,384]{3,2,1,0:T(8,128)(2,1)}, f32[3,2,1024]{2,1,0:T(2,128)S(1)}, f32[8,128]{1,0:T(8,128)}) custom-call(s32[6]{0:T(128)S(1)} %compare_select_fusion.2.valid_ref, s32[6]{0:T(128)S(1)} %get-tuple-element.123.pair_ref, s32[8]{0:T(128)S(1)} %get-tuple-element.113.order_ref, ...), custom_call_target="tpu_custom_call" | custom-call | flops 4026531840 | bytes 12582912 | tf_op jit(solution)/shard_map/attention_backward/pallas_call | solution.py:326
  214.2 3.6 all-to-all-done.1.after.two_ref
  217.7 3.6 all-to-all-start
  221.6 0.8 convert_convert_fusion.bias_hot_ref
  222.3 0.6 concatenate.22.ids_ref
  223.0 0.6 pad_maximum_fusion.bias_ref
  223.6 25.1 %early_gradients.1 = (bf16[4,4,960,128]{3,2,1,0:T(8,128)(2,1)}, bf16[4,4,384,128]{3,2,1,0:T(8,128)(2,1)}) custom-call(bf16[8,128,2048]{2,1,0:T(8,128)(2,1)} %get-tuple-element.69.act_ref, bf16[8,128,768]{2,1,0:T(8,128)(2,1)} %get-tuple-element.55.cot_ref, bf16[8,128,768]{2,1,0:T(8,128)(2,1)} %get-tuple-element.70.normed_ref, ...), custom_call_target="tpu_custom_call" | custom-call | flops 11000000512 | bytes 30000000 | tf_op jit(solution)/shard_map/early_gradients/pallas_call | solution.py:1125
  248.7 2.0 all-to-all-done.one_ref
  250.7 1.4 copy-done.5
  252.2 109.8 %back.1 = (f32[288,768]{1,0:T(8,128)}, f32[96,576]{1,0:T(8,128)}, f32[96,1024]{1,0:T(8,128)}, f32[256,192]{1,0:T(8,128)}, f32[96,192]{1,0:T(8,128)}) custom-call(bf16[8,3,128,384]{3,2,1,0:T(8,128)(2,1)} %copy-done.5, bf16[8,3,128,384]{3,2,1,0:T(8,128)(2,1)} %all-to-all-done.1.after.two_ref, f32[8,128,768]{2,1,0:T(8,128)} %get-tuple-element.54.hidden_ref, ...), custom_call_target="tpu_custom_call" | custom-call | flops 99999997952 | bytes 20000000 | tf_op jit(solution)/shard_map/back/pallas_call | solution.py:978
  362.0 2.8 finish.1
  364.7 1.4 copy.32
  366.1 1.7 copy.33
  (34 shorter events, 1.5 us)
Async XLA Ops:
  0.6 9.3 %copy-start = (f32[32,12]{0,1:T(8,128)S(1)}, f32[32,12]{0,1:T(8,128)}, u32[]{:S(2)}) copy-start(f32[32,12]{0,1:T(8,128)} %param.20) | copy-start | bytes 4612
  1.5 12.2 %collective-permute-start.1 = (s32[8,4]{1,0:T(8,128)S(1)}, s32[8,4]{1,0:T(8,128)S(1)}, u32[]{:S(2)}, u32[]{:S(2)}) collective-permute-start(s32[8,4]{1,0:T(8,128)S(1)} %get-tuple-element.121), channel_id=1, source_target_pairs={{1,0},{2,1},{3,2},{4,3},{5,4},{6,5},{7,6},{9,8},{10,9},{11,10},{12... | collective-permute-start | bytes 392 | tf_op jit(solution)/shard_map/ppermute | solution.py:1461
  2.8 10.9 %collective-permute-start = (s32[8,4]{1,0:T(8,128)S(1)}, s32[8,4]{1,0:T(8,128)S(1)}, u32[]{:S(2)}, u32[]{:S(2)}) collective-permute-start(s32[8,4]{1,0:T(8,128)S(1)} %get-tuple-element.120), channel_id=1, source_target_pairs={{0,1},{1,2},{2,3},{3,4},{4,5},{5,6},{6,7},{8,9},{9,10},{10,11},{11... | collective-permute-start | bytes 392 | tf_op jit(solution)/shard_map/ppermute | solution.py:1460
  106.7 1.1 copy-start.2
  107.9 59.0 %copy-start.3 = (bf16[8,6,128,128]{3,2,1,0:T(8,128)(2,1)S(1)}, bf16[8,6,128,128]{3,2,1,0:T(8,128)(2,1)}, u32[]{:S(2)}) copy-start(bf16[8,6,128,128]{3,2,1,0:T(8,128)(2,1)} %copy-done.2) | copy-start | bytes 4718596
  166.9 0.7 copy-start.4
  183.9 33.9 %all-to-all-start.1 = ((bf16[8,3,128,384]{3,2,1,0:T(8,128)(2,1)}), bf16[8,3,128,384]{3,2,1,0:T(8,128)(2,1)}, u32[]{:S(2)}, u32[]{:S(2)}) async-start(bf16[8,3,128,384]{3,2,1,0:T(8,128)(2,1)} %get-tuple-element.62), calls=%async_computation.1 | async-start | bytes 4718592 | tf_op jit(solution)/shard_map/all_to_all | solution.py:1477
  217.7 33.0 %all-to-all-start = ((bf16[8,3,128,384]{3,2,1,0:T(8,128)(2,1)}), bf16[8,3,128,384]{3,2,1,0:T(8,128)(2,1)S(1)}, u32[]{:S(2)}, u32[]{:S(2)}) async-start(bf16[8,3,128,384]{3,2,1,0:T(8,128)(2,1)} %get-tuple-element.61), calls=%async_computation | async-start | bytes 4718592 | tf_op jit(solution)/shard_map/all_to_all | solution.py:1477
  250.7 1.4 copy-start.5
  252.2 115.7 %copy-start.1 = (f32[32,12]{0,1:T(8,128)S(1)}, f32[32,12]{0,1:T(8,128)}, u32[]{:S(2)}) copy-start(f32[32,12]{0,1:T(8,128)} %param.20) | copy-start | bytes 4612

commit v4 on v3

--- a/solution.py
+++ b/solution.py
@@ -62,16 +62,22 @@
     ka[head] = jnp.where(own, keys, extra.astype(BF16))
 
 
-def move_rows(item, order_ref, source, buffer, target, sems, sorting):
+def item_length(lengths_ref, item):
+    length = jnp.int32(0)
+    for number, rank in enumerate(ranks_of(lengths_ref)):
+        length = jnp.where(rank == item // 6, lengths_ref[number], length)
+    return (length + 1) // 2
+
+
+def move_rows(item, lengths_ref, source, buffer, target, sems, sorting):
     def inward(number):
-        place = order_ref[number] if sorting else number
-        return pltpu.make_async_copy(source.at[place], buffer.at[number], sems.at[0, number])
+        return pltpu.make_async_copy(source.at[number if sorting else ranks[number]], buffer.at[number], sems.at[0, number])
 
     def outward(number):
-        place = number if sorting else order_ref[number]
-        return pltpu.make_async_copy(buffer.at[number], target.at[place], sems.at[1, number])
+        return pltpu.make_async_copy(buffer.at[number], target.at[ranks[number] if sorting else number], sems.at[1, number])
 
     count = source.shape[0]
+    ranks = ranks_of(lengths_ref)
 
     @pl.when(item == 0)
     def _():
@@ -94,12 +100,12 @@
 
 
 def fwd_kernel(
-    blocks, valid_ref, pair_ref, order_ref, qkv_ref, row_ref, cot_ref, out_ref, aug_ref, sorted_ref,
+    blocks, lengths_ref, place_ref, qkv_ref, row_ref, cot_ref, out_ref, aug_ref, sorted_ref,
     qa, ka, vt, strip, peak, acc, probs, moving, sems,
 ):
     item = pl.program_id(0)
-    finish = move_rows(item, order_ref, cot_ref, moving, sorted_ref, sems, True)
-    valid = valid_ref[item]
+    finish = move_rows(item, lengths_ref, cot_ref, moving, sorted_ref, sems, True)
+    valid = item_length(lengths_ref, place_ref[0] + qkv_ref.shape[0] * item)
     tokens = blocks * KB
     joined = qkv_ref[:, 0].reshape(tokens, 384)
     queries = joined[:, 0:128]
@@ -119,9 +125,9 @@
     def step(block, unused):
         first = pl.multiple_of(block * KB, KB)
         shift = pl.multiple_of((blocks - 1 - block) * KB, KB)
-        for head in range(2):
-            alphas = []
-            for part in range(blocks):
+        alphas = [[], []]
+        for part in range(blocks):
+            for head in range(2):
                 here = slice(part * KB, part * KB + KB)
                 logits = dot(ka[head, pl.ds(first, KB), :], qa[head, here, :], NT)
                 logits = logits + strip[head, :, pl.ds(shift + part * KB, KB)]
@@ -129,10 +135,9 @@
                 after = jnp.maximum(before, jnp.max(logits, axis=0, keepdims=True))
                 probs[head, :, here] = jnp.exp(logits - after).astype(BF16)
                 peak[head, :, here] = after
-                alphas.append(jnp.exp(before - after))
-            acc[head] = acc[head] * jnp.concatenate(alphas, axis=1) + dot(
-                    vt[head, :, pl.ds(first, KB)], probs[head], NN
-                )
+                alphas[head].append(jnp.exp(before - after))
+        for head in range(2):
+            acc[head] = acc[head] * jnp.concatenate(alphas[head], axis=1) + dot(vt[head, :, pl.ds(first, KB)], probs[head], NN)
         return unused
 
     lax.fori_loop(0, (valid + KB - 1) // KB, step, 0)
@@ -154,12 +159,12 @@
 
 
 def bwd_kernel(
-    blocks, base_slot, moves, valid_ref, pair_ref, order_ref, qkv_ref, out_ref, aug_ref, grad_ref, row_ref, layer_ref, after,
+    blocks, base_slot, moves, lengths_ref, place_ref, qkv_ref, out_ref, aug_ref, grad_ref, row_ref, layer_ref, after,
     dqkv_ref, bias_ref, moved_ref, qa, ka, va, ga, kt, strip, tally, probs, slopes, dq, *moving,
 ):
     item = pl.program_id(0)
-    finish = move_rows(item, order_ref, layer_ref, moving[0], moved_ref, moving[1], False) if moves else lambda: None
-    valid = valid_ref[item + base_slot]
+    finish = move_rows(item, lengths_ref, layer_ref, moving[0], moved_ref, moving[1], False) if moves else lambda: None
+    valid = item_length(lengths_ref, place_ref[0] + qkv_ref.shape[0] * (item + base_slot))
     tokens = blocks * KB
     width = KB * (2 * blocks - 1)
     local = qkv_ref.shape[2]
@@ -195,8 +200,8 @@
         shift = pl.multiple_of((blocks - 1 - block) * KB, KB)
         key_parts = []
         value_parts = []
-        for head in range(2):
-            for part in range(blocks):
+        for part in range(blocks):
+            for head in range(2):
                 here = slice(part * KB, part * KB + KB)
                 there = pl.ds(shift + part * KB, KB)
                 logits = dot(ka[head, pl.ds(first, KB), :], qa[head, here, :], NT)
@@ -206,6 +211,7 @@
                 tally[head, :, there] += slope
                 probs[head, :, here] = weights.astype(BF16)
                 slopes[head, :, here] = slope.astype(BF16)
+        for head in range(2):
             value_parts.append(dot(probs[head], ga[head], NN))
             key_parts.append(dot(slopes[head], qa[head], NN))
             dq[pl.ds(64 * head, 64), :] += dot(kt[pl.ds(64 * head, 64), pl.ds(first, KB)], slopes[head], NN)
@@ -239,22 +245,22 @@
     finish()
 
 
-def attention_forward(qkv, rows, valid, pair, order, cot):
+def attention_forward(qkv, rows, lengths, place, cot):
     sources, items, local, unused = qkv.shape
     blocks = sources * local // KB
     tokens = sources * local
     width = KB * (2 * blocks - 1)
     spec = pltpu.PrefetchScalarGridSpec(
-        num_scalar_prefetch=3,
+        num_scalar_prefetch=2,
         grid=(items,),
         in_specs=[
-            pl.BlockSpec((sources, 1, local, 384), lambda i, v, p, o: (0, i, 0, 0)),
-            pl.BlockSpec((1, 2, NEAR), lambda i, v, p, o: (p[i], 0, 0)),
+            pl.BlockSpec((sources, 1, local, 384), lambda i, l, p: (0, i, 0, 0)),
+            pl.BlockSpec((1, 2, NEAR), lambda i, l, p: (lax.rem(p[0] + sources * i, 6), 0, 0)),
             pl.BlockSpec(memory_space=pl.ANY),
         ],
         out_specs=[
-            pl.BlockSpec((sources, 1, local, 128), lambda i, v, p, o: (0, i, 0, 0)),
-            pl.BlockSpec((1, tokens, 128), lambda i, v, p, o: (i, 0, 0)),
+            pl.BlockSpec((sources, 1, local, 128), lambda i, l, p: (0, i, 0, 0)),
+            pl.BlockSpec((1, tokens, 128), lambda i, l, p: (i, 0, 0)),
             pl.BlockSpec(memory_space=pl.ANY),
         ],
         scratch_shapes=[
@@ -280,10 +286,10 @@
         compiler_params=pltpu.CompilerParams(vmem_limit_bytes=50 * 2**20),
         cost_estimate=pl.CostEstimate(flops=items * tokens * tokens * 512, bytes_accessed=items * tokens * 2048, transcendentals=items * tokens * tokens * 2),
         name="attention_forward",
-    )(valid, pair, order, qkv, rows, cot)
-
-
-def attention_backward(qkv, outs, aug, grads, rows, valid, pair, order, layer, after, first, items):
+    )(lengths, place, qkv, rows, cot)
+
+
+def attention_backward(qkv, outs, aug, grads, rows, lengths, place, layer, after, first, items, grads_at):
     sources, unused, local, unused = qkv.shape
     moves = layer is not None
     layer = after if layer is None else layer
@@ -291,22 +297,22 @@
     blocks = sources * local // KB
     tokens = sources * local
     width = KB * (2 * blocks - 1)
-    big = lambda lanes: pl.BlockSpec((sources, 1, local, lanes), lambda i, v, p, o: (0, i + first, 0, 0))
+    big = lambda lanes: pl.BlockSpec((sources, 1, local, lanes), lambda i, l, p: (0, i + first, 0, 0))
     spec = pltpu.PrefetchScalarGridSpec(
-        num_scalar_prefetch=3,
+        num_scalar_prefetch=2,
         grid=(items,),
         in_specs=[
             big(384),
             big(128),
-            pl.BlockSpec((1, tokens, 128), lambda i, v, p, o: (i + first, 0, 0)),
-            big(128),
-            pl.BlockSpec((1, 2, NEAR), lambda i, v, p, o: (p[i + first], 0, 0)),
+            pl.BlockSpec((1, tokens, 128), lambda i, l, p: (i + first, 0, 0)),
+            pl.BlockSpec((sources, 1, local, 128), lambda i, l, p: (0, i + grads_at, 0, 0)),
+            pl.BlockSpec((1, 2, NEAR), lambda i, l, p: (lax.rem(p[0] + sources * (i + first), 6), 0, 0)),
             pl.BlockSpec(memory_space=pl.ANY),
             pl.BlockSpec(memory_space=pl.ANY),
         ],
         out_specs=[
-            pl.BlockSpec((sources, 1, local, 384), lambda i, v, p, o: (0, i, 0, 0)),
-            pl.BlockSpec((1, 2, NEAR), lambda i, v, p, o: (i, 0, 0)),
+            pl.BlockSpec((sources, 1, local, 384), lambda i, l, p: (0, i, 0, 0)),
+            pl.BlockSpec((1, 2, NEAR), lambda i, l, p: (i, 0, 0)),
             pl.BlockSpec(memory_space=pl.ANY),
         ],
         scratch_shapes=[
@@ -334,7 +340,7 @@
         compiler_params=pltpu.CompilerParams(vmem_limit_bytes=50 * 2**20),
         cost_estimate=pl.CostEstimate(flops=items * tokens * tokens * 1280, bytes_accessed=items * tokens * 4096, transcendentals=items * tokens * tokens * 2),
         name="attention_backward",
-    )(valid, pair, order, qkv, outs, aug, grads, rows, layer, after)
+    )(lengths, place, qkv, outs, aug, grads, rows, layer, after)
 
 
 VPAD = 384
@@ -443,9 +449,69 @@
     lax.fori_loop(0, devices * per_device, wait, 0)
 
 
+def ranks_of(lengths_ref):
+    count = lengths_ref.shape[0]
+    ranks = []
+    for one in range(count):
+        rank = jnp.int32(0)
+        for two in range(count):
+            if two != one:
+                ahead = lengths_ref[two] > lengths_ref[one] if two > one else lengths_ref[two] >= lengths_ref[one]
+                rank = rank + ahead.astype(jnp.int32)
+        ranks.append(rank)
+    return ranks
+
+
+def spread_ids(lengths_ref, ids_ref, from_left, from_right, extended, sems, me, devices):
+    sequences, local_bytes = ids_ref.shape
+    left_copy = pltpu.make_async_remote_copy(
+        src_ref=ids_ref.at[:, 0:128], dst_ref=from_right, send_sem=sems.at[0], recv_sem=sems.at[1],
+        device_id={"seq": jnp.maximum(me - 1, 0)}, device_id_type=pl.DeviceIdType.MESH,
+    )
+    right_copy = pltpu.make_async_remote_copy(
+        src_ref=ids_ref.at[:, local_bytes - 128 : local_bytes], dst_ref=from_left, send_sem=sems.at[2], recv_sem=sems.at[3],
+        device_id={"seq": jnp.minimum(me + 1, devices - 1)}, device_id_type=pl.DeviceIdType.MESH,
+    )
+
+    @pl.when(me > 0)
+    def _():
+        left_copy.start()
+
+    @pl.when(me < devices - 1)
+    def _():
+        right_copy.start()
+
+    @pl.when(me > 0)
+    def _():
+        left_copy.wait_send()
+        right_copy.wait_recv()
+
+    @pl.when(me < devices - 1)
+    def _():
+        right_copy.wait_send()
+        left_copy.wait_recv()
+
+    joined = jnp.concatenate([from_left[...], ids_ref[...], from_right[...]], axis=1).astype(F32)
+    width = joined.shape[1]
+    moved = pltpu.roll(joined, width - 124, 1)
+    row = lax.broadcasted_iota(jnp.int32, (sequences, width), 0)
+    lane = lax.broadcasted_iota(jnp.int32, (sequences, width), 1)
+    position = me * local_bytes - 4 + lane
+    length = jnp.zeros((sequences, width), jnp.int32)
+    for one in range(sequences):
+        length = jnp.where(row == one, lengths_ref[one], length)
+    outside = (position < 0) | (position >= local_bytes * devices) | (lane >= local_bytes + 8)
+    picked = jnp.where(outside, -1.0, jnp.where(position < length, moved, 0.0))
+    ordered = jnp.zeros((sequences, width), F32)
+    for one, rank in enumerate(ranks_of(lengths_ref)):
+        ordered = jnp.where(row == rank, picked[one : one + 1, :], ordered)
+    extended[...] = ordered
+
+
 def front_kernel(
-    sizes, ids_ref, table_ref, weight_ref, vectors_ref,
-    hidden_ref, normed_ref, conv_ref, mix_ref, share_ref, items_ref, masks, wide, permuted, stage, taps, *sems,
+    sizes, lengths_ref, ids_ref, table_ref, weight_ref, vectors_ref,
+    hidden_ref, normed_ref, conv_ref, mix_ref, share_ref, rows_ref, items_ref,
+    masks, wide, permuted, stage, taps, from_left, from_right, extended, side_sems, *sems,
 ):
     local_tokens, window, devices, total = sizes
     step = pl.program_id(0)
@@ -453,26 +519,35 @@
 
     @pl.when(step == 0)
     def _():
+        from_left[...] = jnp.zeros_like(from_left)
+        from_right[...] = jnp.zeros_like(from_right)
         greet("seq", me, devices)
         block_masks(masks, me * 2 * local_tokens, devices * 2 * local_tokens)
         permute_weight(weight_ref, permuted)
         table = table_ref[...].astype(F32)
+        taps[...] = jnp.zeros_like(taps)
         for tap in range(5):
-            taps[tap] = (vectors_ref[tap : tap + 1, :] * table).astype(BF16)
-
-    together = ids_ref.shape[0]
+            taps[tap, 0 : table.shape[0], :] = (vectors_ref[tap : tap + 1, :] * table).astype(BF16)
+        pl.semaphore_wait(pltpu.get_barrier_semaphore(), devices - 1)
+        spread_ids(lengths_ref, ids_ref, from_left, from_right, extended, side_sems, me, devices)
+
+    together = 1
+    width_ids = extended.shape[1]
+    row = jnp.broadcast_to(extended[pl.ds(step, 1), :], (8, width_ids))
+    rows = pltpu.roll(pltpu.roll(row, width_ids - 4, 1), 0, 1, stride=1, stride_axis=0)
+    rows_ref[0] = rows
+    ids = rows.T[0:window]
     score = vectors_ref[7:8, :]
     gain = vectors_ref[5:6, :]
     model = score.shape[1]
     score_high, score_low = split_two(score)
     row16 = lax.broadcasted_iota(jnp.int32, (16, model), 0)
     score_rows = jnp.where(row16 == 0, score_high.astype(F32), jnp.where(row16 == 1, score_low.astype(F32), 0.0)).astype(BF16)
-    lane = lax.broadcasted_iota(jnp.int32, (together * window, VPAD), 1)
+    lane = lax.broadcasted_iota(jnp.int32, (together * window, VPAD), 1).astype(F32)
     width = masks.shape[3]
-    ids = ids_ref[...].reshape(together * window, 8)
     conv_all = jnp.zeros((together * window, model), F32)
     for tap in range(5):
-        hot = jnp.where(ids[:, tap : tap + 1] == lane, 1.0, 0.0).astype(BF16)
+        hot = jnp.where(ids[:, 4 - tap : 5 - tap] == lane, 1.0, 0.0).astype(BF16)
         conv_all = conv_all + dot(hot, taps[tap], NN)
     for one in range(together):
         high, low = split_two(conv_all[one * window : (one + 1) * window])
@@ -512,16 +587,110 @@
             other, slot = lax.rem(item, devices), item // devices
             stage[other, slot] = piece[one * local_tokens : (one + 1) * local_tokens]
 
-    @pl.when(step == 0)
-    def _():
-        pl.semaphore_wait(pltpu.get_barrier_semaphore(), devices - 1)
-
+    if devices == 8:
+
+        def send(at, unused):
+            item = step * PAIRS + at
+            other, slot = lax.rem(item, 8), item // 8
+
+            @pl.when(other != me)
+            def _():
+                to_device(other, stage.at[other, slot], items_ref.at[me, slot], sems[0].at[0], sems[1].at[0]).start()
+
+            return unused
+
+        lax.fori_loop(0, PAIRS, send, 0)
+
+        @pl.when(step == pl.num_programs(0) - 1)
+        def _():
+            finish_back(me, stage, items_ref, sems)
+
+        return
     send_items(devices, me, step * together * PAIRS, together * PAIRS, stage, items_ref, sems)
 
     @pl.when(step == pl.num_programs(0) - 1)
     def _():
         finish_sends(devices, me, total, lambda other, slot: stage.at[other, slot], lambda other, slot: items_ref.at[me, slot], sems)
         finish_receives(devices, me, total, lambda other, slot: stage.at[other, slot], lambda other, slot: items_ref.at[other, slot], sems)
+
+
+def to_device(other, source, target, send, recv):
+    return pltpu.make_async_remote_copy(
+        src_ref=source, dst_ref=target, send_sem=send, recv_sem=recv, device_id={"seq": other}, device_id_type=pl.DeviceIdType.MESH
+    )
+
+
+SLOT_GROUPS = ((0, 2), (2, 1), (3, 2), (5, 1))
+
+
+def send_slots(me, number, source, arrived, sems):
+    first, count = SLOT_GROUPS[number]
+    slots = pl.ds(first, count)
+
+    def send(offset, unused):
+        other = lax.rem(me + offset, 8)
+        to_device(other, source.at[other, slots], arrived.at[me, slots], sems[0].at[number], sems[1].at[number]).start()
+        return unused
+
+    lax.fori_loop(1, 8, send, 0)
+    pltpu.make_async_copy(source.at[me, slots], arrived.at[me, slots], sems[2].at[number]).start()
+
+
+def wait_slots(me, number, source, arrived, sems, sends):
+    first, count = SLOT_GROUPS[number]
+    slots = pl.ds(first, count)
+    seven = pl.ds(0, 7)
+    copies = to_device(lax.rem(me + 1, 8), source.at[seven, slots], arrived.at[seven, slots], sems[0].at[number], sems[1].at[number])
+    if sends:
+        copies.wait_send()
+    else:
+        copies.wait_recv()
+        pltpu.make_async_copy(source.at[me, slots], arrived.at[me, slots], sems[2].at[number]).wait()
+
+
+def send_back(me, step, stage, target, sems):
+    base, base_to = 3, 0
+    for parity in range(2):
+
+        def send(offset, unused):
+            other = lax.rem(me + offset, 8)
+
+            @pl.when(other < 4)
+            def _():
+                first, count = (0, 2) if parity == 0 else (2, 1)
+                to_device(other, stage.at[other, pl.ds(base + first, count)], target.at[me, pl.ds(base_to + first, count)], sems[0].at[0], sems[1].at[0]).start()
+
+            @pl.when(other >= 4)
+            def _():
+                first, count = (0, 1) if parity == 0 else (1, 2)
+                to_device(other, stage.at[other, pl.ds(base + first, count)], target.at[me, pl.ds(base_to + first, count)], sems[0].at[0], sems[1].at[0]).start()
+
+            return unused
+
+        @pl.when(lax.rem(step, 2) == parity)
+        def _():
+            lax.fori_loop(1, 8, send, 0)
+
+
+def finish_half(me, stage, target, sems):
+    slots = pl.ds(3, 3)
+    local = pltpu.make_async_copy(stage.at[me, slots], target.at[me], sems[2].at[0])
+    local.start()
+    seven = pl.ds(0, 7)
+    copies = to_device(lax.rem(me + 1, 8), stage.at[seven, slots], target.at[seven], sems[0].at[0], sems[1].at[0])
+    copies.wait_send()
+    copies.wait_recv()
+    local.wait()
+
+
+def finish_back(me, stage, target, sems):
+    local = pltpu.make_async_copy(stage.at[me], target.at[me], sems[2].at[0])
+    local.start()
+    seven = pl.ds(0, 7)
+    copies = to_device(lax.rem(me + 1, 8), stage.at[seven], target.at[seven], sems[0].at[0], sems[1].at[0])
+    copies.wait_send()
+    copies.wait_recv()
+    local.wait()
 
 
 def send_group(devices, me, total, group, number, source, arrived, sems):
@@ -585,7 +754,7 @@
 
 def mid_kernel(
     sizes, att_ref, hidden_ref, cot_ref, out_weight_ref, in_weight_ref, down_ref, vectors_ref,
-    layer_ref, act_ref, gate_up_ref, normed_ref, attended_ref, branch_ref, residual_ref, items_ref, gain_out,
+    layer_ref, act_ref, gate_up_ref, normed_ref, attended_ref, branch_ref, residual_ref, items_ref, gain_out, rest_ref,
     arrived, stage, keep_gain, grad_act, *sems,
 ):
     local_tokens, devices, total = sizes
@@ -601,29 +770,42 @@
 
     together = hidden_ref.shape[0]
     group = together * PAIRS
+    turn = lax.rem(step + 2, 4) if devices == 8 else step
     rows = together * local_tokens
     model = vectors_ref.shape[1]
 
-    here_rows = pl.ds(pl.multiple_of(step * rows, 128), rows)
+    here_rows = pl.ds(pl.multiple_of(turn * rows, 128), rows)
 
     @pl.when(step == 0)
     def _():
-        send_group(devices, me, total, group, 0, att_ref, arrived, in_sems)
+        if devices == 8:
+            for number in (2, 3, 0, 1):
+                send_slots(me, number, att_ref, arrived, in_sems)
+        else:
+            send_group(devices, me, total, group, 0, att_ref, arrived, in_sems)
         every = cot_ref[...].reshape(grad_act.shape[0], model)
         for first in range(0, down_ref.shape[0], 512):
             grad_act[:, first : first + 512] = dot(every, down_ref[first : first + 512, :], NT)
 
-    take_items(devices, me, step * group, group, att_ref, arrived, in_sems)
-
-    @pl.when(step + 1 < pl.num_programs(0))
-    def _():
-        send_group(devices, me, total, group, step + 1, att_ref, arrived, in_sems)
+    if devices == 8:
+        for number in range(4):
+
+            @pl.when(turn == number)
+            def _():
+                wait_slots(me, number, att_ref, arrived, in_sems, False)
+
+    else:
+        take_items(devices, me, step * group, group, att_ref, arrived, in_sems)
+
+        @pl.when(step + 1 < pl.num_programs(0))
+        def _():
+            send_group(devices, me, total, group, step + 1, att_ref, arrived, in_sems)
 
     gathered = []
     for one in range(together):
         pieces = []
         for pair in range(PAIRS):
-            item = (step * together + one) * PAIRS + pair
+            item = (turn * together + one) * PAIRS + pair
             other, slot = lax.rem(item, devices), item // devices
             pieces.append(arrived[other, slot])
         gathered.append(jnp.concatenate(pieces, axis=1))
@@ -634,7 +816,7 @@
     scale = lax.rsqrt(jnp.mean(residual * residual, axis=1, keepdims=True) + 1e-06)
     normed = (residual * scale * gain).astype(BF16)
     normed_ref[...] = normed.reshape(normed_ref.shape)
-    cot = cot_ref[pl.ds(step * together, together)].reshape(rows, model)
+    cot = cot_ref[pl.ds(turn * together, together)].reshape(rows, model)
     hidden_units = down_ref.shape[0]
     chunk = 512
     layer = residual
@@ -669,11 +851,24 @@
     grad_attended = dot(branch, out_weight_ref[...], NT).astype(BF16)
     for one in range(together):
         for pair in range(PAIRS):
-            item = (step * together + one) * PAIRS + pair
+            item = (turn * together + one) * PAIRS + pair
             other, slot = lax.rem(item, devices), item // devices
             stage[other, slot] = grad_attended[one * local_tokens : (one + 1) * local_tokens, pair * 128 : pair * 128 + 128]
     keep_gain[...] += jnp.sum((back * residual * scale).reshape(rows // 8, 8, model), axis=0)
     gain_out[...] = jnp.sum(keep_gain[...], axis=0, keepdims=True)
+    if devices == 8:
+        @pl.when(step < 2)
+        def _():
+            send_back(me, turn, stage, items_ref, out_sems)
+
+        @pl.when(step == 3)
+        def _():
+            for number in range(4):
+                wait_slots(me, number, att_ref, arrived, in_sems, True)
+            finish_half(me, stage, items_ref, out_sems)
+            rest_ref[...] = stage[:, 0:3]
+
+        return
     send_items(devices, me, step * group, group, stage, items_ref, out_sems)
 
     @pl.when(step == pl.num_programs(0) - 1)
@@ -731,67 +926,87 @@
 
         @pl.when(step == 1)
         def _():
-            reduce.second()
-
-        @pl.when(step == 5)
+            reduce.in_two()
+
+        @pl.when(step == 2)
         def _():
-            reduce.third()
-            reduce.between()
+            reduce.late_one()
+
+        @pl.when(step == 3)
+        def _():
+            reduce.in_three()
+            reduce.rest_two()
 
     @pl.when(step == 0)
     def _():
         block_masks(masks, me * 2 * local_tokens, devices * 2 * local_tokens)
         permute_weight(weight_ref, permuted)
 
-    projected = jnp.concatenate([block_of(step * PAIRS + pair) for pair in range(PAIRS)], axis=1)
+    together = hidden_ref.shape[0]
+    rows = together * local_tokens
+    projected = jnp.concatenate(
+        [
+            jnp.concatenate([block_of((step * together + one) * PAIRS + pair) for pair in range(PAIRS)], axis=1)
+            for one in range(together)
+        ],
+        axis=0,
+    )
     if not custom:
-        flat_out[0] = projected
+        flat_out[...] = projected.reshape(flat_out.shape)
     width = masks.shape[3]
     grad_normed = dot(projected, permuted[...], NT)
-    hidden = hidden_ref[0]
+    hidden = hidden_ref[...].reshape(rows, model)
     gain = vectors_ref[5:6, :]
     score = vectors_ref[7:8, :]
     scale = lax.rsqrt(jnp.mean(hidden * hidden, axis=1, keepdims=True) + 1e-06)
     weighted = gain * grad_normed
     inner_mean = jnp.mean(hidden * weighted, axis=1, keepdims=True)
-    grad_hidden = residual_ref[0] + scale * weighted - hidden * (scale * scale * scale * inner_mean)
-    keep_gain[...] += jnp.sum((grad_normed * hidden * scale).reshape(local_tokens // 8, 8, model), axis=0)
-    high, low = split_two(grad_hidden)
+    grad_hidden = residual_ref[...].reshape(rows, model) + scale * weighted - hidden * (scale * scale * scale * inner_mean)
+    keep_gain[...] += jnp.sum((grad_normed * hidden * scale).reshape(rows // 8, 8, model), axis=0)
+    high_all, low_all = split_two(grad_hidden)
     vector = jnp.broadcast_to(score.astype(BF16), (local_tokens, model))
-    conv = conv_ref[0]
-    cross = 0.5 * (dot(high, conv, NT) + dot(low, conv, NT))
-    kept = share_ref[0]
-    total = jnp.zeros((local_tokens, width), F32)
-    for side in range(2):
-        shares = [kept[:, 4 * side + k : 4 * side + k + 1] for k in range(4)]
-        grads = [jnp.sum(masks[side, k] * cross, axis=1, keepdims=True) for k in range(4)]
-        mean = sum(share * grad for share, grad in zip(shares, grads))
-        for k in range(4):
-            total = total + (shares[k] * (grads[k] - mean)) * masks[side, k]
-    column = jnp.sum(total, axis=0, keepdims=True)
-    column_high, column_low = split_two(column)
     row16 = lax.broadcasted_iota(jnp.int32, (16, width), 0)
-    column_rows = jnp.where(row16 == 0, column_high.astype(F32), jnp.where(row16 == 1, column_low.astype(F32), 0.0)).astype(BF16)
-    keep_score[...] += dot(column_rows, conv, NN)
-    left = jnp.concatenate([mix_ref[0], total.astype(BF16)], axis=0)
-    right = jnp.concatenate([high, vector], axis=0)
-    slope = dot(left, right, TN)
-    slope = slope[0:window].astype(BF16)
-    row = lax.broadcasted_iota(jnp.int32, (SMALL_ROWS, window), 0)
-    hots = [jnp.where(ids_ref[0, tap : tap + 1, :] == row, 1.0, 0.0).astype(BF16) for tap in range(5)]
+    slopes = []
+    for one in range(together):
+        own = slice(one * local_tokens, (one + 1) * local_tokens)
+        high, low = high_all[own], low_all[own]
+        conv = conv_ref[one]
+        cross = 0.5 * (dot(high, conv, NT) + dot(low, conv, NT))
+        kept = share_ref[one]
+        total = jnp.zeros((local_tokens, width), F32)
+        for side in range(2):
+            shares = [kept[:, 4 * side + k : 4 * side + k + 1] for k in range(4)]
+            grads = [jnp.sum(masks[side, k] * cross, axis=1, keepdims=True) for k in range(4)]
+            mean = sum(share * grad for share, grad in zip(shares, grads))
+            for k in range(4):
+                total = total + (shares[k] * (grads[k] - mean)) * masks[side, k]
+        column = jnp.sum(total, axis=0, keepdims=True)
+        column_high, column_low = split_two(column)
+        column_rows = jnp.where(row16 == 0, column_high.astype(F32), jnp.where(row16 == 1, column_low.astype(F32), 0.0)).astype(BF16)
+        keep_score[...] += dot(column_rows, conv, NN)
+        left = jnp.concatenate([mix_ref[one], total.astype(BF16)], axis=0)
+        right = jnp.concatenate([high, vector], axis=0)
+        slopes.append(dot(left, right, TN)[0:window].astype(BF16))
+    slope = jnp.concatenate(slopes, axis=0)
+    row = lax.broadcasted_iota(jnp.int32, (SMALL_ROWS, window), 0).astype(F32)
     for tap in range(5):
-        tap_sums[tap] += dot(hots[tap], slope, NN)
+        hot = jnp.concatenate(
+            [jnp.where(ids_ref[one, 4 - tap : 5 - tap, 0:window] == row, 1.0, 0.0).astype(BF16) for one in range(together)], axis=1
+        )
+        tap_sums[tap] += dot(hot, slope, NN)
 
     @pl.when(last)
     def _():
+        if custom:
+            reduce.late_two()
         table_grad = jnp.zeros((SMALL_ROWS, model), F32)
-        table = table_ref[0:SMALL_ROWS, :].astype(F32)
+        table = table_ref[...].astype(F32)
         place = lax.broadcasted_iota(jnp.int32, (SMALL_ROWS, model), 0)
         extra = []
         for tap in range(5):
             sums = tap_sums[tap]
             table_grad = table_grad + vectors_ref[tap : tap + 1, :] * sums
-            extra.append(jnp.sum(sums * table, axis=0, keepdims=True))
+            extra.append(jnp.sum(sums[0 : table.shape[0]] * table, axis=0, keepdims=True))
         extra.append(jnp.sum(keep_gain[...], axis=0, keepdims=True))
         extra.append(jnp.sum(keep_score[...], axis=0, keepdims=True))
         extra.append(gain_two_ref[...])
@@ -808,15 +1023,19 @@
         block[272:288, 0:128] = heads
         small.pack()
         small.one_start()
+        small.one_middle()
         if custom:
-            reduce.fourth()
+            reduce.late_three()
         small.one_finish()
+        if custom:
+            reduce.finish_rest(down_out)
+        if custom:
+            reduce.finish_in(in_out, weight_out)
         small.two_finish()
         if custom:
-            reduce.finish(in_out, down_out, weight_out)
+            reduce.finish_late(qkv_out)
         small.three_finish()
-        if custom:
-            reduce.finish_late(qkv_out)
+        small.three_more()
         small.four_finish()
 
 
@@ -851,6 +1070,8 @@
 
 def item_sems(devices, per_device):
     dma = pltpu.SemaphoreType.DMA
+    if devices == 8:
+        return [dma((4,)), dma((4,)), dma((4,))]
     return [dma((devices, per_device)), dma((devices, per_device)), dma((per_device,))]
 
 
@@ -869,20 +1090,23 @@
     return pltpu.CompilerParams(vmem_limit_bytes=VMEM_LIMIT, collective_id=number, has_side_effects=True)
 
 
-def call_front(ids, table, weight, vectors, local_tokens, devices, per_device):
-    sequences, window, unused = ids.shape
+def call_front(lengths, ids, table, weight, vectors, devices, per_device):
+    sequences, local_bytes = ids.shape
+    local_tokens = local_bytes // 2
+    window = local_bytes + 16
     width = -(-window // 128) * 128
     model = weight.shape[0]
     return pl.pallas_call(
         functools.partial(front_kernel, (local_tokens, window, devices, sequences * PAIRS)),
         grid=(sequences,),
-        in_specs=[part(1, window, 8), whole(*table.shape), whole(*weight.shape), whole(*vectors.shape)],
+        in_specs=[pl.BlockSpec(memory_space=pltpu.SMEM), whole(*ids.shape), whole(*table.shape), whole(*weight.shape), whole(*vectors.shape)],
         out_specs=[
             part(1, local_tokens, model),
             part(1, local_tokens, model),
             part(1, width, model),
             part(1, local_tokens, width),
             part(1, local_tokens, 128),
+            part(1, 8, local_bytes + 256),
             ANYWHERE,
         ],
         scratch_shapes=[
@@ -890,7 +1114,11 @@
             pltpu.VMEM((1, 2, width, model), BF16),
             pltpu.VMEM(weight.shape, BF16),
             pltpu.VMEM((devices, per_device, local_tokens, 384), BF16),
-            pltpu.VMEM((5,) + table.shape, BF16),
+            pltpu.VMEM((5, VPAD, model), BF16),
+            pltpu.VMEM((sequences, 128), jnp.int32),
+            pltpu.VMEM((sequences, 128), jnp.int32),
+            pltpu.VMEM((sequences, local_bytes + 256), F32),
+            pltpu.SemaphoreType.DMA((4,)),
         ]
         + item_sems(devices, per_device),
         out_shape=[
@@ -899,19 +1127,23 @@
             jax.ShapeDtypeStruct((sequences, width, model), BF16),
             jax.ShapeDtypeStruct((sequences, local_tokens, width), BF16),
             jax.ShapeDtypeStruct((sequences, local_tokens, 128), F32),
+            jax.ShapeDtypeStruct((sequences, 8, local_bytes + 256), F32),
             jax.ShapeDtypeStruct((devices, per_device, local_tokens, 384), BF16),
         ],
         compiler_params=remote_params(3),
         cost_estimate=pl.CostEstimate(flops=5 * 10**10, bytes_accessed=2 * 10**7, transcendentals=10**5),
         name="front",
-    )(ids, table, weight, vectors)
+    )(lengths, ids, table, weight, vectors)
 
 
 def call_mid(att, hidden, cot, out_weight, in_weight, down_weight, vectors):
     devices, per_device, local_tokens, unused = att.shape
     sequences, unused, model = hidden.shape
     hidden_units = down_weight.shape[0]
-    rows = lambda lanes: part(TOGETHER, local_tokens, lanes)
+    fast = devices == 8
+    rows = lambda lanes: pl.BlockSpec((TOGETHER, local_tokens, lanes), lambda s: (lax.rem(s + 2, 4) if fast else s, 0, 0))
+    shape = (devices, per_device // 2 if fast else per_device, local_tokens, 128)
+    rest = shape if fast else (1, 1, 8, 128)
     full = lambda lanes, kind: jax.ShapeDtypeStruct((sequences, local_tokens, lanes), kind)
     return pl.pallas_call(
         functools.partial(mid_kernel, (local_tokens, devices, sequences * PAIRS)),
@@ -935,6 +1167,7 @@
             rows(model),
             ANYWHERE,
             whole(1, model),
+            whole(*rest),
         ],
         scratch_shapes=[pltpu.VMEM(att.shape, BF16), pltpu.VMEM(att.shape, BF16), pltpu.VMEM((8, model), F32), pltpu.VMEM((sequences * local_tokens, hidden_units), F32)]
         + item_sems(devices, per_device)
@@ -947,8 +1180,9 @@
             full(model, BF16),
             full(model, BF16),
             full(model, F32),
-            jax.ShapeDtypeStruct(att.shape, BF16),
+            jax.ShapeDtypeStruct(shape, BF16),
             jax.ShapeDtypeStruct((1, model), F32),
+            jax.ShapeDtypeStruct(rest, BF16),
         ],
         compiler_params=remote_params(4),
         cost_estimate=pl.CostEstimate(flops=5 * 10**10, bytes_accessed=4 * 10**7, transcendentals=10**6),
@@ -960,7 +1194,7 @@
     devices, unused, local_tokens, unused = one.shape
     sequences, unused, model = hidden.shape
     width = conv.shape[1]
-    window = ids.shape[2]
+    window = 2 * local_tokens + 16
     bias_hot = jnp.pad(near_one_hot(), ((0, 0), (0, 96))).astype(BF16)
     out_specs = [whole(SMALL_ROWS, model)]
     out_shape = [jax.ShapeDtypeStruct((SMALL_ROWS, model), F32)]
@@ -973,20 +1207,20 @@
         out_shape = out_shape + [jax.ShapeDtypeStruct(shape, F32) for shape in sums]
         scratch = weight_scratch(model, sequences * local_tokens)
     else:
-        out_specs = out_specs + [part(1, local_tokens, PAIRS * 384)]
+        out_specs = out_specs + [part(TOGETHER, local_tokens, PAIRS * 384)]
         out_shape = out_shape + [jax.ShapeDtypeStruct((sequences, local_tokens, PAIRS * 384), BF16)]
     return pl.pallas_call(
         functools.partial(back_kernel, (local_tokens, window, devices), custom),
-        grid=(sequences,),
+        grid=(sequences // TOGETHER,),
         in_specs=[
             whole(*one.shape),
             whole(*two.shape),
-            part(1, local_tokens, model),
-            part(1, local_tokens, model),
-            part(1, width, model),
-            part(1, local_tokens, width),
-            part(1, local_tokens, 128),
-            part(1, 8, window),
+            part(TOGETHER, local_tokens, model),
+            part(TOGETHER, local_tokens, model),
+            part(TOGETHER, width, model),
+            part(TOGETHER, local_tokens, width),
+            part(TOGETHER, local_tokens, 128),
+            part(TOGETHER, 8, ids.shape[2]),
             whole(*weight.shape),
             whole(*table.shape),
             whole(*vectors.shape),
@@ -1152,19 +1386,76 @@
     )(act, cot, normed, gate_up, attended, branch, after)
 
 
+class ChipSums:
+    def __init__(self, source, buffers, sems, chip, core):
+        self.source, self.first, self.relay, self.second = (source,) + tuple(buffers)
+        self.send, self.recv = sems
+        self.chip, self.core = chip, core
+        self.beside = chip + 1 - 2 * lax.rem(chip, 2)
+        self.above = lax.rem(chip + 2, 4)
+
+    def copy(self, other, source, target, number):
+        return pltpu.make_async_remote_copy(
+            src_ref=source, dst_ref=target, send_sem=self.send.at[number], recv_sem=self.recv.at[number],
+            device_id={"seq": 2 * other + self.core}, device_id_type=pl.DeviceIdType.MESH,
+        )
+
+    def ways(self):
+        return ((0, self.beside, self.above), (1, self.above, self.beside))
+
+    def one(self):
+        made = []
+        for way, near, other in self.ways():
+            columns = pl.ds(2 * way, 2)
+            made.append(self.copy(near, self.source.at[near, columns], self.first.at[way, 0], 2 * way))
+            made.append(self.copy(near, self.source.at[3 - self.chip, columns], self.first.at[way, 1], 2 * way + 1))
+        return made
+
+    def two(self):
+        return [self.copy(other, self.relay.at[way], self.second.at[way], 4 + way) for way, near, other in self.ways()]
+
+    def start(self):
+        for copy in self.one():
+            copy.start()
+
+    def middle(self):
+        for copy in self.one():
+            copy.wait()
+        for way, near, other in self.ways():
+            for at in range(2):
+                total = self.source[other, 2 * way + at].astype(F32) + self.first[way, 1, at].astype(F32)
+                self.relay[way, at] = total.astype(BF16)
+        for copy in self.two():
+            copy.start()
+
+    def finish(self, target):
+        for copy in self.two():
+            copy.wait()
+        for way in range(2):
+            for at in range(2):
+                total = self.source[self.chip, 2 * way + at].astype(F32) + self.first[way, 0, at].astype(F32)
+                target[2 * way + at] = (total + self.second[way, at].astype(F32)).astype(BF16)
+
+
+def chip_scratch(rows):
+    return [pltpu.VMEM((2, 2, 2, rows, 128), BF16), pltpu.VMEM((2, 2, rows, 128), BF16), pltpu.VMEM((2, 2, rows, 128), BF16)]
+
+
 class WeightSums:
     def __init__(self, normed_ref, across_ref, planes_ref, block_of, refs):
         self.normed, self.across, self.planes, self.block_of = normed_ref, across_ref, planes_ref, block_of
         (
             self.in_sum, self.in_got, self.rest_got, self.rest_sum, self.rest_chips, self.normed_t, self.result,
-            self.keep, self.other, self.got, self.chips, self.late_sum, self.late_got, self.in_chips,
-        ) = refs[:14]
+            self.keep, self.other, self.got, self.late_sum, self.late_got,
+        ) = refs[:12]
         (
             self.send_in, self.recv_in, self.send_rest, self.recv_rest, self.send_chip, self.recv_chip,
-            self.send_a, self.recv_a, self.send_b, self.recv_b, self.send_c, self.recv_c, self.send_i, self.recv_i,
-        ) = refs[14:]
+            self.send_a, self.recv_a, self.send_c, self.recv_c,
+        ) = refs[18:28]
         self.me, self.plane = lax.axis_index("seq"), lax.axis_index("dp")
         self.core, self.chip = lax.rem(self.me, 2), self.me // 2
+        self.in_chips = ChipSums(across_ref, refs[12:15], refs[28:30], self.chip, self.core)
+        self.late_chips = ChipSums(self.keep, refs[15:18], refs[30:32], self.chip, self.core)
 
     def to_plane(self, offset, source, target, send, recv):
         return pltpu.make_async_remote_copy(
@@ -1172,13 +1463,6 @@
             device_id={"dp": lax.rem(self.plane + offset, 4)}, device_id_type=pl.DeviceIdType.MESH,
         )
 
-    def to_chip(self, offset, source, target, send, recv):
-        other = lax.rem(self.chip + offset, 4)
-        return pltpu.make_async_remote_copy(
-            src_ref=source, dst_ref=target, send_sem=send, recv_sem=recv,
-            device_id={"seq": 2 * other + self.core}, device_id_type=pl.DeviceIdType.MESH,
-        )
-
     def rest_plane(self, offset):
         peer = lax.rem(self.plane + offset, 4)
         return self.to_plane(offset, self.planes.at[peer], self.rest_got.at[offset - 1], self.send_rest, self.recv_rest)
@@ -1193,24 +1477,18 @@
 
     def rest_chip(self, offset):
         other = lax.rem(self.chip + offset, 4)
-        return self.to_chip(offset, self.rest_sum.at[other], self.rest_chips.at[offset - 1], self.send_chip.at[offset - 1], self.recv_chip.at[offset - 1])
-
-    def late_chip(self, offset, column):
-        other = lax.rem(self.chip + offset, 4)
-        return self.to_chip(
-            offset, self.keep.at[other, column], self.chips.at[offset - 1, column], self.send_b.at[offset - 1, column], self.recv_b.at[offset - 1, column]
+        return pltpu.make_async_remote_copy(
+            src_ref=self.rest_sum.at[other], dst_ref=self.rest_chips.at[offset - 1],
+            send_sem=self.send_chip.at[offset - 1], recv_sem=self.recv_chip.at[offset - 1],
+            device_id={"seq": 2 * other + self.core}, device_id_type=pl.DeviceIdType.MESH,
         )
 
     def late_core(self, column):
         return to_sibling(self.core, self.other.at[:, column], self.got.at[:, column], self.send_a.at[column], self.recv_a.at[column])
 
-    def in_chip(self, offset):
-        other = lax.rem(self.chip + offset, 4)
-        return self.to_chip(offset, self.across.at[other], self.in_chips.at[offset - 1], self.send_i.at[offset - 1], self.recv_i.at[offset - 1])
-
     def begin(self):
+        self.in_chips.start()
         for offset in (1, 2, 3):
-            self.in_chip(offset).start()
             self.rest_plane(offset).start()
 
     def late(self):
@@ -1234,26 +1512,20 @@
         for column in range(4):
             self.late_core(column).start()
 
-    def second(self):
+    def late_one(self):
         for column in range(4):
             self.late_core(column).wait()
             for at in range(4):
                 self.keep[at, column] = (self.keep[at, column].astype(F32) + self.got[at, column].astype(F32)).astype(BF16)
-            for offset in (1, 2, 3):
-                self.late_chip(offset, column).start()
-
-    def third(self):
-        for offset in (1, 2, 3):
-            self.in_chip(offset).wait()
-        for column in range(4):
-            total = self.across[self.chip, column].astype(F32)
-            for slot in range(3):
-                total = total + self.in_chips[slot, column].astype(F32)
-            self.in_sum[column] = total.astype(BF16)
-        for offset in (1, 2, 3):
-            self.in_plane(offset).start()
-
-    def between(self):
+        self.late_chips.start()
+
+    def in_two(self):
+        self.in_chips.middle()
+
+    def late_two(self):
+        self.late_chips.middle()
+
+    def rest_two(self):
         for offset in (1, 2, 3):
             self.rest_plane(offset).wait()
         for chip in range(4):
@@ -1264,13 +1536,13 @@
         for offset in (1, 2, 3):
             self.rest_chip(offset).start()
 
-    def fourth(self):
-        for column in range(4):
-            total = self.keep[self.chip, column].astype(F32)
-            for offset in (1, 2, 3):
-                self.late_chip(offset, column).wait()
-                total = total + self.chips[offset - 1, column].astype(F32)
-            self.late_sum[column] = total.astype(BF16)
+    def in_three(self):
+        self.in_chips.finish(self.in_sum)
+        for offset in (1, 2, 3):
+            self.in_plane(offset).start()
+
+    def late_three(self):
+        self.late_chips.finish(self.late_sum)
         for offset in (1, 2, 3):
             self.late_plane(offset).start()
 
@@ -1279,7 +1551,15 @@
         count = block.shape[1]
         return jnp.where(odd, pltpu.roll(block, count - 64, 1), block)[:, :columns]
 
-    def finish(self, in_out, down_out, weight_out):
+    def finish_rest(self, down_out):
+        total = self.rest_sum[self.chip].astype(F32)
+        for offset in (1, 2, 3):
+            self.rest_chip(offset).wait()
+            total = total + self.rest_chips[offset - 1].astype(F32)
+        down_out[0:128, :] = total[0:192].T
+        down_out[128:256, :] = total[192:384].T
+
+    def finish_in(self, in_out, weight_out):
         total = self.in_sum[self.plane].astype(F32)
         for offset in (1, 2, 3):
             self.in_plane(offset).wait()
@@ -1287,12 +1567,6 @@
         for tile in range(8):
             in_out[:, 128 * tile : 128 * tile + 128] = total[96 * tile : 96 * tile + 96]
         weight_out[...] = self.joined(jnp.concatenate([total[768:864], total[864:960]], axis=1), 192)
-        total = self.rest_sum[self.chip].astype(F32)
-        for offset in (1, 2, 3):
-            self.rest_chip(offset).wait()
-            total = total + self.rest_chips[offset - 1].astype(F32)
-        down_out[0:128, :] = total[0:192].T
-        down_out[128:256, :] = total[192:384].T
 
     def finish_late(self, qkv_out):
         total = self.late_sum[self.plane].astype(F32)
@@ -1305,24 +1579,26 @@
 def weight_scratch(model, tokens):
     dma = pltpu.SemaphoreType.DMA
     late = (4, 4, LATE_ROWS, 128)
-    return [
-        pltpu.VMEM((4, IN_ROWS, 128), BF16),
-        pltpu.VMEM((3, IN_ROWS, 128), BF16),
-        pltpu.VMEM((3, 4, REST_ROWS, 128), BF16),
-        pltpu.VMEM((4, REST_ROWS, 128), BF16),
-        pltpu.VMEM((3, REST_ROWS, 128), BF16),
-        pltpu.VMEM((model, tokens), BF16),
-        pltpu.VMEM((3 * PAIRS, model, 128), BF16),
-        pltpu.VMEM(late, BF16),
-        pltpu.VMEM(late, BF16),
-        pltpu.VMEM(late, BF16),
-        pltpu.VMEM((3, 4, LATE_ROWS, 128), BF16),
-        pltpu.VMEM((4, LATE_ROWS, 128), BF16),
-        pltpu.VMEM((3, LATE_ROWS, 128), BF16),
-        pltpu.VMEM((3, 4, IN_ROWS, 128), BF16),
-        dma((3,)), dma((3,)), dma((3,)), dma((3,)), dma((3,)), dma((3,)),
-        dma((4,)), dma((4,)), dma((3, 4)), dma((3, 4)), dma((3,)), dma((3,)), dma((3,)), dma((3,)),
-    ]
+    return (
+        [
+            pltpu.VMEM((4, IN_ROWS, 128), BF16),
+            pltpu.VMEM((3, IN_ROWS, 128), BF16),
+            pltpu.VMEM((3, 4, REST_ROWS, 128), BF16),
+            pltpu.VMEM((4, REST_ROWS, 128), BF16),
+            pltpu.VMEM((3, REST_ROWS, 128), BF16),
+            pltpu.VMEM((model, tokens), BF16),
+            pltpu.VMEM((3 * PAIRS, model, 128), BF16),
+            pltpu.VMEM(late, BF16),
+            pltpu.VMEM(late, BF16),
+            pltpu.VMEM(late, BF16),
+            pltpu.VMEM((4, LATE_ROWS, 128), BF16),
+            pltpu.VMEM((3, LATE_ROWS, 128), BF16),
+        ]
+        + chip_scratch(IN_ROWS)
+        + chip_scratch(LATE_ROWS)
+        + [dma((3,)), dma((3,)), dma((3,)), dma((3,)), dma((3,)), dma((3,)), dma((4,)), dma((4,)), dma((3,)), dma((3,))]
+        + [dma((6,)), dma((6,)), dma((6,)), dma((6,))]
+    )
 
 
 SMALL_ROWS = 288
@@ -1335,6 +1611,9 @@
         self.sems = sems
         self.me, self.plane = lax.axis_index("seq"), lax.axis_index("dp")
         self.across, self.along = self.held.shape[0], self.held.shape[1]
+        self.paired = self.across == 8
+        self.core, self.chip = lax.rem(self.me, 2), self.me // 2
+        self.mine = self.across // 2 * self.core + self.chip
 
     def places(self):
         half = self.held.shape[2] // 2
@@ -1356,29 +1635,48 @@
                 self.held[spot] = self.block[source].astype(BF16)
 
     def copies(self, axis, source, target, number):
-        here, count = (self.me, self.across) if axis == "seq" else (self.plane, self.along)
+        here, count = {"seq": (self.me, self.across), "chip": (self.chip, self.across // 2), "dp": (self.plane, self.along)}[axis]
         send, recv = self.sems[2 * number], self.sems[2 * number + 1]
         made = []
         for step in range(1, count):
             peer = lax.rem(here + step, count)
+            device = {"seq": 2 * peer + self.core} if axis == "chip" else {axis: peer}
             made.append(
                 pltpu.make_async_remote_copy(
                     src_ref=source(peer), dst_ref=target(step - 1), send_sem=send.at[step - 1], recv_sem=recv.at[step - 1],
-                    device_id={axis: peer}, device_id_type=pl.DeviceIdType.MESH,
+                    device_id=device, device_id_type=pl.DeviceIdType.MESH,
                 )
             )
         for copy in made:
             copy.start()
         return made
 
+    def sibling(self, source, target, number):
+        made = [to_sibling(self.core, source, target, self.sems[2 * number].at[6], self.sems[2 * number + 1].at[6])]
+        made[0].start()
+        return made
+
     def one_start(self):
+        if self.paired:
+            half = pl.ds(4 * (1 - self.core), 4)
+            self.waiting = self.sibling(self.held.at[half], self.got_seq.at[pl.ds(3, 4)], 0)
+            return
         self.waiting = self.copies("seq", lambda peer: self.held.at[peer], lambda slot: self.got_seq.at[slot], 0)
+
+    def one_middle(self):
+        if self.paired:
+            for copy in self.waiting:
+                copy.wait()
+            for chip in range(4):
+                at = 4 * self.core + chip
+                self.held[at] = (self.held[at].astype(F32) + self.got_seq[3 + chip].astype(F32)).astype(BF16)
+            self.waiting = self.copies("chip", lambda peer: self.held.at[4 * self.core + peer], lambda slot: self.got_seq.at[slot], 0)
 
     def one_finish(self):
         for copy in self.waiting:
             copy.wait()
-        total = self.held[self.me].astype(F32)
-        for slot in range(self.across - 1):
+        total = self.held[self.mine if self.paired else self.me].astype(F32)
+        for slot in range(3 if self.paired else self.across - 1):
             total = total + self.got_seq[slot].astype(F32)
         self.planes[...] = total.astype(BF16)
         self.waiting = self.copies("dp", lambda peer: self.planes.at[peer], lambda slot: self.got_dp.at[slot], 1)
@@ -1389,13 +1687,22 @@
         mine = self.planes[self.plane].astype(F32)
         for slot in range(self.along - 1):
             mine = mine + self.got_dp[slot].astype(F32)
-        self.whole[self.me, self.plane] = mine.astype(BF16)
-        self.waiting = self.copies("dp", lambda peer: self.whole.at[self.me, self.plane], lambda slot: self.whole.at[self.me, self.plane], 2)
+        own = self.mine if self.paired else self.me
+        self.whole[own, self.plane] = mine.astype(BF16)
+        self.waiting = self.copies("dp", lambda peer: self.whole.at[own, self.plane], lambda slot: self.whole.at[own, self.plane], 2)
 
     def three_finish(self):
         for copy in self.waiting:
             copy.wait()
-        self.waiting = self.copies("seq", lambda peer: self.whole.at[self.me], lambda slot: self.whole.at[self.me], 3)
+        own = self.mine if self.paired else self.me
+        self.waiting = self.copies("chip" if self.paired else "seq", lambda peer: self.whole.at[own], lambda slot: self.whole.at[own], 3)
+
+    def three_more(self):
+        if self.paired:
+            for copy in self.waiting:
+                copy.wait()
+            half = pl.ds(4 * self.core, 4)
+            self.waiting = self.sibling(self.whole.at[half], self.whole.at[half], 3)
 
     def four_finish(self):
         for copy in self.waiting:
@@ -1439,46 +1746,19 @@
     sequences, local_bytes = byte_ids.shape
     local_tokens = local_bytes // 2
     total_bytes = local_bytes * devices
-    first_byte = me * local_bytes
     vocab, model = byte_table.shape
-    window = local_bytes + 16
     total = sequences * PAIRS
     per_device = -(-total // devices)
-
-    number = jnp.arange(sequences, dtype=jnp.int32)
-    ahead = (lengths[None, :] > lengths[:, None]) | (
-        (lengths[None, :] == lengths[:, None]) & (number[None, :] < number[:, None])
-    )
-    rank = jnp.sum(ahead.astype(jnp.int32), axis=1)
-    placed = rank[None, :] == number[:, None]
-    order = jnp.sum(jnp.where(placed, number[None, :], 0), axis=1)
-    sorted_lengths = jnp.sum(jnp.where(placed, lengths[None, :], 0), axis=1)
-    positions = first_byte + jnp.arange(local_bytes, dtype=jnp.int32)
-    picked = jnp.where(positions[None, :] < lengths[:, None], byte_ids, 0)
-    forward = [(i, i + 1) for i in range(devices - 1)]
-    backward = [(target, source) for source, target in forward]
-    before = jnp.where(me > 0, lax.ppermute(picked[:, -4:], "seq", forward), -1)
-    after = jnp.where(me < devices - 1, lax.ppermute(picked[:, :4], "seq", backward), -1)
-    outside = jnp.full((sequences, 12), -1, jnp.int32)
-    extended = jnp.concatenate([before, picked, after, outside], axis=1)
-    extended = jnp.sum(jnp.where(placed[:, :, None], extended[None, :, :], 0), axis=1)
-    shifted = jnp.stack([extended[:, tap : tap + window] for tap in range(5)])
-    ids_columns = jnp.concatenate([jnp.moveaxis(shifted, 0, 2), jnp.full((sequences, window, 3), -1, jnp.int32)], axis=2)
-
-    table_padded = jnp.concatenate([byte_table, jnp.zeros((VPAD - vocab, model), BF16)], axis=0)
+    place = jnp.reshape(me, (1,)).astype(jnp.int32)
     vectors = jnp.concatenate([conv_kernel, norm_gain_one[None, :], norm_gain_two[None, :], score_vector[None, :]], axis=0)
     rows = jnp.dot(near_one_hot(), bias_table, precision="highest").T.reshape(PAIRS, 2, NEAR)
 
-    item = me + devices * jnp.arange(per_device, dtype=jnp.int32)
-    length = jnp.sum(jnp.where((item // PAIRS)[:, None] == number[None, :], sorted_lengths[None, :], 0), axis=1)
-    valid = jnp.where(item < total, (length + 1) // 2, 0).astype(jnp.int32)
-    pair = lax.rem(item, PAIRS).astype(jnp.int32)
     def exchange(items):
         return lax.all_to_all(items, "seq", split_axis=0, concat_axis=0, tiled=True)
 
-    hidden, normed, conv, mix, share, received = call_front(ids_columns, table_padded, qkv_weight, vectors, local_tokens, devices, per_device)
-    out, aug, cot = attention_forward(received, rows, valid, pair, order, cotangent)
-    layer, act, gate_up, normed_two, attended, branch, grad_residual, grad_items, grad_gain_two = call_mid(
+    hidden, normed, conv, mix, share, ids_rows, received = call_front(lengths, byte_ids, byte_table, qkv_weight, vectors, devices, per_device)
+    out, aug, cot = attention_forward(received, rows, lengths, place, cotangent)
+    layer, act, gate_up, normed_two, attended, branch, grad_residual, grad_items, grad_gain_two, grad_rest = call_mid(
         out, hidden, cot, out_weight, in_weight, down_weight, vectors
     )
     along_count = lax.axis_size("dp")
@@ -1493,17 +1773,19 @@
         summed_in = scatter(jnp.einsum("btd,bti->di", normed_two, gate_up, preferred_element_type=F32).astype(BF16))
         summed_out = scatter(jnp.einsum("btd,bte->de", attended, branch, preferred_element_type=F32).astype(BF16))
     half = per_device // 2
-    dqkv_two, bias_two, layer_out = attention_backward(received, out, aug, grad_items, rows, valid, pair, order, layer, grad_gain_two, half, per_device - half)
+    grads_two, grads_one, at_two = (grad_items, exchange(grad_rest), 0) if devices == 8 else (grad_items, grad_items, half)
+    dqkv_two, bias_two, layer_out = attention_backward(
+        received, out, aug, grads_two, rows, lengths, place, layer, grad_gain_two, half, per_device - half, at_two
+    )
     items_two = exchange(dqkv_two)
-    dqkv_one, bias_one, unused = attention_backward(received, out, aug, grad_items, rows, valid, pair, order, None, bias_two, 0, half)
+    dqkv_one, bias_one, unused = attention_backward(received, out, aug, grads_one, rows, lengths, place, None, bias_two, 0, half, 0)
     items_one = exchange(dqkv_one)
     bias_rows = jnp.concatenate([bias_one, bias_two], axis=0)
     if custom:
         in_chips, rest_planes = call_early(act, cot, normed_two, gate_up, attended, branch, items_two)
-    ids_rows = jnp.concatenate([jnp.moveaxis(shifted, 0, 1), jnp.full((sequences, 3, window), -1, jnp.int32)], axis=1)
     extra = (normed, in_chips, rest_planes) if custom else ()
     results = call_back(
-        custom, items_one, items_two, hidden, grad_residual, conv, mix, share, ids_rows, qkv_weight, table_padded, vectors, bias_rows, grad_gain_two, along_count, extra
+        custom, items_one, items_two, hidden, grad_residual, conv, mix, share, ids_rows, qkv_weight, byte_table, vectors, bias_rows, grad_gain_two, along_count, extra
     )
     if custom:
         summed_qkv, summed_in, summed_down, summed_out, *smalls = call_finish(results[0], results[1:])

time: 375 us -> 350 us (0.933); the launches traced: 368 us -> 352 us
  Pallas kernels: 330 us -> 302 us
  starting transfers between devices: 12.3 us -> 27.9 us
    all_to_all x2 -> x3, starting transfers between devices: 8 us -> 27.9 us  [exchange(): return lax.all_to_all(items, 'seq', split_axis=0, concat_axis=0, tiled=True)]
    pallas_call x1, Pallas kernels: 110 us -> 93 us  [call_back(): pl.pallas_call(functools.partial(back_kernel, (local_tokens, window, devi...]
    pallas_call x1, Pallas kernels: 59 us -> 46.6 us  [call_mid(): pl.pallas_call(functools.partial(mid_kernel, (local_tokens, devices, sequ...]
    unnamed x15 -> x24, local copies, waits for them, and re-layouts: 6.79 us -> 11.5 us
    ppermute x2 -> x0, starting transfers between devices: 4.31 us -> none  [the longest x1 3.03 us: body(): before = jnp.where(me > 0, lax.ppermute(picked[:, -4:], 'seq', forward), -1)]
  transfers between devices with their start and end apart: 4 -> 3, of which waited for: 2 -> 2; matrix products, arithmetic and copies ran while one was open for 3% -> 0% of each run, Pallas kernels for 14% -> 20%
where the time goes in v4:
time: 350 us; the launch traced here: 352 us
  Pallas kernels  302 us (86%)
  starting transfers between devices  27.9 us (8%)
  local copies, waits for them, and re-layouts  13.6 us (4%)
  waiting for transfers between devices  4.45 us (1%)
    pallas_call x1, Pallas kernels, call_back(): pl.pallas_call(functools.partial(back_kernel, (local_tokens, window, devi...  93 us
    pallas_call x1, Pallas kernels, call_front(): pl.pallas_call(functools.partial(front_kernel, (local_tokens, window, dev...  64.7 us
    pallas_call x1, Pallas kernels, call_mid(): pl.pallas_call(functools.partial(mid_kernel, (local_tokens, devices, sequ...  46.6 us
    pallas_call x2, Pallas kernels, attention_backward(): pl.pallas_call(functools.partial(bwd_kernel, blocks, first, moves), grid_...  43.7 us
    all_to_all x3, starting transfers between devices, exchange(): return lax.all_to_all(items, 'seq', split_axis=0, concat_axis=0, tiled=True)  27.9 us
    pallas_call x1, Pallas kernels, attention_forward(): pl.pallas_call(functools.partial(fwd_kernel, blocks), grid_spec=spec, out...  26.1 us
    pallas_call x1, Pallas kernels, call_early(): pl.pallas_call(early_kernel, grid=(8,), in_specs=[pl.BlockSpec((sequences...  25.1 us
    unnamed x24, local copies, waits for them, and re-layouts  11.5 us
  transfers between devices with their start and end apart: 3, of which 2 were waited for; matrix products, arithmetic and copies ran while one was open for 0% of the time, Pallas kernels for 20%

profile of v4, /device:TPU:0, one launch (start us, length us, event | category | flops | bytes accessed | tf_op | source)
XLA Modules:
  0.0 352.4 jit_solution(17149726565612959297)
XLA Ops:
  0.6 0.0 copy-start
  0.7 0.7 broadcast_in_dim.15
  1.4 0.7 broadcast_in_dim.14
  2.1 0.7 broadcast_in_dim.6
  2.8 0.4 convolution_bitcast_fusion
  3.3 1.4 pad_maximum_fusion.1.vectors_ref
  4.6 64.7 %front.1 = (f32[8,128,768]{2,1,0:T(8,128)}, bf16[8,128,768]{2,1,0:T(8,128)(2,1)}, bf16[8,384,768]{2,1,0:T(8,128)(2,1)}, bf16[8,128,384]{2,1,0:T(8,128)(2,1)}, f3...) custom-call(s32[8]{0:T(128)} %lengths_ref.7, s32[8,256]{1,0:T(8,128)} %ids_ref.1, ...), custom_call_target="tpu_custom_call" | custom-call | flops 49999998976 | bytes 20000000 | tf_op jit(solution)/shard_map/front/pallas_call | solution.py:1099
  69.4 26.1 %attention_forward.1 = (bf16[8,6,128,128]{3,2,1,0:T(8,128)(2,1)S(1)}, bf16[6,1024,128]{2,1,0:T(8,128)(2,1)S(1)}, bf16[8,128,768]{2,1,0:T(8,128)(2,1)}) custom-call(s32[8]{0:T(128)S(1)} %copy-done.2, s32[1]{0:T(128)} %bitcast.place_ref, bf16[8,6,128,384]{3,2,1,0:T(8,128)(2,1)} %get-tuple-element.53.qkv_ref, f32[6,2,1024]{2,1,0:T(2,128)S(1)} %reshape.65.row_ref, ...), custom_call_target="tpu_custom_call" | custom-call | flops 3221225472 | bytes 12582912 | tf_op jit(solution)/shard_map/attention_forward/pallas_call | solution.py:278
  95.5 0.0 copy-start.3
  95.5 1.1 copy-done.3
  96.7 1.1 copy-done.5
  97.8 46.6 %middle.1 = (f32[8,128,768]{2,1,0:T(8,128)}, bf16[8,128,2048]{2,1,0:T(8,128)(2,1)}, bf16[8,128,4096]{2,1,0:T(8,128)(2,1)}, bf16[8,128,768]{2,1,0:T(8,128)(2,1)},...) custom-call(bf16[8,6,128,128]{3,2,1,0:T(8,128)(2,1)} %copy-done.3, ...), custom_call_target="tpu_custom_call" | custom-call | flops 49999998976 | bytes 40000000 | tf_op jit(solution)/shard_map/middle/pallas_call | solution.py:1148
  144.4 4.5 %all-to-all-start = ((bf16[8,3,128,128]{3,2,1,0:T(8,128)(2,1)}), bf16[8,3,128,128]{3,2,1,0:T(8,128)(2,1)S(1)}, u32[]{:S(2)}, u32[]{:S(2)}) async-start(bf16[8,3,128,128]{3,2,1,0:T(8,128)(2,1)} %get-tuple-element.62), calls=%async_computation | async-start | bytes 1572864 | tf_op jit(solution)/shard_map/all_to_all | solution.py:1757
  148.9 1.4 copy-done.6
  150.3 1.1 copy-done.8
  151.4 0.7 copy-done.9
  152.1 17.7 %attention_backward.2 = (bf16[8,3,128,384]{3,2,1,0:T(8,128)(2,1)}, f32[3,2,1024]{2,1,0:T(2,128)S(1)}, f32[8,128,768]{2,1,0:T(8,128)}) custom-call(s32[8]{0:T(128)S(1)} %copy-done.2, s32[1]{0:T(128)} %bitcast.place_ref, bf16[8,6,128,384]{3,2,1,0:T(8,128)(2,1)} %get-tuple-element.53.qkv_ref, bf16[8,6,128,128]{3,2,1,0:T(8,128)(2,1)S(1)} %copy-done.4, ...), custom_call_target="tpu_custom_call" | custom-call | flops 4026531840 | bytes 12582912 | tf_op jit(solution)/shard_map/attention_backward/pallas_call | solution.py:332
  169.8 19.8 %all-to-all-start.2 = ((bf16[8,3,128,384]{3,2,1,0:T(8,128)(2,1)}), bf16[8,3,128,384]{3,2,1,0:T(8,128)(2,1)}, u32[]{:S(2)}, u32[]{:S(2)}) async-start(bf16[8,3,128,384]{3,2,1,0:T(8,128)(2,1)} %get-tuple-element.65), calls=%async_computation.2 | async-start | bytes 4718592 | tf_op jit(solution)/shard_map/all_to_all | solution.py:1757
  189.6 1.4 copy-done.7
  191.0 26.0 %attention_backward.3 = (bf16[8,3,128,384]{3,2,1,0:T(8,128)(2,1)}, f32[3,2,1024]{2,1,0:T(2,128)S(1)}, f32[8,128]{1,0:T(8,128)}) custom-call(s32[8]{0:T(128)S(1)} %copy-done.2, s32[1]{0:T(128)} %bitcast.place_ref, bf16[8,6,128,384]{3,2,1,0:T(8,128)(2,1)} %get-tuple-element.53.qkv_ref, bf16[8,6,128,128]{3,2,1,0:T(8,128)(2,1)S(1)} %copy-done.4, ...), custom_call_target="tpu_custom_call" | custom-call | flops 4026531840 | bytes 12582912 | tf_op jit(solution)/shard_map/attention_backward/pallas_call | solution.py:332
  217.0 1.8 all-to-all-done.2.after.two_ref
  218.8 3.6 %all-to-all-start.1 = ((bf16[8,3,128,384]{3,2,1,0:T(8,128)(2,1)}), bf16[8,3,128,384]{3,2,1,0:T(8,128)(2,1)S(1)}, u32[]{:S(2)}, u32[]{:S(2)}) async-start(bf16[8,3,128,384]{3,2,1,0:T(8,128)(2,1)} %get-tuple-element.64), calls=%async_computation.1 | async-start | bytes 4718592 | tf_op jit(solution)/shard_map/all_to_all | solution.py:1757
  222.5 0.2 iota_compare_fusion
  222.7 0.8 convert_convert_fusion.bias_hot_ref
  223.4 0.6 pad_maximum_fusion.bias_ref
  224.1 25.1 %early_gradients.1 = (bf16[4,4,960,128]{3,2,1,0:T(8,128)(2,1)}, bf16[4,4,384,128]{3,2,1,0:T(8,128)(2,1)}) custom-call(bf16[8,128,2048]{2,1,0:T(8,128)(2,1)} %get-tuple-element.73.act_ref, bf16[8,128,768]{2,1,0:T(8,128)(2,1)} %get-tuple-element.57.cot_ref, bf16[8,128,768]{2,1,0:T(8,128)(2,1)} %get-tuple-element.74.normed_ref, ...), custom_call_target="tpu_custom_call" | custom-call | flops 11000000512 | bytes 30000000 | tf_op jit(solution)/shard_map/early_gradients/pallas_call | solution.py:1359
  249.2 2.7 all-to-all-done.1.one_ref
  251.8 1.4 copy-done.10
  253.3 93.0 %back.1 = (f32[288,768]{1,0:T(8,128)}, f32[96,576]{1,0:T(8,128)}, f32[96,1024]{1,0:T(8,128)}, f32[256,192]{1,0:T(8,128)}, f32[96,192]{1,0:T(8,128)}) custom-call(bf16[8,3,128,384]{3,2,1,0:T(8,128)(2,1)} %copy-done.10, bf16[8,3,128,384]{3,2,1,0:T(8,128)(2,1)} %all-to-all-done.2.after.two_ref, f32[8,128,768]{2,1,0:T(8,128)} %get-tuple-element.56.hidden_ref, ...), custom_call_target="tpu_custom_call" | custom-call | flops 99999997952 | bytes 20000000 | tf_op jit(solution)/shard_map/back/pallas_call | solution.py:1212
  346.3 2.8 finish.1
  349.1 1.4 copy.24
  350.5 1.7 copy.25
  (16 shorter events, 0.1 us)
Async XLA Ops:
  0.6 2.1 copy-start
  4.6 64.8 %copy-start.2 = (s32[8]{0:T(128)S(1)}, s32[8]{0:T(128)}, u32[]{:S(2)}) copy-start(s32[8]{0:T(128)} %lengths_ref.7) | copy-start | bytes 100
  95.5 1.1 copy-start.3
  96.7 1.1 copy-start.5
  97.8 51.1 %copy-start.4 = (bf16[8,6,128,128]{3,2,1,0:T(8,128)(2,1)S(1)}, bf16[8,6,128,128]{3,2,1,0:T(8,128)(2,1)}, u32[]{:S(2)}) copy-start(bf16[8,6,128,128]{3,2,1,0:T(8,128)(2,1)} %copy-done.3) | copy-start | bytes 4718596
  144.4 25.4 %all-to-all-start = ((bf16[8,3,128,128]{3,2,1,0:T(8,128)(2,1)}), bf16[8,3,128,128]{3,2,1,0:T(8,128)(2,1)S(1)}, u32[]{:S(2)}, u32[]{:S(2)}) async-start(bf16[8,3,128,128]{3,2,1,0:T(8,128)(2,1)} %get-tuple-element.62), calls=%async_computation | async-start | bytes 1572864 | tf_op jit(solution)/shard_map/all_to_all | solution.py:1757
  148.9 1.4 copy-start.6
  150.3 1.1 copy-start.8
  151.4 0.7 copy-start.9
  169.8 49.0 %all-to-all-start.2 = ((bf16[8,3,128,384]{3,2,1,0:T(8,128)(2,1)}), bf16[8,3,128,384]{3,2,1,0:T(8,128)(2,1)}, u32[]{:S(2)}, u32[]{:S(2)}) async-start(bf16[8,3,128,384]{3,2,1,0:T(8,128)(2,1)} %get-tuple-element.65), calls=%async_computation.2 | async-start | bytes 4718592 | tf_op jit(solution)/shard_map/all_to_all | solution.py:1757
  189.6 1.4 copy-start.7
  218.8 33.0 %all-to-all-start.1 = ((bf16[8,3,128,384]{3,2,1,0:T(8,128)(2,1)}), bf16[8,3,128,384]{3,2,1,0:T(8,128)(2,1)S(1)}, u32[]{:S(2)}, u32[]{:S(2)}) async-start(bf16[8,3,128,384]{3,2,1,0:T(8,128)(2,1)} %get-tuple-element.64), calls=%async_computation.1 | async-start | bytes 4718592 | tf_op jit(solution)/shard_map/all_to_all | solution.py:1757
  251.8 1.4 copy-start.10
  253.3 98.9 %copy-start.1 = (f32[32,12]{0,1:T(8,128)S(1)}, f32[32,12]{0,1:T(8,128)}, u32[]{:S(2)}) copy-start(f32[32,12]{0,1:T(8,128)} %param.20) | copy-start | bytes 4612

commit v5 on v4

--- a/solution.py
+++ b/solution.py
@@ -32,20 +32,24 @@
     return lax.dot_general(a, b, dims, preferred_element_type=F32)
 
 
-def fill_bias(strip, head, row, blocks):
-    base = KB * (blocks - 2)
-    width = KB * (2 * blocks - 1)
+STRIP = 5 * KB
+
+
+def strip_at(block, part):
+    return pl.ds(pl.multiple_of((jnp.clip(part - block, -2, 2) + 2) * KB, KB), KB)
+
+
+def fill_bias(strip, head, row):
     spread = jnp.broadcast_to(row, (128, NEAR))
     rolled = pltpu.roll(spread, 0, 1, stride=1, stride_axis=0)
     far_right = jnp.broadcast_to(row[:, NEAR - 1 :], (KB, 128))
     far_left = jnp.broadcast_to(row[:, 768:769], (KB, 128))
-    for start in range(0, base, 128):
+    for start in range(0, KB, 128):
         strip[head, :, start : start + 128] = far_right
-    strip[head, 0:128, base : base + 768] = rolled[:, :768]
-    strip[head, 128:256, base : base + 128] = far_right[:128]
-    strip[head, 128:256, base + 128 : base + 768] = rolled[:, :640]
-    for start in range(base + 768, width, 128):
-        strip[head, :, start : start + 128] = far_left
+        strip[head, :, KB + 768 + start : KB + 896 + start] = far_left
+    strip[head, 0:128, KB : KB + 768] = rolled[:, :768]
+    strip[head, 128:256, KB : KB + 128] = far_right[:128]
+    strip[head, 128:256, KB + 128 : KB + 768] = rolled[:, :640]
 
 
 def lanes_of(head, shape):
@@ -118,19 +122,18 @@
         fill_keys(ka, head, keys, valid)
         vt[head, 0:64] = turned[64 * head : 64 * head + 64]
         vt[head, 64:80] = filler
-        fill_bias(strip, head, row_ref[0, head : head + 1, :], blocks)
+        fill_bias(strip, head, row_ref[0, head : head + 1, :])
     peak[...] = jnp.full_like(peak, -1e30)
     acc[...] = jnp.zeros_like(acc)
 
     def step(block, unused):
         first = pl.multiple_of(block * KB, KB)
-        shift = pl.multiple_of((blocks - 1 - block) * KB, KB)
         alphas = [[], []]
         for part in range(blocks):
             for head in range(2):
                 here = slice(part * KB, part * KB + KB)
                 logits = dot(ka[head, pl.ds(first, KB), :], qa[head, here, :], NT)
-                logits = logits + strip[head, :, pl.ds(shift + part * KB, KB)]
+                logits = logits + strip[head, :, strip_at(block, part)]
                 before = peak[head, :, here]
                 after = jnp.maximum(before, jnp.max(logits, axis=0, keepdims=True))
                 probs[head, :, here] = jnp.exp(logits - after).astype(BF16)
@@ -166,7 +169,6 @@
     finish = move_rows(item, lengths_ref, layer_ref, moving[0], moved_ref, moving[1], False) if moves else lambda: None
     valid = item_length(lengths_ref, place_ref[0] + qkv_ref.shape[0] * (item + base_slot))
     tokens = blocks * KB
-    width = KB * (2 * blocks - 1)
     local = qkv_ref.shape[2]
     joined = qkv_ref[:, 0].reshape(tokens, 384)
     queries = joined[:, 0:128]
@@ -190,20 +192,19 @@
         fill_keys(ka, head, keys, valid)
         va[head] = jnp.where(own, values, jnp.where((spare == 0) | (spare == 1), 1.0, 0.0).astype(BF16))
         ga[head] = jnp.where(own, grads, jnp.where(spare == 0, shift_high, jnp.where(spare == 1, shift_low, jnp.zeros_like(shift_low))))
-        fill_bias(strip, head, row_ref[0, head : head + 1, :], blocks)
+        fill_bias(strip, head, row_ref[0, head : head + 1, :])
     tally[...] = jnp.zeros_like(tally)
     dq[...] = jnp.zeros_like(dq)
     dqkv_ref[...] = jnp.zeros_like(dqkv_ref)
 
     def step(block, unused):
         first = pl.multiple_of(block * KB, KB)
-        shift = pl.multiple_of((blocks - 1 - block) * KB, KB)
         key_parts = []
         value_parts = []
         for part in range(blocks):
             for head in range(2):
                 here = slice(part * KB, part * KB + KB)
-                there = pl.ds(shift + part * KB, KB)
+                there = strip_at(block, part)
                 logits = dot(ka[head, pl.ds(first, KB), :], qa[head, here, :], NT)
                 weights = jnp.exp(logits + strip[head, :, there])
                 change = dot(va[head, pl.ds(first, KB), :], ga[head, here, :], NT)
@@ -224,16 +225,14 @@
 
     lax.fori_loop(0, (valid + KB - 1) // KB, step, 0)
     dqkv_ref[:, 0, :, 0:128] = dq[...].T.astype(BF16).reshape(dqkv_ref.shape[0], local, 128)
-    base = KB * (blocks - 2)
     lane = lax.broadcasted_iota(jnp.int32, (1, NEAR), 1)
     flip = jnp.where(row_at + lane_at == 127, 1.0, 0.0).astype(BF16)
     for head in range(2):
-        far_right = sum(tally[head, :, start : start + 128] for start in range(0, base, 128)) if base else jnp.zeros((KB, 128), F32)
-        far_right = far_right[:128] + far_right[128:] + tally[head, 128:256, base : base + 128]
-        left_list = [tally[head, :, start : start + 128] for start in range(base + 768, width, 128)]
-        far_left = sum(left_list) if left_list else jnp.zeros((KB, 128), F32)
-        near = tally[head, 0:128, base : base + 768]
-        near_low = tally[head, 128:256, base + 128 : base + 768]
+        far_right = tally[head, :, 0:128] + tally[head, :, 128:256]
+        far_right = far_right[:128] + far_right[128:] + tally[head, 128:256, KB : KB + 128]
+        far_left = tally[head, :, KB + 768 : KB + 896] + tally[head, :, KB + 896 : STRIP]
+        near = tally[head, 0:128, KB : KB + 768]
+        near_low = tally[head, 128:256, KB + 128 : KB + 768]
         near = near + jnp.concatenate([near_low, jnp.zeros((128, 128), F32)], axis=1)
         near = jnp.concatenate([near, jnp.zeros((128, NEAR - 768), F32)], axis=1)
         near_high = near.astype(BF16)
@@ -249,7 +248,6 @@
     sources, items, local, unused = qkv.shape
     blocks = sources * local // KB
     tokens = sources * local
-    width = KB * (2 * blocks - 1)
     spec = pltpu.PrefetchScalarGridSpec(
         num_scalar_prefetch=2,
         grid=(items,),
@@ -267,7 +265,7 @@
             pltpu.VMEM((2, tokens, 128), BF16),
             pltpu.VMEM((2, tokens, 128), BF16),
             pltpu.VMEM((2, 80, tokens), BF16),
-            pltpu.VMEM((2, KB, width), F32),
+            pltpu.VMEM((2, KB, STRIP), F32),
             pltpu.VMEM((2, 1, tokens), F32),
             pltpu.VMEM((2, 80, tokens), F32),
             pltpu.VMEM((2, KB, tokens), BF16),
@@ -283,7 +281,7 @@
             jax.ShapeDtypeStruct((items, tokens, 128), BF16),
             jax.ShapeDtypeStruct(cot.shape, cot.dtype),
         ],
-        compiler_params=pltpu.CompilerParams(vmem_limit_bytes=50 * 2**20),
+        compiler_params=pltpu.CompilerParams(vmem_limit_bytes=60 * 2**20),
         cost_estimate=pl.CostEstimate(flops=items * tokens * tokens * 512, bytes_accessed=items * tokens * 2048, transcendentals=items * tokens * tokens * 2),
         name="attention_forward",
     )(lengths, place, qkv, rows, cot)
@@ -296,7 +294,6 @@
     moved = layer if moves else jnp.zeros((8, 128), F32)
     blocks = sources * local // KB
     tokens = sources * local
-    width = KB * (2 * blocks - 1)
     big = lambda lanes: pl.BlockSpec((sources, 1, local, lanes), lambda i, l, p: (0, i + first, 0, 0))
     spec = pltpu.PrefetchScalarGridSpec(
         num_scalar_prefetch=2,
@@ -321,8 +318,8 @@
             pltpu.VMEM((2, tokens, 128), BF16),
             pltpu.VMEM((2, tokens, 128), BF16),
             pltpu.VMEM((128, tokens), BF16),
-            pltpu.VMEM((2, KB, width), F32),
-            pltpu.VMEM((2, KB, width), F32),
+            pltpu.VMEM((2, KB, STRIP), F32),
+            pltpu.VMEM((2, KB, STRIP), F32),
             pltpu.VMEM((2, KB, tokens), BF16),
             pltpu.VMEM((2, KB, tokens), BF16),
             pltpu.VMEM((128, tokens), F32),
@@ -337,7 +334,7 @@
             jax.ShapeDtypeStruct((items, 2, NEAR), F32),
             jax.ShapeDtypeStruct(moved.shape, moved.dtype),
         ],
-        compiler_params=pltpu.CompilerParams(vmem_limit_bytes=50 * 2**20),
+        compiler_params=pltpu.CompilerParams(vmem_limit_bytes=60 * 2**20),
         cost_estimate=pl.CostEstimate(flops=items * tokens * tokens * 1280, bytes_accessed=items * tokens * 4096, transcendentals=items * tokens * tokens * 2),
         name="attention_backward",
     )(lengths, place, qkv, outs, aug, grads, rows, layer, after)
@@ -924,10 +921,6 @@
             reduce.begin()
             reduce.late()
 
-        @pl.when(step == 1)
-        def _():
-            reduce.in_two()
-
         @pl.when(step == 2)
         def _():
             reduce.late_one()
@@ -968,6 +961,16 @@
     row16 = lax.broadcasted_iota(jnp.int32, (16, width), 0)
     slopes = []
     for one in range(together):
+        if custom and one == 1:
+
+            @pl.when(step == 1)
+            def _():
+                reduce.in_two()
+
+            @pl.when(last)
+            def _():
+                reduce.late_two()
+
         own = slice(one * local_tokens, (one + 1) * local_tokens)
         high, low = high_all[own], low_all[own]
         conv = conv_ref[one]
@@ -998,7 +1001,7 @@
     @pl.when(last)
     def _():
         if custom:
-            reduce.late_two()
+            reduce.late_three()
         table_grad = jnp.zeros((SMALL_ROWS, model), F32)
         table = table_ref[...].astype(F32)
         place = lax.broadcasted_iota(jnp.int32, (SMALL_ROWS, model), 0)
@@ -1025,17 +1028,14 @@
         small.one_start()
         small.one_middle()
         if custom:
-            reduce.late_three()
+            reduce.finish_rest(down_out)
         small.one_finish()
-        if custom:
-            reduce.finish_rest(down_out)
+        small.two_finish()
+        small.three_finish()
+        small.three_more()
         if custom:
             reduce.finish_in(in_out, weight_out)
-        small.two_finish()
-        if custom:
             reduce.finish_late(qkv_out)
-        small.three_finish()
-        small.three_more()
         small.four_finish()
 
 
@@ -1050,7 +1050,7 @@
     one_out[...] = block[264, :]
     score_out[...] = block[265, :]
     two_out[...] = block[266, :]
-    bias_out[...] = block[272:288, 0:128].T[0:32, 0:12]
+    bias_out[...] = block[272:284, 0:32]
 
 
 def call_finish(block, sums):
@@ -1058,13 +1058,13 @@
     shape = lambda *dims: jax.ShapeDtypeStruct(dims, F32)
     return pl.pallas_call(
         finish_kernel,
-        out_shape=[shape(*x.shape) for x in sums] + [shape(259, model), shape(5, model), shape(model), shape(model), shape(model), shape(32, 12)],
+        out_shape=[shape(*x.shape) for x in sums] + [shape(259, model), shape(5, model), shape(model), shape(model), shape(model), shape(12, 32)],
         compiler_params=pltpu.CompilerParams(vmem_limit_bytes=VMEM_LIMIT),
         name="finish",
     )(block, *sums)
 
 
-VMEM_LIMIT = 58 * 2**20
+VMEM_LIMIT = 60 * 2**20
 TOGETHER = 2
 
 
@@ -1202,7 +1202,7 @@
     specs = []
     if custom:
         specs = [whole(*x.shape) for x in extra]
-        sums = [(96, 576), (96, 1024), (256, 192), (96, 192)]
+        sums = [(96, 576), (96, 1024), (192, 256), (96, 192)]
         out_specs = out_specs + [whole(*shape) for shape in sums]
         out_shape = out_shape + [jax.ShapeDtypeStruct(shape, F32) for shape in sums]
         scratch = weight_scratch(model, sequences * local_tokens)
@@ -1556,8 +1556,8 @@
         for offset in (1, 2, 3):
             self.rest_chip(offset).wait()
             total = total + self.rest_chips[offset - 1].astype(F32)
-        down_out[0:128, :] = total[0:192].T
-        down_out[128:256, :] = total[192:384].T
+        down_out[:, 0:128] = total[0:192]
+        down_out[:, 128:256] = total[192:384]
 
     def finish_in(self, in_out, weight_out):
         total = self.in_sum[self.plane].astype(F32)
@@ -1789,6 +1789,7 @@
     )
     if custom:
         summed_qkv, summed_in, summed_down, summed_out, *smalls = call_finish(results[0], results[1:])
+        summed_down = summed_down.T
     else:
         smalls = call_finish(results[0], ())
         grad_qkv = jnp.einsum("btd,bte->de", normed, results[1], preferred_element_type=F32).astype(BF16)
@@ -1802,7 +1803,7 @@
         grad_score,
         grad_gain_one,
         summed_qkv,
-        grad_bias,
+        grad_bias.T,
         summed_out,
         grad_gain_two,
         summed_in,

time: 350 us -> 343 us (0.980)
  local copies, waits for them, and re-layouts: 13.6 us -> 5.01 us
    unnamed x24 -> x12, local copies, waits for them, and re-layouts: 11.5 us -> 2.28 us
    pallas_call x1, Pallas kernels: 93 us -> 89.3 us  [call_back(): pl.pallas_call(functools.partial(back_kernel, (local_tokens, window, devi...]
where the time goes in v5:
time: 343 us; the launch traced here: 344 us
  Pallas kernels  300 us (87%)
  starting transfers between devices  27.8 us (8%)
  waiting for transfers between devices  6.13 us (2%)
  local copies, waits for them, and re-layouts  5.01 us (1%)
    pallas_call x1, Pallas kernels, call_back(): pl.pallas_call(functools.partial(back_kernel, (local_tokens, window, devi...  89.3 us
    pallas_call x1, Pallas kernels, call_front(): pl.pallas_call(functools.partial(front_kernel, (local_tokens, window, dev...  64.7 us
    pallas_call x1, Pallas kernels, call_mid(): pl.pallas_call(functools.partial(mid_kernel, (local_tokens, devices, sequ...  48.4 us
    pallas_call x2, Pallas kernels, attention_backward(): pl.pallas_call(functools.partial(bwd_kernel, blocks, first, moves), grid_...  43.2 us
    all_to_all x3, starting transfers between devices, exchange(): return lax.all_to_all(items, 'seq', split_axis=0, concat_axis=0, tiled=True)  27.8 us
    pallas_call x1, Pallas kernels, attention_forward(): pl.pallas_call(functools.partial(fwd_kernel, blocks), grid_spec=spec, out...  26.9 us
    pallas_call x1, Pallas kernels, call_early(): pl.pallas_call(early_kernel, grid=(8,), in_specs=[pl.BlockSpec((sequences...  25.1 us
  transfers between devices with their start and end apart: 3, of which 2 were waited for; matrix products, arithmetic and copies ran while one was open for 0% of the time, Pallas kernels for 20%

profile of v5, /device:TPU:0, one launch (start us, length us, event | category | flops | bytes accessed | tf_op | source)
XLA Modules:
  0.0 343.7 jit_solution(10306678229989369927)
XLA Ops:
  0.6 0.0 copy-start
  0.7 0.7 broadcast_in_dim.15
  1.4 0.7 broadcast_in_dim.14
  2.1 0.7 broadcast_in_dim.6
  2.8 0.0 copy-done
  2.8 0.4 convolution_bitcast_fusion
  3.2 0.7 reshape.65.row_ref
  3.9 1.4 pad_maximum_fusion.1.vectors_ref
  5.2 64.7 %front.1 = (f32[8,128,768]{2,1,0:T(8,128)}, bf16[8,128,768]{2,1,0:T(8,128)(2,1)}, bf16[8,384,768]{2,1,0:T(8,128)(2,1)}, bf16[8,128,384]{2,1,0:T(8,128)(2,1)}, f3...) custom-call(s32[8]{0:T(128)} %lengths_ref.7, s32[8,256]{1,0:T(8,128)} %ids_ref.1, ...), custom_call_target="tpu_custom_call" | custom-call | flops 49999998976 | bytes 20000000 | tf_op jit(solution)/shard_map/front/pallas_call | solution.py:1099
  69.9 26.9 %attention_forward.1 = (bf16[8,6,128,128]{3,2,1,0:T(8,128)(2,1)}, bf16[6,1024,128]{2,1,0:T(8,128)(2,1)}, bf16[8,128,768]{2,1,0:T(8,128)(2,1)}) custom-call(s32[8]{0:T(128)} %lengths_ref.7, s32[1]{0:T(128)} %bitcast.place_ref, bf16[8,6,128,384]{3,2,1,0:T(8,128)(2,1)} %get-tuple-element.53.qkv_ref, f32[6,2,1024]{2,1,0:T(2,128)} %reshape.65.row_ref, ...), custom_call_target="tpu_custom_call" | custom-call | flops 3221225472 | bytes 12582912 | tf_op jit(solution)/shard_map/attention_forward/pallas_call | solution.py:276
  96.8 48.4 %middle.1 = (f32[8,128,768]{2,1,0:T(8,128)}, bf16[8,128,2048]{2,1,0:T(8,128)(2,1)}, bf16[8,128,4096]{2,1,0:T(8,128)(2,1)}, bf16[8,128,768]{2,1,0:T(8,128)(2,1)},...) custom-call(bf16[8,6,128,128]{3,2,1,0:T(8,128)(2,1)} %get-tuple-elem, ...), custom_call_target="tpu_custom_call" | custom-call | flops 49999998976 | bytes 40000000 | tf_op jit(solution)/shard_map/middle/pallas_call | solution.py:1148
  145.2 4.5 %all-to-all-start = ((bf16[8,3,128,128]{3,2,1,0:T(8,128)(2,1)}), bf16[8,3,128,128]{3,2,1,0:T(8,128)(2,1)S(1)}, u32[]{:S(2)}, u32[]{:S(2)}) async-start(bf16[8,3,128,128]{3,2,1,0:T(8,128)(2,1)} %get-tuple-element.62), calls=%async_computation | async-start | bytes 1572864 | tf_op jit(solution)/shard_map/all_to_all | solution.py:1757
  149.7 17.5 %attention_backward.2 = (bf16[8,3,128,384]{3,2,1,0:T(8,128)(2,1)}, f32[3,2,1024]{2,1,0:T(2,128)}, f32[8,128,768]{2,1,0:T(8,128)}) custom-call(s32[8]{0:T(128)} %lengths_ref.7, s32[1]{0:T(128)} %bitcast.place_ref, bf16[8,6,128,384]{3,2,1,0:T(8,128)(2,1)} %get-tuple-element.53.qkv_ref, bf16[8,6,128,128]{3,2,1,0:T(8,128)(2,1)} %get-tuple-element.54.att_ref.out_ref, ...), custom_call_target="tpu_custom_call" | custom-call | flops 4026531840 | bytes 12582912 | tf_op jit(solution)/shard_map/attention_backward/pallas_call | solution.py:329
  167.2 0.0 all-to-all-done.grad_ref
  167.2 0.0 copy-start.3
  167.2 0.9 copy-done.3
  168.1 19.0 %all-to-all-start.2 = ((bf16[8,3,128,384]{3,2,1,0:T(8,128)(2,1)}), bf16[8,3,128,384]{3,2,1,0:T(8,128)(2,1)S(1)}, u32[]{:S(2)}, u32[]{:S(2)}) async-start(bf16[8,3,128,384]{3,2,1,0:T(8,128)(2,1)} %get-tuple-element.65), calls=%async_computation.2 | async-start | bytes 4718592 | tf_op jit(solution)/shard_map/all_to_all | solution.py:1757
  187.1 25.8 %attention_backward.3 = (bf16[8,3,128,384]{3,2,1,0:T(8,128)(2,1)}, f32[3,2,1024]{2,1,0:T(2,128)}, f32[8,128]{1,0:T(8,128)}) custom-call(s32[8]{0:T(128)} %lengths_ref.7, s32[1]{0:T(128)} %bitcast.place_ref, bf16[8,6,128,384]{3,2,1,0:T(8,128)(2,1)} %get-tuple-element.53.qkv_ref, bf16[8,6,128,128]{3,2,1,0:T(8,128)(2,1)} %get-tuple-element.54.att_ref.out_ref, ...), custom_call_target="tpu_custom_call" | custom-call | flops 4026531840 | bytes 12582912 | tf_op jit(solution)/shard_map/attention_backward/pallas_call | solution.py:329
  212.8 3.4 all-to-all-done.2.after.two_ref
  216.2 0.0 copy-start.2
  216.2 1.4 copy-done.2
  217.6 4.4 %all-to-all-start.1 = ((bf16[8,3,128,384]{3,2,1,0:T(8,128)(2,1)}), bf16[8,3,128,384]{3,2,1,0:T(8,128)(2,1)}, u32[]{:S(2)}, u32[]{:S(2)}) async-start(bf16[8,3,128,384]{3,2,1,0:T(8,128)(2,1)} %get-tuple-element.64), calls=%async_computation.1 | async-start | bytes 4718592 | tf_op jit(solution)/shard_map/all_to_all | solution.py:1757
  222.0 0.2 iota_compare_fusion
  222.2 0.8 convert_convert_fusion.bias_hot_ref
  222.9 0.0 copy-done.4
  222.9 0.0 copy-done.5
  222.9 0.6 pad_maximum_fusion.bias_ref
  223.6 25.1 %early_gradients.1 = (bf16[4,4,960,128]{3,2,1,0:T(8,128)(2,1)}, bf16[4,4,384,128]{3,2,1,0:T(8,128)(2,1)}) custom-call(bf16[8,128,2048]{2,1,0:T(8,128)(2,1)} %get-tuple-element.73.act_ref, bf16[8,128,768]{2,1,0:T(8,128)(2,1)} %get-tuple-element.57.cot_ref, bf16[8,128,768]{2,1,0:T(8,128)(2,1)} %get-tuple-element.74.normed_ref, ...), custom_call_target="tpu_custom_call" | custom-call | flops 11000000512 | bytes 30000000 | tf_op jit(solution)/shard_map/early_gradients/pallas_call | solution.py:1359
  248.7 2.8 all-to-all-done.1.one_ref
  251.4 89.3 %back.1 = (f32[288,768]{1,0:T(8,128)}, f32[96,576]{1,0:T(8,128)}, f32[96,1024]{1,0:T(8,128)}, f32[192,256]{1,0:T(8,128)}, f32[96,192]{1,0:T(8,128)}) custom-call(bf16[8,3,128,384]{3,2,1,0:T(8,128)(2,1)} %all-to-all-done.1.one_ref, bf16[8,3,128,384]{3,2,1,0:T(8,128)(2,1)} %copy-done.2, f32[8,128,768]{2,1,0:T(8,128)} %get-tuple-element.56.hidden_ref, ...), custom_call_target="tpu_custom_call" | custom-call | flops 99999997952 | bytes 20000000 | tf_op jit(solution)/shard_map/back/pallas_call | solution.py:1212
  340.7 2.7 finish.1
  343.5 0.0 copy-done.1
  (4 shorter events, 0.0 us)
Async XLA Ops:
  0.6 2.1 copy-start
  145.2 21.9 %all-to-all-start = ((bf16[8,3,128,128]{3,2,1,0:T(8,128)(2,1)}), bf16[8,3,128,128]{3,2,1,0:T(8,128)(2,1)S(1)}, u32[]{:S(2)}, u32[]{:S(2)}) async-start(bf16[8,3,128,128]{3,2,1,0:T(8,128)(2,1)} %get-tuple-element.62), calls=%async_computation | async-start | bytes 1572864 | tf_op jit(solution)/shard_map/all_to_all | solution.py:1757
  167.2 0.9 copy-start.3
  168.1 48.1 %all-to-all-start.2 = ((bf16[8,3,128,384]{3,2,1,0:T(8,128)(2,1)}), bf16[8,3,128,384]{3,2,1,0:T(8,128)(2,1)S(1)}, u32[]{:S(2)}, u32[]{:S(2)}) async-start(bf16[8,3,128,384]{3,2,1,0:T(8,128)(2,1)} %get-tuple-element.65), calls=%async_computation.2 | async-start | bytes 4718592 | tf_op jit(solution)/shard_map/all_to_all | solution.py:1757
  216.2 1.4 copy-start.2
  216.2 6.7 %copy-start.4 = (f32[3,2,1024]{2,1,0:T(2,128)S(1)}, f32[3,2,1024]{2,1,0:T(2,128)}, u32[]{:S(2)}) copy-start(f32[3,2,1024]{2,1,0:T(2,128)} %get-tuple-element.63.layer_ref.after) | copy-start | bytes 73732
  216.2 6.7 %copy-start.5 = (f32[3,2,1024]{2,1,0:T(2,128)S(1)}, f32[3,2,1024]{2,1,0:T(2,128)}, u32[]{:S(2)}) copy-start(f32[3,2,1024]{2,1,0:T(2,128)} %get-tuple-element.71) | copy-start | bytes 73732
  217.6 33.8 %all-to-all-start.1 = ((bf16[8,3,128,384]{3,2,1,0:T(8,128)(2,1)}), bf16[8,3,128,384]{3,2,1,0:T(8,128)(2,1)}, u32[]{:S(2)}, u32[]{:S(2)}) async-start(bf16[8,3,128,384]{3,2,1,0:T(8,128)(2,1)} %get-tuple-element.64), calls=%async_computation.1 | async-start | bytes 4718592 | tf_op jit(solution)/shard_map/all_to_all | solution.py:1757
  251.4 92.1 %copy-start.1 = (f32[32,12]{0,1:T(8,128)S(1)}, f32[32,12]{0,1:T(8,128)}, u32[]{:S(2)}) copy-start(f32[32,12]{0,1:T(8,128)} %param.20) | copy-start | bytes 4612

commit v6 on v5

--- a/solution.py
+++ b/solution.py
@@ -506,9 +506,9 @@
 
 
 def front_kernel(
-    sizes, lengths_ref, ids_ref, table_ref, weight_ref, vectors_ref,
+    sizes, lengths_ref, ids_ref, table_ref, weight_source, vectors_ref,
     hidden_ref, normed_ref, conv_ref, mix_ref, share_ref, rows_ref, items_ref,
-    masks, wide, permuted, stage, taps, from_left, from_right, extended, side_sems, *sems,
+    masks, wide, permuted, stage, taps, from_left, from_right, extended, side_sems, weight_ref, weight_sem, *sems,
 ):
     local_tokens, window, devices, total = sizes
     step = pl.program_id(0)
@@ -516,15 +516,17 @@
 
     @pl.when(step == 0)
     def _():
+        pltpu.make_async_copy(weight_source, weight_ref, weight_sem).start()
         from_left[...] = jnp.zeros_like(from_left)
         from_right[...] = jnp.zeros_like(from_right)
         greet("seq", me, devices)
         block_masks(masks, me * 2 * local_tokens, devices * 2 * local_tokens)
-        permute_weight(weight_ref, permuted)
         table = table_ref[...].astype(F32)
         taps[...] = jnp.zeros_like(taps)
         for tap in range(5):
             taps[tap, 0 : table.shape[0], :] = (vectors_ref[tap : tap + 1, :] * table).astype(BF16)
+        pltpu.make_async_copy(weight_source, weight_ref, weight_sem).wait()
+        permute_weight(weight_ref, permuted)
         pl.semaphore_wait(pltpu.get_barrier_semaphore(), devices - 1)
         spread_ids(lengths_ref, ids_ref, from_left, from_right, extended, side_sems, me, devices)
 
@@ -750,9 +752,9 @@
 
 
 def mid_kernel(
-    sizes, att_ref, hidden_ref, cot_ref, out_weight_ref, in_weight_ref, down_ref, vectors_ref,
+    sizes, att_ref, hidden_ref, cot_ref, out_weight_ref, in_source, down_ref, vectors_ref,
     layer_ref, act_ref, gate_up_ref, normed_ref, attended_ref, branch_ref, residual_ref, items_ref, gain_out, rest_ref,
-    arrived, stage, keep_gain, grad_act, *sems,
+    arrived, stage, keep_gain, grad_act, in_weight_ref, in_sem, *sems,
 ):
     local_tokens, devices, total = sizes
     in_sems, out_sems = sems[:3], sems[3:]
@@ -762,6 +764,7 @@
     @pl.when(step == 0)
     def _():
         greet("seq", me, devices)
+        pltpu.make_async_copy(in_source, in_weight_ref, in_sem).start()
         keep_gain[...] = jnp.zeros_like(keep_gain)
         pl.semaphore_wait(pltpu.get_barrier_semaphore(), devices - 1)
 
@@ -783,6 +786,7 @@
         every = cot_ref[...].reshape(grad_act.shape[0], model)
         for first in range(0, down_ref.shape[0], 512):
             grad_act[:, first : first + 512] = dot(every, down_ref[first : first + 512, :], NT)
+        pltpu.make_async_copy(in_source, in_weight_ref, in_sem).wait()
 
     if devices == 8:
         for number in range(4):
@@ -876,7 +880,7 @@
 
 
 def back_kernel(
-    sizes, custom, one_ref, two_ref, hidden_ref, residual_ref, conv_ref, mix_ref, share_ref, ids_ref, weight_ref,
+    sizes, custom, one_ref, two_ref, hidden_ref, residual_ref, conv_ref, mix_ref, share_ref, ids_ref, weight_source,
     table_ref, vectors_ref, bias_ref, bias_hot_ref, gain_two_ref, *refs,
 ):
     local_tokens, window, devices = sizes
@@ -891,13 +895,14 @@
         refs = refs[8:]
     else:
         block, flat_out, refs = refs[0], refs[1], refs[2:]
-    masks, permuted, tap_sums, keep_gain, keep_score = refs[:5]
-    refs = refs[5:]
-    small = SmallSums(block, refs[:5], refs[5:13])
-    refs = refs[13:]
+    masks, permuted, tap_sums, keep_gain, keep_score, weight_ref, weight_sem = refs[:7]
+    refs = refs[7:]
+    small = SmallSums(block, refs[:4], refs[4:10])
+    refs = refs[10:]
 
     @pl.when(step == 0)
     def _():
+        pltpu.make_async_copy(weight_source, weight_ref, weight_sem).start()
         greet("seq", me, devices)
         greet("dp", plane, small.along)
         keep_gain[...] = jnp.zeros_like(keep_gain)
@@ -933,6 +938,7 @@
     @pl.when(step == 0)
     def _():
         block_masks(masks, me * 2 * local_tokens, devices * 2 * local_tokens)
+        pltpu.make_async_copy(weight_source, weight_ref, weight_sem).wait()
         permute_weight(weight_ref, permuted)
 
     together = hidden_ref.shape[0]
@@ -1000,8 +1006,6 @@
 
     @pl.when(last)
     def _():
-        if custom:
-            reduce.late_three()
         table_grad = jnp.zeros((SMALL_ROWS, model), F32)
         table = table_ref[...].astype(F32)
         place = lax.broadcasted_iota(jnp.int32, (SMALL_ROWS, model), 0)
@@ -1027,12 +1031,12 @@
         small.pack()
         small.one_start()
         small.one_middle()
+        small.one_finish()
         if custom:
+            reduce.late_three()
             reduce.finish_rest(down_out)
-        small.one_finish()
         small.two_finish()
         small.three_finish()
-        small.three_more()
         if custom:
             reduce.finish_in(in_out, weight_out)
             reduce.finish_late(qkv_out)
@@ -1099,7 +1103,7 @@
     return pl.pallas_call(
         functools.partial(front_kernel, (local_tokens, window, devices, sequences * PAIRS)),
         grid=(sequences,),
-        in_specs=[pl.BlockSpec(memory_space=pltpu.SMEM), whole(*ids.shape), whole(*table.shape), whole(*weight.shape), whole(*vectors.shape)],
+        in_specs=[pl.BlockSpec(memory_space=pltpu.SMEM), whole(*ids.shape), whole(*table.shape), ANYWHERE, whole(*vectors.shape)],
         out_specs=[
             part(1, local_tokens, model),
             part(1, local_tokens, model),
@@ -1119,6 +1123,8 @@
             pltpu.VMEM((sequences, 128), jnp.int32),
             pltpu.VMEM((sequences, local_bytes + 256), F32),
             pltpu.SemaphoreType.DMA((4,)),
+            pltpu.VMEM(weight.shape, BF16),
+            pltpu.SemaphoreType.DMA,
         ]
         + item_sems(devices, per_device),
         out_shape=[
@@ -1153,7 +1159,7 @@
             rows(model),
             whole(*cot.shape),
             whole(*out_weight.shape),
-            whole(*in_weight.shape),
+            ANYWHERE,
             whole(*down_weight.shape),
             whole(*vectors.shape),
         ],
@@ -1169,7 +1175,10 @@
             whole(1, model),
             whole(*rest),
         ],
-        scratch_shapes=[pltpu.VMEM(att.shape, BF16), pltpu.VMEM(att.shape, BF16), pltpu.VMEM((8, model), F32), pltpu.VMEM((sequences * local_tokens, hidden_units), F32)]
+        scratch_shapes=[pltpu.VMEM(att.shape, BF16), pltpu.VMEM(att.shape, BF16), pltpu.VMEM((8, model), F32), pltpu.VMEM((sequences * local_tokens, hidden_units), F32),
+            pltpu.VMEM(in_weight.shape, BF16),
+            pltpu.SemaphoreType.DMA,
+        ]
         + item_sems(devices, per_device)
         + item_sems(devices, per_device),
         out_shape=[
@@ -1221,7 +1230,7 @@
             part(TOGETHER, local_tokens, width),
             part(TOGETHER, local_tokens, 128),
             part(TOGETHER, 8, ids.shape[2]),
-            whole(*weight.shape),
+            ANYWHERE,
             whole(*table.shape),
             whole(*vectors.shape),
             whole(*bias_rows.shape),
@@ -1236,6 +1245,8 @@
             pltpu.VMEM((5, SMALL_ROWS, model), F32),
             pltpu.VMEM((8, model), F32),
             pltpu.VMEM((16, model), F32),
+            pltpu.VMEM(weight.shape, BF16),
+            pltpu.SemaphoreType.DMA,
         ]
         + small_scratch(devices, along)
         + scratch,
@@ -1607,7 +1618,7 @@
 class SmallSums:
     def __init__(self, block, buffers, sems):
         self.block = block
-        self.held, self.got_seq, self.planes, self.got_dp, self.whole = buffers
+        self.held, self.got_seq, self.planes, self.whole = buffers
         self.sems = sems
         self.me, self.plane = lax.axis_index("seq"), lax.axis_index("dp")
         self.across, self.along = self.held.shape[0], self.held.shape[1]
@@ -1678,31 +1689,25 @@
         total = self.held[self.mine if self.paired else self.me].astype(F32)
         for slot in range(3 if self.paired else self.across - 1):
             total = total + self.got_seq[slot].astype(F32)
-        self.planes[...] = total.astype(BF16)
-        self.waiting = self.copies("dp", lambda peer: self.planes.at[peer], lambda slot: self.got_dp.at[slot], 1)
+        self.planes[self.plane] = total.astype(BF16)
+        self.waiting = self.copies("dp", lambda peer: self.planes.at[self.plane], lambda slot: self.planes.at[self.plane], 1)
 
     def two_finish(self):
         for copy in self.waiting:
             copy.wait()
-        mine = self.planes[self.plane].astype(F32)
-        for slot in range(self.along - 1):
-            mine = mine + self.got_dp[slot].astype(F32)
+        total = self.planes[0].astype(F32)
+        for plane in range(1, self.along):
+            total = total + self.planes[plane].astype(F32)
         own = self.mine if self.paired else self.me
-        self.whole[own, self.plane] = mine.astype(BF16)
-        self.waiting = self.copies("dp", lambda peer: self.whole.at[own, self.plane], lambda slot: self.whole.at[own, self.plane], 2)
+        self.whole[own] = total.astype(BF16)
+        self.waiting = self.copies("chip" if self.paired else "seq", lambda peer: self.whole.at[own], lambda slot: self.whole.at[own], 2)
 
     def three_finish(self):
-        for copy in self.waiting:
-            copy.wait()
-        own = self.mine if self.paired else self.me
-        self.waiting = self.copies("chip" if self.paired else "seq", lambda peer: self.whole.at[own], lambda slot: self.whole.at[own], 3)
-
-    def three_more(self):
         if self.paired:
             for copy in self.waiting:
                 copy.wait()
             half = pl.ds(4 * self.core, 4)
-            self.waiting = self.sibling(self.whole.at[half], self.whole.at[half], 3)
+            self.waiting = self.sibling(self.whole.at[half], self.whole.at[half], 2)
 
     def four_finish(self):
         for copy in self.waiting:
@@ -1718,11 +1723,9 @@
     return [
         pltpu.VMEM((across, along, chunk, 128), BF16),
         pltpu.VMEM((across - 1, along, chunk, 128), BF16),
-        pltpu.VMEM((along, chunk, 128), BF16),
-        pltpu.VMEM((along - 1, chunk, 128), BF16),
+        pltpu.VMEM((along, along, chunk, 128), BF16),
         pltpu.VMEM((across, along, chunk, 128), BF16),
-        dma(across - 1), dma(across - 1), dma(along - 1), dma(along - 1),
-        dma(along - 1), dma(along - 1), dma(across - 1), dma(across - 1),
+        dma(across - 1), dma(across - 1), dma(along - 1), dma(along - 1), dma(across - 1), dma(across - 1),
     ]
 
 

time: 343 us -> 338 us (0.985)
    pallas_call x1, Pallas kernels: 89.3 us -> 93.5 us  [call_back(): pl.pallas_call(functools.partial(back_kernel, (local_tokens, window, devi...]
  transfers between devices with their start and end apart: 3 -> 3, of which waited for: 2 -> 2; matrix products, arithmetic and copies ran while one was open for 0% -> 0% of each run, Pallas kernels for 20% -> 19%
where the time goes in v6:
time: 338 us; the launch traced here: 340 us
  Pallas kernels  297 us (88%)
  starting transfers between devices  27.7 us (8%)
  waiting for transfers between devices  6.13 us (2%)
  local copies, waits for them, and re-layouts  5.01 us (1%)
    pallas_call x1, Pallas kernels, call_back(): pl.pallas_call(functools.partial(back_kernel, (local_tokens, window, devi...  93.5 us
    pallas_call x1, Pallas kernels, call_front(): pl.pallas_call(functools.partial(front_kernel, (local_tokens, window, dev...  64.1 us
    pallas_call x1, Pallas kernels, call_mid(): pl.pallas_call(functools.partial(mid_kernel, (local_tokens, devices, sequ...  46.1 us
    pallas_call x2, Pallas kernels, attention_backward(): pl.pallas_call(functools.partial(bwd_kernel, blocks, first, moves), grid_...  40.3 us
    all_to_all x3, starting transfers between devices, exchange(): return lax.all_to_all(items, 'seq', split_axis=0, concat_axis=0, tiled=True)  27.7 us
    pallas_call x1, Pallas kernels, call_early(): pl.pallas_call(early_kernel, grid=(8,), in_specs=[pl.BlockSpec((sequences...  25.1 us
    pallas_call x1, Pallas kernels, attention_forward(): pl.pallas_call(functools.partial(fwd_kernel, blocks), grid_spec=spec, out...  25 us
  transfers between devices with their start and end apart: 3, of which 2 were waited for; matrix products, arithmetic and copies ran while one was open for 0% of the time, Pallas kernels for 19%

profile of v6, /device:TPU:0, one launch (start us, length us, event | category | flops | bytes accessed | tf_op | source)
XLA Modules:
  0.0 340.0 jit_solution(382676541080014258)
XLA Ops:
  0.6 0.0 copy-start
  0.7 0.7 broadcast_in_dim.15
  1.4 0.7 broadcast_in_dim.14
  2.1 0.7 broadcast_in_dim.6
  2.8 0.0 copy-done
  2.8 0.4 convolution_bitcast_fusion
  3.2 0.7 reshape.65.row_ref
  3.9 1.4 pad_maximum_fusion.1.vectors_ref
  5.2 64.1 %front.1 = (f32[8,128,768]{2,1,0:T(8,128)}, bf16[8,128,768]{2,1,0:T(8,128)(2,1)}, bf16[8,384,768]{2,1,0:T(8,128)(2,1)}, bf16[8,128,384]{2,1,0:T(8,128)(2,1)}, f3...) custom-call(s32[8]{0:T(128)} %lengths_ref.7, s32[8,256]{1,0:T(8,128)} %ids_ref.1, ...), custom_call_target="tpu_custom_call" | custom-call | flops 49999998976 | bytes 20000000 | tf_op jit(solution)/shard_map/front/pallas_call | solution.py:1103
  69.4 25.0 %attention_forward.1 = (bf16[8,6,128,128]{3,2,1,0:T(8,128)(2,1)}, bf16[6,1024,128]{2,1,0:T(8,128)(2,1)}, bf16[8,128,768]{2,1,0:T(8,128)(2,1)}) custom-call(s32[8]{0:T(128)} %lengths_ref.7, s32[1]{0:T(128)} %bitcast.place_ref, bf16[8,6,128,384]{3,2,1,0:T(8,128)(2,1)} %get-tuple-element.53.qkv_ref, f32[6,2,1024]{2,1,0:T(2,128)} %reshape.65.row_ref, ...), custom_call_target="tpu_custom_call" | custom-call | flops 3221225472 | bytes 12582912 | tf_op jit(solution)/shard_map/attention_forward/pallas_call | solution.py:276
  94.3 46.1 %middle.1 = (f32[8,128,768]{2,1,0:T(8,128)}, bf16[8,128,2048]{2,1,0:T(8,128)(2,1)}, bf16[8,128,4096]{2,1,0:T(8,128)(2,1)}, bf16[8,128,768]{2,1,0:T(8,128)(2,1)},...) custom-call(bf16[8,6,128,128]{3,2,1,0:T(8,128)(2,1)} %get-tuple-elem, ...), custom_call_target="tpu_custom_call" | custom-call | flops 49999998976 | bytes 40000000 | tf_op jit(solution)/shard_map/middle/pallas_call | solution.py:1154
  140.5 4.5 %all-to-all-start = ((bf16[8,3,128,128]{3,2,1,0:T(8,128)(2,1)}), bf16[8,3,128,128]{3,2,1,0:T(8,128)(2,1)S(1)}, u32[]{:S(2)}, u32[]{:S(2)}) async-start(bf16[8,3,128,128]{3,2,1,0:T(8,128)(2,1)} %get-tuple-element.62), calls=%async_computation | async-start | bytes 1572864 | tf_op jit(solution)/shard_map/all_to_all | solution.py:1760
  144.9 14.5 %attention_backward.2 = (bf16[8,3,128,384]{3,2,1,0:T(8,128)(2,1)}, f32[3,2,1024]{2,1,0:T(2,128)}, f32[8,128,768]{2,1,0:T(8,128)}) custom-call(s32[8]{0:T(128)} %lengths_ref.7, s32[1]{0:T(128)} %bitcast.place_ref, bf16[8,6,128,384]{3,2,1,0:T(8,128)(2,1)} %get-tuple-element.53.qkv_ref, bf16[8,6,128,128]{3,2,1,0:T(8,128)(2,1)} %get-tuple-element.54.att_ref.out_ref, ...), custom_call_target="tpu_custom_call" | custom-call | flops 4026531840 | bytes 12582912 | tf_op jit(solution)/shard_map/attention_backward/pallas_call | solution.py:329
  159.5 0.0 all-to-all-done.grad_ref
  159.5 0.0 copy-start.3
  159.5 0.9 copy-done.3
  160.4 18.8 %all-to-all-start.2 = ((bf16[8,3,128,384]{3,2,1,0:T(8,128)(2,1)}), bf16[8,3,128,384]{3,2,1,0:T(8,128)(2,1)S(1)}, u32[]{:S(2)}, u32[]{:S(2)}) async-start(bf16[8,3,128,384]{3,2,1,0:T(8,128)(2,1)} %get-tuple-element.65), calls=%async_computation.2 | async-start | bytes 4718592 | tf_op jit(solution)/shard_map/all_to_all | solution.py:1760
  179.2 25.8 %attention_backward.3 = (bf16[8,3,128,384]{3,2,1,0:T(8,128)(2,1)}, f32[3,2,1024]{2,1,0:T(2,128)}, f32[8,128]{1,0:T(8,128)}) custom-call(s32[8]{0:T(128)} %lengths_ref.7, s32[1]{0:T(128)} %bitcast.place_ref, bf16[8,6,128,384]{3,2,1,0:T(8,128)(2,1)} %get-tuple-element.53.qkv_ref, bf16[8,6,128,128]{3,2,1,0:T(8,128)(2,1)} %get-tuple-element.54.att_ref.out_ref, ...), custom_call_target="tpu_custom_call" | custom-call | flops 4026531840 | bytes 12582912 | tf_op jit(solution)/shard_map/attention_backward/pallas_call | solution.py:329
  205.0 3.4 all-to-all-done.2.after.two_ref
  208.4 0.0 copy-start.2
  208.4 1.4 copy-done.2
  209.7 4.4 %all-to-all-start.1 = ((bf16[8,3,128,384]{3,2,1,0:T(8,128)(2,1)}), bf16[8,3,128,384]{3,2,1,0:T(8,128)(2,1)}, u32[]{:S(2)}, u32[]{:S(2)}) async-start(bf16[8,3,128,384]{3,2,1,0:T(8,128)(2,1)} %get-tuple-element.64), calls=%async_computation.1 | async-start | bytes 4718592 | tf_op jit(solution)/shard_map/all_to_all | solution.py:1760
  214.1 0.2 iota_compare_fusion
  214.3 0.8 convert_convert_fusion.bias_hot_ref
  215.1 0.0 copy-done.4
  215.1 0.0 copy-done.5
  215.1 0.6 pad_maximum_fusion.bias_ref
  215.7 25.1 %early_gradients.1 = (bf16[4,4,960,128]{3,2,1,0:T(8,128)(2,1)}, bf16[4,4,384,128]{3,2,1,0:T(8,128)(2,1)}) custom-call(bf16[8,128,2048]{2,1,0:T(8,128)(2,1)} %get-tuple-element.73.act_ref, bf16[8,128,768]{2,1,0:T(8,128)(2,1)} %get-tuple-element.57.cot_ref, bf16[8,128,768]{2,1,0:T(8,128)(2,1)} %get-tuple-element.74.normed_ref, ...), custom_call_target="tpu_custom_call" | custom-call | flops 11000000512 | bytes 30000000 | tf_op jit(solution)/shard_map/early_gradients/pallas_call | solution.py:1370
  240.8 2.8 all-to-all-done.1.one_ref
  243.6 93.5 %back.1 = (f32[288,768]{1,0:T(8,128)}, f32[96,576]{1,0:T(8,128)}, f32[96,1024]{1,0:T(8,128)}, f32[192,256]{1,0:T(8,128)}, f32[96,192]{1,0:T(8,128)}) custom-call(bf16[8,3,128,384]{3,2,1,0:T(8,128)(2,1)} %all-to-all-done.1.one_ref, bf16[8,3,128,384]{3,2,1,0:T(8,128)(2,1)} %copy-done.2, f32[8,128,768]{2,1,0:T(8,128)} %get-tuple-element.56.hidden_ref, ...), custom_call_target="tpu_custom_call" | custom-call | flops 99999997952 | bytes 20000000 | tf_op jit(solution)/shard_map/back/pallas_call | solution.py:1221
  337.1 2.7 finish.1
  339.8 0.0 copy-done.1
  (4 shorter events, 0.0 us)
Async XLA Ops:
  0.6 2.1 copy-start
  140.5 19.0 %all-to-all-start = ((bf16[8,3,128,128]{3,2,1,0:T(8,128)(2,1)}), bf16[8,3,128,128]{3,2,1,0:T(8,128)(2,1)S(1)}, u32[]{:S(2)}, u32[]{:S(2)}) async-start(bf16[8,3,128,128]{3,2,1,0:T(8,128)(2,1)} %get-tuple-element.62), calls=%async_computation | async-start | bytes 1572864 | tf_op jit(solution)/shard_map/all_to_all | solution.py:1760
  159.5 0.9 copy-start.3
  160.4 48.0 %all-to-all-start.2 = ((bf16[8,3,128,384]{3,2,1,0:T(8,128)(2,1)}), bf16[8,3,128,384]{3,2,1,0:T(8,128)(2,1)S(1)}, u32[]{:S(2)}, u32[]{:S(2)}) async-start(bf16[8,3,128,384]{3,2,1,0:T(8,128)(2,1)} %get-tuple-element.65), calls=%async_computation.2 | async-start | bytes 4718592 | tf_op jit(solution)/shard_map/all_to_all | solution.py:1760
  208.4 1.4 copy-start.2
  208.4 6.7 %copy-start.4 = (f32[3,2,1024]{2,1,0:T(2,128)S(1)}, f32[3,2,1024]{2,1,0:T(2,128)}, u32[]{:S(2)}) copy-start(f32[3,2,1024]{2,1,0:T(2,128)} %get-tuple-element.63.layer_ref.after) | copy-start | bytes 73732
  208.4 6.7 %copy-start.5 = (f32[3,2,1024]{2,1,0:T(2,128)S(1)}, f32[3,2,1024]{2,1,0:T(2,128)}, u32[]{:S(2)}) copy-start(f32[3,2,1024]{2,1,0:T(2,128)} %get-tuple-element.71) | copy-start | bytes 73732
  209.7 33.8 %all-to-all-start.1 = ((bf16[8,3,128,384]{3,2,1,0:T(8,128)(2,1)}), bf16[8,3,128,384]{3,2,1,0:T(8,128)(2,1)}, u32[]{:S(2)}, u32[]{:S(2)}) async-start(bf16[8,3,128,384]{3,2,1,0:T(8,128)(2,1)} %get-tuple-element.64), calls=%async_computation.1 | async-start | bytes 4718592 | tf_op jit(solution)/shard_map/all_to_all | solution.py:1760
  243.6 96.2 %copy-start.1 = (f32[32,12]{0,1:T(8,128)S(1)}, f32[32,12]{0,1:T(8,128)}, u32[]{:S(2)}) copy-start(f32[32,12]{0,1:T(8,128)} %param.20) | copy-start | bytes 4612

commit v7 on v6

--- a/solution.py
+++ b/solution.py
@@ -589,7 +589,7 @@
     if devices == 8:
 
         def send(at, unused):
-            item = step * PAIRS + at
+            item = step * PAIRS + lax.rem(at + me, PAIRS)
             other, slot = lax.rem(item, 8), item // 8
 
             @pl.when(other != me)

time: 338 us -> 344 us (1.018)
  the two profiles are of different devices: /device:TPU:0 before, /device:TPU:9 now
where the time goes in v7:
time: 344 us; the launch traced here: 338 us
  Pallas kernels  299 us (87%)
  starting transfers between devices  29.7 us (9%)
  local copies, waits for them, and re-layouts  5.01 us (1%)
    pallas_call x1, Pallas kernels, call_back(): pl.pallas_call(functools.partial(back_kernel, (local_tokens, window, devi...  90.5 us
    pallas_call x1, Pallas kernels, call_front(): pl.pallas_call(functools.partial(front_kernel, (local_tokens, window, dev...  65.1 us
    pallas_call x1, Pallas kernels, call_mid(): pl.pallas_call(functools.partial(mid_kernel, (local_tokens, devices, sequ...  45.7 us
    pallas_call x2, Pallas kernels, attention_backward(): pl.pallas_call(functools.partial(bwd_kernel, blocks, first, moves), grid_...  43.2 us
    all_to_all x3, starting transfers between devices, exchange(): return lax.all_to_all(items, 'seq', split_axis=0, concat_axis=0, tiled=True)  29.7 us
    pallas_call x1, Pallas kernels, attention_forward(): pl.pallas_call(functools.partial(fwd_kernel, blocks), grid_spec=spec, out...  26.9 us
    pallas_call x1, Pallas kernels, call_early(): pl.pallas_call(early_kernel, grid=(8,), in_specs=[pl.BlockSpec((sequences...  25.1 us
  transfers between devices with their start and end apart: 3, of which 1 were waited for; matrix products, arithmetic and copies ran while one was open for 0% of the time, Pallas kernels for 20%

profile of v7, /device:TPU:9, one launch (start us, length us, event | category | flops | bytes accessed | tf_op | source)
XLA Modules:
  0.0 338.5 jit_solution(2623281482820014292)
XLA Ops:
  0.6 0.0 copy-start
  0.7 0.7 broadcast_in_dim.15
  1.4 0.7 broadcast_in_dim.14
  2.1 0.7 broadcast_in_dim.6
  2.8 0.0 copy-done
  2.8 0.4 convolution_bitcast_fusion
  3.2 0.7 reshape.65.row_ref
  3.9 1.4 pad_maximum_fusion.1.vectors_ref
  5.2 65.1 %front.1 = (f32[8,128,768]{2,1,0:T(8,128)}, bf16[8,128,768]{2,1,0:T(8,128)(2,1)}, bf16[8,384,768]{2,1,0:T(8,128)(2,1)}, bf16[8,128,384]{2,1,0:T(8,128)(2,1)}, f3...) custom-call(s32[8]{0:T(128)} %lengths_ref.7, s32[8,256]{1,0:T(8,128)} %ids_ref.1, ...), custom_call_target="tpu_custom_call" | custom-call | flops 49999998976 | bytes 20000000 | tf_op jit(solution)/shard_map/front/pallas_call | solution.py:1103
  70.3 26.9 %attention_forward.1 = (bf16[8,6,128,128]{3,2,1,0:T(8,128)(2,1)}, bf16[6,1024,128]{2,1,0:T(8,128)(2,1)}, bf16[8,128,768]{2,1,0:T(8,128)(2,1)}) custom-call(s32[8]{0:T(128)} %lengths_ref.7, s32[1]{0:T(128)} %bitcast.place_ref, bf16[8,6,128,384]{3,2,1,0:T(8,128)(2,1)} %get-tuple-element.53.qkv_ref, f32[6,2,1024]{2,1,0:T(2,128)} %reshape.65.row_ref, ...), custom_call_target="tpu_custom_call" | custom-call | flops 3221225472 | bytes 12582912 | tf_op jit(solution)/shard_map/attention_forward/pallas_call | solution.py:276
  97.2 45.7 %middle.1 = (f32[8,128,768]{2,1,0:T(8,128)}, bf16[8,128,2048]{2,1,0:T(8,128)(2,1)}, bf16[8,128,4096]{2,1,0:T(8,128)(2,1)}, bf16[8,128,768]{2,1,0:T(8,128)(2,1)},...) custom-call(bf16[8,6,128,128]{3,2,1,0:T(8,128)(2,1)} %get-tuple-elem, ...), custom_call_target="tpu_custom_call" | custom-call | flops 49999998976 | bytes 40000000 | tf_op jit(solution)/shard_map/middle/pallas_call | solution.py:1154
  142.9 3.5 %all-to-all-start = ((bf16[8,3,128,128]{3,2,1,0:T(8,128)(2,1)}), bf16[8,3,128,128]{3,2,1,0:T(8,128)(2,1)S(1)}, u32[]{:S(2)}, u32[]{:S(2)}) async-start(bf16[8,3,128,128]{3,2,1,0:T(8,128)(2,1)} %get-tuple-element.62), calls=%async_computation | async-start | bytes 1572864 | tf_op jit(solution)/shard_map/all_to_all | solution.py:1760
  146.4 17.5 %attention_backward.2 = (bf16[8,3,128,384]{3,2,1,0:T(8,128)(2,1)}, f32[3,2,1024]{2,1,0:T(2,128)}, f32[8,128,768]{2,1,0:T(8,128)}) custom-call(s32[8]{0:T(128)} %lengths_ref.7, s32[1]{0:T(128)} %bitcast.place_ref, bf16[8,6,128,384]{3,2,1,0:T(8,128)(2,1)} %get-tuple-element.53.qkv_ref, bf16[8,6,128,128]{3,2,1,0:T(8,128)(2,1)} %get-tuple-element.54.att_ref.out_ref, ...), custom_call_target="tpu_custom_call" | custom-call | flops 4026531840 | bytes 12582912 | tf_op jit(solution)/shard_map/attention_backward/pallas_call | solution.py:329
  163.9 0.0 all-to-all-done.grad_ref
  163.9 0.0 copy-start.3
  163.9 0.9 copy-done.3
  164.8 18.8 %all-to-all-start.2 = ((bf16[8,3,128,384]{3,2,1,0:T(8,128)(2,1)}), bf16[8,3,128,384]{3,2,1,0:T(8,128)(2,1)S(1)}, u32[]{:S(2)}, u32[]{:S(2)}) async-start(bf16[8,3,128,384]{3,2,1,0:T(8,128)(2,1)} %get-tuple-element.65), calls=%async_computation.2 | async-start | bytes 4718592 | tf_op jit(solution)/shard_map/all_to_all | solution.py:1760
  183.6 25.8 %attention_backward.3 = (bf16[8,3,128,384]{3,2,1,0:T(8,128)(2,1)}, f32[3,2,1024]{2,1,0:T(2,128)}, f32[8,128]{1,0:T(8,128)}) custom-call(s32[8]{0:T(128)} %lengths_ref.7, s32[1]{0:T(128)} %bitcast.place_ref, bf16[8,6,128,384]{3,2,1,0:T(8,128)(2,1)} %get-tuple-element.53.qkv_ref, bf16[8,6,128,128]{3,2,1,0:T(8,128)(2,1)} %get-tuple-element.54.att_ref.out_ref, ...), custom_call_target="tpu_custom_call" | custom-call | flops 4026531840 | bytes 12582912 | tf_op jit(solution)/shard_map/attention_backward/pallas_call | solution.py:329
  209.3 0.2 all-to-all-done.2.after.two_ref
  209.6 1.4 copy-done.2
  211.0 7.4 %all-to-all-start.1 = ((bf16[8,3,128,384]{3,2,1,0:T(8,128)(2,1)}), bf16[8,3,128,384]{3,2,1,0:T(8,128)(2,1)}, u32[]{:S(2)}, u32[]{:S(2)}) async-start(bf16[8,3,128,384]{3,2,1,0:T(8,128)(2,1)} %get-tuple-element.64), calls=%async_computation.1 | async-start | bytes 4718592 | tf_op jit(solution)/shard_map/all_to_all | solution.py:1760
  218.3 0.2 iota_compare_fusion
  218.5 0.8 convert_convert_fusion.bias_hot_ref
  219.3 0.0 copy-done.4
  219.3 0.0 copy-done.5
  219.3 0.6 pad_maximum_fusion.bias_ref
  220.0 25.1 %early_gradients.1 = (bf16[4,4,960,128]{3,2,1,0:T(8,128)(2,1)}, bf16[4,4,384,128]{3,2,1,0:T(8,128)(2,1)}) custom-call(bf16[8,128,2048]{2,1,0:T(8,128)(2,1)} %get-tuple-element.73.act_ref, bf16[8,128,768]{2,1,0:T(8,128)(2,1)} %get-tuple-element.57.cot_ref, bf16[8,128,768]{2,1,0:T(8,128)(2,1)} %get-tuple-element.74.normed_ref, ...), custom_call_target="tpu_custom_call" | custom-call | flops 11000000512 | bytes 30000000 | tf_op jit(solution)/shard_map/early_gradients/pallas_call | solution.py:1370
  245.0 0.0 all-to-all-done.1.one_ref
  245.0 0.0 copy-start.1
  245.0 90.5 %back.1 = (f32[288,768]{1,0:T(8,128)}, f32[96,576]{1,0:T(8,128)}, f32[96,1024]{1,0:T(8,128)}, f32[192,256]{1,0:T(8,128)}, f32[96,192]{1,0:T(8,128)}) custom-call(bf16[8,3,128,384]{3,2,1,0:T(8,128)(2,1)} %all-to-all-done.1.one_ref, bf16[8,3,128,384]{3,2,1,0:T(8,128)(2,1)} %copy-done.2, f32[8,128,768]{2,1,0:T(8,128)} %get-tuple-element.56.hidden_ref, ...), custom_call_target="tpu_custom_call" | custom-call | flops 99999997952 | bytes 20000000 | tf_op jit(solution)/shard_map/back/pallas_call | solution.py:1221
  335.5 2.7 finish.1
  338.3 0.0 copy-done.1
  (4 shorter events, 0.0 us)
Async XLA Ops:
  0.6 2.1 copy-start
  142.9 21.0 %all-to-all-start = ((bf16[8,3,128,128]{3,2,1,0:T(8,128)(2,1)}), bf16[8,3,128,128]{3,2,1,0:T(8,128)(2,1)S(1)}, u32[]{:S(2)}, u32[]{:S(2)}) async-start(bf16[8,3,128,128]{3,2,1,0:T(8,128)(2,1)} %get-tuple-element.62), calls=%async_computation | async-start | bytes 1572864 | tf_op jit(solution)/shard_map/all_to_all | solution.py:1760
  163.9 0.9 copy-start.3
  164.8 44.8 %all-to-all-start.2 = ((bf16[8,3,128,384]{3,2,1,0:T(8,128)(2,1)}), bf16[8,3,128,384]{3,2,1,0:T(8,128)(2,1)S(1)}, u32[]{:S(2)}, u32[]{:S(2)}) async-start(bf16[8,3,128,384]{3,2,1,0:T(8,128)(2,1)} %get-tuple-element.65), calls=%async_computation.2 | async-start | bytes 4718592 | tf_op jit(solution)/shard_map/all_to_all | solution.py:1760
  209.6 1.4 copy-start.2
  209.6 9.7 %copy-start.4 = (f32[3,2,1024]{2,1,0:T(2,128)S(1)}, f32[3,2,1024]{2,1,0:T(2,128)}, u32[]{:S(2)}) copy-start(f32[3,2,1024]{2,1,0:T(2,128)} %get-tuple-element.63.layer_ref.after) | copy-start | bytes 73732
  209.6 9.7 %copy-start.5 = (f32[3,2,1024]{2,1,0:T(2,128)S(1)}, f32[3,2,1024]{2,1,0:T(2,128)}, u32[]{:S(2)}) copy-start(f32[3,2,1024]{2,1,0:T(2,128)} %get-tuple-element.71) | copy-start | bytes 73732
  211.0 34.1 %all-to-all-start.1 = ((bf16[8,3,128,384]{3,2,1,0:T(8,128)(2,1)}), bf16[8,3,128,384]{3,2,1,0:T(8,128)(2,1)}, u32[]{:S(2)}, u32[]{:S(2)}) async-start(bf16[8,3,128,384]{3,2,1,0:T(8,128)(2,1)} %get-tuple-element.64), calls=%async_computation.1 | async-start | bytes 4718592 | tf_op jit(solution)/shard_map/all_to_all | solution.py:1760
  245.0 93.3 %copy-start.1 = (f32[32,12]{0,1:T(8,128)S(1)}, f32[32,12]{0,1:T(8,128)}, u32[]{:S(2)}) copy-start(f32[32,12]{0,1:T(8,128)} %param.20) | copy-start | bytes 4612
